TPU v7x, 32 devices: a whole 2x2x4 slice. The times are simulated.
32 devices in a mesh: dp: 8 (over z, x), seq: 4 (over y, core).
Axes of the slice: x: 2, y: 2, z: 4, core: 2. Of those that a mesh axis runs over, the one named last changes fastest.
Arguments:
- inputs: bfloat16 [64, 512, 768], P('dp', 'seq'), may hold values from -6 to 6
- lengths: int32 [64], P('dp'), may hold values from 1 to 512, as said below
- query_key_value_weight: bfloat16 [768, 2304], P(('dp', 'seq')), may hold values from -0.21875 to 0.21875
- query_bias: bfloat16 [768], P(('dp', 'seq')), may hold values from -3 to 3
- value_bias: bfloat16 [768], P(('dp', 'seq')), may hold values from -0.29882812 to 0.29882812
- output_weight: bfloat16 [768, 768], P(('dp', 'seq')), may hold values from -1.75 to 1.75
- output_bias: bfloat16 [768], P(('dp', 'seq')), may hold values from -1.1953125 to 1.1953125
- norm1_gain: bfloat16 [768], P(('dp', 'seq')), may hold values from 0.5 to 1.5
- norm1_shift: bfloat16 [768], P(('dp', 'seq')), may hold values from -1.1953125 to 1.1953125
- in_weight: bfloat16 [768, 3072], P(('dp', 'seq')), may hold values from -0.21875 to 0.21875
- in_bias: bfloat16 [3072], P(('dp', 'seq')), may hold values from -1.1953125 to 1.1953125
- down_weight: bfloat16 [3072, 768], P(('dp', 'seq')), may hold values from -0.109375 to 0.109375
- down_bias: bfloat16 [768], P(('dp', 'seq')), may hold values from -1.1953125 to 1.1953125
- norm2_gain: bfloat16 [768], P(('dp', 'seq')), may hold values from 0.5 to 1.5
- norm2_shift: bfloat16 [768], P(('dp', 'seq')), may hold values from -1.1953125 to 1.1953125
- cotangent: bfloat16 [64, 512, 768], P('dp', 'seq'), may hold values from -6 to 6
Outputs:
- outputs: bfloat16 [64, 512, 768], P('dp', 'seq')
- grad_inputs: bfloat16 [64, 512, 768], P('dp', 'seq')
- grad_qkv_weight: float32 [768, 2304], P(('dp', 'seq'))
- grad_query_bias: float32 [768], P(('dp', 'seq'))
- grad_value_bias: float32 [768], P(('dp', 'seq'))
- grad_out_weight: float32 [768, 768], P(('dp', 'seq'))
- grad_out_bias: float32 [768], P(('dp', 'seq'))
- grad_norm1_gain: float32 [768], P(('dp', 'seq'))
- grad_norm1_shift: float32 [768], P(('dp', 'seq'))
- grad_in_weight: float32 [768, 3072], P(('dp', 'seq'))
- grad_in_bias: float32 [3072], P(('dp', 'seq'))
- grad_down_weight: float32 [3072, 768], P(('dp', 'seq'))
- grad_down_bias: float32 [768], P(('dp', 'seq'))
- grad_norm2_gain: float32 [768], P(('dp', 'seq'))
- grad_norm2_shift: float32 [768], P(('dp', 'seq'))
Inputs may be any that keep to these rules, and one draw needn't show every extreme that they name: `lengths`: in each aligned block of 8 sequences, one drawn from the seed has length 512.
All inputs are finite; a program needn't handle non-finite values.
Results may differ from a plain program's by a relative error of at most 0.017.
Values may be sent and summed in bfloat16 or wider, within the bound.
No kernel may reach another device: no remote copies, remote signals or barrier semaphores. Data moves between devices by JAX's collectives and lax.ppermute only.
A program may use at most 192 MiB of HBM per device.

v0:
```python
import jax
import jax.numpy as jnp
from jax import lax
from jax.sharding import PartitionSpec as P

HD = 64


def layer_norm(value, gain, shift):
    center = jnp.mean(value, -1, keepdims=True)
    centered = value - center
    spread = jnp.mean(centered * centered, -1, keepdims=True)
    return centered * lax.rsqrt(spread + 1e-12) * gain + shift


def gelu_exact(value):
    return jax.nn.gelu(value, approximate=False)


def over_rows(left, right):
    return lax.dot_general(
        left, right, (((0,), (0,)), ((), ())), preferred_element_type=jnp.float32
    )


def times_transposed(left, right):
    return lax.dot_general(
        left, right, (((1,), (1,)), ((), ())), preferred_element_type=jnp.float32
    )


def split_pairs(block):
    groups, count, width = block.shape
    return (
        block.reshape(groups, count, width // 128, 128)
        .transpose(0, 2, 1, 3)
        .reshape(-1, count, 128)
    )


def join_pairs(block, groups):
    items, count, lanes = block.shape
    pairs = items // groups
    return (
        block.reshape(groups, pairs, count, lanes)
        .transpose(0, 2, 1, 3)
        .reshape(groups, count, pairs * lanes)
    )


def head_view(block):
    return block.reshape(block.shape[0], 128 // HD, HD)


def scores_of(query_blk, key_blk, limit):
    scores = (
        jnp.einsum(
            "qhd,khd->hqk",
            head_view(query_blk),
            head_view(key_blk),
            preferred_element_type=jnp.float32,
        )
        * 0.125
    )
    valid = jnp.arange(key_blk.shape[0], dtype=jnp.int32) < limit
    return jnp.where(valid[None, None, :], scores, -1e30)


def attend_forward(item):
    query_blk, key_blk, value_blk, limit = item
    scores = scores_of(query_blk, key_blk, limit)
    highest_precision = jnp.max(scores, -1, keepdims=True)
    raised = jnp.exp(scores - highest_precision)
    total = jnp.sum(raised, -1, keepdims=True)
    probs = (raised / total).astype(jnp.bfloat16)
    mixed_heads = jnp.einsum(
        "hqk,khd->qhd", probs, head_view(value_blk), preferred_element_type=jnp.float32
    )
    return (mixed_heads.reshape(-1, 128), (highest_precision + jnp.log(total))[..., 0])


def attend_backward(item):
    query_blk, key_blk, value_blk, limit, logsum, grad_blk = item
    scores = scores_of(query_blk, key_blk, limit)
    probs = jnp.exp(scores - logsum[..., None])
    grad_heads = head_view(grad_blk)
    grad_probs = jnp.einsum(
        "qhd,khd->hqk", grad_heads, head_view(value_blk), preferred_element_type=jnp.float32
    )
    inner = jnp.sum(probs * grad_probs, -1, keepdims=True)
    grad_scores = (probs * (grad_probs - inner)).astype(jnp.bfloat16)
    grad_values = jnp.einsum(
        "hqk,qhd->khd", probs.astype(jnp.bfloat16), grad_heads, preferred_element_type=jnp.float32
    )
    grad_queries = (
        jnp.einsum(
            "hqk,khd->qhd", grad_scores, head_view(key_blk), preferred_element_type=jnp.float32
        )
        * 0.125
    )
    grad_keys = (
        jnp.einsum(
            "hqk,qhd->khd", grad_scores, head_view(query_blk), preferred_element_type=jnp.float32
        )
        * 0.125
    )
    return (grad_queries.reshape(-1, 128), grad_keys.reshape(-1, 128), grad_values.reshape(-1, 128))


def on_device(
    inputs,
    lengths,
    query_key_value_weight,
    query_bias,
    value_bias,
    output_weight,
    output_bias,
    norm1_gain,
    norm1_shift,
    in_weight,
    in_bias,
    down_weight,
    down_bias,
    norm2_gain,
    norm2_shift,
    cotangent,
):
    groups, local_len, width = inputs.shape
    rows = groups * local_len
    (
        wide_qkv,
        full_query_bias,
        full_value_bias,
        wide_out,
        full_out_bias,
        gain_one,
        shift_one,
        wide_in,
        full_in_bias,
        wide_down,
        full_down_bias,
        gain_two,
        shift_two,
    ) = (
        lax.all_gather(query_key_value_weight, ("dp", "seq"), axis=0, tiled=True),
        lax.all_gather(query_bias, ("dp", "seq"), axis=0, tiled=True),
        lax.all_gather(value_bias, ("dp", "seq"), axis=0, tiled=True),
        lax.all_gather(output_weight, ("dp", "seq"), axis=0, tiled=True),
        lax.all_gather(output_bias, ("dp", "seq"), axis=0, tiled=True),
        lax.all_gather(norm1_gain, ("dp", "seq"), axis=0, tiled=True),
        lax.all_gather(norm1_shift, ("dp", "seq"), axis=0, tiled=True),
        lax.all_gather(in_weight, ("dp", "seq"), axis=0, tiled=True),
        lax.all_gather(in_bias, ("dp", "seq"), axis=0, tiled=True),
        lax.all_gather(down_weight, ("dp", "seq"), axis=0, tiled=True),
        lax.all_gather(down_bias, ("dp", "seq"), axis=0, tiled=True),
        lax.all_gather(norm2_gain, ("dp", "seq"), axis=0, tiled=True),
        lax.all_gather(norm2_shift, ("dp", "seq"), axis=0, tiled=True),
    )
    flat = inputs.reshape(rows, width)
    bias_vector = jnp.concatenate(
        [
            full_query_bias.astype(jnp.float32),
            jnp.zeros((width,), jnp.float32),
            full_value_bias.astype(jnp.float32),
        ]
    )
    packed_tokens = (
        jnp.dot(flat, wide_qkv, preferred_element_type=jnp.float32) + bias_vector
    ).astype(jnp.bfloat16)
    queries = packed_tokens[:, :width].reshape(groups, local_len, width)
    keys_local = packed_tokens[:, width : 2 * width].reshape(groups, local_len, width)
    values_local = packed_tokens[:, 2 * width :].reshape(groups, local_len, width)
    keys, values = (
        lax.all_gather(keys_local, "seq", axis=1, tiled=True),
        lax.all_gather(values_local, "seq", axis=1, tiled=True),
    )
    pairs = width // 128
    limits = jnp.repeat(lengths, pairs, total_repeat_length=groups * pairs)
    query_items = split_pairs(queries)
    key_items = split_pairs(keys)
    value_items = split_pairs(values)
    mixed_items, logsum = lax.map(attend_forward, (query_items, key_items, value_items, limits))
    mixed_heads = join_pairs(mixed_items, groups).reshape(rows, width).astype(jnp.bfloat16)
    attention_branch = jnp.dot(
        mixed_heads, wide_out, preferred_element_type=jnp.float32
    ) + full_out_bias.astype(jnp.float32)
    first, norm_one_pull = jax.vjp(
        layer_norm,
        flat.astype(jnp.float32) + attention_branch,
        gain_one.astype(jnp.float32),
        shift_one.astype(jnp.float32),
    )
    first_low = first.astype(jnp.bfloat16)
    hidden = jnp.dot(first_low, wide_in, preferred_element_type=jnp.float32) + full_in_bias.astype(
        jnp.float32
    )
    active, gelu_pull = jax.vjp(gelu_exact, hidden)
    active_low = active.astype(jnp.bfloat16)
    branch_two = jnp.dot(
        active_low, wide_down, preferred_element_type=jnp.float32
    ) + full_down_bias.astype(jnp.float32)
    result, norm_two_pull = jax.vjp(
        layer_norm,
        first_low.astype(jnp.float32) + branch_two,
        gain_two.astype(jnp.float32),
        shift_two.astype(jnp.float32),
    )
    outputs = result.astype(jnp.bfloat16).reshape(groups, local_len, width)
    back_qkv, back_out, back_in, back_down = (
        lax.all_gather(query_key_value_weight, ("dp", "seq"), axis=0, tiled=True),
        lax.all_gather(output_weight, ("dp", "seq"), axis=0, tiled=True),
        lax.all_gather(in_weight, ("dp", "seq"), axis=0, tiled=True),
        lax.all_gather(down_weight, ("dp", "seq"), axis=0, tiled=True),
    )
    grad_second, grad_gain_two, grad_shift_two = norm_two_pull(
        cotangent.reshape(rows, width).astype(jnp.float32)
    )
    grad_branch_two = grad_second.astype(jnp.bfloat16)
    grad_down = over_rows(active_low, grad_branch_two)
    grad_down_bias = jnp.sum(grad_branch_two.astype(jnp.float32), 0)
    (grad_hidden,) = gelu_pull(times_transposed(grad_branch_two, back_down))
    grad_hidden_low = grad_hidden.astype(jnp.bfloat16)
    grad_in = over_rows(first_low, grad_hidden_low)
    grad_in_bias = jnp.sum(grad_hidden_low.astype(jnp.float32), 0)
    grad_first = times_transposed(grad_hidden_low, back_in) + grad_second
    grad_residual, grad_gain_one, grad_shift_one = norm_one_pull(grad_first)
    grad_branch_one = grad_residual.astype(jnp.bfloat16)
    grad_out = over_rows(mixed_heads, grad_branch_one)
    grad_out_bias = jnp.sum(grad_branch_one.astype(jnp.float32), 0)
    grad_mixed = times_transposed(grad_branch_one, back_out).astype(jnp.bfloat16)
    grad_mixed_seq = grad_mixed.reshape(groups, local_len, width)
    grad_items = split_pairs(grad_mixed_seq)
    query_terms, key_terms, value_terms = lax.map(
        attend_backward, (query_items, key_items, value_items, limits, logsum, grad_items)
    )
    grad_queries = join_pairs(query_terms, groups)
    grad_keys, grad_values = (
        lax.psum_scatter(
            join_pairs(key_terms, groups).astype(jnp.bfloat16),
            "seq",
            scatter_dimension=1,
            tiled=True,
        ).astype(jnp.float32),
        lax.psum_scatter(
            join_pairs(value_terms, groups).astype(jnp.bfloat16),
            "seq",
            scatter_dimension=1,
            tiled=True,
        ).astype(jnp.float32),
    )
    grad_packed = jnp.concatenate([grad_queries, grad_keys, grad_values], -1).reshape(
        rows, 3 * width
    )
    grad_packed = grad_packed.astype(jnp.bfloat16)
    grad_qkv = over_rows(flat, grad_packed)
    column_sums = jnp.sum(grad_packed.astype(jnp.float32), 0)
    grad_inputs = times_transposed(grad_packed, back_qkv) + grad_residual
    (
        grad_qkv_weight,
        grad_query_bias,
        grad_value_bias,
        grad_out_weight,
        grad_out_shift,
        grad_norm1_gain,
        grad_norm1_shift,
        grad_in_weight,
        grad_in_shift,
        grad_down_weight,
        grad_down_shift,
        grad_norm2_gain,
        grad_norm2_shift,
    ) = (
        lax.psum_scatter(grad_qkv, ("dp", "seq"), scatter_dimension=0, tiled=True),
        lax.psum_scatter(column_sums[:width], ("dp", "seq"), scatter_dimension=0, tiled=True),
        lax.psum_scatter(column_sums[2 * width :], ("dp", "seq"), scatter_dimension=0, tiled=True),
        lax.psum_scatter(grad_out, ("dp", "seq"), scatter_dimension=0, tiled=True),
        lax.psum_scatter(grad_out_bias, ("dp", "seq"), scatter_dimension=0, tiled=True),
        lax.psum_scatter(grad_gain_one, ("dp", "seq"), scatter_dimension=0, tiled=True),
        lax.psum_scatter(grad_shift_one, ("dp", "seq"), scatter_dimension=0, tiled=True),
        lax.psum_scatter(grad_in, ("dp", "seq"), scatter_dimension=0, tiled=True),
        lax.psum_scatter(grad_in_bias, ("dp", "seq"), scatter_dimension=0, tiled=True),
        lax.psum_scatter(grad_down, ("dp", "seq"), scatter_dimension=0, tiled=True),
        lax.psum_scatter(grad_down_bias, ("dp", "seq"), scatter_dimension=0, tiled=True),
        lax.psum_scatter(grad_gain_two, ("dp", "seq"), scatter_dimension=0, tiled=True),
        lax.psum_scatter(grad_shift_two, ("dp", "seq"), scatter_dimension=0, tiled=True),
    )
    return (
        outputs,
        grad_inputs.astype(jnp.bfloat16).reshape(groups, local_len, width),
        grad_qkv_weight,
        grad_query_bias,
        grad_value_bias,
        grad_out_weight,
        grad_out_shift,
        grad_norm1_gain,
        grad_norm1_shift,
        grad_in_weight,
        grad_in_shift,
        grad_down_weight,
        grad_down_shift,
        grad_norm2_gain,
        grad_norm2_shift,
    )


def solution(mesh):
    placed = (
        P("dp", "seq", None),
        P("dp"),
        P(("dp", "seq"), None),
        P(("dp", "seq")),
        P(("dp", "seq")),
        P(("dp", "seq"), None),
        P(("dp", "seq")),
        P(("dp", "seq")),
        P(("dp", "seq")),
        P(("dp", "seq"), None),
        P(("dp", "seq")),
        P(("dp", "seq"), None),
        P(("dp", "seq")),
        P(("dp", "seq")),
        P(("dp", "seq")),
        P("dp", "seq", None),
    )
    return jax.shard_map(
        on_device,
        mesh=mesh,
        in_specs=placed,
        out_specs=(
            P("dp", "seq", None),
            P("dp", "seq", None),
            P(("dp", "seq"), None),
            P(("dp", "seq")),
            P(("dp", "seq")),
            P(("dp", "seq"), None),
            P(("dp", "seq")),
            P(("dp", "seq")),
            P(("dp", "seq")),
            P(("dp", "seq"), None),
            P(("dp", "seq")),
            P(("dp", "seq"), None),
            P(("dp", "seq")),
            P(("dp", "seq")),
            P(("dp", "seq")),
        ),
        check_vma=False,
    )
```

profile of v0, /device:TPU:0, one launch (start us, length us, event | category | flops | bytes accessed | tf_op | source)
XLA Modules:
  0.0 1546.9 jit_solution(3724551556821933747)
XLA Ops:
  15.5 42.4 %all-reduce.19 = (bf16[768]{0:T(1024)(128)(2,1)S(1)}, bf16[768]{0:T(1024)(128)(2,1)S(1)}, bf16[768]{0:T(1024)(128)(2,1)S(1)}, bf16[768]{0:T(1024)(128)(2,1)S(1)}...) all-reduce(bf16[768]{0:T(1024)(128)(2,1)S(1)} %dynamic-update-slice, ...), channel_id=1, replica_groups=mesh['dp'=8,'seq'=4] {'dp','seq'}, use_global_device_ids=true, to_apply=%add.2 | all-reduce | flops 9216 | bytes 36864
  58.0 15.9 %all-gather.7.cloned.1.call-done = bf16[768,2304]{1,0:T(8,128)(2,1)} async-done(((bf16[24,2304]{1,0:T(8,128)(2,1)}), bf16[768,2304]{1,0:T(8,128)(2,1)}) %all-gather.7.cloned.1.call-update) | async-done | bytes 3538960 | tf_op jit(solution)/shard_map/all_gather | solution.py:145
  98.2 32.2 %all-gather.9.cloned.1.call-done = bf16[8,512,768]{1,2,0:T(8,128)(2,1)} async-done(((bf16[8,128,768]{1,2,0:T(8,128)(2,1)}), bf16[8,512,768]{1,2,0:T(8,128)(2,1)}) %all-gather.9.cloned.1.call-update) | async-done | bytes 6291472 | tf_op jit(solution)/shard_map/all_gather | solution.py:175
  130.5 48.8 %all-gather.11.cloned.1.call-done = bf16[8,512,768]{1,2,0:T(8,128)(2,1)} async-done(((bf16[8,128,768]{1,2,0:T(8,128)(2,1)}), bf16[8,512,768]{1,2,0:T(8,128)(2,1)}) %all-gather.11.cloned.1.call-update) | async-done | bytes 6291472 | tf_op jit(solution)/shard_map/all_gather | solution.py:174
  179.6 217.4 %while.27 = (s32[]{:T(128)}, bf16[48,128,128]{1,2,0:T(8,128)(2,1)S(1)}, f32[48,2,128]{2,1,0:T(2,128)}, bf16[48,512,128]{1,2,0:T(8,128)(2,1)}, s32[48]{0:T(128)S(...) while((s32[]{:T(128)}, bf16[48,128,128]{1,2,0:T(8,128)(2,1)S(1)}, ...), condition=%wide.region_3.4_spmd, body=%wide.region_0.3_spmd.sunk | while | flops 34603264 | bytes 2565245 | solution.py:182
  403.7 35.8 %multiply_convert_fusion.1 = (bf16[1024,3072]{1,0:T(8,128)(2,1)}, f32[1024,3072]{1,0:T(8,128)}, f32[1024,3072]{1,0:T(8,128)}) fusion(f32[3072]{0:T(1024)S(1)} %convert_element_type.142, bf16[768,3072]{1,0:T(8,128)(2,1)} %all-gather.15.cloned.1.call-done, f32[1024,768]{1,0:T(8,128)S(1)} %get-tuple-element.308, f32[768]{0:T(1024)S(1)} %convert_element_type.139, ...), kind=kOutput, calls=%fused_computation.36 | convolution fusion | flops 5043388416 | bytes 39348224 | tf_op jit(solution)/shard_map/dot_general | solution.py:194
  439.4 9.0 fusion.34
  455.2 18.2 %convert_reduce_fusion = (f32[3072]{0:T(1024)S(1)}, bf16[1024,3072]{1,0:T(8,128)(2,1)}) fusion(f32[1024,3072]{1,0:T(8,128)} %get-tuple-element.284, bf16[1024,768]{1,0:T(8,128)(2,1)} %get-tuple-element.276, bf16[3072,768]{1,0:T(8,128)(2,1)} %all-gather.17.cloned.1.call-done, f32[1024,3072]{1,0:T(8,128)} %get-tuple-element.309, ...), kind=kOutput, calls=%fused_computation.34 | convolution fusion | flops 4885312512 | bytes 37773312 | tf_op jit(solution)/shard_map/dot_general | solution.py:27
  473.4 9.5 multiply_reduce_fusion.1
  500.5 389.9 %while.28 = (s32[]{:T(128)}, bf16[48,128,128]{1,2,0:T(8,128)(2,1)}, bf16[48,512,128]{1,2,0:T(8,128)(2,1)}, bf16[48,512,128]{1,2,0:T(8,128)(2,1)}, bf16[48,512,12...) while((s32[]{:T(128)}, bf16[48,128,128]{1,2,0:T(8,128)(2,1)}, ...), condition=%wide.region_14.15_spmd, body=%wide.region_12.14_spmd.sunk | while | flops 85229824 | bytes 6068385 | solution.py:233
  890.4 9.3 copy.81
  907.1 9.5 copy.79
  916.6 8.2 copy.92
  929.5 10.7 fusion.35
  941.6 10.2 fusion.37
  954.7 10.8 reduce-scatter.21.cloned.1.call-done
  969.2 57.4 %reduce-scatter.19.cloned.1.call-done = bf16[128,6144]{1,0:T(8,128)(2,1)} async-done(((bf16[512,6144]{1,0:T(8,128)(2,1)}), bf16[128,6144]{1,0:T(8,128)(2,1)}) %reduce-scatter.19.cloned.1.call-update) | async-done | bytes 1572880
  1030.3 9.1 convolution_bitcast_fusion
  1052.1 40.4 %all-reduce.18 = (f32[768]{0:T(1024)S(1)}, f32[768]{0:T(1024)S(1)}, f32[768]{0:T(1024)S(1)}, f32[768]{0:T(1024)S(1)}, f32[768]{0:T(1024)S(1)}, /*index=5*/f32[30...) all-reduce(f32[768]{0:T(1024)S(1)} %get-tuple-element.298, ...), channel_id=5, replica_groups=mesh['dp'=8,'seq'=4] {'dp','seq'}, use_global_device_ids=true, to_apply=%region_19.20.clone | all-reduce | flops 9216 | bytes 73728
  1097.8 8.7 add_convert_fusion.2
  1106.5 25.1 %reduce-scatter.13.cloned.1.call-done = f32[24,768]{1,0:T(8,128)} async-done(((f32[768,768]{1,0:T(8,128)}), f32[24,768]{1,0:T(8,128)}) %reduce-scatter.13.cloned.1.call-update) | async-done | bytes 73744 | tf_op jit(solution)/shard_map/reduce_scatter | solution.py:276
  1131.6 142.0 %reduce-scatter.15.cloned.1.call-done = f32[24,3072]{1,0:T(8,128)} async-done(((f32[768,3072]{1,0:T(8,128)}), f32[24,3072]{1,0:T(8,128)}) %reduce-scatter.15.cloned.1.call-update) | async-done | bytes 294928 | tf_op jit(solution)/shard_map/reduce_scatter | solution.py:280
  1273.6 141.1 %reduce-scatter.17.cloned.1.call-done = f32[96,768]{1,0:T(8,128)} async-done(((f32[3072,768]{1,0:T(8,128)}), f32[96,768]{1,0:T(8,128)}) %reduce-scatter.17.cloned.1.call-update) | async-done | bytes 294928 | tf_op jit(solution)/shard_map/reduce_scatter | solution.py:282
  1414.7 125.2 %reduce-scatter.23.cloned.1.call-done = f32[24,2304]{1,0:T(8,128)} async-done(((f32[768,2304]{1,0:T(8,128)}), f32[24,2304]{1,0:T(8,128)}) %reduce-scatter.23.cloned.1.call-update) | async-done | bytes 221200
  (1353 shorter events, 708.6 us)
Async XLA Ops:
  7.2 66.7 %all-gather.7.cloned.1.call-start = ((), (), s32[]{:S(2)}) async-start(), calls=%async_computation.6 | async-start | bytes 3649536 | tf_op jit(solution)/shard_map/all_gather | solution.py:145
  7.9 122.5 %all-gather.9.cloned.1.call-start = ((), (), s32[]{:S(2)}) async-start(), calls=%async_computation.7 | async-start | bytes 7864320 | tf_op jit(solution)/shard_map/all_gather | solution.py:175
  84.2 4.1 copy-start.8
  84.2 4.8 copy-start.11
  84.2 4.8 copy-start.12
  84.2 4.8 copy-start.13
  84.2 4.8 copy-start.14
  84.2 4.8 copy-start.15
  84.2 4.8 copy-start.16
  84.3 4.8 copy-start.17
  84.3 95.0 %all-gather.11.cloned.1.call-start = ((), (), s32[]{:S(2)}) async-start(), calls=%async_computation.8 | async-start | bytes 7864320 | tf_op jit(solution)/shard_map/all_gather | solution.py:174
  86.0 313.3 %all-gather.13.cloned.1.call-start = ((), (), s32[]{:S(2)}) async-start(), calls=%async_computation.9 | async-start | bytes 1216512 | tf_op jit(solution)/shard_map/all_gather | solution.py:148
  86.5 317.1 %all-gather.15.cloned.1.call-start = ((), (), s32[]{:S(2)}) async-start(), calls=%async_computation.10 | async-start | bytes 4866048 | tf_op jit(solution)/shard_map/all_gather | solution.py:152
  87.1 352.3 %all-gather.17.cloned.1.call-start = ((), (), s32[]{:S(2)}) async-start(), calls=%async_computation.11 | async-start | bytes 4866048 | tf_op jit(solution)/shard_map/all_gather | solution.py:154
  87.7 877.8 %reduce-scatter.21.cloned.1.call-start = ((), (), s32[]{:S(2)}) async-start(), calls=%async_computation.16 | async-start | bytes 7864320
  484.5 3.2 copy-start.18
  495.9 4.7 copy-start.10
  907.1 119.6 %reduce-scatter.19.cloned.1.call-start = ((), (), s32[]{:S(2)}) async-start(), calls=%async_computation.15 | async-start | bytes 7864320
  924.8 206.8 %reduce-scatter.13.cloned.1.call-start = ((), (), s32[]{:S(2)}) async-start(), calls=%async_computation.12 | async-start | bytes 2433024 | tf_op jit(solution)/shard_map/reduce_scatter | solution.py:276
  929.5 344.1 %reduce-scatter.15.cloned.1.call-start = ((), (), s32[]{:S(2)}) async-start(), calls=%async_computation.13 | async-start | bytes 9732096 | tf_op jit(solution)/shard_map/reduce_scatter | solution.py:280
  940.2 474.4 %reduce-scatter.17.cloned.1.call-start = ((), (), s32[]{:S(2)}) async-start(), calls=%async_computation.14 | async-start | bytes 9732096 | tf_op jit(solution)/shard_map/reduce_scatter | solution.py:282
  951.8 588.1 %reduce-scatter.23.cloned.1.call-start = ((), (), s32[]{:S(2)}) async-start(), calls=%async_computation.17 | async-start | bytes 7299072
  954.7 75.6 %copy-start.5 = (bf16[96,8,8,128]{3,1,2,0:T(8,128)(2,1)}, bf16[96,8,8,128]{3,1,2,0:T(8,128)(2,1)S(1)}, u32[]{:S(2)}) copy-start(bf16[96,8,8,128]{3,1,2,0:T(8,128)(2,1)S(1)} %copy.107) | copy-start | bytes 4718596
  1049.2 48.6 %copy-start.3 = (f32[1024,768]{1,0:T(8,128)S(1)}, f32[1024,768]{1,0:T(8,128)}, u32[]{:S(2)}) copy-start(f32[1024,768]{1,0:T(8,128)} %copy-done.2) | copy-start | bytes 9437188
  (7 other events, 10.7 us)
Sparse Core Ops, SparseCore 0:
  10.9 62.9 all-gather.6
  84.4 45.9 all-gather.8
  132.0 47.2 all-gather.10
  182.0 54.1 all-gather.12
  238.9 62.5 all-gather.14
  304.3 62.7 all-gather.16
  907.2 58.3 reduce-scatter.20
  968.2 58.3 reduce-scatter.18
  1032.5 99.0 reduce-scatter.12
  1138.9 134.6 reduce-scatter.14
  1280.1 134.5 reduce-scatter.16
  1421.7 118.1 reduce-scatter.22
where the time goes:
time: 1570 us; the launch traced here: 1550 us
  waiting for transfers between devices  601 us (38%)
  local copies, waits for them, and re-layouts  499 us (32%)
  matrix products  220 us (14%)
  other arithmetic  123 us (8%)
  blocking collectives  82.8 us (5%)
    dynamic_slice x432, local copies, waits for them, and re-layouts, on_device(): lax.map(attend_forward, (query_items, key_items, value_items, limits))  307 us
    unnamed x15, waiting for transfers between devices  196 us
    reduce_scatter x1, waiting for transfers between devices, on_device(): lax.psum_scatter(grad_in, ('dp', 'seq'), scatter_dimension=0, tiled=True)  142 us
    reduce_scatter x1, waiting for transfers between devices, on_device(): lax.psum_scatter(grad_down, ('dp', 'seq'), scatter_dimension=0, tiled=True)  141 us
    unnamed x2, blocking collectives  82.8 us
    unnamed x75, local copies, waits for them, and re-layouts  69.9 us
    lt x96, other arithmetic, scores_of(): valid = jnp.arange(key_blk.shape[0], dtype=jnp.int32) < limit  62.3 us
    all_gather x1, waiting for transfers between devices, on_device(): lax.all_gather(keys_local, 'seq', axis=1, tiled=True)  48.8 us
  transfers between devices with their start and end apart: 12, of which 9 were waited for; matrix products, arithmetic and copies ran while one was open for 24% of the time, Pallas kernels for 0%

commit v1 on v0

v1 whole, which is shorter than its diff:
```python
import functools

import jax
import jax.numpy as jnp
from jax import lax
from jax.experimental import pallas as pl
from jax.experimental.pallas import tpu as pltpu
from jax.sharding import PartitionSpec as P

BF = jnp.bfloat16
F32 = jnp.float32
HD = 64
BOTH = ("dp", "seq")

def layer_norm(value, gain, shift):
    center = jnp.mean(value, -1, keepdims=True)
    centered = value - center
    spread = jnp.mean(centered * centered, -1, keepdims=True)
    return centered * lax.rsqrt(spread + 1e-12) * gain + shift


def gelu_exact(value):
    return jax.nn.gelu(value, approximate=False)


def over_rows(left, right):
    return lax.dot_general(
        left, right, (((0,), (0,)), ((), ())), preferred_element_type=jnp.float32
    )


def times_transposed(left, right):
    return lax.dot_general(
        left, right, (((1,), (1,)), ((), ())), preferred_element_type=jnp.float32
    )


def nt(a,b): return lax.dot_general(a,b,(((1,),(1,)),((),())),preferred_element_type=F32)
def tn(a,b): return lax.dot_general(a,b,(((0,),(0,)),((),())),preferred_element_type=F32)
def nn(a,b): return lax.dot_general(a,b,(((1,),(0,)),((),())),preferred_element_type=F32)

def masked_pair(q, k, bias, head, lane):
    mine = (lane >= head*HD) & (lane < (head+1)*HD)
    spare = lane == (HD if head==0 else 0)
    zero=jnp.zeros((),BF)
    qh = jnp.where(mine, q*BF(0.125), jnp.where(spare, jnp.ones((),BF), zero))
    kh = jnp.where(mine, k, jnp.where(spare, bias, zero))
    return qh, kh

def fwd_kernel(cq, q_ref,k_ref,v_ref,b_ref,o_ref,lse_ref):
    n=q_ref.shape[0]
    lane=lax.broadcasted_iota(jnp.int32,(n,128),1)
    q=q_ref[...]; k=k_ref[...]; v=v_ref[...]; bias=b_ref[0]
    pairs=[masked_pair(q,k,bias,h,lane) for h in range(2)]
    for c in range(n//cq):
        sl=slice(c*cq,(c+1)*cq)
        halves=[]
        for h in range(2):
            qh,kh=pairs[h]
            s=nt(kh,qh[sl])
            m=jnp.max(s,0,keepdims=True)
            e=jnp.exp(s-m)
            l=jnp.sum(e,0,keepdims=True)
            ot=tn(v[:,h*HD:(h+1)*HD],e.astype(BF))
            halves.append(ot*(1.0/l))
            lse_ref[0,h:h+1,sl]=m+jnp.log(l)
        o_ref[sl,:]=jnp.concatenate(halves,0).T.astype(BF)

def bwd_kernel(cq, q_ref,k_ref,v_ref,b_ref,lse_ref,g_ref,dq_ref,dk_ref,dv_ref):
    n=q_ref.shape[0]
    lane=lax.broadcasted_iota(jnp.int32,(n,128),1)
    q=q_ref[...]; k=k_ref[...]; v=v_ref[...]; bias=b_ref[0]; g=g_ref[...]
    qs=q*BF(0.125); ks=k*BF(0.125)
    zero=jnp.zeros((),BF)
    dks=[];dvs=[]
    dq=[[None,None] for _ in range(n//cq)]
    for h in range(2):
        qh,kh=masked_pair(q,k,bias,h,lane)
        mine = (lane >= h*HD) & (lane < (h+1)*HD)
        vh=jnp.where(mine,v,zero)
        kth=ks[:,h*HD:(h+1)*HD]
        dk=dv=None
        for c in range(n//cq):
            sl=slice(c*cq,(c+1)*cq)
            s=nt(kh,qh[sl])
            p=jnp.exp(s-lse_ref[0,h:h+1,sl])
            gp=nt(vh,g[sl])
            inner=jnp.sum(p*gp,0,keepdims=True)
            ds=(p*(gp-inner)).astype(BF)
            a=nn(p.astype(BF),g[sl]); b=nn(ds,qs[sl])
            dv=a if dv is None else dv+a
            dk=b if dk is None else dk+b
            dq[c][h]=tn(kth,ds)
        dks.append(dk);dvs.append(dv)
    for c in range(n//cq):
        sl=slice(c*cq,(c+1)*cq)
        dq_ref[sl,:]=jnp.concatenate(dq[c],0).T.astype(BF)
    first=lane<HD
    dk_ref[...]=jnp.where(first,dks[0],dks[1]).astype(BF)
    dv_ref[...]=jnp.where(first,dvs[0],dvs[1]).astype(BF)

def attention_forward(packed,bias,length,cq=512):
    rows,wide=packed.shape; width=wide//3; pairs=width//128; seqs=rows//length
    blk=lambda off: pl.BlockSpec((length,128),lambda s,p:(s,off*pairs+p))
    return pl.pallas_call(functools.partial(fwd_kernel,cq),grid=(seqs,pairs),
      in_specs=[blk(0),blk(1),blk(2),pl.BlockSpec((1,length,128),lambda s,p:(s,0,0))],
      out_specs=[blk(0),pl.BlockSpec((1,2,length),lambda s,p:(s*pairs+p,0,0))],
      out_shape=[jax.ShapeDtypeStruct((rows,width),BF),jax.ShapeDtypeStruct((seqs*pairs,2,length),F32)],
      compiler_params=pltpu.CompilerParams(vmem_limit_bytes=48*2**20),name="attention_forward",
      cost_estimate=pl.CostEstimate(flops=4*rows*length*width,bytes_accessed=rows*width*8,transcendentals=rows*length*width//HD))(packed,packed,packed,bias)

def attention_backward(packed,bias,lse,grad,length,cq=512):
    rows,wide=packed.shape; width=wide//3; pairs=width//128; seqs=rows//length
    blk=lambda off: pl.BlockSpec((length,128),lambda s,p:(s,off*pairs+p))
    o=jax.ShapeDtypeStruct((rows,width),BF)
    return pl.pallas_call(functools.partial(bwd_kernel,cq),grid=(seqs,pairs),
      in_specs=[blk(0),blk(1),blk(2),pl.BlockSpec((1,length,128),lambda s,p:(s,0,0)),pl.BlockSpec((1,2,length),lambda s,p:(s*pairs+p,0,0)),blk(0)],
      out_specs=[blk(0)]*3,out_shape=[o,o,o],
      compiler_params=pltpu.CompilerParams(vmem_limit_bytes=48*2**20),name="attention_backward",
      cost_estimate=pl.CostEstimate(flops=10*rows*length*width,bytes_accessed=rows*width*14,transcendentals=rows*length*width//HD))(packed,packed,packed,bias,lse,grad)

def to_sequences(block):
    return lax.all_to_all(block, "seq", 0, 1, tiled=True)


def to_positions(block):
    return lax.all_to_all(block, "seq", 1, 0, tiled=True)


def gather_rows(block):
    return lax.all_gather(block, BOTH, axis=0, tiled=True)


def on_device(
    inputs,
    lengths,
    query_key_value_weight,
    query_bias,
    value_bias,
    output_weight,
    output_bias,
    norm1_gain,
    norm1_shift,
    in_weight,
    in_bias,
    down_weight,
    down_bias,
    norm2_gain,
    norm2_shift,
    cotangent,
):
    groups, local_len, width = inputs.shape
    rows = groups * local_len
    members = lax.axis_size("seq")
    devices = lax.axis_size("dp") * members
    kept = groups // members
    length = local_len * members
    flat = to_sequences(inputs).reshape(rows, width)
    wide_qkv = gather_rows(query_key_value_weight)
    vectors = (
        query_bias,
        value_bias,
        output_bias,
        norm1_gain,
        norm1_shift,
        in_bias,
        down_bias,
        norm2_gain,
        norm2_shift,
    )
    sizes = [v.shape[0] for v in vectors]
    gathered = gather_rows(jnp.concatenate(vectors)[None])
    full = []
    at = 0
    for size in sizes:
        full.append(gathered[:, at : at + size].reshape(-1).astype(F32))
        at += size
    (
        full_query_bias,
        full_value_bias,
        full_out_bias,
        gain_one,
        shift_one,
        full_in_bias,
        full_down_bias,
        gain_two,
        shift_two,
    ) = full
    wide_out = gather_rows(output_weight)
    wide_in = gather_rows(in_weight)
    wide_down = gather_rows(down_weight)
    cot = to_sequences(cotangent).reshape(rows, width)
    bias_vector = jnp.concatenate([full_query_bias, jnp.zeros((width,), F32), full_value_bias])
    packed = (jnp.dot(flat, wide_qkv, preferred_element_type=F32) + bias_vector).astype(BF)
    mine = lax.dynamic_slice(lengths, (lax.axis_index("seq") * kept,), (kept,))
    positions = jnp.arange(length, dtype=jnp.int32)
    mask = jnp.where(positions[None, :] < mine[:, None], 0.0, -1e30).astype(BF)
    mask = jnp.broadcast_to(mask[:, :, None], (kept, length, 128))
    mixed, logsum = attention_forward(packed, mask, length)
    attention_branch = jnp.dot(mixed, wide_out, preferred_element_type=F32) + full_out_bias
    first, norm_one_pull = jax.vjp(
        layer_norm, flat.astype(F32) + attention_branch, gain_one, shift_one
    )
    first_low = first.astype(BF)
    hidden = jnp.dot(first_low, wide_in, preferred_element_type=F32) + full_in_bias
    active, gelu_pull = jax.vjp(gelu_exact, hidden)
    active_low = active.astype(BF)
    branch_two = jnp.dot(active_low, wide_down, preferred_element_type=F32) + full_down_bias
    result, norm_two_pull = jax.vjp(
        layer_norm, first_low.astype(F32) + branch_two, gain_two, shift_two
    )
    outputs = to_positions(result.astype(BF).reshape(kept, length, width))
    grad_second, grad_gain_two, grad_shift_two = norm_two_pull(cot.astype(F32))
    grad_branch_two = grad_second.astype(BF)
    grad_down = over_rows(active_low, grad_branch_two)
    grad_down_bias = jnp.sum(grad_branch_two.astype(F32), 0)
    (grad_hidden,) = gelu_pull(times_transposed(grad_branch_two, wide_down))
    grad_hidden_low = grad_hidden.astype(BF)
    grad_in = over_rows(first_low, grad_hidden_low)
    grad_in_bias = jnp.sum(grad_hidden_low.astype(F32), 0)
    grad_first = times_transposed(grad_hidden_low, wide_in) + grad_second
    grad_residual, grad_gain_one, grad_shift_one = norm_one_pull(grad_first)
    grad_branch_one = grad_residual.astype(BF)
    grad_out = over_rows(mixed, grad_branch_one)
    grad_out_bias = jnp.sum(grad_branch_one.astype(F32), 0)
    grad_mixed = times_transposed(grad_branch_one, wide_out).astype(BF)
    grad_queries, grad_keys, grad_values = attention_backward(
        packed, mask, logsum, grad_mixed, length
    )
    grad_packed = jnp.concatenate([grad_queries, grad_keys, grad_values], -1)
    grad_inputs = times_transposed(grad_packed, wide_qkv) + grad_residual
    grad_inputs = to_positions(grad_inputs.astype(BF).reshape(kept, length, width))
    grad_qkv = over_rows(flat, grad_packed)
    column_sums = jnp.sum(grad_packed.astype(F32), 0)

    def scatter(total):
        return lax.psum_scatter(total.astype(BF), BOTH, scatter_dimension=0, tiled=True).astype(F32)

    sums = (
        column_sums[:width],
        column_sums[2 * width :],
        grad_out_bias,
        grad_gain_one,
        grad_shift_one,
        grad_in_bias,
        grad_down_bias,
        grad_gain_two,
        grad_shift_two,
    )
    joined = jnp.concatenate([v.reshape(devices, -1) for v in sums], 1)
    joined = lax.psum_scatter(joined, BOTH, scatter_dimension=0, tiled=True)[0]
    parts = []
    at = 0
    for size in sizes:
        parts.append(joined[at : at + size])
        at += size
    return (
        outputs,
        grad_inputs,
        scatter(grad_qkv),
        parts[0],
        parts[1],
        scatter(grad_out),
        parts[2],
        parts[3],
        parts[4],
        scatter(grad_in),
        parts[5],
        scatter(grad_down),
        parts[6],
        parts[7],
        parts[8],
    )


def solution(mesh):
    placed = (
        P("dp", "seq", None),
        P("dp"),
        P(("dp", "seq"), None),
        P(("dp", "seq")),
        P(("dp", "seq")),
        P(("dp", "seq"), None),
        P(("dp", "seq")),
        P(("dp", "seq")),
        P(("dp", "seq")),
        P(("dp", "seq"), None),
        P(("dp", "seq")),
        P(("dp", "seq"), None),
        P(("dp", "seq")),
        P(("dp", "seq")),
        P(("dp", "seq")),
        P("dp", "seq", None),
    )
    return jax.shard_map(
        on_device,
        mesh=mesh,
        in_specs=placed,
        out_specs=(
            P("dp", "seq", None),
            P("dp", "seq", None),
            P(("dp", "seq"), None),
            P(("dp", "seq")),
            P(("dp", "seq")),
            P(("dp", "seq"), None),
            P(("dp", "seq")),
            P(("dp", "seq")),
            P(("dp", "seq")),
            P(("dp", "seq"), None),
            P(("dp", "seq")),
            P(("dp", "seq"), None),
            P(("dp", "seq")),
            P(("dp", "seq")),
            P(("dp", "seq")),
        ),
        check_vma=False,
    )
```

time: 1570 us -> 754 us (0.48); the launches traced: 1550 us -> 748 us
  local copies, waits for them, and re-layouts: 499 us -> 35.5 us
  waiting for transfers between devices: 601 us -> 372 us
  other arithmetic: 123 us -> 16.6 us
  matrix products: 220 us -> 125 us
  blocking collectives: 82.8 us -> 130 us
  Pallas kernels: 0 us -> 42 us
    dynamic_slice x432 -> x1, local copies, waits for them, and re-layouts: 307 us -> 0.08 us  [on_device(): mine = lax.dynamic_slice(lengths, (lax.axis_index('seq') * kept,), (kept,))]
    unnamed x15 -> x9, waiting for transfers between devices: 196 us -> 50.2 us
    dot_general x340 -> x4, matrix products: 147 us -> 58 us  [the longest x1 38.4 us: on_device(): jnp.dot(first_low, wide_in, preferred_element_type=F32) + full_in_bias]
    reduce_scatter x3, waiting for transfers between devices: 308 us -> 220 us  [scatter(): lax.psum_scatter(total.astype(BF), BOTH, scatter_dimension=0, tiled=True)]
    dynamic_update_slice x144 -> x0, local copies, waits for them, and re-layouts: 64.7 us -> none  [the longest x48 34.8 us: on_device(): lax.map(attend_backward, (query_items, key_items, value_items, limits, lo...]
    lt x96 -> x0, other arithmetic: 62.3 us -> none  [scores_of(): valid = jnp.arange(key_blk.shape[0], dtype=jnp.int32) < limit]
    unnamed x75 -> x57, local copies, waits for them, and re-layouts: 69.9 us -> 17.8 us
    pallas_call x0 -> x2, Pallas kernels: none -> 42 us  [the longest x1 24.7 us: attention_backward(): pl.pallas_call(functools.partial(bwd_kernel, cq), grid=(seqs, pairs), in_...]
  transfers between devices with their start and end apart: 12 -> 11, of which waited for: 9 -> 7; matrix products, arithmetic and copies ran while one was open for 24% -> 16% of each run, Pallas kernels for 0% -> 6%
where the time goes in v1:
time: 754 us; the launch traced here: 748 us
  waiting for transfers between devices  372 us (49%)
  blocking collectives  130 us (17%)
  matrix products  125 us (17%)
  Pallas kernels  42 us (6%)
  local copies, waits for them, and re-layouts  35.5 us (5%)
  other arithmetic  16.6 us (2%)
  between operations  15.2 us (2%)
  starting transfers between devices  12 us (2%)
    reduce_scatter x3, waiting for transfers between devices, scatter(): lax.psum_scatter(total.astype(BF), BOTH, scatter_dimension=0, tiled=True)  220 us
    unnamed x2, blocking collectives  104 us
    all_gather x4, waiting for transfers between devices, gather_rows(): return lax.all_gather(block, BOTH, axis=0, tiled=True)  91.7 us
    unnamed x9, waiting for transfers between devices  50.2 us
    dot_general x4, matrix products, times_transposed(): lax.dot_general(left, right, (((1,), (1,)), ((), ())), preferred_element_...  39.5 us
    dot_general x1, matrix products, on_device(): jnp.dot(first_low, wide_in, preferred_element_type=F32) + full_in_bias  38.4 us
    dot_general x4, matrix products, over_rows(): lax.dot_general(left, right, (((0,), (0,)), ((), ())), preferred_element_...  27 us
    all_to_all x1, blocking collectives, to_sequences(): return lax.all_to_all(block, 'seq', 0, 1, tiled=True)  25.3 us
  transfers between devices with their start and end apart: 11, of which 7 were waited for; matrix products, arithmetic and copies ran while one was open for 16% of the time, Pallas kernels for 6%

profile of v1, /device:TPU:0, one launch (start us, length us, event | category | flops | bytes accessed | tf_op | source)
XLA Modules:
  0.0 747.8 jit_solution(6912927585909273106)
XLA Ops:
  9.5 25.3 %all_to_all.60 = bf16[8,128,768]{2,1,0:T(8,128)(2,1)S(1)} all-to-all(bf16[8,128,768]{2,1,0:T(8,128)(2,1)} %param.16), channel_id=1, replica_groups=mesh['dp'=8,'seq'=4] {'seq'}, dimensions={0} | all-to-all | bytes 3145728 | tf_op jit(solution)/shard_map/all_to_all | solution.py:123
  39.4 55.6 %all-reduce = bf16[9216]{0:T(1024)(128)(2,1)S(1)} all-reduce(bf16[9216]{0:T(1024)(128)(2,1)S(1)} %dynamic-update-slice), channel_id=2, replica_groups=mesh['dp'=8,'seq'=4] {'dp','seq'}, use_global_device_ids=true, to_apply=%add | all-reduce | flops 9216 | bytes 36864
  100.0 7.5 %add_convert_fusion.1.q_ref.k_ref.v_ref = bf16[1024,2304]{1,0:T(8,128)(2,1)} fusion(bf16[1024,768]{1,0:T(8,128)(2,1)S(1)} %bitcast.76, bf16[768,2304]{1,0:T(8,128)(2,1)} %all-gather.6.cloned.1.call-done, f32[2304]{0:T(1024)S(1)} %pad_maximum_fusion), kind=kOutput, calls=%fused_computation.19 | convolution fusion | flops 3628597248 | bytes 9839616 | tf_op jit(solution)/shard_map/dot_general | solution.py:194
  107.7 17.2 %attention_forward.1 = (bf16[1024,768]{1,0:T(8,128)(2,1)S(1)}, f32[12,2,512]{2,1,0:T(2,128)S(1)}) custom-call(bf16[1024,2304]{1,0:T(8,128)(2,1)} %add_convert_fusion.1.q_ref.k_ref.v_ref, bf16[1024,2304]{1,0:T(8,128)(2,1)} %add_convert_fusion.1.q_ref.k_ref.v_ref, bf16[1024,2304]{1,0:T(8,128)(2,1)} %add_convert_fusion.1.q_ref.k_ref.v_ref, ...), custom_call_target="tpu_custom_call" | custom-call | flops 1610612736 | bytes 6291456 | tf_op jit(solution)/shard_map/attention_forward/pallas_call | solution.py:105
  125.6 5.1 all-gather.8.cloned.1.call-done
  136.4 59.8 %all-gather.10.cloned.1.call-done = bf16[768,3072]{1,0:T(8,128)(2,1)} async-done(((bf16[24,3072]{1,0:T(8,128)(2,1)}), bf16[768,3072]{1,0:T(8,128)(2,1)}) %all-gather.10.cloned.1.call-update) | async-done | bytes 4718608 | tf_op jit(solution)/shard_map/all_gather | solution.py:131
  196.1 38.4 %multiply_convert_fusion = (bf16[1024,3072]{1,0:T(8,128)(2,1)}, f32[1024,3072]{1,0:T(8,128)}, f32[1024,3072]{1,0:T(8,128)}) fusion(f32[3072]{0:T(1024)S(1)} %reshape.266, bf16[768,3072]{1,0:T(8,128)(2,1)} %all-gather.10.cloned.1.call-done, f32[1024,768]{1,0:T(8,128)} %copy-done.7, f32[768]{0:T(1024)S(1)} %reshape.265, f32[768]{0:T(1024)S(1)} %reshape.264, ...), kind=kOutput, calls=%fused_computation.4 | convolution fusion | flops 5043388416 | bytes 39348224 | tf_op jit(solution)/shard_map/dot_general | solution.py:205
  234.5 26.8 %all-gather.12.cloned.1.call-done = bf16[3072,768]{1,0:T(8,128)(2,1)} async-done(((bf16[96,768]{1,0:T(8,128)(2,1)}), bf16[3072,768]{1,0:T(8,128)(2,1)}) %all-gather.12.cloned.1.call-update) | async-done | bytes 4718608 | tf_op jit(solution)/shard_map/all_gather | solution.py:131
  261.4 8.8 %fusion.16 = (f32[1024]{0:T(1024)S(1)}, f32[1024,768]{1,0:T(8,128)S(1)}) fusion(f32[768]{0:T(1024)S(1)} %reshape.267, bf16[1024,3072]{1,0:T(8,128)(2,1)} %get-tuple-element.83, bf16[3072,768]{1,0:T(8,128)(2,1)} %all-gather.12.cloned.1.call-done, f32[768]{0:T(1024)S(1)} %reshape.265, f32[768]{0:T(1024)S(1)} %reshape.264, f32[1024]{0:T(1024)S(1)} %fusion.9, ...), kind=kOutput, calls=%fused_computation.85 | convolution fusion | flops 4838915072 | bytes 17323008 | tf_op jit(solution)/shard_map/dot_general | solution.py:208
  277.5 18.3 %convert_reduce_fusion = (f32[3072]{0:T(1024)S(1)}, bf16[1024,3072]{1,0:T(8,128)(2,1)}) fusion(f32[1024,3072]{1,0:T(8,128)} %get-tuple-element.84, bf16[1024,768]{1,0:T(8,128)(2,1)} %get-tuple-element.76, bf16[3072,768]{1,0:T(8,128)(2,1)} %all-gather.12.cloned.1.call-done, f32[1024,3072]{1,0:T(8,128)} %get-tuple-element.106, f32[3072]{0:T(1024)S(1)} %reshape.266), kind=kOutput, calls=%fused_computation.2 | convolution fusion | flops 4885312512 | bytes 37773312 | tf_op jit(solution)/shard_map/dot_general | solution.py:33
  295.8 9.5 %multiply_reduce_fusion = (f32[768]{0:T(1024)S(1)}, f32[1024]{0:T(1024)S(1)}, f32[768]{0:T(1024)S(1)}, f32[1024,768]{1,0:T(8,128)S(1)}) fusion(f32[1024,768]{1,0:T(8,128)S(1)} %copy-done.8, f32[1024]{0:T(1024)S(1)} %fusion.9, f32[1024]{0:T(1024)S(1)} %broadcast_multiply_fusion.1, f32[768]{0:T(1024)S(1)} %reshape.264, ...), kind=kOutput, calls=%fused_computation.30 | convolution fusion | flops 4839699456 | bytes 20472832 | tf_op jit(solution)/shard_map/dot_general | solution.py:33
  312.5 4.4 convolution_convert_fusion.3.g_ref
  316.9 24.7 %attention_backward.1 = (bf16[1024,768]{1,0:T(8,128)(2,1)S(1)}, bf16[1024,768]{1,0:T(8,128)(2,1)S(1)}, bf16[1024,768]{1,0:T(8,128)(2,1)S(1)}) custom-call(bf16[1024,2304]{1,0:T(8,128)(2,1)} %add_convert_fusion.1.q_ref.k_ref.v_ref, bf16[1024,2304]{1,0:T(8,128)(2,1)} %add_convert_fusion.1.q_ref.k_ref.v_ref, ...), custom_call_target="tpu_custom_call" | custom-call | flops 4026531840 | bytes 11010048 | tf_op jit(solution)/shard_map/attention_backward/pallas_call | solution.py:116
  344.2 5.4 fusion.6
  349.5 5.8 copy.48
  355.4 9.1 %convolution_convert_fusion = bf16[3072,768]{1,0:T(8,128)(2,1)} fusion(bf16[1024,3072]{1,0:T(8,128)(2,1)} %get-tuple-element.83, bf16[1024,768]{1,0:T(8,128)(2,1)} %get-tuple-element.76), kind=kOutput, calls=%fused_computation.20 | convolution fusion | flops 4834197504 | bytes 12582912 | tf_op jit(solution)/shard_map/dot_general | solution.py:27
  364.6 10.0 %convolution_convert_fusion.1 = bf16[768,3072]{1,0:T(8,128)(2,1)} fusion(bf16[1024,3072]{1,0:T(8,128)(2,1)} %get-tuple-element.111, f32[1024,768]{1,0:T(8,128)S(1)} %copy-done.8, f32[768]{0:T(1024)S(1)} %reshape.265, f32[768]{0:T(1024)S(1)} %reshape.264, f32[1024]{0:T(1024)S(1)} %fusion.9, f32[1024]{0:T(1024)S(1)} %broadcast_multiply_fusion.1), kind=kOutput, calls=%fused_computation.21 | convolution fusion | flops 4838129664 | bytes 14170112 | tf_op jit(solution)/shard_map/dot_general | solution.py:27
  378.9 4.6 all-to-all-start.1
  383.6 7.3 add_convert_fusion.2
  393.7 10.2 %all-to-all-done.1 = bf16[2,512,768]{2,0,1:T(2,128)(2,1)} async-done(((bf16[2,512,768]{2,0,1:T(2,128)(2,1)}), bf16[2,512,768]{2,0,1:T(2,128)(2,1)}, u32[]{:S(2)}, u32[]{:S(2)}) %all-to-all-start.1) | async-done | bytes 1572896 | tf_op jit(solution)/shard_map/all_to_all | solution.py:127
  411.7 48.9 %all-reduce.1 = f32[32,288]{1,0:T(8,128)S(1)} all-reduce(f32[32,288]{1,0:T(8,128)S(1)} %concatenate.15), channel_id=4, replica_groups=mesh['dp'=8,'seq'=4] {'dp','seq'}, use_global_device_ids=true, to_apply=%region_17.18.clone | all-reduce | flops 9216 | bytes 73728
  467.3 47.6 %reduce-scatter.13.cloned.1.call-done = bf16[24,2304]{1,0:T(8,128)(2,1)} async-done(((bf16[768,2304]{1,0:T(8,128)(2,1)}), bf16[24,2304]{1,0:T(8,128)(2,1)}) %reduce-scatter.13.cloned.1.call-update) | async-done | bytes 110608
  517.1 109.3 %reduce-scatter.11.cloned.1.call-done = bf16[96,768]{1,0:T(8,128)(2,1)} async-done(((bf16[3072,768]{1,0:T(8,128)(2,1)}), bf16[96,768]{1,0:T(8,128)(2,1)}) %reduce-scatter.11.cloned.1.call-update) | async-done | bytes 147472 | tf_op jit(solution)/shard_map/reduce_scatter | solution.py:237
  628.0 110.8 %reduce-scatter.9.cloned.1.call-done = bf16[24,3072]{1,0:T(8,128)(2,1)} async-done(((bf16[768,3072]{1,0:T(8,128)(2,1)}), bf16[24,3072]{1,0:T(8,128)(2,1)}) %reduce-scatter.9.cloned.1.call-update) | async-done | bytes 147472 | tf_op jit(solution)/shard_map/reduce_scatter | solution.py:237
  (138 shorter events, 62.2 us)
Async XLA Ops:
  7.2 92.2 %all-gather.6.cloned.1.call-start = ((), (), s32[]{:S(2)}) async-start(), calls=%async_computation.8 | async-start | bytes 3649536 | tf_op jit(solution)/shard_map/all_gather | solution.py:131
  7.9 122.8 %all-gather.8.cloned.1.call-start = ((), (), s32[]{:S(2)}) async-start(), calls=%async_computation.9 | async-start | bytes 1216512 | tf_op jit(solution)/shard_map/all_gather | solution.py:131
  8.7 187.5 %all-gather.10.cloned.1.call-start = ((), (), s32[]{:S(2)}) async-start(), calls=%async_computation.10 | async-start | bytes 4866048 | tf_op jit(solution)/shard_map/all_gather | solution.py:131
  9.4 29.6 %copy-start.15 = (bf16[24]{0:T(256)(128)(2,1)S(1)}, bf16[24]{0:T(256)(128)(2,1)}, u32[]{:S(2)}) copy-start(bf16[24]{0:T(256)(128)(2,1)} %param.19) | copy-start | bytes 148
  9.4 29.6 %copy-start.16 = (bf16[24]{0:T(256)(128)(2,1)S(1)}, bf16[24]{0:T(256)(128)(2,1)}, u32[]{:S(2)}) copy-start(bf16[24]{0:T(256)(128)(2,1)} %param.20) | copy-start | bytes 148
  9.4 29.6 %copy-start.17 = (bf16[24]{0:T(256)(128)(2,1)S(1)}, bf16[24]{0:T(256)(128)(2,1)}, u32[]{:S(2)}) copy-start(bf16[24]{0:T(256)(128)(2,1)} %param.22) | copy-start | bytes 148
  9.4 29.6 %copy-start.18 = (bf16[24]{0:T(256)(128)(2,1)S(1)}, bf16[24]{0:T(256)(128)(2,1)}, u32[]{:S(2)}) copy-start(bf16[24]{0:T(256)(128)(2,1)} %param.23) | copy-start | bytes 148
  9.4 29.6 %copy-start.19 = (bf16[24]{0:T(256)(128)(2,1)S(1)}, bf16[24]{0:T(256)(128)(2,1)}, u32[]{:S(2)}) copy-start(bf16[24]{0:T(256)(128)(2,1)} %param.24) | copy-start | bytes 148
  9.5 29.6 %copy-start.20 = (bf16[96]{0:T(256)(128)(2,1)S(1)}, bf16[96]{0:T(256)(128)(2,1)}, u32[]{:S(2)}) copy-start(bf16[96]{0:T(256)(128)(2,1)} %param.26) | copy-start | bytes 580
  9.5 29.6 %copy-start.21 = (bf16[24]{0:T(256)(128)(2,1)S(1)}, bf16[24]{0:T(256)(128)(2,1)}, u32[]{:S(2)}) copy-start(bf16[24]{0:T(256)(128)(2,1)} %param.28) | copy-start | bytes 148
  9.5 29.6 %copy-start.22 = (bf16[24]{0:T(256)(128)(2,1)S(1)}, bf16[24]{0:T(256)(128)(2,1)}, u32[]{:S(2)}) copy-start(bf16[24]{0:T(256)(128)(2,1)} %param.29) | copy-start | bytes 148
  9.5 29.6 %copy-start.23 = (bf16[24]{0:T(256)(128)(2,1)S(1)}, bf16[24]{0:T(256)(128)(2,1)}, u32[]{:S(2)}) copy-start(bf16[24]{0:T(256)(128)(2,1)} %param.30) | copy-start | bytes 148
  9.5 86.5 %copy-start.24 = (s32[8]{0:T(128)S(1)}, s32[8]{0:T(128)}, u32[]{:S(2)}) copy-start(s32[8]{0:T(128)} %param.17) | copy-start | bytes 100
  34.8 62.7 %all-to-all-start.2 = ((bf16[8,128,768]{2,1,0:T(8,128)(2,1)}), bf16[8,128,768]{2,1,0:T(8,128)(2,1)S(1)}, u32[]{:S(2)}, u32[]{:S(2)}) async-start(bf16[8,128,768]{2,1,0:T(8,128)(2,1)} %param.31), calls=%async_computation.2 | async-start | bytes 3145728 | tf_op jit(solution)/shard_map/all_to_all | solution.py:123
  38.3 223.0 %all-gather.12.cloned.1.call-start = ((), (), s32[]{:S(2)}) async-start(), calls=%async_computation.11 | async-start | bytes 4866048 | tf_op jit(solution)/shard_map/all_gather | solution.py:131
  38.9 427.0 %reduce-scatter.7.cloned.1.call-start = ((), (), s32[]{:S(2)}) async-start(), calls=%async_computation.12 | async-start | bytes 1216512 | tf_op jit(solution)/shard_map/reduce_scatter | solution.py:237
  97.5 10.0 %copy-start.5 = (bf16[8,128,768]{2,1,0:T(8,128)(2,1)}, bf16[8,128,768]{2,1,0:T(8,128)(2,1)S(1)}, u32[]{:S(2)}) copy-start(bf16[8,128,768]{2,1,0:T(8,128)(2,1)S(1)} %all-to-all-done.2) | copy-start | bytes 4718596
  136.3 125.0 %copy-start.8 = (f32[1024,768]{1,0:T(8,128)S(1)}, f32[1024,768]{1,0:T(8,128)}, u32[]{:S(2)}) copy-start(f32[1024,768]{1,0:T(8,128)} %copy-done.7) | copy-start | bytes 9437188
  312.5 202.4 %reduce-scatter.13.cloned.1.call-start = ((), (), s32[]{:S(2)}) async-start(), calls=%async_computation.15 | async-start | bytes 3649536
  355.3 271.0 %reduce-scatter.11.cloned.1.call-start = ((), (), s32[]{:S(2)}) async-start(), calls=%async_computation.14 | async-start | bytes 4866048 | tf_op jit(solution)/shard_map/reduce_scatter | solution.py:237
  364.5 374.3 %reduce-scatter.9.cloned.1.call-start = ((), (), s32[]{:S(2)}) async-start(), calls=%async_computation.13 | async-start | bytes 4866048 | tf_op jit(solution)/shard_map/reduce_scatter | solution.py:237
  378.9 25.0 %all-to-all-start.1 = ((bf16[2,512,768]{2,0,1:T(2,128)(2,1)}), bf16[2,512,768]{2,0,1:T(2,128)(2,1)}, u32[]{:S(2)}, u32[]{:S(2)}) async-start(bf16[2,512,768]{2,0,1:T(2,128)(2,1)} %copy.42), calls=%async_computation.1 | async-start | bytes 3145728 | tf_op jit(solution)/shard_map/all_to_all | solution.py:127
  390.9 16.6 %copy-start.6 = (bf16[8,128,768]{2,1,0:T(8,128)(2,1)S(1)}, bf16[8,128,768]{2,1,0:T(8,128)(2,1)}, u32[]{:S(2)}) copy-start(bf16[8,128,768]{2,1,0:T(8,128)(2,1)} %copy-done.5) | copy-start | bytes 4718596
  403.9 60.6 %all-to-all-start.3 = ((bf16[2,512,768]{2,0,1:T(2,128)(2,1)}), bf16[2,512,768]{2,0,1:T(2,128)(2,1)S(1)}, u32[]{:S(2)}, u32[]{:S(2)}) async-start(bf16[2,512,768]{2,0,1:T(2,128)(2,1)} %copy.45), calls=%async_computation.3 | async-start | bytes 3145728 | tf_op jit(solution)/shard_map/all_to_all | solution.py:127
  (12 other events, 39.1 us)
Sparse Core Ops, SparseCore 0:
  10.9 63.7 all-gather.5
  77.7 53.0 all-gather.7
  133.7 62.4 all-gather.9
  198.9 62.4 all-gather.11
  312.6 94.9 reduce-scatter.6
  412.9 101.9 reduce-scatter.12
  520.4 105.9 reduce-scatter.10
  632.8 106.0 reduce-scatter.8

commit v2 on v1

--- a/solution.py
+++ b/solution.py
@@ -118,17 +118,126 @@
       out_specs=[blk(0)]*3,out_shape=[o,o,o],
       compiler_params=pltpu.CompilerParams(vmem_limit_bytes=48*2**20),name="attention_backward",
       cost_estimate=pl.CostEstimate(flops=10*rows*length*width,bytes_accessed=rows*width*14,transcendentals=rows*length*width//HD))(packed,packed,packed,bias,lse,grad)
-
-def to_sequences(block):
-    return lax.all_to_all(block, "seq", 0, 1, tiled=True)
-
-
-def to_positions(block):
-    return lax.all_to_all(block, "seq", 1, 0, tiled=True)
-
-
-def gather_rows(block):
-    return lax.all_gather(block, BOTH, axis=0, tiled=True)
+def swap(block, distance, devices):
+    return lax.ppermute(block, BOTH, [(i, i ^ distance) for i in range(devices)])
+
+
+def place_kernel(ids, counts, spans, me_ref, *refs):
+    pieces, rest = refs[: len(counts)], refs[len(counts) :]
+    outs, sems = rest[: len(spans)], rest[len(spans)]
+    me = me_ref[0]
+    copies = []
+    at = 0
+    for piece, count in zip(pieces, counts):
+        for j in range(count):
+            spot = me ^ ids[at]
+            for out, (start, size) in zip(outs, spans):
+                source = piece.at[j] if len(spans) == 1 else piece.at[j, :, pl.ds(start, size)]
+                copy = pltpu.make_async_copy(source, out.at[spot], sems.at[len(copies)])
+                copy.start()
+                copies.append(copy)
+            at += 1
+    for copy in copies:
+        copy.wait()
+
+
+def place(pieces, ids, me, spans=None):
+    counts = [p.shape[0] for p in pieces]
+    total = sum(counts)
+    tail = pieces[0].shape[1:]
+    spans = spans or [(0, tail[-1])]
+    any_space = pl.BlockSpec(memory_space=pl.ANY)
+    return pl.pallas_call(
+        functools.partial(place_kernel, ids, counts, spans),
+        in_specs=[pl.BlockSpec(memory_space=pltpu.SMEM)] + [any_space] * len(pieces),
+        out_specs=[any_space] * len(spans),
+        out_shape=[
+            jax.ShapeDtypeStruct((total,) + tail[:-1] + (size,), pieces[0].dtype)
+            for _, size in spans
+        ],
+        scratch_shapes=[pltpu.SemaphoreType.DMA((total * len(spans),))],
+        name="place_blocks",
+    )(me.reshape(1), *pieces)
+
+
+def gather_blocks(block, me, devices, plan, spans=None):
+    swapped = lambda b, distance: swap(b, distance, devices)
+    own, own_ids = block[None], [0]
+    distance = 32
+    while distance < devices:
+        own = jnp.concatenate([own, swapped(own, distance)])
+        own_ids = own_ids + [i ^ distance for i in own_ids]
+        distance *= 2
+    far = [own] + [swapped(own, 8 * k) for k in (1, 2, 3)]
+    far_ids = [[i ^ (8 * k) for i in own_ids] for k in range(4)]
+    if plan == "split":
+        parts = [((0, 1), (4, 2)), ((2, 3), (2, 4))]
+    else:
+        parts = [((0, 1, 2, 3), (4, 2) if plan == "xy" else (2, 4))]
+    pieces, ids = [], []
+    for which, order in parts:
+        held = jnp.concatenate([far[k] for k in which])
+        held_ids = [i for k in which for i in far_ids[k]]
+        got = swapped(held, order[0])
+        got_ids = [i ^ order[0] for i in held_ids]
+        both = jnp.concatenate([held, got])
+        both_ids = held_ids + got_ids
+        last = swapped(both, order[1])
+        last_ids = [i ^ order[1] for i in both_ids]
+        for b, b_ids in ((both, both_ids), (last, last_ids)):
+            pieces += [b, swapped(b, 1)]
+            ids += b_ids + [i ^ 1 for i in b_ids]
+    return place(pieces, ids, me, spans)
+
+
+def pick(block, axis, index):
+    return lax.dynamic_index_in_dim(block, index, axis, keepdims=False)
+
+
+def fold(block, axis, me, distance, devices):
+    digit = (me // distance) % 2
+    got = swap(pick(block, axis, 1 - digit), distance, devices)
+    return (pick(block, axis, digit).astype(F32) + got.astype(F32)).astype(BF)
+
+
+def scatter_blocks(total, me, devices, plan):
+    tail = total.shape[1:]
+    distance = devices // 2
+    while distance >= 32:
+        total = fold(total.reshape((2, distance) + tail), 0, me, distance, devices)
+        distance //= 2
+    total = fold(total.reshape((16, 2) + tail), 1, me, 1, devices)
+    total = total.reshape((4, 2, 2) + tail)
+    z = (me // 8) % 4
+    if plan == "split":
+        upper = [pick(total.reshape((2, 2, 2, 2) + tail), 0, i) for i in (z // 2, 1 - z // 2)]
+        near = fold(fold(upper[0], 1, me, 4, devices), 1, me, 2, devices)
+        away = fold(fold(upper[1], 2, me, 2, devices), 1, me, 4, devices)
+        odd = z % 2
+        mine = [pick(near, 0, odd), pick(near, 0, 1 - odd), pick(away, 0, odd), pick(away, 0, 1 - odd)]
+    else:
+        if plan == "xy":
+            total = fold(fold(total, 1, me, 4, devices), 1, me, 2, devices)
+        else:
+            total = fold(fold(total, 2, me, 2, devices), 1, me, 4, devices)
+        mine = [pick(total, 0, z ^ k) for k in range(4)]
+    got = [swap(mine[k], 8 * k, devices).astype(F32) for k in (1, 2, 3)]
+    return mine[0].astype(F32) + got[0] + got[1] + got[2]
+
+
+def to_sequences(block, seat, members, devices):
+    groups, count, width = block.shape
+    parts = block.reshape(members, groups // members, count, width)
+    pieces = [pick(parts, 0, seat)]
+    pieces += [swap(pick(parts, 0, seat ^ k), k, devices) for k in range(1, members)]
+    return jnp.stack(pieces, 1).reshape(groups * count, width)
+
+
+def to_positions(block, seat, members, devices):
+    pieces = [block[:, 0][None]]
+    pieces += [swap(block[:, k][None], k, devices) for k in range(1, members)]
+    (placed,) = place(pieces, list(range(members)), seat)
+    return placed.reshape((-1,) + placed.shape[2:])
 
 
 def on_device(
@@ -155,8 +264,9 @@
     devices = lax.axis_size("dp") * members
     kept = groups // members
     length = local_len * members
-    flat = to_sequences(inputs).reshape(rows, width)
-    wide_qkv = gather_rows(query_key_value_weight)
+    seat = lax.axis_index("seq")
+    me = lax.axis_index("dp") * members + seat
+    flat = to_sequences(inputs, seat, members, devices)
     vectors = (
         query_bias,
         value_bias,
@@ -169,7 +279,19 @@
         norm2_shift,
     )
     sizes = [v.shape[0] for v in vectors]
-    gathered = gather_rows(jnp.concatenate(vectors)[None])
+    share = query_key_value_weight.shape[0]
+    vector_block = jnp.concatenate(vectors).reshape(share, -1)
+    used = vector_block.shape[1]
+    vector_block = jnp.pad(vector_block, ((0, 0), (0, 128 - used)))
+    wide_qkv, gathered = gather_blocks(
+        jnp.concatenate([query_key_value_weight, vector_block], 1),
+        me,
+        devices,
+        "split",
+        [(0, 3 * width), (3 * width, 128)],
+    )
+    wide_qkv = wide_qkv.reshape(width, 3 * width)
+    gathered = gathered[:, :, :used].reshape(devices, -1)
     full = []
     at = 0
     for size in sizes:
@@ -186,14 +308,24 @@
         gain_two,
         shift_two,
     ) = full
-    wide_out = gather_rows(output_weight)
-    wide_in = gather_rows(in_weight)
-    wide_down = gather_rows(down_weight)
-    cot = to_sequences(cotangent).reshape(rows, width)
+    inner_width = in_weight.shape[1]
+    wide_in, wide_out = gather_blocks(
+        jnp.concatenate([in_weight, output_weight], 1),
+        me,
+        devices,
+        "yx",
+        [(0, inner_width), (inner_width, width)],
+    )
+    wide_in = wide_in.reshape(width, inner_width)
+    wide_out = wide_out.reshape(width, width)
+    (wide_down,) = gather_blocks(down_weight, me, devices, "xy")
+    wide_down = wide_down.reshape(inner_width, width)
+    cot = to_sequences(cotangent, seat, members, devices)
     bias_vector = jnp.concatenate([full_query_bias, jnp.zeros((width,), F32), full_value_bias])
     packed = (jnp.dot(flat, wide_qkv, preferred_element_type=F32) + bias_vector).astype(BF)
-    mine = lax.dynamic_slice(lengths, (lax.axis_index("seq") * kept,), (kept,))
-    positions = jnp.arange(length, dtype=jnp.int32)
+    mine = lax.dynamic_slice(lengths, (seat * kept,), (kept,))
+    slots = jnp.arange(length, dtype=jnp.int32)
+    positions = ((slots // local_len) ^ seat) * local_len + slots % local_len
     mask = jnp.where(positions[None, :] < mine[:, None], 0.0, -1e30).astype(BF)
     mask = jnp.broadcast_to(mask[:, :, None], (kept, length, 128))
     mixed, logsum = attention_forward(packed, mask, length)
@@ -209,7 +341,9 @@
     result, norm_two_pull = jax.vjp(
         layer_norm, first_low.astype(F32) + branch_two, gain_two, shift_two
     )
-    outputs = to_positions(result.astype(BF).reshape(kept, length, width))
+    outputs = to_positions(
+        result.astype(BF).reshape(kept, members, local_len, width), seat, members, devices
+    )
     grad_second, grad_gain_two, grad_shift_two = norm_two_pull(cot.astype(F32))
     grad_branch_two = grad_second.astype(BF)
     grad_down = over_rows(active_low, grad_branch_two)
@@ -229,12 +363,11 @@
     )
     grad_packed = jnp.concatenate([grad_queries, grad_keys, grad_values], -1)
     grad_inputs = times_transposed(grad_packed, wide_qkv) + grad_residual
-    grad_inputs = to_positions(grad_inputs.astype(BF).reshape(kept, length, width))
+    grad_inputs = to_positions(
+        grad_inputs.astype(BF).reshape(kept, members, local_len, width), seat, members, devices
+    )
     grad_qkv = over_rows(flat, grad_packed)
     column_sums = jnp.sum(grad_packed.astype(F32), 0)
-
-    def scatter(total):
-        return lax.psum_scatter(total.astype(BF), BOTH, scatter_dimension=0, tiled=True).astype(F32)
 
     sums = (
         column_sums[:width],
@@ -248,7 +381,27 @@
         grad_shift_two,
     )
     joined = jnp.concatenate([v.reshape(devices, -1) for v in sums], 1)
-    joined = lax.psum_scatter(joined, BOTH, scatter_dimension=0, tiled=True)[0]
+    joined = jnp.pad(joined.reshape(devices, share, used), ((0, 0), (0, 0), (0, 128 - used)))
+    down_part = scatter_blocks(
+        grad_down.astype(BF).reshape(devices, -1, width), me, devices, "xy"
+    )
+    in_part = scatter_blocks(
+        jnp.concatenate([grad_in.astype(BF), grad_out.astype(BF)], 1).reshape(
+            devices, share, inner_width + width
+        ),
+        me,
+        devices,
+        "yx",
+    )
+    qkv_part = scatter_blocks(
+        jnp.concatenate(
+            [grad_qkv.astype(BF).reshape(devices, share, 3 * width), joined.astype(BF)], 2
+        ),
+        me,
+        devices,
+        "split",
+    )
+    joined = qkv_part[:, 3 * width : 3 * width + used].reshape(-1)
     parts = []
     at = 0
     for size in sizes:
@@ -257,16 +410,16 @@
     return (
         outputs,
         grad_inputs,
-        scatter(grad_qkv),
+        qkv_part[:, : 3 * width],
         parts[0],
         parts[1],
-        scatter(grad_out),
+        in_part[:, inner_width:],
         parts[2],
         parts[3],
         parts[4],
-        scatter(grad_in),
+        in_part[:, :inner_width],
         parts[5],
-        scatter(grad_down),
+        down_part,
         parts[6],
         parts[7],
         parts[8],

time: 754 us -> 1020 us (1.35)
  Pallas kernels: 42 us -> 579 us
  waiting for transfers between devices: 372 us -> 155 us
  blocking collectives: 130 us -> 0 us
  starting transfers between devices: 12 us -> 59.9 us
  local copies, waits for them, and re-layouts: 35.5 us -> 64.1 us
  other arithmetic: 16.6 us -> 38.3 us
  between operations: 15.2 us -> 2.09 us
    pallas_call x0 -> x5, Pallas kernels: none -> 537 us  [place(): pl.pallas_call(functools.partial(place_kernel, ids, counts, spans), in_sp...]
    reduce_scatter x3 -> x0, waiting for transfers between devices: 220 us -> none  [scatter(): lax.psum_scatter(total.astype(BF), BOTH, scatter_dimension=0, tiled=True)]
    ppermute x0 -> x57, waiting for transfers between devices: none -> 155 us  [swap(): lax.ppermute(block, BOTH, [(i, i ^ distance) for i in range(devices)])]
    unnamed x2 -> x0, blocking collectives: 104 us -> none
    all_gather x4 -> x0, waiting for transfers between devices: 91.7 us -> none  [gather_rows(): return lax.all_gather(block, BOTH, axis=0, tiled=True)]
    ppermute x0 -> x57, starting transfers between devices: none -> 59.9 us  [swap(): lax.ppermute(block, BOTH, [(i, i ^ distance) for i in range(devices)])]
    unnamed x9 -> x0, waiting for transfers between devices: 50.2 us -> none
    all_to_all x1 -> x0, blocking collectives: 25.3 us -> none  [to_sequences(): return lax.all_to_all(block, 'seq', 0, 1, tiled=True)]
  transfers between devices with their start and end apart: 11 -> 57, of which waited for: 7 -> 16; matrix products, arithmetic and copies ran while one was open for 16% -> 9% of each run, Pallas kernels for 6% -> 37%
where the time goes in v2:
time: 1020 us
  Pallas kernels  579 us (57%)
  waiting for transfers between devices  155 us (15%)
  matrix products  118 us (12%)
  local copies, waits for them, and re-layouts  64.1 us (6%)
  starting transfers between devices  59.9 us (6%)
  other arithmetic  38.3 us (4%)
    pallas_call x5, Pallas kernels, place(): pl.pallas_call(functools.partial(place_kernel, ids, counts, spans), in_sp...  537 us
    ppermute x57, waiting for transfers between devices, swap(): lax.ppermute(block, BOTH, [(i, i ^ distance) for i in range(devices)])  155 us
    ppermute x57, starting transfers between devices, swap(): lax.ppermute(block, BOTH, [(i, i ^ distance) for i in range(devices)])  59.9 us
    dot_general x4, matrix products, times_transposed(): lax.dot_general(left, right, (((1,), (1,)), ((), ())), preferred_element_...  39.2 us
    dot_general x1, matrix products, on_device(): jnp.dot(first_low, wide_in, preferred_element_type=F32) + full_in_bias  35.4 us
    dot_general x4, matrix products, over_rows(): lax.dot_general(left, right, (((0,), (0,)), ((), ())), preferred_element_...  26.5 us
    pallas_call x1, Pallas kernels, attention_backward(): pl.pallas_call(functools.partial(bwd_kernel, cq), grid=(seqs, pairs), in_...  24.8 us
  transfers between devices with their start and end apart: 57, of which 16 were waited for; matrix products, arithmetic and copies ran while one was open for 9% of the time, Pallas kernels for 37%

profile of v2, /device:TPU:0, one launch (start us, length us, event | category | flops | bytes accessed | tf_op | source)
XLA Modules:
  0.0 1017.5 jit_solution(15328916613484887204)
XLA Ops:
  0.7 6.2 concatenate.58
  40.8 8.1 collective-permute-done.22
  56.0 34.7 %collective-permute-done.17 = bf16[4,24,3840]{2,1,0:T(8,128)(2,1)S(1)} collective-permute-done((bf16[4,24,3840]{2,1,0:T(8,128)(2,1)S(1)}, bf16[4,24,3840]{2,1,0:T(8,128)(2,1)S(1)}, u32[]{:S(2)}, u32[]{:S(2)}) %collective-permute-start.17) | collective-permute-done | bytes 737312 | tf_op jit(solution)/shard_map/ppermute | solution.py:122
  110.1 5.9 collective-permute-done.24
  120.0 35.3 %collective-permute-done.12.refs_6_ = bf16[4,24,2432]{2,1,0:T(8,128)(2,1)} collective-permute-done((bf16[4,24,2432]{2,1,0:T(8,128)(2,1)}, bf16[4,24,2432]{2,1,0:T(8,128)(2,1)}, u32[]{:S(2)}, u32[]{:S(2)}) %collective-permute-start.12) | collective-permute-done | bytes 466976 | tf_op jit(solution)/shard_map/ppermute | solution.py:122
  161.1 114.9 %place_blocks.5 = (bf16[32,24,2304]{2,1,0:T(8,128)(2,1)}, bf16[32,24,128]{2,1,0:T(8,128)(2,1)}) custom-call(s32[1]{0:T(128)} %bitcast.10.me_ref, bf16[4,24,2432]{2,1,0:T(8,128)(2,1)} %copy-done.14, bf16[4,24,2432]{2,1,0:T(8,128)(2,1)} %collective-permute-done.5.refs_1_, bf16[4,24,2432]{2,1,0:T(8,128)(2,1)} %collective-permute-done.6.refs_2_, ...), custom_call_target="tpu_custom_call" | custom-call | tf_op jit(solution)/shard_map/place_blocks/pallas_call | solution.py:150
  280.1 8.4 add_convert_fusion.1.q_ref.k_ref.v_ref
  288.7 17.5 %attention_forward.1 = (bf16[1024,768]{1,0:T(8,128)(2,1)S(1)}, f32[12,2,512]{2,1,0:T(2,128)S(1)}) custom-call(bf16[1024,2304]{1,0:T(8,128)(2,1)} %add_convert_fusion.1.q_ref.k_ref.v_ref, bf16[1024,2304]{1,0:T(8,128)(2,1)} %add_convert_fusion.1.q_ref.k_ref.v_ref, bf16[1024,2304]{1,0:T(8,128)(2,1)} %add_convert_fusion.1.q_ref.k_ref.v_ref, ...), custom_call_target="tpu_custom_call" | custom-call | flops 1610612736 | bytes 6291456 | tf_op jit(solution)/shard_map/attention_forward/pallas_call | solution.py:105
  306.2 144.3 %place_blocks.7 = bf16[32,96,768]{2,1,0:T(8,128)(2,1)} custom-call(s32[1]{0:T(128)} %bitcast.10.me_ref, bf16[8,96,768]{2,1,0:T(8,128)(2,1)} %constant_dynamic-update-slice_fusion.8.refs_0_, bf16[8,96,768]{2,1,0:T(8,128)(2,1)} %collective-permute-done.25.refs_1_, bf16[8,96,768]{2,1,0:T(8,128)(2,1)} %collective-permute-done.26.refs_2_, ...), custom_call_target="tpu_custom_call" | custom-call | tf_op jit(solution)/shard_map/place_blocks/pallas_call | solution.py:150
  450.6 180.4 %place_blocks.6 = (bf16[32,24,3072]{2,1,0:T(8,128)(2,1)}, bf16[32,24,768]{2,1,0:T(8,128)(2,1)}) custom-call(s32[1]{0:T(128)} %bitcast.10.me_ref, bf16[8,24,3840]{2,1,0:T(8,128)(2,1)} %constant_dynamic-update-slice_fusion.3.refs_0_, bf16[8,24,3840]{2,1,0:T(8,128)(2,1)} %collective-permute-done.18.refs_1_, ...), custom_call_target="tpu_custom_call" | custom-call | tf_op jit(solution)/shard_map/place_blocks/pallas_call | solution.py:150
  635.1 35.4 %multiply_convert_fusion = (bf16[1024,3072]{1,0:T(8,128)(2,1)S(1)}, f32[1024,3072]{1,0:T(8,128)}, f32[1024,3072]{1,0:T(8,128)}) fusion(f32[3072]{0:T(1024)S(1)} %reshape.408, bf16[768,3072]{1,0:T(8,128)(2,1)S(1)} %bitcast.248, f32[1024,768]{1,0:T(8,128)S(1)} %get-tuple-element.95, f32[768]{0:T(1024)S(1)} %reshape.407, f32[768]{0:T(1024)S(1)} %reshape.406, ...), kind=kOutput, calls=%fused_computation.3 | convolution fusion | flops 5043388416 | bytes 39348224 | tf_op jit(solution)/shard_map/dot_general | solution.py:337
  683.7 6.9 convolution_convert_fusion
  690.6 19.1 %fusion.57 = (bf16[3072]{0:T(1024)(128)(2,1)}, bf16[1024,3072]{1,0:T(8,128)(2,1)}) fusion(f32[1024,3072]{1,0:T(8,128)} %get-tuple-element.47, bf16[1024,768]{1,0:T(8,128)(2,1)} %copy-done.16, bf16[3072,768]{1,0:T(8,128)(2,1)} %bitcast.221, f32[1024,3072]{1,0:T(8,128)} %get-tuple-element.96, f32[3072]{0:T(1024)S(1)} %reshape.408), kind=kOutput, calls=%fused_computation.185 | convolution fusion | flops 4882166784 | bytes 37767168 | tf_op jit(solution)/shard_map/dot_general | solution.py:33
  709.7 10.1 multiply_reduce_fusion
  729.0 24.8 %attention_backward.1 = (bf16[1024,768]{1,0:T(8,128)(2,1)S(1)}, bf16[1024,768]{1,0:T(8,128)(2,1)S(1)}, bf16[1024,768]{1,0:T(8,128)(2,1)S(1)}) custom-call(bf16[1024,2304]{1,0:T(8,128)(2,1)} %add_convert_fusion.1.q_ref.k_ref.v_ref, bf16[1024,2304]{1,0:T(8,128)(2,1)} %add_convert_fusion.1.q_ref.k_ref.v_ref, ...), custom_call_target="tpu_custom_call" | custom-call | flops 4026531840 | bytes 11010048 | tf_op jit(solution)/shard_map/attention_backward/pallas_call | solution.py:116
  761.4 6.8 convolution_convert_fusion.2
  768.3 7.4 add_convert_fusion.2
  798.4 10.2 %convolution_convert_fusion.1 = bf16[768,3072]{1,0:T(8,128)(2,1)} fusion(bf16[1024,3072]{1,0:T(8,128)(2,1)} %get-tuple-element.101, f32[1024,768]{1,0:T(8,128)S(1)} %copy-done.6, f32[768]{0:T(1024)S(1)} %copy-done.38, f32[768]{0:T(1024)S(1)} %reshape.406, f32[1024]{0:T(1024)S(1)} %copy-done.36, f32[1024]{0:T(1024)S(1)} %broadcast_multiply_fusion.1), kind=kOutput, calls=%fused_computation.22 | convolution fusion | flops 4838129664 | bytes 14170112 | tf_op jit(solution)/shard_map/dot_general | solution.py:27
  822.2 6.3 collective-permute-done.29.refs_2_
  829.3 48.8 %place_blocks.9 = bf16[4,2,128,768]{3,2,1,0:T(8,128)(2,1)} custom-call(s32[1]{0:T(128)} %bitcast.me_ref, bf16[1,2,128,768]{3,2,1,0:T(8,128)(2,1)} %get-tuple-element.59.refs_0_, bf16[1,2,128,768]{3,2,1,0:T(8,128)(2,1)} %collective-permute-done.34.refs_1_, bf16[1,2,128,768]{3,2,1,0:T(8,128)(2,1)} %collective-permute-done.35.refs_2_, ...), custom_call_target="tpu_custom_call" | custom-call | tf_op jit(solution)/shard_map/place_blocks/pallas_call | solution.py:150
  878.1 48.8 %place_blocks.8 = bf16[4,2,128,768]{3,2,1,0:T(8,128)(2,1)} custom-call(s32[1]{0:T(128)} %bitcast.me_ref, bf16[1,2,128,768]{3,2,1,0:T(8,128)(2,1)} %get-tuple-element.63.refs_0_, bf16[1,2,128,768]{3,2,1,0:T(8,128)(2,1)} %copy-done.29, bf16[1,2,128,768]{3,2,1,0:T(8,128)(2,1)} %copy-done.30, bf16[1,2,128,768]{3,2,1,0:T(8,128)(2,1)} %collective-permute-done.30.refs_3_), custom_call_target="tpu_custom_call" | custom-call | tf_op jit(solution)/shard_map/place_blocks/pallas_call | solution.py:150
  943.3 17.6 %collective-permute-done.52 = bf16[4,2,96,768]{3,2,1,0:T(8,128)(2,1)S(1)} collective-permute-done((bf16[4,2,96,768]{3,2,1,0:T(8,128)(2,1)S(1)}, bf16[4,2,96,768]{3,2,1,0:T(8,128)(2,1)S(1)}, u32[]{:S(2)}, u32[]{:S(2)}) %collective-permute-start.52) | collective-permute-done | bytes 1179680 | tf_op jit(solution)/shard_map/ppermute | solution.py:122
  963.7 9.7 collective-permute-done.46
  1001.9 13.6 %collective-permute-done.49 = bf16[24,3840]{1,0:T(8,128)(2,1)S(1)} collective-permute-done((bf16[24,3840]{1,0:T(8,128)(2,1)S(1)}, bf16[24,3840]{1,0:T(8,128)(2,1)S(1)}, u32[]{:S(2)}, u32[]{:S(2)}) %collective-permute-start.49) | collective-permute-done | bytes 184352 | tf_op jit(solution)/shard_map/ppermute | solution.py:122
  (354 shorter events, 194.2 us)
Async XLA Ops:
  14.5 37.0 %collective-permute-start.14 = (bf16[1,24,3840]{2,1,0:T(8,128)(2,1)S(1)}, bf16[1,24,3840]{2,1,0:T(8,128)(2,1)S(1)}, u32[]{:S(2)}, u32[]{:S(2)}) collective-permute-start(bf16[1,24,3840]{2,1,0:T(8,128)(2,1)S(1)} %maximum_bitcast_fusion), channel_id=1, source_target_pairs={{0,8},{1,9},{2,10},{3,11},{4,12},{5,13},{6,14},{7,15},{8,0},{9,1},... | collective-permute-start | bytes 552968 | tf_op jit(solution)/shard_map/ppermute | solution.py:122
  16.4 35.3 %collective-permute-start.15 = (bf16[1,24,3840]{2,1,0:T(8,128)(2,1)S(1)}, bf16[1,24,3840]{2,1,0:T(8,128)(2,1)S(1)}, u32[]{:S(2)}, u32[]{:S(2)}) collective-permute-start(bf16[1,24,3840]{2,1,0:T(8,128)(2,1)S(1)} %maximum_bitcast_fusion), channel_id=1, source_target_pairs={{0,16},{1,17},{2,18},{3,19},{4,20},{5,21},{6,22},{7,23},{8,24},{9,... | collective-permute-start | bytes 552968 | tf_op jit(solution)/shard_map/ppermute | solution.py:122
  48.9 50.8 %collective-permute-start = (bf16[2,128,768]{2,1,0:T(8,128)(2,1)}, bf16[2,128,768]{2,1,0:T(8,128)(2,1)}, u32[]{:S(2)}, u32[]{:S(2)}) collective-permute-start(bf16[2,128,768]{2,1,0:T(8,128)(2,1)} %get-tuple-element.67), channel_id=1, source_target_pairs={{0,1},{1,0},{2,3},{3,2},{4,5},{5,4},{6,7},{7,6},{8,9},{9,8},{10,11... | collective-permute-start | bytes 1179656 | tf_op jit(solution)/shard_map/ppermute | solution.py:122
  49.6 51.7 %collective-permute-start.1 = (bf16[2,128,768]{2,1,0:T(8,128)(2,1)}, bf16[2,128,768]{2,1,0:T(8,128)(2,1)S(1)}, u32[]{:S(2)}, u32[]{:S(2)}) collective-permute-start(bf16[2,128,768]{2,1,0:T(8,128)(2,1)} %get-tuple-element.66), channel_id=1, source_target_pairs={{0,2},{1,3},{2,0},{3,1},{4,6},{5,7},{6,4},{7,5},{8,10},{9,11},{10,... | collective-permute-start | bytes 1179656 | tf_op jit(solution)/shard_map/ppermute | solution.py:122
  51.5 50.3 %collective-permute-start.2 = (bf16[2,128,768]{2,1,0:T(8,128)(2,1)}, bf16[2,128,768]{2,1,0:T(8,128)(2,1)S(1)}, u32[]{:S(2)}, u32[]{:S(2)}) collective-permute-start(bf16[2,128,768]{2,1,0:T(8,128)(2,1)} %get-tuple-element.65), channel_id=1, source_target_pairs={{0,3},{1,2},{2,1},{3,0},{4,7},{5,6},{6,5},{7,4},{8,11},{9,10},{10,... | collective-permute-start | bytes 1179656 | tf_op jit(solution)/shard_map/ppermute | solution.py:122
  51.7 41.6 %collective-permute-start.10 = (bf16[2,24,2432]{2,1,0:T(8,128)(2,1)S(1)}, bf16[2,24,2432]{2,1,0:T(8,128)(2,1)S(1)}, u32[]{:S(2)}, u32[]{:S(2)}) collective-permute-start(bf16[2,24,2432]{2,1,0:T(8,128)(2,1)S(1)} %pad_maximum_fusion.7), channel_id=1, source_target_pairs={{0,2},{1,3},{2,0},{3,1},{4,6},{5,7},{6,4},{7,5},{8,10},{9,11},{10,... | collective-permute-start | bytes 700424 | tf_op jit(solution)/shard_map/ppermute | solution.py:122
  53.5 37.1 %collective-permute-start.17 = (bf16[4,24,3840]{2,1,0:T(8,128)(2,1)S(1)}, bf16[4,24,3840]{2,1,0:T(8,128)(2,1)S(1)}, u32[]{:S(2)}, u32[]{:S(2)}) collective-permute-start(bf16[4,24,3840]{2,1,0:T(8,128)(2,1)S(1)} %pad_maximum_fusion.3), channel_id=1, source_target_pairs={{0,2},{1,3},{2,0},{3,1},{4,6},{5,7},{6,4},{7,5},{8,10},{9,11},{10,... | collective-permute-start | bytes 2211848 | tf_op jit(solution)/shard_map/ppermute | solution.py:122
  101.2 175.8 %collective-permute-start.19 = (bf16[8,24,3840]{2,1,0:T(8,128)(2,1)}, bf16[8,24,3840]{2,1,0:T(8,128)(2,1)}, u32[]{:S(2)}, u32[]{:S(2)}) collective-permute-start(bf16[8,24,3840]{2,1,0:T(8,128)(2,1)} %constant_dynamic-update-slice_fusion.3.refs_0_), channel_id=1, source_target_pairs={{0,4},{1,5},{2,6},{3,7},{4,0},{5,1},{6,2},{7,3},{8,12},{9,13},{10,... | collective-permute-start | bytes 4423688 | tf_op jit(solution)/shard_map/ppermute | solution.py:122
  102.8 52.5 %collective-permute-start.12 = (bf16[4,24,2432]{2,1,0:T(8,128)(2,1)}, bf16[4,24,2432]{2,1,0:T(8,128)(2,1)}, u32[]{:S(2)}, u32[]{:S(2)}) collective-permute-start(bf16[4,24,2432]{2,1,0:T(8,128)(2,1)} %constant_dynamic-update-slice_fusion.refs_4_), channel_id=1, source_target_pairs={{0,4},{1,5},{2,6},{3,7},{4,0},{5,1},{6,2},{7,3},{8,12},{9,13},{10,... | collective-permute-start | bytes 1400840 | tf_op jit(solution)/shard_map/ppermute | solution.py:122
  110.1 45.2 %collective-permute-start.11 = (bf16[4,24,2432]{2,1,0:T(8,128)(2,1)}, bf16[4,24,2432]{2,1,0:T(8,128)(2,1)S(1)}, u32[]{:S(2)}, u32[]{:S(2)}) collective-permute-start(bf16[4,24,2432]{2,1,0:T(8,128)(2,1)} %constant_dynamic-update-slice_fusion.refs_4_), channel_id=1, source_target_pairs={{0,1},{1,0},{2,3},{3,2},{4,5},{5,4},{6,7},{7,6},{8,9},{9,8},{10,11... | collective-permute-start | bytes 1400840 | tf_op jit(solution)/shard_map/ppermute | solution.py:122
  116.0 39.8 %collective-permute-start.6 = (bf16[4,24,2432]{2,1,0:T(8,128)(2,1)S(1)}, bf16[4,24,2432]{2,1,0:T(8,128)(2,1)}, u32[]{:S(2)}, u32[]{:S(2)}) collective-permute-start(bf16[4,24,2432]{2,1,0:T(8,128)(2,1)S(1)} %pad_maximum_fusion.5.refs_0_), channel_id=1, source_target_pairs={{0,2},{1,3},{2,0},{3,1},{4,6},{5,7},{6,4},{7,5},{8,10},{9,11},{10,... | collective-permute-start | bytes 1400840 | tf_op jit(solution)/shard_map/ppermute | solution.py:122
  117.9 162.0 %collective-permute-start.26 = (bf16[8,96,768]{2,1,0:T(8,128)(2,1)}, bf16[8,96,768]{2,1,0:T(8,128)(2,1)}, u32[]{:S(2)}, u32[]{:S(2)}) collective-permute-start(bf16[8,96,768]{2,1,0:T(8,128)(2,1)} %constant_dynamic-update-slice_fusion.8.refs_0_), channel_id=1, source_target_pairs={{0,2},{1,3},{2,0},{3,1},{4,6},{5,7},{6,4},{7,5},{8,10},{9,11},{10,... | collective-permute-start | bytes 3538952 | tf_op jit(solution)/shard_map/ppermute | solution.py:122
  160.5 145.8 %collective-permute-start.25 = (bf16[8,96,768]{2,1,0:T(8,128)(2,1)}, bf16[8,96,768]{2,1,0:T(8,128)(2,1)}, u32[]{:S(2)}, u32[]{:S(2)}) collective-permute-start(bf16[8,96,768]{2,1,0:T(8,128)(2,1)} %constant_dynamic-update-slice_fusion.8.refs_0_), channel_id=1, source_target_pairs={{0,1},{1,0},{2,3},{3,2},{4,5},{5,4},{6,7},{7,6},{8,9},{9,8},{10,11... | collective-permute-start | bytes 3538952 | tf_op jit(solution)/shard_map/ppermute | solution.py:122
  161.0 289.6 %collective-permute-start.18 = (bf16[8,24,3840]{2,1,0:T(8,128)(2,1)}, bf16[8,24,3840]{2,1,0:T(8,128)(2,1)}, u32[]{:S(2)}, u32[]{:S(2)}) collective-permute-start(bf16[8,24,3840]{2,1,0:T(8,128)(2,1)} %constant_dynamic-update-slice_fusion.3.refs_0_), channel_id=1, source_target_pairs={{0,1},{1,0},{2,3},{3,2},{4,5},{5,4},{6,7},{7,6},{8,9},{9,8},{10,11... | collective-permute-start | bytes 4423688 | tf_op jit(solution)/shard_map/ppermute | solution.py:122
  277.0 173.5 %collective-permute-start.20 = (bf16[8,24,3840]{2,1,0:T(8,128)(2,1)}, bf16[8,24,3840]{2,1,0:T(8,128)(2,1)}, u32[]{:S(2)}, u32[]{:S(2)}) collective-permute-start(bf16[8,24,3840]{2,1,0:T(8,128)(2,1)} %collective-permute-done.19.refs_2_), channel_id=1, source_target_pairs={{0,1},{1,0},{2,3},{3,2},{4,5},{5,4},{6,7},{7,6},{8,9},{9,8},{10,11... | collective-permute-start | bytes 4423688 | tf_op jit(solution)/shard_map/ppermute | solution.py:122
  777.3 152.1 %collective-permute-start.51 = (bf16[16,96,768]{2,1,0:T(8,128)(2,1)}, bf16[16,96,768]{2,1,0:T(8,128)(2,1)}, u32[]{:S(2)}, u32[]{:S(2)}) collective-permute-start(bf16[16,96,768]{2,1,0:T(8,128)(2,1)} %dynamic-slice_bitcast_fusion.1), channel_id=1, source_target_pairs={{0,1},{1,0},{2,3},{3,2},{4,5},{5,4},{6,7},{7,6},{8,9},{9,8},{10,11... | collective-permute-start | bytes 7077896 | tf_op jit(solution)/shard_map/ppermute | solution.py:122
  817.0 61.1 %collective-permute-start.30 = (bf16[1,2,128,768]{3,2,1,0:T(8,128)(2,1)}, bf16[1,2,128,768]{3,2,1,0:T(8,128)(2,1)}, u32[]{:S(2)}, u32[]{:S(2)}) collective-permute-start(bf16[1,2,128,768]{3,2,1,0:T(8,128)(2,1)} %get-tuple-element.60), channel_id=1, source_target_pairs={{0,3},{1,2},{2,1},{3,0},{4,7},{5,6},{6,5},{7,4},{8,11},{9,10},{10,... | collective-permute-start | bytes 1179656 | tf_op jit(solution)/shard_map/ppermute | solution.py:122
  818.4 108.5 %collective-permute-start.41 = (bf16[2,2,24,2432]{3,2,1,0:T(8,128)(2,1)}, bf16[2,2,24,2432]{3,2,1,0:T(8,128)(2,1)S(1)}, u32[]{:S(2)}, u32[]{:S(2)}) collective-permute-start(bf16[2,2,24,2432]{3,2,1,0:T(8,128)(2,1)} %dynamic-slice_bitcast_fusion.6), channel_id=1, source_target_pairs={{0,2},{1,3},{2,0},{3,1},{4,6},{5,7},{6,4},{7,5},{8,10},{9,11},{10,... | collective-permute-start | bytes 1400840 | tf_op jit(solution)/shard_map/ppermute | solution.py:122
  818.7 108.2 %collective-permute-start.38 = (bf16[2,2,24,2432]{3,2,1,0:T(8,128)(2,1)S(1)}, bf16[2,2,24,2432]{3,2,1,0:T(8,128)(2,1)S(1)}, u32[]{:S(2)}, u32[]{:S(2)}) collective-permute-start(bf16[2,2,24,2432]{3,2,1,0:T(8,128)(2,1)S(1)} %dynamic-slice_bitcast_fusion.7), channel_id=1, source_target_pairs={{0,4},{1,5},{2,6},{3,7},{4,0},{5,1},{6,2},{7,3},{8,12},{9,13},{10,... | collective-permute-start | bytes 1400840 | tf_op jit(solution)/shard_map/ppermute | solution.py:122
  829.3 106.2 %collective-permute-start.45 = (bf16[16,24,3840]{2,1,0:T(8,128)(2,1)}, bf16[16,24,3840]{2,1,0:T(8,128)(2,1)}, u32[]{:S(2)}, u32[]{:S(2)}) collective-permute-start(bf16[16,24,3840]{2,1,0:T(8,128)(2,1)} %dynamic-slice_bitcast_fusion), channel_id=1, source_target_pairs={{0,1},{1,0},{2,3},{3,2},{4,5},{5,4},{6,7},{7,6},{8,9},{9,8},{10,11... | collective-permute-start | bytes 8847368 | tf_op jit(solution)/shard_map/ppermute | solution.py:122
  938.2 35.3 %collective-permute-start.46 = (bf16[4,2,24,3840]{3,2,1,0:T(8,128)(2,1)S(1)}, bf16[4,2,24,3840]{3,2,1,0:T(8,128)(2,1)S(1)}, u32[]{:S(2)}, u32[]{:S(2)}) collective-permute-start(bf16[4,2,24,3840]{3,2,1,0:T(8,128)(2,1)S(1)} %dynamic-slice_bitcast_fusion.2), channel_id=1, source_target_pairs={{0,2},{1,3},{2,0},{3,1},{4,6},{5,7},{6,4},{7,5},{8,10},{9,11},{10,... | collective-permute-start | bytes 4423688 | tf_op jit(solution)/shard_map/ppermute | solution.py:122
  938.7 37.6 %collective-permute-start.40 = (bf16[24,2432]{1,0:T(8,128)(2,1)S(1)}, bf16[24,2432]{1,0:T(8,128)(2,1)S(1)}, u32[]{:S(2)}, u32[]{:S(2)}) collective-permute-start(bf16[24,2432]{1,0:T(8,128)(2,1)S(1)} %dynamic-slice_bitcast_fusion.26), channel_id=1, source_target_pairs={{0,8},{1,9},{2,10},{3,11},{4,12},{5,13},{6,14},{7,15},{8,0},{9,1},... | collective-permute-start | bytes 350216 | tf_op jit(solution)/shard_map/ppermute | solution.py:122
  939.3 37.0 %collective-permute-start.43 = (bf16[24,2432]{1,0:T(8,128)(2,1)S(1)}, bf16[24,2432]{1,0:T(8,128)(2,1)S(1)}, u32[]{:S(2)}, u32[]{:S(2)}) collective-permute-start(bf16[24,2432]{1,0:T(8,128)(2,1)S(1)} %get-tuple-element.82), channel_id=1, source_target_pairs={{0,16},{1,17},{2,18},{3,19},{4,20},{5,21},{6,22},{7,23},{8,24},{9,... | collective-permute-start | bytes 350216 | tf_op jit(solution)/shard_map/ppermute | solution.py:122
  942.0 34.2 %collective-permute-start.44 = (bf16[24,2432]{1,0:T(8,128)(2,1)S(1)}, bf16[24,2432]{1,0:T(8,128)(2,1)S(1)}, u32[]{:S(2)}, u32[]{:S(2)}) collective-permute-start(bf16[24,2432]{1,0:T(8,128)(2,1)S(1)} %get-tuple-element.83), channel_id=1, source_target_pairs={{0,24},{1,25},{2,26},{3,27},{4,28},{5,29},{6,30},{7,31},{8,16},{9,... | collective-permute-start | bytes 350216 | tf_op jit(solution)/shard_map/ppermute | solution.py:122
  (83 other events, 2177.2 us)

commit v3 on v2

--- a/solution.py
+++ b/solution.py
@@ -150,12 +150,13 @@
     return pl.pallas_call(
         functools.partial(place_kernel, ids, counts, spans),
         in_specs=[pl.BlockSpec(memory_space=pltpu.SMEM)] + [any_space] * len(pieces),
-        out_specs=[any_space] * len(spans),
+        out_specs=[pl.BlockSpec(memory_space=pltpu.VMEM)] * len(spans),
         out_shape=[
             jax.ShapeDtypeStruct((total,) + tail[:-1] + (size,), pieces[0].dtype)
             for _, size in spans
         ],
         scratch_shapes=[pltpu.SemaphoreType.DMA((total * len(spans),))],
+        compiler_params=pltpu.CompilerParams(vmem_limit_bytes=32 * 2**20),
         name="place_blocks",
     )(me.reshape(1), *pieces)
 

time: 1020 us -> 515 us (0.50)
  Pallas kernels: 579 us -> 55.7 us
  waiting for transfers between devices: 155 us -> 169 us
    pallas_call x5, Pallas kernels: 537 us -> 13.4 us  [place(): pl.pallas_call(functools.partial(place_kernel, ids, counts, spans), in_sp...]
    ppermute x57, waiting for transfers between devices: 155 us -> 169 us  [swap(): lax.ppermute(block, BOTH, [(i, i ^ distance) for i in range(devices)])]
  transfers between devices with their start and end apart: 57 -> 57, of which waited for: 16 -> 17; matrix products, arithmetic and copies ran while one was open for 9% -> 17% of each run, Pallas kernels for 37% -> 5%
where the time goes in v3:
time: 515 us; the launch traced here: 510 us
  waiting for transfers between devices  169 us (33%)
  matrix products  117 us (23%)
  starting transfers between devices  62.5 us (12%)
  local copies, waits for them, and re-layouts  61.6 us (12%)
  Pallas kernels  55.7 us (11%)
  other arithmetic  42.8 us (8%)
    ppermute x57, waiting for transfers between devices, swap(): lax.ppermute(block, BOTH, [(i, i ^ distance) for i in range(devices)])  169 us
    ppermute x57, starting transfers between devices, swap(): lax.ppermute(block, BOTH, [(i, i ^ distance) for i in range(devices)])  62.5 us
    dot_general x4, matrix products, times_transposed(): lax.dot_general(left, right, (((1,), (1,)), ((), ())), preferred_element_...  39.7 us
    dot_general x1, matrix products, on_device(): jnp.dot(first_low, wide_in, preferred_element_type=F32) + full_in_bias  35.2 us
    dot_general x4, matrix products, over_rows(): lax.dot_general(left, right, (((0,), (0,)), ((), ())), preferred_element_...  26.4 us
    pallas_call x1, Pallas kernels, attention_backward(): pl.pallas_call(functools.partial(bwd_kernel, cq), grid=(seqs, pairs), in_...  24.9 us
    pallas_call x1, Pallas kernels, attention_forward(): pl.pallas_call(functools.partial(fwd_kernel, cq), grid=(seqs, pairs), in_...  17.3 us
    unnamed x121, local copies, waits for them, and re-layouts  14.4 us
  transfers between devices with their start and end apart: 57, of which 17 were waited for; matrix products, arithmetic and copies ran while one was open for 17% of the time, Pallas kernels for 5%

profile of v3, /device:TPU:0, one launch (start us, length us, event | category | flops | bytes accessed | tf_op | source)
XLA Modules:
  0.0 509.7 jit_solution(7923317167344135522)
XLA Ops:
  0.6 6.1 %concatenate.58 = bf16[288]{0:T(512)(128)(2,1)S(1)} concatenate(bf16[24]{0:T(256)(128)(2,1)} %param.19, bf16[24]{0:T(256)(128)(2,1)} %param.20, bf16[24]{0:T(256)(128)(2,1)} %param.22, bf16[24]{0:T(256)(128)(2,1)} %param.23, bf16[24]{0:T(256)(128)(2,1)} %param.24, bf16[96]{0:T(256)(128)(2,1)} %param.26, bf16[24]{0:T(256)(128)(2,1)} %param.28, bf16[24]{0:T(256)(128)(2,1)} %param.29, ...), dimensions={0} | concatenate | bytes 1152 | tf_op jit(solution)/shard_map/concatenate | solution.py:284
  29.1 7.3 %collective-permute-done.21 = bf16[1,96,768]{2,1,0:T(8,128)(2,1)S(1)} collective-permute-done((bf16[1,96,768]{2,1,0:T(8,128)(2,1)S(1)}, bf16[1,96,768]{2,1,0:T(8,128)(2,1)S(1)}, u32[]{:S(2)}, u32[]{:S(2)}) %collective-permute-start.21) | collective-permute-done | bytes 147488 | tf_op jit(solution)/shard_map/ppermute | solution.py:122
  40.6 8.1 %collective-permute-done.22 = bf16[1,96,768]{2,1,0:T(8,128)(2,1)S(1)} collective-permute-done((bf16[1,96,768]{2,1,0:T(8,128)(2,1)S(1)}, bf16[1,96,768]{2,1,0:T(8,128)(2,1)S(1)}, u32[]{:S(2)}, u32[]{:S(2)}) %collective-permute-start.22) | collective-permute-done | bytes 147488 | tf_op jit(solution)/shard_map/ppermute | solution.py:122
  53.8 36.7 %collective-permute-done.17 = bf16[4,24,3840]{2,1,0:T(8,128)(2,1)S(1)} collective-permute-done((bf16[4,24,3840]{2,1,0:T(8,128)(2,1)S(1)}, bf16[4,24,3840]{2,1,0:T(8,128)(2,1)S(1)}, u32[]{:S(2)}, u32[]{:S(2)}) %collective-permute-start.17) | collective-permute-done | bytes 737312 | tf_op jit(solution)/shard_map/ppermute | solution.py:122
  92.4 5.5 %collective-permute-done.4 = bf16[2,24,2432]{2,1,0:T(8,128)(2,1)S(1)} collective-permute-done((bf16[2,24,2432]{2,1,0:T(8,128)(2,1)S(1)}, bf16[2,24,2432]{2,1,0:T(8,128)(2,1)S(1)}, u32[]{:S(2)}, u32[]{:S(2)}) %collective-permute-start.4) | collective-permute-done | bytes 233504 | tf_op jit(solution)/shard_map/ppermute | solution.py:122
  103.4 6.5 %collective-permute-done.32 = bf16[2,128,768]{2,1,0:T(8,128)(2,1)S(1)} collective-permute-done((bf16[2,128,768]{2,1,0:T(8,128)(2,1)S(1)}, bf16[2,128,768]{2,1,0:T(8,128)(2,1)S(1)}, u32[]{:S(2)}, u32[]{:S(2)}) %collective-permute-start.32) | collective-permute-done | bytes 393248 | tf_op jit(solution)/shard_map/ppermute | solution.py:122
  122.7 32.3 %collective-permute-done.12.refs_6_ = bf16[4,24,2432]{2,1,0:T(8,128)(2,1)S(1)} collective-permute-done((bf16[4,24,2432]{2,1,0:T(8,128)(2,1)S(1)}, bf16[4,24,2432]{2,1,0:T(8,128)(2,1)S(1)}, u32[]{:S(2)}, u32[]{:S(2)}) %collective-permute-start.12) | collective-permute-done | bytes 466976 | tf_op jit(solution)/shard_map/ppermute | solution.py:122
  171.7 8.4 %add_convert_fusion.1.q_ref.k_ref.v_ref = bf16[1024,2304]{1,0:T(8,128)(2,1)} fusion(bf16[1024,768]{1,0:T(8,128)(2,1)} %bitcast.233, bf16[768,2304]{1,0:T(8,128)(2,1)} %bitcast.208, f32[2304]{0:T(1024)S(1)} %pad_maximum_fusion.8), kind=kOutput, calls=%fused_computation.17 | convolution fusion | flops 3628597248 | bytes 9839616 | tf_op jit(solution)/shard_map/dot_general | solution.py:326
  180.4 17.3 %attention_forward.1 = (bf16[1024,768]{1,0:T(8,128)(2,1)S(1)}, f32[12,2,512]{2,1,0:T(2,128)S(1)}) custom-call(bf16[1024,2304]{1,0:T(8,128)(2,1)} %add_convert_fusion.1.q_ref.k_ref.v_ref, bf16[1024,2304]{1,0:T(8,128)(2,1)} %add_convert_fusion.1.q_ref.k_ref.v_ref, bf16[1024,2304]{1,0:T(8,128)(2,1)} %add_convert_fusion.1.q_ref.k_ref.v_ref, ...), custom_call_target="tpu_custom_call" | custom-call | flops 1610612736 | bytes 6291456 | tf_op jit(solution)/shard_map/attention_forward/pallas_call | solution.py:105
  206.5 35.2 %multiply_convert_fusion = (bf16[1024,3072]{1,0:T(8,128)(2,1)S(1)}, f32[1024,3072]{1,0:T(8,128)}, f32[1024,3072]{1,0:T(8,128)}) fusion(f32[3072]{0:T(1024)S(1)} %reshape.408, bf16[768,3072]{1,0:T(8,128)(2,1)S(1)} %bitcast.206, f32[1024,768]{1,0:T(8,128)S(1)} %get-tuple-element.95, f32[768]{0:T(1024)S(1)} %reshape.407, f32[768]{0:T(1024)S(1)} %reshape.406, ...), kind=kOutput, calls=%fused_computation.3 | convolution fusion | flops 5043388416 | bytes 39348224 | tf_op jit(solution)/shard_map/dot_general | solution.py:338
  241.7 5.5 %fusion.56 = (f32[1024]{0:T(1024)S(1)}, f32[1024,768]{1,0:T(8,128)S(1)}) fusion(f32[768]{0:T(1024)S(1)} %reshape.409, bf16[1024,3072]{1,0:T(8,128)(2,1)S(1)} %get-tuple-element.46, bf16[3072,768]{1,0:T(8,128)(2,1)S(1)} %bitcast.203, f32[768]{0:T(1024)S(1)} %reshape.407, f32[768]{0:T(1024)S(1)} %reshape.406, f32[1024]{0:T(1024)S(1)} %fusion.39, ...), kind=kOutput, calls=%fused_computation.184 | convolution fusion | flops 4838915072 | bytes 17323008 | tf_op jit(solution)/shard_map/dot_general | solution.py:341
  255.7 6.9 %convolution_convert_fusion = bf16[3072,768]{1,0:T(8,128)(2,1)} fusion(bf16[1024,3072]{1,0:T(8,128)(2,1)S(1)} %get-tuple-element.46, bf16[1024,768]{1,0:T(8,128)(2,1)S(1)} %get-tuple-element.39), kind=kOutput, calls=%fused_computation.21 | convolution fusion | flops 4834197504 | bytes 12582912 | tf_op jit(solution)/shard_map/dot_general | solution.py:27
  262.7 16.8 %fusion.57 = (bf16[3072]{0:T(1024)(128)(2,1)}, bf16[1024,3072]{1,0:T(8,128)(2,1)}) fusion(f32[1024,3072]{1,0:T(8,128)} %get-tuple-element.47, bf16[1024,768]{1,0:T(8,128)(2,1)} %copy-done.24, bf16[3072,768]{1,0:T(8,128)(2,1)S(1)} %bitcast.204, f32[1024,3072]{1,0:T(8,128)} %get-tuple-element.96, f32[3072]{0:T(1024)S(1)} %reshape.408), kind=kOutput, calls=%fused_computation.185 | convolution fusion | flops 4882166784 | bytes 37767168 | tf_op jit(solution)/shard_map/dot_general | solution.py:33
  279.5 11.6 %multiply_reduce_fusion = (bf16[768]{0:T(1024)(128)(2,1)}, f32[1024]{0:T(1024)S(1)}, bf16[768]{0:T(1024)(128)(2,1)}, f32[1024,768]{1,0:T(8,128)S(1)}) fusion(f32[1024,768]{1,0:T(8,128)} %copy-done.13, f32[1024]{0:T(1024)S(1)} %fusion.39, f32[1024]{0:T(1024)S(1)} %broadcast_multiply_fusion.1, f32[768]{0:T(1024)S(1)} %reshape.406, ...), kind=kOutput, calls=%fused_computation.40 | convolution fusion | flops 4839699456 | bytes 20469760 | tf_op jit(solution)/shard_map/dot_general | solution.py:33
  300.3 24.9 %attention_backward.1 = (bf16[1024,768]{1,0:T(8,128)(2,1)S(1)}, bf16[1024,768]{1,0:T(8,128)(2,1)S(1)}, bf16[1024,768]{1,0:T(8,128)(2,1)S(1)}) custom-call(bf16[1024,2304]{1,0:T(8,128)(2,1)} %add_convert_fusion.1.q_ref.k_ref.v_ref, bf16[1024,2304]{1,0:T(8,128)(2,1)} %add_convert_fusion.1.q_ref.k_ref.v_ref, ...), custom_call_target="tpu_custom_call" | custom-call | flops 4026531840 | bytes 11010048 | tf_op jit(solution)/shard_map/attention_backward/pallas_call | solution.py:116
  332.8 6.8 %convolution_convert_fusion.2 = bf16[768,2304]{1,0:T(8,128)(2,1)S(1)} fusion(bf16[1024,768]{1,0:T(8,128)(2,1)} %bitcast.234, bf16[1024,2304]{1,0:T(8,128)(2,1)} %constant_dynamic-update-slice_fusion.13), kind=kOutput, calls=%fused_computation.23 | convolution fusion | flops 3625648128 | bytes 9830400 | tf_op jit(solution)/shard_map/dot_general | solution.py:27
  339.7 8.7 %add_convert_fusion.2 = bf16[1024,768]{1,0:T(8,128)(2,1)} fusion(f32[1024,768]{1,0:T(8,128)S(1)} %copy-done.17, bf16[1024,2304]{1,0:T(8,128)(2,1)} %constant_dynamic-update-slice_fusion.13, bf16[768,2304]{1,0:T(8,128)(2,1)S(1)} %bitcast.209, f32[1024]{0:T(1024)S(1)} %negate_multiply_fusion.1), kind=kOutput, calls=%fused_computation.41 | convolution fusion | flops 3626237952 | bytes 12980224 | tf_op jit(solution)/shard_map/dot_general | solution.py:33
  370.4 10.1 %convolution_convert_fusion.1 = bf16[768,3072]{1,0:T(8,128)(2,1)} fusion(bf16[1024,3072]{1,0:T(8,128)(2,1)} %get-tuple-element.101, f32[1024,768]{1,0:T(8,128)S(1)} %copy-done.15, f32[768]{0:T(1024)S(1)} %copy-done.45, f32[768]{0:T(1024)S(1)} %reshape.406, f32[1024]{0:T(1024)S(1)} %copy-done.43, f32[1024]{0:T(1024)S(1)} %broadcast_multiply_fusion.1), kind=kOutput, calls=%fused_computation.22 | convolution fusion | flops 4838129664 | bytes 14170112 | tf_op jit(solution)/shard_map/dot_general | solution.py:27
  395.8 6.3 %collective-permute-done.29.refs_2_ = bf16[1,2,128,768]{3,2,1,0:T(8,128)(2,1)S(1)} collective-permute-done((bf16[1,2,128,768]{3,2,1,0:T(8,128)(2,1)}, bf16[1,2,128,768]{3,2,1,0:T(8,128)(2,1)S(1)}, u32[]{:S(2)}, u32[]{:S(2)}) %collective-permute-start.29) | collective-permute-done | bytes 393248 | tf_op jit(solution)/shard_map/ppermute | solution.py:122
  404.1 5.9 %collective-permute-done.30.refs_3_ = bf16[1,2,128,768]{3,2,1,0:T(8,128)(2,1)S(1)} collective-permute-done((bf16[1,2,128,768]{3,2,1,0:T(8,128)(2,1)S(1)}, bf16[1,2,128,768]{3,2,1,0:T(8,128)(2,1)S(1)}, u32[]{:S(2)}, u32[]{:S(2)}) %collective-permute-start.30) | collective-permute-done | bytes 393248 | tf_op jit(solution)/shard_map/ppermute | solution.py:122
  411.9 8.5 %collective-permute-done.41 = bf16[2,2,24,2432]{3,2,1,0:T(8,128)(2,1)} collective-permute-done((bf16[2,2,24,2432]{3,2,1,0:T(8,128)(2,1)}, bf16[2,2,24,2432]{3,2,1,0:T(8,128)(2,1)}, u32[]{:S(2)}, u32[]{:S(2)}) %collective-permute-start.41) | collective-permute-done | bytes 466976 | tf_op jit(solution)/shard_map/ppermute | solution.py:122
  437.1 17.6 %collective-permute-done.52 = bf16[4,2,96,768]{3,2,1,0:T(8,128)(2,1)S(1)} collective-permute-done((bf16[4,2,96,768]{3,2,1,0:T(8,128)(2,1)S(1)}, bf16[4,2,96,768]{3,2,1,0:T(8,128)(2,1)S(1)}, u32[]{:S(2)}, u32[]{:S(2)}) %collective-permute-start.52) | collective-permute-done | bytes 1179680 | tf_op jit(solution)/shard_map/ppermute | solution.py:122
  457.6 9.8 %collective-permute-done.46 = bf16[4,2,24,3840]{3,2,1,0:T(8,128)(2,1)S(1)} collective-permute-done((bf16[4,2,24,3840]{3,2,1,0:T(8,128)(2,1)S(1)}, bf16[4,2,24,3840]{3,2,1,0:T(8,128)(2,1)S(1)}, u32[]{:S(2)}, u32[]{:S(2)}) %collective-permute-start.46) | collective-permute-done | bytes 1474592 | tf_op jit(solution)/shard_map/ppermute | solution.py:122
  495.1 12.9 %collective-permute-done.49 = bf16[24,3840]{1,0:T(8,128)(2,1)S(1)} collective-permute-done((bf16[24,3840]{1,0:T(8,128)(2,1)S(1)}, bf16[24,3840]{1,0:T(8,128)(2,1)S(1)}, u32[]{:S(2)}, u32[]{:S(2)}) %collective-permute-start.49) | collective-permute-done | bytes 184352 | tf_op jit(solution)/shard_map/ppermute | solution.py:122
  (354 shorter events, 192.0 us)
Async XLA Ops:
  14.4 37.0 %collective-permute-start.14 = (bf16[1,24,3840]{2,1,0:T(8,128)(2,1)S(1)}, bf16[1,24,3840]{2,1,0:T(8,128)(2,1)S(1)}, u32[]{:S(2)}, u32[]{:S(2)}) collective-permute-start(bf16[1,24,3840]{2,1,0:T(8,128)(2,1)S(1)} %maximum_bitcast_fusion), channel_id=1, source_target_pairs={{0,8},{1,9},{2,10},{3,11},{4,12},{5,13},{6,14},{7,15},{8,0},{9,1},... | collective-permute-start | bytes 552968 | tf_op jit(solution)/shard_map/ppermute | solution.py:122
  16.3 35.3 %collective-permute-start.15 = (bf16[1,24,3840]{2,1,0:T(8,128)(2,1)S(1)}, bf16[1,24,3840]{2,1,0:T(8,128)(2,1)S(1)}, u32[]{:S(2)}, u32[]{:S(2)}) collective-permute-start(bf16[1,24,3840]{2,1,0:T(8,128)(2,1)S(1)} %maximum_bitcast_fusion), channel_id=1, source_target_pairs={{0,16},{1,17},{2,18},{3,19},{4,20},{5,21},{6,22},{7,23},{8,24},{9,... | collective-permute-start | bytes 552968 | tf_op jit(solution)/shard_map/ppermute | solution.py:122
  24.5 28.8 %collective-permute-start.16 = (bf16[1,24,3840]{2,1,0:T(8,128)(2,1)S(1)}, bf16[1,24,3840]{2,1,0:T(8,128)(2,1)S(1)}, u32[]{:S(2)}, u32[]{:S(2)}) collective-permute-start(bf16[1,24,3840]{2,1,0:T(8,128)(2,1)S(1)} %maximum_bitcast_fusion), channel_id=1, source_target_pairs={{0,24},{1,25},{2,26},{3,27},{4,28},{5,29},{6,30},{7,31},{8,16},{9,... | collective-permute-start | bytes 552968 | tf_op jit(solution)/shard_map/ppermute | solution.py:122
  48.8 50.8 %collective-permute-start = (bf16[2,128,768]{2,1,0:T(8,128)(2,1)}, bf16[2,128,768]{2,1,0:T(8,128)(2,1)S(1)}, u32[]{:S(2)}, u32[]{:S(2)}) collective-permute-start(bf16[2,128,768]{2,1,0:T(8,128)(2,1)} %get-tuple-element.67), channel_id=1, source_target_pairs={{0,1},{1,0},{2,3},{3,2},{4,5},{5,4},{6,7},{7,6},{8,9},{9,8},{10,11... | collective-permute-start | bytes 1179656 | tf_op jit(solution)/shard_map/ppermute | solution.py:122
  49.4 51.7 %collective-permute-start.1 = (bf16[2,128,768]{2,1,0:T(8,128)(2,1)}, bf16[2,128,768]{2,1,0:T(8,128)(2,1)S(1)}, u32[]{:S(2)}, u32[]{:S(2)}) collective-permute-start(bf16[2,128,768]{2,1,0:T(8,128)(2,1)} %get-tuple-element.66), channel_id=1, source_target_pairs={{0,2},{1,3},{2,0},{3,1},{4,6},{5,7},{6,4},{7,5},{8,10},{9,11},{10,... | collective-permute-start | bytes 1179656 | tf_op jit(solution)/shard_map/ppermute | solution.py:122
  51.4 50.3 %collective-permute-start.2 = (bf16[2,128,768]{2,1,0:T(8,128)(2,1)}, bf16[2,128,768]{2,1,0:T(8,128)(2,1)S(1)}, u32[]{:S(2)}, u32[]{:S(2)}) collective-permute-start(bf16[2,128,768]{2,1,0:T(8,128)(2,1)} %get-tuple-element.65), channel_id=1, source_target_pairs={{0,3},{1,2},{2,1},{3,0},{4,7},{5,6},{6,5},{7,4},{8,11},{9,10},{10,... | collective-permute-start | bytes 1179656 | tf_op jit(solution)/shard_map/ppermute | solution.py:122
  51.6 40.7 %collective-permute-start.10 = (bf16[2,24,2432]{2,1,0:T(8,128)(2,1)S(1)}, bf16[2,24,2432]{2,1,0:T(8,128)(2,1)S(1)}, u32[]{:S(2)}, u32[]{:S(2)}) collective-permute-start(bf16[2,24,2432]{2,1,0:T(8,128)(2,1)S(1)} %pad_maximum_fusion.7), channel_id=1, source_target_pairs={{0,2},{1,3},{2,0},{3,1},{4,6},{5,7},{6,4},{7,5},{8,10},{9,11},{10,... | collective-permute-start | bytes 700424 | tf_op jit(solution)/shard_map/ppermute | solution.py:122
  53.4 37.1 %collective-permute-start.17 = (bf16[4,24,3840]{2,1,0:T(8,128)(2,1)S(1)}, bf16[4,24,3840]{2,1,0:T(8,128)(2,1)S(1)}, u32[]{:S(2)}, u32[]{:S(2)}) collective-permute-start(bf16[4,24,3840]{2,1,0:T(8,128)(2,1)S(1)} %pad_maximum_fusion.3), channel_id=1, source_target_pairs={{0,2},{1,3},{2,0},{3,1},{4,6},{5,7},{6,4},{7,5},{8,10},{9,11},{10,... | collective-permute-start | bytes 2211848 | tf_op jit(solution)/shard_map/ppermute | solution.py:122
  101.1 67.6 %collective-permute-start.19 = (bf16[8,24,3840]{2,1,0:T(8,128)(2,1)S(1)}, bf16[8,24,3840]{2,1,0:T(8,128)(2,1)}, u32[]{:S(2)}, u32[]{:S(2)}) collective-permute-start(bf16[8,24,3840]{2,1,0:T(8,128)(2,1)S(1)} %constant_dynamic-update-slice_fusion.3.refs_0_), channel_id=1, source_target_pairs={{0,4},{1,5},{2,6},{3,7},{4,0},{5,1},{6,2},{7,3},{8,12},{9,13},{10,... | collective-permute-start | bytes 4423688 | tf_op jit(solution)/shard_map/ppermute | solution.py:122
  101.8 53.1 %collective-permute-start.12 = (bf16[4,24,2432]{2,1,0:T(8,128)(2,1)S(1)}, bf16[4,24,2432]{2,1,0:T(8,128)(2,1)S(1)}, u32[]{:S(2)}, u32[]{:S(2)}) collective-permute-start(bf16[4,24,2432]{2,1,0:T(8,128)(2,1)S(1)} %constant_dynamic-update-slice_fusion.refs_4_), channel_id=1, source_target_pairs={{0,4},{1,5},{2,6},{3,7},{4,0},{5,1},{6,2},{7,3},{8,12},{9,13},{10,... | collective-permute-start | bytes 1400840 | tf_op jit(solution)/shard_map/ppermute | solution.py:122
  109.9 45.1 %collective-permute-start.11 = (bf16[4,24,2432]{2,1,0:T(8,128)(2,1)S(1)}, bf16[4,24,2432]{2,1,0:T(8,128)(2,1)S(1)}, u32[]{:S(2)}, u32[]{:S(2)}) collective-permute-start(bf16[4,24,2432]{2,1,0:T(8,128)(2,1)S(1)} %constant_dynamic-update-slice_fusion.refs_4_), channel_id=1, source_target_pairs={{0,1},{1,0},{2,3},{3,2},{4,5},{5,4},{6,7},{7,6},{8,9},{9,8},{10,11... | collective-permute-start | bytes 1400840 | tf_op jit(solution)/shard_map/ppermute | solution.py:122
  115.9 39.6 %collective-permute-start.6 = (bf16[4,24,2432]{2,1,0:T(8,128)(2,1)S(1)}, bf16[4,24,2432]{2,1,0:T(8,128)(2,1)}, u32[]{:S(2)}, u32[]{:S(2)}) collective-permute-start(bf16[4,24,2432]{2,1,0:T(8,128)(2,1)S(1)} %pad_maximum_fusion.5.refs_0_), channel_id=1, source_target_pairs={{0,2},{1,3},{2,0},{3,1},{4,6},{5,7},{6,4},{7,5},{8,10},{9,11},{10,... | collective-permute-start | bytes 1400840 | tf_op jit(solution)/shard_map/ppermute | solution.py:122
  117.7 53.9 %collective-permute-start.26 = (bf16[8,96,768]{2,1,0:T(8,128)(2,1)}, bf16[8,96,768]{2,1,0:T(8,128)(2,1)}, u32[]{:S(2)}, u32[]{:S(2)}) collective-permute-start(bf16[8,96,768]{2,1,0:T(8,128)(2,1)} %constant_dynamic-update-slice_fusion.8.refs_0_), channel_id=1, source_target_pairs={{0,2},{1,3},{2,0},{3,1},{4,6},{5,7},{6,4},{7,5},{8,10},{9,11},{10,... | collective-permute-start | bytes 3538952 | tf_op jit(solution)/shard_map/ppermute | solution.py:122
  161.5 36.2 %collective-permute-start.25 = (bf16[8,96,768]{2,1,0:T(8,128)(2,1)}, bf16[8,96,768]{2,1,0:T(8,128)(2,1)}, u32[]{:S(2)}, u32[]{:S(2)}) collective-permute-start(bf16[8,96,768]{2,1,0:T(8,128)(2,1)} %constant_dynamic-update-slice_fusion.8.refs_0_), channel_id=1, source_target_pairs={{0,1},{1,0},{2,3},{3,2},{4,5},{5,4},{6,7},{7,6},{8,9},{9,8},{10,11... | collective-permute-start | bytes 3538952 | tf_op jit(solution)/shard_map/ppermute | solution.py:122
  162.0 38.7 %collective-permute-start.18 = (bf16[8,24,3840]{2,1,0:T(8,128)(2,1)S(1)}, bf16[8,24,3840]{2,1,0:T(8,128)(2,1)}, u32[]{:S(2)}, u32[]{:S(2)}) collective-permute-start(bf16[8,24,3840]{2,1,0:T(8,128)(2,1)S(1)} %constant_dynamic-update-slice_fusion.3.refs_0_), channel_id=1, source_target_pairs={{0,1},{1,0},{2,3},{3,2},{4,5},{5,4},{6,7},{7,6},{8,9},{9,8},{10,11... | collective-permute-start | bytes 4423688 | tf_op jit(solution)/shard_map/ppermute | solution.py:122
  168.7 32.0 %collective-permute-start.20 = (bf16[8,24,3840]{2,1,0:T(8,128)(2,1)}, bf16[8,24,3840]{2,1,0:T(8,128)(2,1)}, u32[]{:S(2)}, u32[]{:S(2)}) collective-permute-start(bf16[8,24,3840]{2,1,0:T(8,128)(2,1)} %collective-permute-done.19.refs_2_), channel_id=1, source_target_pairs={{0,1},{1,0},{2,3},{3,2},{4,5},{5,4},{6,7},{7,6},{8,9},{9,8},{10,11... | collective-permute-start | bytes 4423688 | tf_op jit(solution)/shard_map/ppermute | solution.py:122
  350.0 74.0 %collective-permute-start.51 = (bf16[16,96,768]{2,1,0:T(8,128)(2,1)}, bf16[16,96,768]{2,1,0:T(8,128)(2,1)}, u32[]{:S(2)}, u32[]{:S(2)}) collective-permute-start(bf16[16,96,768]{2,1,0:T(8,128)(2,1)} %dynamic-slice_bitcast_fusion.1), channel_id=1, source_target_pairs={{0,1},{1,0},{2,3},{3,2},{4,5},{5,4},{6,7},{7,6},{8,9},{9,8},{10,11... | collective-permute-start | bytes 7077896 | tf_op jit(solution)/shard_map/ppermute | solution.py:122
  392.0 28.4 %collective-permute-start.41 = (bf16[2,2,24,2432]{3,2,1,0:T(8,128)(2,1)}, bf16[2,2,24,2432]{3,2,1,0:T(8,128)(2,1)}, u32[]{:S(2)}, u32[]{:S(2)}) collective-permute-start(bf16[2,2,24,2432]{3,2,1,0:T(8,128)(2,1)} %dynamic-slice_bitcast_fusion.6), channel_id=1, source_target_pairs={{0,2},{1,3},{2,0},{3,1},{4,6},{5,7},{6,4},{7,5},{8,10},{9,11},{10,... | collective-permute-start | bytes 1400840 | tf_op jit(solution)/shard_map/ppermute | solution.py:122
  392.4 28.0 %collective-permute-start.38 = (bf16[2,2,24,2432]{3,2,1,0:T(8,128)(2,1)}, bf16[2,2,24,2432]{3,2,1,0:T(8,128)(2,1)}, u32[]{:S(2)}, u32[]{:S(2)}) collective-permute-start(bf16[2,2,24,2432]{3,2,1,0:T(8,128)(2,1)} %dynamic-slice_bitcast_fusion.7), channel_id=1, source_target_pairs={{0,4},{1,5},{2,6},{3,7},{4,0},{5,1},{6,2},{7,3},{8,12},{9,13},{10,... | collective-permute-start | bytes 1400840 | tf_op jit(solution)/shard_map/ppermute | solution.py:122
  427.2 27.6 %collective-permute-start.52 = (bf16[4,2,96,768]{3,2,1,0:T(8,128)(2,1)S(1)}, bf16[4,2,96,768]{3,2,1,0:T(8,128)(2,1)S(1)}, u32[]{:S(2)}, u32[]{:S(2)}) collective-permute-start(bf16[4,2,96,768]{3,2,1,0:T(8,128)(2,1)S(1)} %dynamic-slice_bitcast_fusion.3), channel_id=1, source_target_pairs={{0,4},{1,5},{2,6},{3,7},{4,0},{5,1},{6,2},{7,3},{8,12},{9,13},{10,... | collective-permute-start | bytes 3538952 | tf_op jit(solution)/shard_map/ppermute | solution.py:122
  432.1 35.3 %collective-permute-start.46 = (bf16[4,2,24,3840]{3,2,1,0:T(8,128)(2,1)S(1)}, bf16[4,2,24,3840]{3,2,1,0:T(8,128)(2,1)S(1)}, u32[]{:S(2)}, u32[]{:S(2)}) collective-permute-start(bf16[4,2,24,3840]{3,2,1,0:T(8,128)(2,1)S(1)} %dynamic-slice_bitcast_fusion.2), channel_id=1, source_target_pairs={{0,2},{1,3},{2,0},{3,1},{4,6},{5,7},{6,4},{7,5},{8,10},{9,11},{10,... | collective-permute-start | bytes 4423688 | tf_op jit(solution)/shard_map/ppermute | solution.py:122
  432.5 37.8 %collective-permute-start.40 = (bf16[24,2432]{1,0:T(8,128)(2,1)S(1)}, bf16[24,2432]{1,0:T(8,128)(2,1)S(1)}, u32[]{:S(2)}, u32[]{:S(2)}) collective-permute-start(bf16[24,2432]{1,0:T(8,128)(2,1)S(1)} %dynamic-slice_bitcast_fusion.26), channel_id=1, source_target_pairs={{0,8},{1,9},{2,10},{3,11},{4,12},{5,13},{6,14},{7,15},{8,0},{9,1},... | collective-permute-start | bytes 350216 | tf_op jit(solution)/shard_map/ppermute | solution.py:122
  433.2 37.0 %collective-permute-start.43 = (bf16[24,2432]{1,0:T(8,128)(2,1)S(1)}, bf16[24,2432]{1,0:T(8,128)(2,1)S(1)}, u32[]{:S(2)}, u32[]{:S(2)}) collective-permute-start(bf16[24,2432]{1,0:T(8,128)(2,1)S(1)} %get-tuple-element.82), channel_id=1, source_target_pairs={{0,16},{1,17},{2,18},{3,19},{4,20},{5,21},{6,22},{7,23},{8,24},{9,... | collective-permute-start | bytes 350216 | tf_op jit(solution)/shard_map/ppermute | solution.py:122
  435.9 34.4 %collective-permute-start.44 = (bf16[24,2432]{1,0:T(8,128)(2,1)S(1)}, bf16[24,2432]{1,0:T(8,128)(2,1)S(1)}, u32[]{:S(2)}, u32[]{:S(2)}) collective-permute-start(bf16[24,2432]{1,0:T(8,128)(2,1)S(1)} %get-tuple-element.83), channel_id=1, source_target_pairs={{0,24},{1,25},{2,26},{3,27},{4,28},{5,29},{6,30},{7,31},{8,16},{9,... | collective-permute-start | bytes 350216 | tf_op jit(solution)/shard_map/ppermute | solution.py:122
  (84 other events, 1244.5 us)

commit v4 on v1

--- a/solution.py
+++ b/solution.py
@@ -118,17 +118,205 @@
       out_specs=[blk(0)]*3,out_shape=[o,o,o],
       compiler_params=pltpu.CompilerParams(vmem_limit_bytes=48*2**20),name="attention_backward",
       cost_estimate=pl.CostEstimate(flops=10*rows*length*width,bytes_accessed=rows*width*14,transcendentals=rows*length*width//HD))(packed,packed,packed,bias,lse,grad)
-
-def to_sequences(block):
-    return lax.all_to_all(block, "seq", 0, 1, tiled=True)
-
-
-def to_positions(block):
-    return lax.all_to_all(block, "seq", 1, 0, tiled=True)
-
-
-def gather_rows(block):
-    return lax.all_gather(block, BOTH, axis=0, tiled=True)
+def swap(block, distance, devices):
+    return lax.ppermute(block, BOTH, [(i, i ^ distance) for i in range(devices)])
+
+
+def after(value, *done):
+    return lax.optimization_barrier((value,) + done)[0]
+
+
+def place_kernel(ids, counts, spans, me_ref, *refs):
+    pieces, rest = refs[: len(counts)], refs[len(counts) :]
+    outs, sems = rest[: len(spans)], rest[len(spans)]
+    me = me_ref[0]
+    copies = []
+    at = 0
+    for piece, count in zip(pieces, counts):
+        for j in range(count):
+            spot = me ^ ids[at]
+            for out, (start, size) in zip(outs, spans):
+                source = piece.at[j] if len(spans) == 1 else piece.at[j, :, pl.ds(start, size)]
+                copy = pltpu.make_async_copy(source, out.at[spot], sems.at[len(copies)])
+                copy.start()
+                copies.append(copy)
+            at += 1
+    for copy in copies:
+        copy.wait()
+
+
+def place(pieces, ids, me, spans=None):
+    counts = [p.shape[0] for p in pieces]
+    total = sum(counts)
+    tail = pieces[0].shape[1:]
+    spans = spans or [(0, tail[-1])]
+    any_space = pl.BlockSpec(memory_space=pl.ANY)
+    moved = 2 * sum(p.size * p.dtype.itemsize for p in pieces)
+    return pl.pallas_call(
+        functools.partial(place_kernel, ids, counts, spans),
+        in_specs=[pl.BlockSpec(memory_space=pltpu.SMEM)] + [any_space] * len(pieces),
+        out_specs=[pl.BlockSpec(memory_space=pltpu.VMEM)] * len(spans),
+        out_shape=[
+            jax.ShapeDtypeStruct((total,) + tail[:-1] + (size,), pieces[0].dtype)
+            for _, size in spans
+        ],
+        scratch_shapes=[pltpu.SemaphoreType.DMA((total * len(spans),))],
+        compiler_params=pltpu.CompilerParams(vmem_limit_bytes=32 * 2**20),
+        cost_estimate=pl.CostEstimate(flops=0, bytes_accessed=moved, transcendentals=0),
+        name="place_blocks",
+    )(me.reshape(1), *pieces)
+
+
+def pack_rows(vectors, share):
+    lead = vectors[0].shape[:-1]
+    columns = []
+    for at in range(0, len(vectors), share):
+        rows = []
+        for v in vectors[at : at + share]:
+            rows.append(jnp.pad(v, [(0, 0)] * len(lead) + [(0, 128 - v.shape[-1])]))
+        block = jnp.stack(rows, -2)
+        columns.append(
+            jnp.pad(block, [(0, 0)] * len(lead) + [(0, share - len(rows)), (0, 0)])
+        )
+    return columns[0] if len(columns) == 1 else jnp.concatenate(columns, -1)
+
+
+def unpack_rows(block, sizes):
+    share = block.shape[-2]
+    out = []
+    for i, size in enumerate(sizes):
+        start = i // share * 128
+        out.append(block[..., i % share, start : start + size])
+    return out
+
+
+class Gather:
+    def __init__(self, block, me, devices, plan):
+        self.me, self.devices, self.plan = me, devices, plan
+        self.own, self.own_ids = block[None], [0]
+
+    def swapped(self, block, distance):
+        return swap(block, distance, self.devices)
+
+    def along_z(self, *done):
+        own, own_ids = self.own, self.own_ids
+        if done:
+            own = after(own, *done)
+        distance = 32
+        while distance < self.devices:
+            own = jnp.concatenate([own, self.swapped(own, distance)])
+            own_ids = own_ids + [i ^ distance for i in own_ids]
+            distance *= 2
+        far = [own] + [self.swapped(own, 8 * k) for k in (1, 2, 3)]
+        far_ids = [[i ^ (8 * k) for i in own_ids] for k in range(4)]
+        if self.plan == "split":
+            parts = [((0, 1), (4, 2)), ((2, 3), (2, 4))]
+        else:
+            parts = [((0, 1, 2, 3), (4, 2) if self.plan == "xy" else (2, 4))]
+        self.parts = []
+        for which, order in parts:
+            held = jnp.concatenate([far[k] for k in which])
+            self.parts.append((held, [i for k in which for i in far_ids[k]], order))
+        return far[1]
+
+    def first(self, *done):
+        grown = []
+        for held, ids, order in self.parts:
+            if done:
+                held = after(held, *done)
+            got = self.swapped(held, order[0])
+            grown.append(
+                (jnp.concatenate([held, got]), ids + [i ^ order[0] for i in ids], order)
+            )
+        self.parts = grown
+        return grown[0][0]
+
+    def second(self, spans=None, *done):
+        pieces, piece_ids = [], []
+        for held, ids, order in self.parts:
+            if done:
+                held = after(held, *done)
+            last = self.swapped(held, order[1])
+            last_ids = [i ^ order[1] for i in ids]
+            for b, b_ids in ((held, ids), (last, last_ids)):
+                pieces += [b, self.swapped(b, 1)]
+                piece_ids += b_ids + [i ^ 1 for i in b_ids]
+        return place(pieces, piece_ids, self.me, spans)
+
+
+def pick(block, axis, index):
+    return lax.dynamic_index_in_dim(block, index, axis, keepdims=False)
+
+
+def fold(block, axis, me, distance, devices):
+    digit = (me // distance) % 2
+    got = swap(pick(block, axis, 1 - digit), distance, devices)
+    return (pick(block, axis, digit).astype(F32) + got.astype(F32)).astype(BF)
+
+
+class Scatter:
+    def __init__(self, total, me, devices, plan):
+        self.me, self.devices, self.plan = me, devices, plan
+        self.tail = total.shape[1:]
+        distance = devices // 2
+        while distance >= 32:
+            total = self.fold(total.reshape((2, distance) + self.tail), 0, distance)
+            distance //= 2
+        self.total = self.fold(total.reshape((16, 2) + self.tail), 1, 1)
+
+    def fold(self, block, axis, distance):
+        return fold(block, axis, self.me, distance, self.devices)
+
+    def first(self):
+        total = self.total.reshape((4, 2, 2) + self.tail)
+        if self.plan == "split":
+            z = (self.me // 8) % 4
+            halves = total.reshape((2, 2, 2, 2) + self.tail)
+            self.parts = [
+                self.fold(pick(halves, 0, z // 2), 1, 4),
+                self.fold(pick(halves, 0, 1 - z // 2), 2, 2),
+            ]
+        elif self.plan == "xy":
+            self.parts = [self.fold(total, 1, 4)]
+        else:
+            self.parts = [self.fold(total, 2, 2)]
+        return self.parts
+
+    def second(self):
+        z = (self.me // 8) % 4
+        if self.plan == "split":
+            near = self.fold(self.parts[0], 1, 2)
+            away = self.fold(self.parts[1], 1, 4)
+            odd = z % 2
+            self.mine = [
+                pick(near, 0, odd),
+                pick(near, 0, 1 - odd),
+                pick(away, 0, odd),
+                pick(away, 0, 1 - odd),
+            ]
+        else:
+            total = self.fold(self.parts[0], 1, 2 if self.plan == "xy" else 4)
+            self.mine = [pick(total, 0, z ^ k) for k in range(4)]
+        return self.mine
+
+    def along_z(self):
+        got = [swap(self.mine[k], 8 * k, self.devices).astype(F32) for k in (1, 2, 3)]
+        return self.mine[0].astype(F32) + got[0] + got[1] + got[2]
+
+
+def to_sequences(block, seat, members, devices):
+    groups, count, width = block.shape
+    parts = block.reshape(members, groups // members, count, width)
+    pieces = [pick(parts, 0, seat)]
+    pieces += [swap(pick(parts, 0, seat ^ k), k, devices) for k in range(1, members)]
+    return jnp.stack(pieces, 1).reshape(groups * count, width)
+
+
+def to_positions(block, seat, members, devices):
+    pieces = [block[:, 0][None]]
+    pieces += [swap(block[:, k][None], k, devices) for k in range(1, members)]
+    (placed,) = place(pieces, list(range(members)), seat)
+    return placed.reshape((-1,) + placed.shape[2:])
 
 
 def on_device(
@@ -155,11 +343,15 @@
     devices = lax.axis_size("dp") * members
     kept = groups // members
     length = local_len * members
-    flat = to_sequences(inputs).reshape(rows, width)
-    wide_qkv = gather_rows(query_key_value_weight)
-    vectors = (
-        query_bias,
-        value_bias,
+    seat = lax.axis_index("seq")
+    me = lax.axis_index("dp") * members + seat
+    share = query_key_value_weight.shape[0]
+    inner_width = in_weight.shape[1]
+    early = pack_rows([query_bias, value_bias], share)
+    qkv_gather = Gather(
+        jnp.concatenate([query_key_value_weight, early], 1), me, devices, "split"
+    )
+    late_vectors = [
         output_bias,
         norm1_gain,
         norm1_shift,
@@ -167,17 +359,37 @@
         down_bias,
         norm2_gain,
         norm2_shift,
-    )
-    sizes = [v.shape[0] for v in vectors]
-    gathered = gather_rows(jnp.concatenate(vectors)[None])
-    full = []
-    at = 0
-    for size in sizes:
-        full.append(gathered[:, at : at + size].reshape(-1).astype(F32))
-        at += size
+    ]
+    late = pack_rows(late_vectors, share)
+    in_gather = Gather(
+        jnp.concatenate([in_weight, output_weight, late], 1), me, devices, "split"
+    )
+    down_gather = Gather(down_weight, me, devices, "yx")
+    z_done = qkv_gather.along_z()
+    flat = to_sequences(inputs, seat, members, devices)
+    first_done = qkv_gather.first()
+    in_z_done = in_gather.along_z(z_done)
+    down_z_done = down_gather.along_z(z_done)
+    wide_qkv, early = qkv_gather.second([(0, 3 * width), (3 * width, early.shape[1])])
+    wide_qkv = wide_qkv.reshape(width, 3 * width)
+    full_query_bias, full_value_bias = [
+        v.reshape(-1).astype(F32) for v in unpack_rows(early, [share, share])
+    ]
+    bias_vector = jnp.concatenate([full_query_bias, jnp.zeros((width,), F32), full_value_bias])
+    packed = (jnp.dot(flat, wide_qkv, preferred_element_type=F32) + bias_vector).astype(BF)
+    in_gather.first(packed)
+    mine = lax.dynamic_slice(lengths, (seat * kept,), (kept,))
+    slots = jnp.arange(length, dtype=jnp.int32)
+    positions = ((slots // local_len) ^ seat) * local_len + slots % local_len
+    mask = jnp.where(positions[None, :] < mine[:, None], 0.0, -1e30).astype(BF)
+    mask = jnp.broadcast_to(mask[:, :, None], (kept, length, 128))
+    mixed, logsum = attention_forward(packed, mask, length)
+    wide_in, wide_out, late = in_gather.second(
+        [(0, inner_width), (inner_width, width), (inner_width + width, late.shape[1])]
+    )
+    wide_in = wide_in.reshape(width, inner_width)
+    wide_out = wide_out.reshape(width, width)
     (
-        full_query_bias,
-        full_value_bias,
         full_out_bias,
         gain_one,
         shift_one,
@@ -185,60 +397,46 @@
         full_down_bias,
         gain_two,
         shift_two,
-    ) = full
-    wide_out = gather_rows(output_weight)
-    wide_in = gather_rows(in_weight)
-    wide_down = gather_rows(down_weight)
-    cot = to_sequences(cotangent).reshape(rows, width)
-    bias_vector = jnp.concatenate([full_query_bias, jnp.zeros((width,), F32), full_value_bias])
-    packed = (jnp.dot(flat, wide_qkv, preferred_element_type=F32) + bias_vector).astype(BF)
-    mine = lax.dynamic_slice(lengths, (lax.axis_index("seq") * kept,), (kept,))
-    positions = jnp.arange(length, dtype=jnp.int32)
-    mask = jnp.where(positions[None, :] < mine[:, None], 0.0, -1e30).astype(BF)
-    mask = jnp.broadcast_to(mask[:, :, None], (kept, length, 128))
-    mixed, logsum = attention_forward(packed, mask, length)
+    ) = [
+        v.reshape(-1).astype(F32)
+        for v in unpack_rows(late, [v.shape[0] for v in late_vectors])
+    ]
+    down_gather.first(mixed)
     attention_branch = jnp.dot(mixed, wide_out, preferred_element_type=F32) + full_out_bias
     first, norm_one_pull = jax.vjp(
         layer_norm, flat.astype(F32) + attention_branch, gain_one, shift_one
     )
     first_low = first.astype(BF)
+    cot = to_sequences(after(cotangent, first_low), seat, members, devices)
     hidden = jnp.dot(first_low, wide_in, preferred_element_type=F32) + full_in_bias
     active, gelu_pull = jax.vjp(gelu_exact, hidden)
     active_low = active.astype(BF)
+    (wide_down,) = down_gather.second()
+    wide_down = wide_down.reshape(inner_width, width)
     branch_two = jnp.dot(active_low, wide_down, preferred_element_type=F32) + full_down_bias
     result, norm_two_pull = jax.vjp(
         layer_norm, first_low.astype(F32) + branch_two, gain_two, shift_two
     )
-    outputs = to_positions(result.astype(BF).reshape(kept, length, width))
     grad_second, grad_gain_two, grad_shift_two = norm_two_pull(cot.astype(F32))
     grad_branch_two = grad_second.astype(BF)
-    grad_down = over_rows(active_low, grad_branch_two)
+    grad_down = over_rows(active_low, grad_branch_two).astype(BF)
+    down_scatter = Scatter(grad_down.reshape(devices, -1, width), me, devices, "yx")
     grad_down_bias = jnp.sum(grad_branch_two.astype(F32), 0)
     (grad_hidden,) = gelu_pull(times_transposed(grad_branch_two, wide_down))
     grad_hidden_low = grad_hidden.astype(BF)
-    grad_in = over_rows(first_low, grad_hidden_low)
+    grad_in = over_rows(first_low, grad_hidden_low).astype(BF)
     grad_in_bias = jnp.sum(grad_hidden_low.astype(F32), 0)
+    grad_hidden_low = after(grad_hidden_low, down_scatter.total)
+    down_half = down_scatter.first()
     grad_first = times_transposed(grad_hidden_low, wide_in) + grad_second
     grad_residual, grad_gain_one, grad_shift_one = norm_one_pull(grad_first)
     grad_branch_one = grad_residual.astype(BF)
-    grad_out = over_rows(mixed, grad_branch_one)
+    grad_out = over_rows(mixed, grad_branch_one).astype(BF)
     grad_out_bias = jnp.sum(grad_branch_one.astype(F32), 0)
-    grad_mixed = times_transposed(grad_branch_one, wide_out).astype(BF)
-    grad_queries, grad_keys, grad_values = attention_backward(
-        packed, mask, logsum, grad_mixed, length
-    )
-    grad_packed = jnp.concatenate([grad_queries, grad_keys, grad_values], -1)
-    grad_inputs = times_transposed(grad_packed, wide_qkv) + grad_residual
-    grad_inputs = to_positions(grad_inputs.astype(BF).reshape(kept, length, width))
-    grad_qkv = over_rows(flat, grad_packed)
-    column_sums = jnp.sum(grad_packed.astype(F32), 0)
-
-    def scatter(total):
-        return lax.psum_scatter(total.astype(BF), BOTH, scatter_dimension=0, tiled=True).astype(F32)
-
-    sums = (
-        column_sums[:width],
-        column_sums[2 * width :],
+    outputs = to_positions(
+        result.astype(BF).reshape(kept, members, local_len, width), seat, members, devices
+    )
+    late_sums = [
         grad_out_bias,
         grad_gain_one,
         grad_shift_one,
@@ -246,30 +444,72 @@
         grad_down_bias,
         grad_gain_two,
         grad_shift_two,
-    )
-    joined = jnp.concatenate([v.reshape(devices, -1) for v in sums], 1)
-    joined = lax.psum_scatter(joined, BOTH, scatter_dimension=0, tiled=True)[0]
-    parts = []
-    at = 0
-    for size in sizes:
-        parts.append(joined[at : at + size])
-        at += size
+    ]
+    late_block = pack_rows([v.reshape(devices, -1) for v in late_sums], share).astype(BF)
+    in_scatter = Scatter(
+        jnp.concatenate(
+            [
+                grad_in.reshape(devices, share, inner_width),
+                grad_out.reshape(devices, share, width),
+                late_block,
+            ],
+            2,
+        ),
+        me,
+        devices,
+        "split",
+    )
+    grad_mixed = times_transposed(grad_branch_one, wide_out).astype(BF)
+    grad_mixed = after(grad_mixed, *down_half)
+    down_quarter = down_scatter.second()
+    grad_queries, grad_keys, grad_values = attention_backward(
+        packed, mask, logsum, grad_mixed, length
+    )
+    grad_packed = jnp.concatenate([grad_queries, grad_keys, grad_values], -1)
+    grad_packed = after(grad_packed, in_scatter.total, *down_quarter)
+    in_half = in_scatter.first()
+    down_part = down_scatter.along_z()
+    grad_qkv = over_rows(flat, grad_packed).astype(BF)
+    column_sums = jnp.sum(grad_packed.astype(F32), 0)
+    early_sums = [column_sums[:width], column_sums[2 * width :]]
+    early_block = pack_rows([v.reshape(devices, -1) for v in early_sums], share).astype(BF)
+    qkv_scatter = Scatter(
+        jnp.concatenate([grad_qkv.reshape(devices, share, 3 * width), early_block], 2),
+        me,
+        devices,
+        "split",
+    )
+    grad_inputs = (
+        times_transposed(after(grad_packed, grad_qkv), wide_qkv) + grad_residual
+    ).astype(BF)
+    grad_inputs = to_positions(
+        grad_inputs.reshape(kept, members, local_len, width), seat, members, devices
+    )
+    in_scatter.second()
+    in_part = in_scatter.along_z()
+    qkv_scatter.first()
+    qkv_scatter.second()
+    qkv_part = qkv_scatter.along_z()
+    early_out = unpack_rows(qkv_part[:, 3 * width :], [share, share])
+    late_out = unpack_rows(
+        in_part[:, inner_width + width :], [v.shape[0] for v in late_vectors]
+    )
     return (
         outputs,
         grad_inputs,
-        scatter(grad_qkv),
-        parts[0],
-        parts[1],
-        scatter(grad_out),
-        parts[2],
-        parts[3],
-        parts[4],
-        scatter(grad_in),
-        parts[5],
-        scatter(grad_down),
-        parts[6],
-        parts[7],
-        parts[8],
+        qkv_part[:, : 3 * width],
+        early_out[0],
+        early_out[1],
+        in_part[:, inner_width : inner_width + width],
+        late_out[0],
+        late_out[1],
+        late_out[2],
+        in_part[:, :inner_width],
+        late_out[3],
+        down_part,
+        late_out[4],
+        late_out[5],
+        late_out[6],
     )
 
 

time: 754 us -> 498 us (0.66)
  waiting for transfers between devices: 372 us -> 154 us
  blocking collectives: 130 us -> 0 us
  starting transfers between devices: 12 us -> 73.3 us
  other arithmetic: 16.6 us -> 43 us
  Pallas kernels: 42 us -> 55 us
  between operations: 15.2 us -> 2.22 us
  local copies, waits for them, and re-layouts: 35.5 us -> 45.6 us
  matrix products: 125 us -> 117 us
    reduce_scatter x3 -> x0, waiting for transfers between devices: 220 us -> none  [scatter(): lax.psum_scatter(total.astype(BF), BOTH, scatter_dimension=0, tiled=True)]
    ppermute x0 -> x63, waiting for transfers between devices: none -> 154 us  [swap(): lax.ppermute(block, BOTH, [(i, i ^ distance) for i in range(devices)])]
    unnamed x2 -> x0, blocking collectives: 104 us -> none
    all_gather x4 -> x0, waiting for transfers between devices: 91.7 us -> none  [gather_rows(): return lax.all_gather(block, BOTH, axis=0, tiled=True)]
    ppermute x0 -> x63, starting transfers between devices: none -> 73.3 us  [swap(): lax.ppermute(block, BOTH, [(i, i ^ distance) for i in range(devices)])]
    unnamed x9 -> x0, waiting for transfers between devices: 50.2 us -> none
    all_to_all x1 -> x0, blocking collectives: 25.3 us -> none  [to_sequences(): return lax.all_to_all(block, 'seq', 0, 1, tiled=True)]
    pallas_call x0 -> x5, Pallas kernels: none -> 12.9 us  [place(): pl.pallas_call(functools.partial(place_kernel, ids, counts, spans), in_sp...]
  transfers between devices with their start and end apart: 11 -> 63, of which waited for: 7 -> 22; matrix products, arithmetic and copies ran while one was open for 16% -> 24% of each run, Pallas kernels for 6% -> 10%
where the time goes in v4:
time: 498 us; the launch traced here: 489 us
  waiting for transfers between devices  154 us (31%)
  matrix products  117 us (23%)
  starting transfers between devices  73.3 us (15%)
  Pallas kernels  55 us (11%)
  local copies, waits for them, and re-layouts  45.6 us (9%)
  other arithmetic  43 us (9%)
    ppermute x63, waiting for transfers between devices, swap(): lax.ppermute(block, BOTH, [(i, i ^ distance) for i in range(devices)])  154 us
    ppermute x63, starting transfers between devices, swap(): lax.ppermute(block, BOTH, [(i, i ^ distance) for i in range(devices)])  73.3 us
    dot_general x1, matrix products, on_device(): jnp.dot(first_low, wide_in, preferred_element_type=F32) + full_in_bias  36.8 us
    dot_general x4, matrix products, times_transposed(): lax.dot_general(left, right, (((1,), (1,)), ((), ())), preferred_element_...  34.2 us
    dot_general x4, matrix products, over_rows(): lax.dot_general(left, right, (((0,), (0,)), ((), ())), preferred_element_...  25.3 us
    pallas_call x1, Pallas kernels, attention_backward(): pl.pallas_call(functools.partial(bwd_kernel, cq), grid=(seqs, pairs), in_...  24.7 us
    unnamed x100, local copies, waits for them, and re-layouts  19.6 us
    pallas_call x1, Pallas kernels, attention_forward(): pl.pallas_call(functools.partial(fwd_kernel, cq), grid=(seqs, pairs), in_...  17.3 us
  transfers between devices with their start and end apart: 63, of which 22 were waited for; matrix products, arithmetic and copies ran while one was open for 24% of the time, Pallas kernels for 10%

profile of v4, /device:TPU:0, one launch (start us, length us, event | category | flops | bytes accessed | tf_op | source)
XLA Modules:
  0.0 489.3 jit_solution(7966540335210069640)
XLA Ops:
  51.1 6.7 %collective-permute-done.1 = bf16[2,128,768]{2,1,0:T(8,128)(2,1)S(1)} collective-permute-done((bf16[2,128,768]{2,1,0:T(8,128)(2,1)S(1)}, bf16[2,128,768]{2,1,0:T(8,128)(2,1)S(1)}, u32[]{:S(2)}, u32[]{:S(2)}) %collective-permute-start.1) | collective-permute-done | bytes 393248 | tf_op jit(solution)/shard_map/ppermute | solution.py:122
  59.2 6.1 %collective-permute-done.2 = bf16[2,128,768]{2,1,0:T(8,128)(2,1)S(1)} collective-permute-done((bf16[2,128,768]{2,1,0:T(8,128)(2,1)S(1)}, bf16[2,128,768]{2,1,0:T(8,128)(2,1)S(1)}, u32[]{:S(2)}, u32[]{:S(2)}) %collective-permute-start.2) | collective-permute-done | bytes 393248 | tf_op jit(solution)/shard_map/ppermute | solution.py:122
  72.6 7.5 %add_convert_fusion.1.q_ref.k_ref.v_ref = bf16[1024,2304]{1,0:T(8,128)(2,1)} fusion(bf16[1024,768]{1,0:T(8,128)(2,1)} %bitcast.283, bf16[768,2304]{1,0:T(8,128)(2,1)S(1)} %bitcast.264, f32[2304]{0:T(1024)S(1)} %pad_maximum_fusion.9), kind=kOutput, calls=%fused_computation.17 | convolution fusion | flops 3628597248 | bytes 9839616 | tf_op jit(solution)/shard_map/dot_general | solution.py:379
  83.5 17.3 %attention_forward.1 = (bf16[1024,768]{1,0:T(8,128)(2,1)S(1)}, f32[12,2,512]{2,1,0:T(2,128)S(1)}) custom-call(bf16[1024,2304]{1,0:T(8,128)(2,1)} %add_convert_fusion.1.q_ref.k_ref.v_ref, bf16[1024,2304]{1,0:T(8,128)(2,1)} %add_convert_fusion.1.q_ref.k_ref.v_ref, bf16[1024,2304]{1,0:T(8,128)(2,1)} %add_convert_fusion.1.q_ref.k_ref.v_ref, ...), custom_call_target="tpu_custom_call" | custom-call | flops 1610612736 | bytes 6291456 | tf_op jit(solution)/shard_map/attention_forward/pallas_call | solution.py:105
  105.7 12.6 %collective-permute-done.28 = bf16[4,96,768]{2,1,0:T(8,128)(2,1)S(1)} collective-permute-done((bf16[4,96,768]{2,1,0:T(8,128)(2,1)S(1)}, bf16[4,96,768]{2,1,0:T(8,128)(2,1)S(1)}, u32[]{:S(2)}, u32[]{:S(2)}) %collective-permute-start.28) | collective-permute-done | bytes 589856 | tf_op jit(solution)/shard_map/ppermute | solution.py:122
  122.6 10.8 %collective-permute-done.17.refs_2_ = bf16[4,24,3968]{2,1,0:T(8,128)(2,1)S(1)} collective-permute-done((bf16[4,24,3968]{2,1,0:T(8,128)(2,1)S(1)}, bf16[4,24,3968]{2,1,0:T(8,128)(2,1)S(1)}, u32[]{:S(2)}, u32[]{:S(2)}) %collective-permute-start.17) | collective-permute-done | bytes 761888 | tf_op jit(solution)/shard_map/ppermute | solution.py:122
  133.8 12.6 %collective-permute-done.30.refs_2_ = bf16[8,96,768]{2,1,0:T(8,128)(2,1)} collective-permute-done((bf16[8,96,768]{2,1,0:T(8,128)(2,1)}, bf16[8,96,768]{2,1,0:T(8,128)(2,1)}, u32[]{:S(2)}, u32[]{:S(2)}) %collective-permute-start.30) | collective-permute-done | bytes 1179680 | tf_op jit(solution)/shard_map/ppermute | solution.py:122
  167.8 36.8 %multiply_convert_fusion = (bf16[1024,3072]{1,0:T(8,128)(2,1)}, f32[1024,3072]{1,0:T(8,128)}, f32[1024,3072]{1,0:T(8,128)}) fusion(f32[3072]{0:T(1024)S(1)} %reshape.390, bf16[1024,768]{1,0:T(8,128)(2,1)} %add_convert_fusion.4, bf16[768,3072]{1,0:T(8,128)(2,1)} %bitcast.262), kind=kOutput, calls=%fused_computation.3 | convolution fusion | flops 5039456256 | bytes 37761024 | tf_op jit(solution)/shard_map/dot_general | solution.py:411
  208.4 7.4 %fusion.56 = (f32[1024]{0:T(1024)S(1)}, f32[1024,768]{1,0:T(8,128)S(1)}) fusion(f32[768]{0:T(1024)S(1)} %reshape.391, bf16[1024,3072]{1,0:T(8,128)(2,1)} %get-tuple-element.78, bf16[3072,768]{1,0:T(8,128)(2,1)S(1)} %bitcast.260, bf16[1024,768]{1,0:T(8,128)(2,1)S(1)} %copy-done.22), kind=kOutput, calls=%fused_computation.225 | convolution fusion | flops 4834982912 | bytes 15735808 | tf_op jit(solution)/shard_map/dot_general | solution.py:416
  222.3 6.0 %convolution_convert_fusion.1 = bf16[3072,768]{1,0:T(8,128)(2,1)S(1)} fusion(bf16[1024,3072]{1,0:T(8,128)(2,1)S(1)} %bitcast.304, bf16[1024,768]{1,0:T(8,128)(2,1)S(1)} %get-tuple-element.71), kind=kOutput, calls=%fused_computation.21 | convolution fusion | flops 4834197504 | bytes 12582912 | tf_op jit(solution)/shard_map/dot_general | solution.py:27
  232.7 16.0 %fusion.57 = (bf16[3072]{0:T(1024)(128)(2,1)S(1)}, bf16[1024,3072]{1,0:T(8,128)(2,1)}) fusion(f32[1024,3072]{1,0:T(8,128)} %get-tuple-element.79, bf16[1024,768]{1,0:T(8,128)(2,1)} %copy-done.20, bf16[3072,768]{1,0:T(8,128)(2,1)S(1)} %bitcast.261, f32[1024,3072]{1,0:T(8,128)} %get-tuple-element.123, f32[3072]{0:T(1024)S(1)} %reshape.390), kind=kOutput, calls=%fused_computation.226 | convolution fusion | flops 4882166784 | bytes 37767168 | tf_op jit(solution)/shard_map/dot_general | solution.py:33
  248.9 7.9 %convolution_convert_fusion = bf16[768,3072]{1,0:T(8,128)(2,1)S(1)} fusion(bf16[1024,768]{1,0:T(8,128)(2,1)} %add_convert_fusion.4, bf16[1024,3072]{1,0:T(8,128)(2,1)} %get-tuple-element.48), kind=kOutput, calls=%fused_computation.20 | convolution fusion | flops 4834197504 | bytes 12582912 | tf_op jit(solution)/shard_map/dot_general | solution.py:27
  265.5 9.4 %multiply_reduce_fusion = (bf16[768]{0:T(1024)(128)(2,1)S(1)}, f32[1024]{0:T(1024)S(1)}, bf16[768]{0:T(1024)(128)(2,1)S(1)}, f32[1024,768]{1,0:T(8,128)S(1)}) fusion(f32[1024,768]{1,0:T(8,128)} %get-tuple-element.122, f32[1024]{0:T(1024)S(1)} %copy-done.34, f32[1024]{0:T(1024)S(1)} %copy-done.27, f32[768]{0:T(1024)S(1)} %copy-done.32, ...), kind=kOutput, calls=%fused_computation.39 | convolution fusion | flops 4839699456 | bytes 20469760 | tf_op jit(solution)/shard_map/dot_general | solution.py:33
  300.2 23.9 %collective-permute-done.33.refs_2_ = bf16[1,2,128,768]{3,2,1,0:T(8,128)(2,1)S(1)} collective-permute-done((bf16[1,2,128,768]{3,2,1,0:T(8,128)(2,1)}, bf16[1,2,128,768]{3,2,1,0:T(8,128)(2,1)S(1)}, u32[]{:S(2)}, u32[]{:S(2)}) %collective-permute-start.33) | collective-permute-done | bytes 393248 | tf_op jit(solution)/shard_map/ppermute | solution.py:122
  324.1 6.6 %collective-permute-done.34.refs_3_ = bf16[1,2,128,768]{3,2,1,0:T(8,128)(2,1)S(1)} collective-permute-done((bf16[1,2,128,768]{3,2,1,0:T(8,128)(2,1)S(1)}, bf16[1,2,128,768]{3,2,1,0:T(8,128)(2,1)S(1)}, u32[]{:S(2)}, u32[]{:S(2)}) %collective-permute-start.34) | collective-permute-done | bytes 393248 | tf_op jit(solution)/shard_map/ppermute | solution.py:122
  337.6 24.7 %attention_backward.1 = (bf16[1024,768]{1,0:T(8,128)(2,1)S(1)}, bf16[1024,768]{1,0:T(8,128)(2,1)S(1)}, bf16[1024,768]{1,0:T(8,128)(2,1)S(1)}) custom-call(bf16[1024,2304]{1,0:T(8,128)(2,1)} %add_convert_fusion.1.q_ref.k_ref.v_ref, bf16[1024,2304]{1,0:T(8,128)(2,1)} %add_convert_fusion.1.q_ref.k_ref.v_ref, ...), custom_call_target="tpu_custom_call" | custom-call | flops 4026531840 | bytes 11010048 | tf_op jit(solution)/shard_map/attention_backward/pallas_call | solution.py:116
  370.9 7.8 %collective-permute-done.61 = bf16[96,768]{1,0:T(8,128)(2,1)S(1)} collective-permute-done((bf16[96,768]{1,0:T(8,128)(2,1)S(1)}, bf16[96,768]{1,0:T(8,128)(2,1)S(1)}, u32[]{:S(2)}, u32[]{:S(2)}) %collective-permute-start.61) | collective-permute-done | bytes 147488 | tf_op jit(solution)/shard_map/ppermute | solution.py:122
  385.2 8.5 %convolution_convert_fusion.2 = bf16[768,2304]{1,0:T(8,128)(2,1)} fusion(bf16[1024,768]{1,0:T(8,128)(2,1)} %bitcast.285, bf16[1024,2304]{1,0:T(8,128)(2,1)} %pad_maximum_fusion), kind=kOutput, calls=%fused_computation.22 | convolution fusion | flops 3625648128 | bytes 9830400 | tf_op jit(solution)/shard_map/dot_general | solution.py:27
  402.8 6.2 %add_convert_fusion.2 = bf16[1024,768]{1,0:T(8,128)(2,1)S(1)} fusion(f32[1024,768]{1,0:T(8,128)S(1)} %copy-done.10, bf16[1024,2304]{1,0:T(8,128)(2,1)} %pad_maximum_fusion, bf16[768,2304]{1,0:T(8,128)(2,1)S(1)} %bitcast.265, f32[1024]{0:T(1024)S(1)} %negate_multiply_fusion.1), kind=kOutput, calls=%fused_computation.38 | convolution fusion | flops 3626237952 | bytes 12980224 | tf_op jit(solution)/shard_map/dot_general | solution.py:33
  411.8 9.4 %collective-permute-done.43.refs_2_ = bf16[1,2,128,768]{3,2,1,0:T(8,128)(2,1)S(1)} collective-permute-done((bf16[1,2,128,768]{3,2,1,0:T(8,128)(2,1)S(1)}, bf16[1,2,128,768]{3,2,1,0:T(8,128)(2,1)S(1)}, u32[]{:S(2)}, u32[]{:S(2)}) %collective-permute-start.43) | collective-permute-done | bytes 393248 | tf_op jit(solution)/shard_map/ppermute | solution.py:122
  421.2 7.6 %collective-permute-done.44.refs_3_ = bf16[1,2,128,768]{3,2,1,0:T(8,128)(2,1)S(1)} collective-permute-done((bf16[1,2,128,768]{3,2,1,0:T(8,128)(2,1)S(1)}, bf16[1,2,128,768]{3,2,1,0:T(8,128)(2,1)S(1)}, u32[]{:S(2)}, u32[]{:S(2)}) %collective-permute-start.44) | collective-permute-done | bytes 393248 | tf_op jit(solution)/shard_map/ppermute | solution.py:122
  434.5 9.4 %collective-permute-done.54 = bf16[2,24,3968]{2,1,0:T(8,128)(2,1)S(1)} collective-permute-done((bf16[2,24,3968]{2,1,0:T(8,128)(2,1)S(1)}, bf16[2,24,3968]{2,1,0:T(8,128)(2,1)S(1)}, u32[]{:S(2)}, u32[]{:S(2)}) %collective-permute-start.54) | collective-permute-done | bytes 380960 | tf_op jit(solution)/shard_map/ppermute | solution.py:122
  454.8 9.7 %collective-permute-done.58 = bf16[24,3968]{1,0:T(8,128)(2,1)S(1)} collective-permute-done((bf16[24,3968]{1,0:T(8,128)(2,1)S(1)}, bf16[24,3968]{1,0:T(8,128)(2,1)S(1)}, u32[]{:S(2)}, u32[]{:S(2)}) %collective-permute-start.58) | collective-permute-done | bytes 190496 | tf_op jit(solution)/shard_map/ppermute | solution.py:122
  481.6 6.0 %collective-permute-done.51 = bf16[24,2432]{1,0:T(8,128)(2,1)S(1)} collective-permute-done((bf16[24,2432]{1,0:T(8,128)(2,1)S(1)}, bf16[24,2432]{1,0:T(8,128)(2,1)S(1)}, u32[]{:S(2)}, u32[]{:S(2)}) %collective-permute-start.51) | collective-permute-done | bytes 116768 | tf_op jit(solution)/shard_map/ppermute | solution.py:122
  (344 shorter events, 210.2 us)
Async XLA Ops:
  14.5 26.9 %collective-permute-start.19 = (bf16[1,24,3968]{2,1,0:T(8,128)(2,1)S(1)}, bf16[1,24,3968]{2,1,0:T(8,128)(2,1)S(1)}, u32[]{:S(2)}, u32[]{:S(2)}) collective-permute-start(bf16[1,24,3968]{2,1,0:T(8,128)(2,1)S(1)} %fusion.32), channel_id=1, source_target_pairs={{0,16},{1,17},{2,18},{3,19},{4,20},{5,21},{6,22},{7,23},{8,24},{9,... | collective-permute-start | bytes 571400 | tf_op jit(solution)/shard_map/ppermute | solution.py:122
  16.5 26.5 %collective-permute-start.14 = (bf16[1,24,3968]{2,1,0:T(8,128)(2,1)S(1)}, bf16[1,24,3968]{2,1,0:T(8,128)(2,1)S(1)}, u32[]{:S(2)}, u32[]{:S(2)}) collective-permute-start(bf16[1,24,3968]{2,1,0:T(8,128)(2,1)S(1)} %fusion.32), channel_id=1, source_target_pairs={{0,8},{1,9},{2,10},{3,11},{4,12},{5,13},{6,14},{7,15},{8,0},{9,1},... | collective-permute-start | bytes 571400 | tf_op jit(solution)/shard_map/ppermute | solution.py:122
  35.8 22.0 %collective-permute-start.6 = (bf16[4,24,2432]{2,1,0:T(8,128)(2,1)S(1)}, bf16[4,24,2432]{2,1,0:T(8,128)(2,1)S(1)}, u32[]{:S(2)}, u32[]{:S(2)}) collective-permute-start(bf16[4,24,2432]{2,1,0:T(8,128)(2,1)S(1)} %pad_maximum_fusion.4.refs_0_), channel_id=1, source_target_pairs={{0,2},{1,3},{2,0},{3,1},{4,6},{5,7},{6,4},{7,5},{8,10},{9,11},{10,... | collective-permute-start | bytes 1400840 | tf_op jit(solution)/shard_map/ppermute | solution.py:122
  80.2 22.4 %collective-permute-start.21 = (bf16[2,24,3968]{2,1,0:T(8,128)(2,1)S(1)}, bf16[2,24,3968]{2,1,0:T(8,128)(2,1)S(1)}, u32[]{:S(2)}, u32[]{:S(2)}) collective-permute-start(bf16[2,24,3968]{2,1,0:T(8,128)(2,1)S(1)} %copy-done.24), channel_id=1, source_target_pairs={{0,2},{1,3},{2,0},{3,1},{4,6},{5,7},{6,4},{7,5},{8,10},{9,11},{10,... | collective-permute-start | bytes 1142792 | tf_op jit(solution)/shard_map/ppermute | solution.py:122
  81.8 21.4 %collective-permute-start.15 = (bf16[2,24,3968]{2,1,0:T(8,128)(2,1)S(1)}, bf16[2,24,3968]{2,1,0:T(8,128)(2,1)S(1)}, u32[]{:S(2)}, u32[]{:S(2)}) collective-permute-start(bf16[2,24,3968]{2,1,0:T(8,128)(2,1)S(1)} %copy-done.23), channel_id=1, source_target_pairs={{0,4},{1,5},{2,6},{3,7},{4,0},{5,1},{6,2},{7,3},{8,12},{9,13},{10,... | collective-permute-start | bytes 1142792 | tf_op jit(solution)/shard_map/ppermute | solution.py:122
  102.6 19.9 %collective-permute-start.23 = (bf16[4,24,3968]{2,1,0:T(8,128)(2,1)S(1)}, bf16[4,24,3968]{2,1,0:T(8,128)(2,1)S(1)}, u32[]{:S(2)}, u32[]{:S(2)}) collective-permute-start(bf16[4,24,3968]{2,1,0:T(8,128)(2,1)S(1)} %constant_dynamic-update-slice_fusion.5.refs_4_), channel_id=1, source_target_pairs={{0,4},{1,5},{2,6},{3,7},{4,0},{5,1},{6,2},{7,3},{8,12},{9,13},{10,... | collective-permute-start | bytes 2285576 | tf_op jit(solution)/shard_map/ppermute | solution.py:122
  103.3 30.1 %collective-permute-start.17 = (bf16[4,24,3968]{2,1,0:T(8,128)(2,1)S(1)}, bf16[4,24,3968]{2,1,0:T(8,128)(2,1)S(1)}, u32[]{:S(2)}, u32[]{:S(2)}) collective-permute-start(bf16[4,24,3968]{2,1,0:T(8,128)(2,1)S(1)} %constant_dynamic-update-slice_fusion.3.refs_0_), channel_id=1, source_target_pairs={{0,2},{1,3},{2,0},{3,1},{4,6},{5,7},{6,4},{7,5},{8,10},{9,11},{10,... | collective-permute-start | bytes 2285576 | tf_op jit(solution)/shard_map/ppermute | solution.py:122
  119.1 27.3 %collective-permute-start.30 = (bf16[8,96,768]{2,1,0:T(8,128)(2,1)}, bf16[8,96,768]{2,1,0:T(8,128)(2,1)}, u32[]{:S(2)}, u32[]{:S(2)}) collective-permute-start(bf16[8,96,768]{2,1,0:T(8,128)(2,1)} %constant_dynamic-update-slice_fusion.7.refs_0_), channel_id=1, source_target_pairs={{0,4},{1,5},{2,6},{3,7},{4,0},{5,1},{6,2},{7,3},{8,12},{9,13},{10,... | collective-permute-start | bytes 3538952 | tf_op jit(solution)/shard_map/ppermute | solution.py:122
  119.6 26.8 %collective-permute-start.16 = (bf16[4,24,3968]{2,1,0:T(8,128)(2,1)S(1)}, bf16[4,24,3968]{2,1,0:T(8,128)(2,1)}, u32[]{:S(2)}, u32[]{:S(2)}) collective-permute-start(bf16[4,24,3968]{2,1,0:T(8,128)(2,1)S(1)} %constant_dynamic-update-slice_fusion.3.refs_0_), channel_id=1, source_target_pairs={{0,1},{1,0},{2,3},{3,2},{4,5},{5,4},{6,7},{7,6},{8,9},{9,8},{10,11... | collective-permute-start | bytes 2285576 | tf_op jit(solution)/shard_map/ppermute | solution.py:122
  122.6 23.9 %collective-permute-start.24 = (bf16[4,24,3968]{2,1,0:T(8,128)(2,1)S(1)}, bf16[4,24,3968]{2,1,0:T(8,128)(2,1)}, u32[]{:S(2)}, u32[]{:S(2)}) collective-permute-start(bf16[4,24,3968]{2,1,0:T(8,128)(2,1)S(1)} %collective-permute-done.23.refs_6_), channel_id=1, source_target_pairs={{0,1},{1,0},{2,3},{3,2},{4,5},{5,4},{6,7},{7,6},{8,9},{9,8},{10,11... | collective-permute-start | bytes 2285576 | tf_op jit(solution)/shard_map/ppermute | solution.py:122
  133.3 72.2 %collective-permute-start.29 = (bf16[8,96,768]{2,1,0:T(8,128)(2,1)}, bf16[8,96,768]{2,1,0:T(8,128)(2,1)}, u32[]{:S(2)}, u32[]{:S(2)}) collective-permute-start(bf16[8,96,768]{2,1,0:T(8,128)(2,1)} %constant_dynamic-update-slice_fusion.7.refs_0_), channel_id=1, source_target_pairs={{0,1},{1,0},{2,3},{3,2},{4,5},{5,4},{6,7},{7,6},{8,9},{9,8},{10,11... | collective-permute-start | bytes 3538952 | tf_op jit(solution)/shard_map/ppermute | solution.py:122
  146.4 59.1 %collective-permute-start.31 = (bf16[8,96,768]{2,1,0:T(8,128)(2,1)}, bf16[8,96,768]{2,1,0:T(8,128)(2,1)}, u32[]{:S(2)}, u32[]{:S(2)}) collective-permute-start(bf16[8,96,768]{2,1,0:T(8,128)(2,1)} %collective-permute-done.30.refs_2_), channel_id=1, source_target_pairs={{0,1},{1,0},{2,3},{3,2},{4,5},{5,4},{6,7},{7,6},{8,9},{9,8},{10,11... | collective-permute-start | bytes 3538952 | tf_op jit(solution)/shard_map/ppermute | solution.py:122
  165.6 39.3 %collective-permute-start.35 = (bf16[2,128,768]{2,1,0:T(8,128)(2,1)S(1)}, bf16[2,128,768]{2,1,0:T(8,128)(2,1)S(1)}, u32[]{:S(2)}, u32[]{:S(2)}) collective-permute-start(bf16[2,128,768]{2,1,0:T(8,128)(2,1)S(1)} %get-tuple-element.94), channel_id=1, source_target_pairs={{0,1},{1,0},{2,3},{3,2},{4,5},{5,4},{6,7},{7,6},{8,9},{9,8},{10,11... | collective-permute-start | bytes 1179656 | tf_op jit(solution)/shard_map/ppermute | solution.py:122
  166.2 38.8 %collective-permute-start.36 = (bf16[2,128,768]{2,1,0:T(8,128)(2,1)S(1)}, bf16[2,128,768]{2,1,0:T(8,128)(2,1)S(1)}, u32[]{:S(2)}, u32[]{:S(2)}) collective-permute-start(bf16[2,128,768]{2,1,0:T(8,128)(2,1)S(1)} %get-tuple-element.93), channel_id=1, source_target_pairs={{0,2},{1,3},{2,0},{3,1},{4,6},{5,7},{6,4},{7,5},{8,10},{9,11},{10,... | collective-permute-start | bytes 1179656 | tf_op jit(solution)/shard_map/ppermute | solution.py:122
  167.7 37.4 %collective-permute-start.37 = (bf16[2,128,768]{2,1,0:T(8,128)(2,1)S(1)}, bf16[2,128,768]{2,1,0:T(8,128)(2,1)S(1)}, u32[]{:S(2)}, u32[]{:S(2)}) collective-permute-start(bf16[2,128,768]{2,1,0:T(8,128)(2,1)S(1)} %get-tuple-element.92), channel_id=1, source_target_pairs={{0,3},{1,2},{2,1},{3,0},{4,7},{5,6},{6,5},{7,4},{8,11},{9,10},{10,... | collective-permute-start | bytes 1179656 | tf_op jit(solution)/shard_map/ppermute | solution.py:122
  232.0 27.5 %collective-permute-start.38 = (bf16[16,96,768]{2,1,0:T(8,128)(2,1)}, bf16[16,96,768]{2,1,0:T(8,128)(2,1)}, u32[]{:S(2)}, u32[]{:S(2)}) collective-permute-start(bf16[16,96,768]{2,1,0:T(8,128)(2,1)} %dynamic-slice_bitcast_fusion.1), channel_id=1, source_target_pairs={{0,1},{1,0},{2,3},{3,2},{4,5},{5,4},{6,7},{7,6},{8,9},{9,8},{10,11... | collective-permute-start | bytes 7077896 | tf_op jit(solution)/shard_map/ppermute | solution.py:122
  286.7 46.0 %collective-permute-start.39 = (bf16[4,2,96,768]{3,2,0,1:T(8,128)(2,1)}, bf16[4,2,96,768]{3,2,0,1:T(8,128)(2,1)}, u32[]{:S(2)}, u32[]{:S(2)}) collective-permute-start(bf16[4,2,96,768]{3,2,0,1:T(8,128)(2,1)} %bitcast.259), channel_id=1, source_target_pairs={{0,2},{1,3},{2,0},{3,1},{4,6},{5,7},{6,4},{7,5},{8,10},{9,11},{10,... | collective-permute-start | bytes 3538952 | tf_op jit(solution)/shard_map/ppermute | solution.py:122
  293.9 85.6 %collective-permute-start.40 = (bf16[16,24,3968]{2,1,0:T(8,128)(2,1)}, bf16[16,24,3968]{2,1,0:T(8,128)(2,1)}, u32[]{:S(2)}, u32[]{:S(2)}) collective-permute-start(bf16[16,24,3968]{2,1,0:T(8,128)(2,1)} %dynamic-slice_bitcast_fusion), channel_id=1, source_target_pairs={{0,1},{1,0},{2,3},{3,2},{4,5},{5,4},{6,7},{7,6},{8,9},{9,8},{10,11... | collective-permute-start | bytes 9142280 | tf_op jit(solution)/shard_map/ppermute | solution.py:122
  295.4 28.7 %collective-permute-start.33 = (bf16[1,2,128,768]{3,2,1,0:T(8,128)(2,1)}, bf16[1,2,128,768]{3,2,1,0:T(8,128)(2,1)S(1)}, u32[]{:S(2)}, u32[]{:S(2)}) collective-permute-start(bf16[1,2,128,768]{3,2,1,0:T(8,128)(2,1)} %get-tuple-element.97), channel_id=1, source_target_pairs={{0,2},{1,3},{2,0},{3,1},{4,6},{5,7},{6,4},{7,5},{8,10},{9,11},{10,... | collective-permute-start | bytes 1179656 | tf_op jit(solution)/shard_map/ppermute | solution.py:122
  295.9 34.7 %collective-permute-start.34 = (bf16[1,2,128,768]{3,2,1,0:T(8,128)(2,1)S(1)}, bf16[1,2,128,768]{3,2,1,0:T(8,128)(2,1)S(1)}, u32[]{:S(2)}, u32[]{:S(2)}) collective-permute-start(bf16[1,2,128,768]{3,2,1,0:T(8,128)(2,1)S(1)} %get-tuple-element.96), channel_id=1, source_target_pairs={{0,3},{1,2},{2,1},{3,0},{4,7},{5,6},{6,5},{7,4},{8,11},{9,10},{10,... | collective-permute-start | bytes 1179656 | tf_op jit(solution)/shard_map/ppermute | solution.py:122
  334.4 27.9 %collective-permute-start.41 = (bf16[4,96,768]{2,1,0:T(8,128)(2,1)S(1)}, bf16[4,96,768]{2,1,0:T(8,128)(2,1)S(1)}, u32[]{:S(2)}, u32[]{:S(2)}) collective-permute-start(bf16[4,96,768]{2,1,0:T(8,128)(2,1)S(1)} %dynamic-slice_bitcast_fusion.5), channel_id=1, source_target_pairs={{0,4},{1,5},{2,6},{3,7},{4,0},{5,1},{6,2},{7,3},{8,12},{9,13},{10,... | collective-permute-start | bytes 1769480 | tf_op jit(solution)/shard_map/ppermute | solution.py:122
  394.6 36.4 %collective-permute-start.56 = (bf16[2,2,24,3968]{3,2,1,0:T(8,128)(2,1)}, bf16[2,2,24,3968]{3,2,1,0:T(8,128)(2,1)}, u32[]{:S(2)}, u32[]{:S(2)}) collective-permute-start(bf16[2,2,24,3968]{3,2,1,0:T(8,128)(2,1)} %dynamic-slice_bitcast_fusion.3), channel_id=1, source_target_pairs={{0,2},{1,3},{2,0},{3,1},{4,6},{5,7},{6,4},{7,5},{8,10},{9,11},{10,... | collective-permute-start | bytes 2285576 | tf_op jit(solution)/shard_map/ppermute | solution.py:122
  397.0 34.0 %collective-permute-start.53 = (bf16[2,2,24,3968]{3,2,1,0:T(8,128)(2,1)}, bf16[2,2,24,3968]{3,2,1,0:T(8,128)(2,1)}, u32[]{:S(2)}, u32[]{:S(2)}) collective-permute-start(bf16[2,2,24,3968]{3,2,1,0:T(8,128)(2,1)} %dynamic-slice_bitcast_fusion.4), channel_id=1, source_target_pairs={{0,4},{1,5},{2,6},{3,7},{4,0},{5,1},{6,2},{7,3},{8,12},{9,13},{10,... | collective-permute-start | bytes 2285576 | tf_op jit(solution)/shard_map/ppermute | solution.py:122
  411.4 39.7 %collective-permute-start.45 = (bf16[16,24,2432]{2,1,0:T(8,128)(2,1)S(1)}, bf16[16,24,2432]{2,1,0:T(8,128)(2,1)S(1)}, u32[]{:S(2)}, u32[]{:S(2)}) collective-permute-start(bf16[16,24,2432]{2,1,0:T(8,128)(2,1)S(1)} %dynamic-slice_bitcast_fusion.2), channel_id=1, source_target_pairs={{0,1},{1,0},{2,3},{3,2},{4,5},{5,4},{6,7},{7,6},{8,9},{9,8},{10,11... | collective-permute-start | bytes 5603336 | tf_op jit(solution)/shard_map/ppermute | solution.py:122
  (82 other events, 845.9 us)

commit v5 on v4

--- a/solution.py
+++ b/solution.py
@@ -35,89 +35,139 @@
     )
 
 
-def nt(a,b): return lax.dot_general(a,b,(((1,),(1,)),((),())),preferred_element_type=F32)
-def tn(a,b): return lax.dot_general(a,b,(((0,),(0,)),((),())),preferred_element_type=F32)
-def nn(a,b): return lax.dot_general(a,b,(((1,),(0,)),((),())),preferred_element_type=F32)
+def nt(a, b):
+    return lax.dot_general(a, b, (((1,), (1,)), ((), ())), preferred_element_type=F32)
+
+
+def tn(a, b):
+    return lax.dot_general(a, b, (((0,), (0,)), ((), ())), preferred_element_type=F32)
+
+
+def nn(a, b):
+    return lax.dot_general(a, b, (((1,), (0,)), ((), ())), preferred_element_type=F32)
+
 
 def masked_pair(q, k, bias, head, lane):
-    mine = (lane >= head*HD) & (lane < (head+1)*HD)
-    spare = lane == (HD if head==0 else 0)
-    zero=jnp.zeros((),BF)
-    qh = jnp.where(mine, q*BF(0.125), jnp.where(spare, jnp.ones((),BF), zero))
+    mine = (lane >= head * HD) & (lane < (head + 1) * HD)
+    spare = lane == (HD if head == 0 else 0)
+    zero = jnp.zeros((), BF)
+    qh = jnp.where(mine, q * BF(0.125), jnp.where(spare, jnp.ones((), BF), zero))
     kh = jnp.where(mine, k, jnp.where(spare, bias, zero))
     return qh, kh
 
-def fwd_kernel(cq, q_ref,k_ref,v_ref,b_ref,o_ref,lse_ref):
-    n=q_ref.shape[0]
-    lane=lax.broadcasted_iota(jnp.int32,(n,128),1)
-    q=q_ref[...]; k=k_ref[...]; v=v_ref[...]; bias=b_ref[0]
-    pairs=[masked_pair(q,k,bias,h,lane) for h in range(2)]
-    for c in range(n//cq):
-        sl=slice(c*cq,(c+1)*cq)
-        halves=[]
-        for h in range(2):
-            qh,kh=pairs[h]
-            s=nt(kh,qh[sl])
-            m=jnp.max(s,0,keepdims=True)
-            e=jnp.exp(s-m)
-            l=jnp.sum(e,0,keepdims=True)
-            ot=tn(v[:,h*HD:(h+1)*HD],e.astype(BF))
-            halves.append(ot*(1.0/l))
-            lse_ref[0,h:h+1,sl]=m+jnp.log(l)
-        o_ref[sl,:]=jnp.concatenate(halves,0).T.astype(BF)
-
-def bwd_kernel(cq, q_ref,k_ref,v_ref,b_ref,lse_ref,g_ref,dq_ref,dk_ref,dv_ref):
-    n=q_ref.shape[0]
-    lane=lax.broadcasted_iota(jnp.int32,(n,128),1)
-    q=q_ref[...]; k=k_ref[...]; v=v_ref[...]; bias=b_ref[0]; g=g_ref[...]
-    qs=q*BF(0.125); ks=k*BF(0.125)
-    zero=jnp.zeros((),BF)
-    dks=[];dvs=[]
-    dq=[[None,None] for _ in range(n//cq)]
+
+def forward_kernel(packed_ref, mask_ref, mixed_ref, logsum_ref):
+    count = packed_ref.shape[0]
+    lane = lax.broadcasted_iota(jnp.int32, (count, 128), 1)
+    q, k, v = (packed_ref[:, i * 128 : (i + 1) * 128] for i in range(3))
+    bias = mask_ref[0]
+    halves = []
     for h in range(2):
-        qh,kh=masked_pair(q,k,bias,h,lane)
-        mine = (lane >= h*HD) & (lane < (h+1)*HD)
-        vh=jnp.where(mine,v,zero)
-        kth=ks[:,h*HD:(h+1)*HD]
-        dk=dv=None
-        for c in range(n//cq):
-            sl=slice(c*cq,(c+1)*cq)
-            s=nt(kh,qh[sl])
-            p=jnp.exp(s-lse_ref[0,h:h+1,sl])
-            gp=nt(vh,g[sl])
-            inner=jnp.sum(p*gp,0,keepdims=True)
-            ds=(p*(gp-inner)).astype(BF)
-            a=nn(p.astype(BF),g[sl]); b=nn(ds,qs[sl])
-            dv=a if dv is None else dv+a
-            dk=b if dk is None else dk+b
-            dq[c][h]=tn(kth,ds)
-        dks.append(dk);dvs.append(dv)
-    for c in range(n//cq):
-        sl=slice(c*cq,(c+1)*cq)
-        dq_ref[sl,:]=jnp.concatenate(dq[c],0).T.astype(BF)
-    first=lane<HD
-    dk_ref[...]=jnp.where(first,dks[0],dks[1]).astype(BF)
-    dv_ref[...]=jnp.where(first,dvs[0],dvs[1]).astype(BF)
-
-def attention_forward(packed,bias,length,cq=512):
-    rows,wide=packed.shape; width=wide//3; pairs=width//128; seqs=rows//length
-    blk=lambda off: pl.BlockSpec((length,128),lambda s,p:(s,off*pairs+p))
-    return pl.pallas_call(functools.partial(fwd_kernel,cq),grid=(seqs,pairs),
-      in_specs=[blk(0),blk(1),blk(2),pl.BlockSpec((1,length,128),lambda s,p:(s,0,0))],
-      out_specs=[blk(0),pl.BlockSpec((1,2,length),lambda s,p:(s*pairs+p,0,0))],
-      out_shape=[jax.ShapeDtypeStruct((rows,width),BF),jax.ShapeDtypeStruct((seqs*pairs,2,length),F32)],
-      compiler_params=pltpu.CompilerParams(vmem_limit_bytes=48*2**20),name="attention_forward",
-      cost_estimate=pl.CostEstimate(flops=4*rows*length*width,bytes_accessed=rows*width*8,transcendentals=rows*length*width//HD))(packed,packed,packed,bias)
-
-def attention_backward(packed,bias,lse,grad,length,cq=512):
-    rows,wide=packed.shape; width=wide//3; pairs=width//128; seqs=rows//length
-    blk=lambda off: pl.BlockSpec((length,128),lambda s,p:(s,off*pairs+p))
-    o=jax.ShapeDtypeStruct((rows,width),BF)
-    return pl.pallas_call(functools.partial(bwd_kernel,cq),grid=(seqs,pairs),
-      in_specs=[blk(0),blk(1),blk(2),pl.BlockSpec((1,length,128),lambda s,p:(s,0,0)),pl.BlockSpec((1,2,length),lambda s,p:(s*pairs+p,0,0)),blk(0)],
-      out_specs=[blk(0)]*3,out_shape=[o,o,o],
-      compiler_params=pltpu.CompilerParams(vmem_limit_bytes=48*2**20),name="attention_backward",
-      cost_estimate=pl.CostEstimate(flops=10*rows*length*width,bytes_accessed=rows*width*14,transcendentals=rows*length*width//HD))(packed,packed,packed,bias,lse,grad)
+        qh, kh = masked_pair(q, k, bias, h, lane)
+        scores = nt(kh, qh)
+        top = jnp.max(scores, 0, keepdims=True)
+        raised = jnp.exp(scores - top)
+        total = jnp.sum(raised, 0, keepdims=True)
+        mixed = tn(v[:, h * HD : (h + 1) * HD], raised.astype(BF))
+        halves.append(mixed * (1.0 / total))
+        logsum_ref[0, h : h + 1, :] = top + jnp.log(total)
+    mixed_ref[...] = jnp.concatenate(halves, 0).T.astype(BF)
+
+
+def backward_kernel(packed_ref, mask_ref, logsum_ref, grad_ref, out_ref, sums_ref):
+    count = packed_ref.shape[0]
+    lane = lax.broadcasted_iota(jnp.int32, (count, 128), 1)
+    q, k, v = (packed_ref[:, i * 128 : (i + 1) * 128] for i in range(3))
+    bias = mask_ref[0]
+    grad = grad_ref[...]
+    q_scaled, k_scaled = q * BF(0.125), k * BF(0.125)
+    dq, dk, dv = [], [], []
+    for h in range(2):
+        qh, kh = masked_pair(q, k, bias, h, lane)
+        mine = (lane >= h * HD) & (lane < (h + 1) * HD)
+        vh = jnp.where(mine, v, jnp.zeros((), BF))
+        probs = jnp.exp(nt(kh, qh) - logsum_ref[0, h : h + 1, :])
+        grad_probs = nt(vh, grad)
+        inner = jnp.sum(probs * grad_probs, 0, keepdims=True)
+        grad_scores = (probs * (grad_probs - inner)).astype(BF)
+        dv.append(nn(probs.astype(BF), grad))
+        dk.append(nn(grad_scores, q_scaled))
+        dq.append(tn(k_scaled[:, h * HD : (h + 1) * HD], grad_scores))
+    low_half = lane < HD
+    parts = (
+        jnp.concatenate(dq, 0).T,
+        jnp.where(low_half, dk[0], dk[1]),
+        jnp.where(low_half, dv[0], dv[1]),
+    )
+    for i, part in enumerate(parts):
+        rounded = part.astype(BF)
+        out_ref[:, i * 128 : (i + 1) * 128] = rounded
+        sums_ref[0, :, i * 128 : (i + 1) * 128] = jnp.sum(
+            rounded.astype(F32), 0, keepdims=True
+        )
+
+
+def attention_specs(packed, length):
+    rows, wide = packed.shape
+    pairs, seqs = wide // 384, rows // length
+    block = lambda size: pl.BlockSpec((length, size), lambda s, p: (s, p))
+    mask = pl.BlockSpec((1, length, 128), lambda s, p: (s, 0, 0))
+    row = lambda count, size: pl.BlockSpec((1, count, size), lambda s, p: (s * pairs + p, 0, 0))
+    return rows, pairs, seqs, block, mask, row
+
+
+def attention_forward(packed, mask, length):
+    rows, pairs, seqs, block, mask_spec, row = attention_specs(packed, length)
+    return pl.pallas_call(
+        forward_kernel,
+        grid=(seqs, pairs),
+        in_specs=[block(384), mask_spec],
+        out_specs=[block(128), row(2, length)],
+        out_shape=[
+            jax.ShapeDtypeStruct((rows, pairs * 128), BF),
+            jax.ShapeDtypeStruct((seqs * pairs, 2, length), F32),
+        ],
+        compiler_params=pltpu.CompilerParams(vmem_limit_bytes=48 * 2**20),
+        name="attention_forward",
+        cost_estimate=pl.CostEstimate(
+            flops=16 * rows * length * pairs * 128,
+            bytes_accessed=rows * pairs * 1024,
+            transcendentals=2 * rows * length * pairs,
+        ),
+    )(packed, mask)
+
+
+def attention_backward(packed, mask, logsum, grad, length):
+    rows, pairs, seqs, block, mask_spec, row = attention_specs(packed, length)
+    return pl.pallas_call(
+        backward_kernel,
+        grid=(seqs, pairs),
+        in_specs=[block(384), mask_spec, row(2, length), block(128)],
+        out_specs=[block(384), row(1, 384)],
+        out_shape=[
+            jax.ShapeDtypeStruct((rows, pairs * 384), BF),
+            jax.ShapeDtypeStruct((seqs * pairs, 1, 384), F32),
+        ],
+        compiler_params=pltpu.CompilerParams(vmem_limit_bytes=48 * 2**20),
+        name="attention_backward",
+        cost_estimate=pl.CostEstimate(
+            flops=28 * rows * length * pairs * 128,
+            bytes_accessed=rows * pairs * 1792,
+            transcendentals=2 * rows * length * pairs,
+        ),
+    )(packed, mask, logsum, grad)
+
+
+def pair_major(block):
+    lead = block.shape[:-1]
+    return block.reshape(lead + (3, -1, 128)).swapaxes(-3, -2).reshape(block.shape)
+
+
+def kind_major(block):
+    lead = block.shape[:-1]
+    return block.reshape(lead + (-1, 3, 128)).swapaxes(-3, -2).reshape(block.shape)
+
+
 def swap(block, distance, devices):
     return lax.ppermute(block, BOTH, [(i, i ^ distance) for i in range(devices)])
 
@@ -231,13 +281,18 @@
         self.parts = grown
         return grown[0][0]
 
-    def second(self, spans=None, *done):
-        pieces, piece_ids = [], []
+    def second(self, *done):
+        grown = []
         for held, ids, order in self.parts:
             if done:
                 held = after(held, *done)
-            last = self.swapped(held, order[1])
-            last_ids = [i ^ order[1] for i in ids]
+            grown.append((held, ids, self.swapped(held, order[1]), [i ^ order[1] for i in ids]))
+        self.parts = grown
+        return [part[2] for part in grown]
+
+    def finish(self, spans=None):
+        pieces, piece_ids = [], []
+        for held, ids, last, last_ids in self.parts:
             for b, b_ids in ((held, ids), (last, last_ids)):
                 pieces += [b, self.swapped(b, 1)]
                 piece_ids += b_ids + [i ^ 1 for i in b_ids]
@@ -312,10 +367,14 @@
     return jnp.stack(pieces, 1).reshape(groups * count, width)
 
 
-def to_positions(block, seat, members, devices):
+def send_positions(block, members, devices):
     pieces = [block[:, 0][None]]
-    pieces += [swap(block[:, k][None], k, devices) for k in range(1, members)]
-    (placed,) = place(pieces, list(range(members)), seat)
+    return pieces + [swap(block[:, k][None], k, devices) for k in range(1, members)]
+
+
+def put_positions(pieces, seat, *done):
+    pieces = [after(pieces[0], *done)] + pieces[1:]
+    (placed,) = place(pieces, list(range(len(pieces))), seat)
     return placed.reshape((-1,) + placed.shape[2:])
 
 
@@ -349,7 +408,7 @@
     inner_width = in_weight.shape[1]
     early = pack_rows([query_bias, value_bias], share)
     qkv_gather = Gather(
-        jnp.concatenate([query_key_value_weight, early], 1), me, devices, "split"
+        jnp.concatenate([pair_major(query_key_value_weight), early], 1), me, devices, "split"
     )
     late_vectors = [
         output_bias,
@@ -365,26 +424,29 @@
         jnp.concatenate([in_weight, output_weight, late], 1), me, devices, "split"
     )
     down_gather = Gather(down_weight, me, devices, "yx")
-    z_done = qkv_gather.along_z()
+    qkv_gather.along_z()
     flat = to_sequences(inputs, seat, members, devices)
     first_done = qkv_gather.first()
-    in_z_done = in_gather.along_z(z_done)
-    down_z_done = down_gather.along_z(z_done)
-    wide_qkv, early = qkv_gather.second([(0, 3 * width), (3 * width, early.shape[1])])
+    last_done = qkv_gather.second()
+    in_gather.along_z(first_done)
+    in_gather.first(*last_done)
+    wide_qkv, early = qkv_gather.finish([(0, 3 * width), (3 * width, early.shape[1])])
+    in_gather.second(wide_qkv)
     wide_qkv = wide_qkv.reshape(width, 3 * width)
     full_query_bias, full_value_bias = [
         v.reshape(-1).astype(F32) for v in unpack_rows(early, [share, share])
     ]
     bias_vector = jnp.concatenate([full_query_bias, jnp.zeros((width,), F32), full_value_bias])
-    packed = (jnp.dot(flat, wide_qkv, preferred_element_type=F32) + bias_vector).astype(BF)
-    in_gather.first(packed)
+    packed = jnp.dot(flat, wide_qkv, preferred_element_type=F32) + pair_major(bias_vector)
+    packed = packed.astype(BF)
+    down_gather.along_z(packed)
     mine = lax.dynamic_slice(lengths, (seat * kept,), (kept,))
     slots = jnp.arange(length, dtype=jnp.int32)
     positions = ((slots // local_len) ^ seat) * local_len + slots % local_len
     mask = jnp.where(positions[None, :] < mine[:, None], 0.0, -1e30).astype(BF)
     mask = jnp.broadcast_to(mask[:, :, None], (kept, length, 128))
     mixed, logsum = attention_forward(packed, mask, length)
-    wide_in, wide_out, late = in_gather.second(
+    wide_in, wide_out, late = in_gather.finish(
         [(0, inner_width), (inner_width, width), (inner_width + width, late.shape[1])]
     )
     wide_in = wide_in.reshape(width, inner_width)
@@ -408,14 +470,18 @@
     )
     first_low = first.astype(BF)
     cot = to_sequences(after(cotangent, first_low), seat, members, devices)
+    down_gather.second(first_low)
     hidden = jnp.dot(first_low, wide_in, preferred_element_type=F32) + full_in_bias
     active, gelu_pull = jax.vjp(gelu_exact, hidden)
     active_low = active.astype(BF)
-    (wide_down,) = down_gather.second()
+    (wide_down,) = down_gather.finish()
     wide_down = wide_down.reshape(inner_width, width)
     branch_two = jnp.dot(active_low, wide_down, preferred_element_type=F32) + full_down_bias
     result, norm_two_pull = jax.vjp(
         layer_norm, first_low.astype(F32) + branch_two, gain_two, shift_two
+    )
+    outputs = send_positions(
+        result.astype(BF).reshape(kept, members, local_len, width), members, devices
     )
     grad_second, grad_gain_two, grad_shift_two = norm_two_pull(cot.astype(F32))
     grad_branch_two = grad_second.astype(BF)
@@ -433,9 +499,6 @@
     grad_branch_one = grad_residual.astype(BF)
     grad_out = over_rows(mixed, grad_branch_one).astype(BF)
     grad_out_bias = jnp.sum(grad_branch_one.astype(F32), 0)
-    outputs = to_positions(
-        result.astype(BF).reshape(kept, members, local_len, width), seat, members, devices
-    )
     late_sums = [
         grad_out_bias,
         grad_gain_one,
@@ -460,17 +523,15 @@
         "split",
     )
     grad_mixed = times_transposed(grad_branch_one, wide_out).astype(BF)
-    grad_mixed = after(grad_mixed, *down_half)
+    grad_mixed = after(grad_mixed, in_scatter.total, *down_half)
+    in_half = in_scatter.first()
     down_quarter = down_scatter.second()
-    grad_queries, grad_keys, grad_values = attention_backward(
-        packed, mask, logsum, grad_mixed, length
-    )
-    grad_packed = jnp.concatenate([grad_queries, grad_keys, grad_values], -1)
-    grad_packed = after(grad_packed, in_scatter.total, *down_quarter)
-    in_half = in_scatter.first()
+    grad_packed, column_sums = attention_backward(packed, mask, logsum, grad_mixed, length)
+    grad_packed = after(grad_packed, *down_quarter, *in_half)
     down_part = down_scatter.along_z()
+    in_quarter = in_scatter.second()
     grad_qkv = over_rows(flat, grad_packed).astype(BF)
-    column_sums = jnp.sum(grad_packed.astype(F32), 0)
+    column_sums = kind_major(column_sums.reshape(kept, 3 * width).sum(0))
     early_sums = [column_sums[:width], column_sums[2 * width :]]
     early_block = pack_rows([v.reshape(devices, -1) for v in early_sums], share).astype(BF)
     qkv_scatter = Scatter(
@@ -482,14 +543,15 @@
     grad_inputs = (
         times_transposed(after(grad_packed, grad_qkv), wide_qkv) + grad_residual
     ).astype(BF)
-    grad_inputs = to_positions(
-        grad_inputs.reshape(kept, members, local_len, width), seat, members, devices
-    )
-    in_scatter.second()
+    grad_inputs = send_positions(
+        grad_inputs.reshape(kept, members, local_len, width), members, devices
+    )
+    qkv_half = qkv_scatter.first()
     in_part = in_scatter.along_z()
-    qkv_scatter.first()
-    qkv_scatter.second()
+    outputs = put_positions(outputs, seat, qkv_scatter.total)
+    qkv_quarter = qkv_scatter.second()
     qkv_part = qkv_scatter.along_z()
+    grad_inputs = put_positions(grad_inputs, seat, *qkv_half)
     early_out = unpack_rows(qkv_part[:, 3 * width :], [share, share])
     late_out = unpack_rows(
         in_part[:, inner_width + width :], [v.shape[0] for v in late_vectors]
@@ -497,7 +559,7 @@
     return (
         outputs,
         grad_inputs,
-        qkv_part[:, : 3 * width],
+        kind_major(qkv_part[:, : 3 * width]),
         early_out[0],
         early_out[1],
         in_part[:, inner_width : inner_width + width],

time: 498 us -> 497 us (level)
  starting transfers between devices: 73.3 us -> 64.7 us
  waiting for transfers between devices: 154 us -> 161 us
  matrix products: 117 us -> 111 us
    ppermute x63, starting transfers between devices: 73.3 us -> 64.7 us  [swap(): lax.ppermute(block, BOTH, [(i, i ^ distance) for i in range(devices)])]
    ppermute x63, waiting for transfers between devices: 154 us -> 161 us  [swap(): lax.ppermute(block, BOTH, [(i, i ^ distance) for i in range(devices)])]
    reduce_sum x6, other arithmetic: 1.67 us -> 8.27 us  [layer_norm(): return centered * lax.rsqrt(spread + 1e-12) * gain + shift]
    unnamed x100 -> x117, local copies, waits for them, and re-layouts: 19.6 us -> 20.4 us
  transfers between devices with their start and end apart: 63 -> 63, of which waited for: 22 -> 25; matrix products, arithmetic and copies ran while one was open for 24% -> 26% of each run, Pallas kernels for 10% -> 9%
where the time goes in v5:
time: 497 us; the launch traced here: 492 us
  waiting for transfers between devices  161 us (32%)
  matrix products  111 us (22%)
  starting transfers between devices  64.7 us (13%)
  Pallas kernels  58.1 us (12%)
  local copies, waits for them, and re-layouts  49.4 us (10%)
  other arithmetic  44.6 us (9%)
    ppermute x63, waiting for transfers between devices, swap(): lax.ppermute(block, BOTH, [(i, i ^ distance) for i in range(devices)])  161 us
    ppermute x63, starting transfers between devices, swap(): lax.ppermute(block, BOTH, [(i, i ^ distance) for i in range(devices)])  64.7 us
    dot_general x1, matrix products, on_device(): jnp.dot(first_low, wide_in, preferred_element_type=F32) + full_in_bias  37 us
    dot_general x4, matrix products, times_transposed(): lax.dot_general(left, right, (((1,), (1,)), ((), ())), preferred_element_...  30.7 us
    pallas_call x1, Pallas kernels, attention_backward(): pl.pallas_call(backward_kernel, grid=(seqs, pairs), in_specs=[block(384),...  24.5 us
    dot_general x4, matrix products, over_rows(): lax.dot_general(left, right, (((0,), (0,)), ((), ())), preferred_element_...  21.1 us
    unnamed x117, local copies, waits for them, and re-layouts  20.4 us
    pallas_call x1, Pallas kernels, attention_forward(): pl.pallas_call(forward_kernel, grid=(seqs, pairs), in_specs=[block(384),...  17 us
  transfers between devices with their start and end apart: 63, of which 25 were waited for; matrix products, arithmetic and copies ran while one was open for 26% of the time, Pallas kernels for 9%

profile of v5, /device:TPU:0, one launch (start us, length us, event | category | flops | bytes accessed | tf_op | source)
XLA Modules:
  0.0 491.6 jit_solution(9827387432493785208)
XLA Ops:
  24.6 5.3 %collective-permute-start.19 = (bf16[1,24,3968]{2,1,0:T(8,128)(2,1)S(1)}, bf16[1,24,3968]{2,1,0:T(8,128)(2,1)S(1)}, u32[]{:S(2)}, u32[]{:S(2)}) collective-permute-start(bf16[1,24,3968]{2,1,0:T(8,128)(2,1)S(1)} %fusion.32), channel_id=1, source_target_pairs={{0,16},{1,17},{2,18},{3,19},{4,20},{5,21},{6,22},{7,23},{8,24},{9,... | collective-permute-start | bytes 571400 | tf_op jit(solution)/shard_map/ppermute | solution.py:172
  32.4 9.7 %collective-permute-done.19 = bf16[1,24,3968]{2,1,0:T(8,128)(2,1)S(1)} collective-permute-done((bf16[1,24,3968]{2,1,0:T(8,128)(2,1)S(1)}, bf16[1,24,3968]{2,1,0:T(8,128)(2,1)S(1)}, u32[]{:S(2)}, u32[]{:S(2)}) %collective-permute-start.19) | collective-permute-done | bytes 190496 | tf_op jit(solution)/shard_map/ppermute | solution.py:172
  73.1 11.1 %collective-permute-done.23.refs_6_ = bf16[4,24,3968]{2,1,0:T(8,128)(2,1)S(1)} collective-permute-done((bf16[4,24,3968]{2,1,0:T(8,128)(2,1)S(1)}, bf16[4,24,3968]{2,1,0:T(8,128)(2,1)S(1)}, u32[]{:S(2)}, u32[]{:S(2)}) %collective-permute-start.23) | collective-permute-done | bytes 761888 | tf_op jit(solution)/shard_map/ppermute | solution.py:172
  88.3 5.6 %collective-permute-done.1 = bf16[2,128,768]{2,1,0:T(8,128)(2,1)} collective-permute-done((bf16[2,128,768]{2,1,0:T(8,128)(2,1)S(1)}, bf16[2,128,768]{2,1,0:T(8,128)(2,1)}, u32[]{:S(2)}, u32[]{:S(2)}) %collective-permute-start.1) | collective-permute-done | bytes 393248 | tf_op jit(solution)/shard_map/ppermute | solution.py:172
  94.2 10.6 %collective-permute-done.2 = bf16[2,128,768]{2,1,0:T(8,128)(2,1)} collective-permute-done((bf16[2,128,768]{2,1,0:T(8,128)(2,1)}, bf16[2,128,768]{2,1,0:T(8,128)(2,1)}, u32[]{:S(2)}, u32[]{:S(2)}) %collective-permute-start.2) | collective-permute-done | bytes 393248 | tf_op jit(solution)/shard_map/ppermute | solution.py:172
  116.4 8.5 %add_convert_fusion.1.packed_ref = bf16[1024,2304]{1,0:T(8,128)(2,1)} fusion(bf16[1024,768]{1,0:T(8,128)(2,1)} %bitcast.291, bf16[768,2304]{1,0:T(8,128)(2,1)} %bitcast.272, f32[2304]{0:T(1024)S(1)} %add.417), kind=kOutput, calls=%fused_computation.17 | convolution fusion | flops 3628597248 | bytes 9839616 | tf_op jit(solution)/shard_map/dot_general | solution.py:440
  129.5 17.0 %attention_forward.1 = (bf16[1024,768]{1,0:T(8,128)(2,1)S(1)}, f32[12,2,512]{2,1,0:T(2,128)S(1)}) custom-call(bf16[1024,2304]{1,0:T(8,128)(2,1)} %add_convert_fusion.1.packed_ref, bf16[2,512,128]{2,1,0:T(8,128)(2,1)S(1)} %broadcast_in_dim.55.mask_ref), custom_call_target="tpu_custom_call" | custom-call | flops 6442450944 | bytes 6291456 | tf_op jit(solution)/shard_map/attention_forward/pallas_call | solution.py:121
  146.7 5.0 %fusion.54 = (f32[1024]{0:T(1024)S(1)}, f32[1024,768]{1,0:T(8,128)}) fusion(f32[768]{0:T(1024)S(1)} %reshape.424, bf16[1024,768]{1,0:T(8,128)(2,1)S(1)} %get-tuple-element.41, bf16[768,768]{1,0:T(8,128)(2,1)S(1)} %bitcast.274, bf16[1024,768]{1,0:T(8,128)(2,1)} %bitcast.292), kind=kOutput, calls=%fused_computation.221 | convolution fusion | flops 1211104256 | bytes 7478272 | tf_op jit(solution)/shard_map/dot_general | solution.py:467
  160.3 6.6 %collective-permute-done.28 = bf16[4,96,768]{2,1,0:T(8,128)(2,1)S(1)} collective-permute-done((bf16[4,96,768]{2,1,0:T(8,128)(2,1)S(1)}, bf16[4,96,768]{2,1,0:T(8,128)(2,1)S(1)}, u32[]{:S(2)}, u32[]{:S(2)}) %collective-permute-start.28) | collective-permute-done | bytes 589856 | tf_op jit(solution)/shard_map/ppermute | solution.py:172
  173.7 19.4 %collective-permute-done.30.refs_2_ = bf16[8,96,768]{2,1,0:T(8,128)(2,1)S(1)} collective-permute-done((bf16[8,96,768]{2,1,0:T(8,128)(2,1)S(1)}, bf16[8,96,768]{2,1,0:T(8,128)(2,1)S(1)}, u32[]{:S(2)}, u32[]{:S(2)}) %collective-permute-start.30) | collective-permute-done | bytes 1179680 | tf_op jit(solution)/shard_map/ppermute | solution.py:172
  193.0 37.0 %multiply_convert_fusion = (bf16[1024,3072]{1,0:T(8,128)(2,1)}, f32[1024,3072]{1,0:T(8,128)}, f32[1024,3072]{1,0:T(8,128)}) fusion(f32[3072]{0:T(1024)} %reshape.427, bf16[1024,768]{1,0:T(8,128)(2,1)} %add_convert_fusion.4, bf16[768,3072]{1,0:T(8,128)(2,1)} %bitcast.270), kind=kOutput, calls=%fused_computation.3 | convolution fusion | flops 5039456256 | bytes 37761024 | tf_op jit(solution)/shard_map/dot_general | solution.py:474
  239.1 6.2 %place_blocks.7 = bf16[32,96,768]{2,1,0:T(8,128)(2,1)S(1)} custom-call(s32[1]{0:T(128)} %bitcast.10.me_ref, bf16[8,96,768]{2,1,0:T(8,128)(2,1)S(1)} %pad_maximum_fusion.2.refs_0_, bf16[8,96,768]{2,1,0:T(8,128)(2,1)S(1)} %collective-permute-done.29.refs_1_, bf16[8,96,768]{2,1,0:T(8,128)(2,1)S(1)} %collective-permute-done.30.refs_2_, ...), custom_call_target="tpu_custom_call" | custom-call | bytes 9437184 | tf_op jit(solution)/shard_map/place_blocks/pallas_call | solution.py:205
  245.4 9.0 %fusion.55 = (f32[1024]{0:T(1024)S(1)}, f32[1024,768]{1,0:T(8,128)S(1)}) fusion(f32[768]{0:T(1024)S(1)} %copy-done.43, bf16[1024,3072]{1,0:T(8,128)(2,1)} %get-tuple-element.88, bf16[3072,768]{1,0:T(8,128)(2,1)S(1)} %bitcast.266, bf16[1024,768]{1,0:T(8,128)(2,1)S(1)} %copy-done.27), kind=kOutput, calls=%fused_computation.222 | convolution fusion | flops 4834982912 | bytes 15735808 | tf_op jit(solution)/shard_map/dot_general | solution.py:479
  260.4 5.8 %convolution_convert_fusion.1 = bf16[3072,768]{1,0:T(8,128)(2,1)S(1)} fusion(bf16[1024,3072]{1,0:T(8,128)(2,1)S(1)} %bitcast.310, bf16[1024,768]{1,0:T(8,128)(2,1)S(1)} %get-tuple-element.81), kind=kOutput, calls=%fused_computation.21 | convolution fusion | flops 4834197504 | bytes 12582912 | tf_op jit(solution)/shard_map/dot_general | solution.py:27
  270.4 16.0 %fusion.56 = (bf16[3072]{0:T(1024)(128)(2,1)S(1)}, bf16[1024,3072]{1,0:T(8,128)(2,1)}) fusion(f32[1024,3072]{1,0:T(8,128)} %get-tuple-element.89, bf16[1024,768]{1,0:T(8,128)(2,1)} %copy-done.25, bf16[3072,768]{1,0:T(8,128)(2,1)S(1)} %bitcast.269, f32[1024,3072]{1,0:T(8,128)} %get-tuple-element.131, f32[3072]{0:T(1024)S(1)} %copy-done.42), kind=kOutput, calls=%fused_computation.223 | convolution fusion | flops 4882166784 | bytes 37767168 | tf_op jit(solution)/shard_map/dot_general | solution.py:33
  286.7 7.9 %convolution_convert_fusion = bf16[768,3072]{1,0:T(8,128)(2,1)S(1)} fusion(bf16[1024,768]{1,0:T(8,128)(2,1)} %add_convert_fusion.4, bf16[1024,3072]{1,0:T(8,128)(2,1)} %get-tuple-element.55), kind=kOutput, calls=%fused_computation.20 | convolution fusion | flops 4834197504 | bytes 12582912 | tf_op jit(solution)/shard_map/dot_general | solution.py:27
  303.4 9.4 %multiply_reduce_fusion = (bf16[768]{0:T(1024)(128)(2,1)S(1)}, f32[1024]{0:T(1024)S(1)}, bf16[768]{0:T(1024)(128)(2,1)S(1)}, f32[1024,768]{1,0:T(8,128)S(1)}) fusion(f32[1024,768]{1,0:T(8,128)} %get-tuple-element.130, f32[1024]{0:T(1024)S(1)} %copy-done.37, f32[1024]{0:T(1024)S(1)} %copy-done.32, f32[768]{0:T(1024)S(1)} %copy-done.35, ...), kind=kOutput, calls=%fused_computation.38 | convolution fusion | flops 4839699456 | bytes 20469760 | tf_op jit(solution)/shard_map/dot_general | solution.py:33
  331.7 20.8 %collective-permute-done.37 = bf16[4,2,96,768]{3,2,0,1:T(8,128)(2,1)} collective-permute-done((bf16[4,2,96,768]{3,2,0,1:T(8,128)(2,1)}, bf16[4,2,96,768]{3,2,0,1:T(8,128)(2,1)}, u32[]{:S(2)}, u32[]{:S(2)}) %collective-permute-start.37) | collective-permute-done | bytes 1179680 | tf_op jit(solution)/shard_map/ppermute | solution.py:172
  357.6 13.4 %collective-permute-done.38 = bf16[4,96,768]{2,1,0:T(8,128)(2,1)} collective-permute-done((bf16[4,96,768]{2,1,0:T(8,128)(2,1)}, bf16[4,96,768]{2,1,0:T(8,128)(2,1)}, u32[]{:S(2)}, u32[]{:S(2)}) %collective-permute-start.38) | collective-permute-done | bytes 589856 | tf_op jit(solution)/shard_map/ppermute | solution.py:172
  379.7 5.9 %collective-permute-done.61 = bf16[96,768]{1,0:T(8,128)(2,1)S(1)} collective-permute-done((bf16[96,768]{1,0:T(8,128)(2,1)S(1)}, bf16[96,768]{1,0:T(8,128)(2,1)S(1)}, u32[]{:S(2)}, u32[]{:S(2)}) %collective-permute-start.61) | collective-permute-done | bytes 147488 | tf_op jit(solution)/shard_map/ppermute | solution.py:172
  390.9 24.5 %attention_backward.1 = (bf16[1024,2304]{1,0:T(8,128)(2,1)}, f32[12,1,384]{2,1,0:T(1,128)S(1)}) custom-call(bf16[1024,2304]{1,0:T(8,128)(2,1)} %add_convert_fusion.1.packed_ref, bf16[2,512,128]{2,1,0:T(8,128)(2,1)S(1)} %copy-done.2, f32[12,2,512]{2,1,0:T(2,128)S(1)} %copy-done.13, bf16[1024,768]{1,0:T(8,128)(2,1)S(1)} %convolution_convert_fusion.3.grad_ref), custom_call_target="tpu_custom_call" | custom-call | flops 11274289152 | bytes 11010048 | tf_op jit(solution)/shard_map/attention_backward/pallas_call | solution.py:142
  439.7 10.0 %collective-permute-done.58 = bf16[24,3968]{1,0:T(8,128)(2,1)S(1)} collective-permute-done((bf16[24,3968]{1,0:T(8,128)(2,1)S(1)}, bf16[24,3968]{1,0:T(8,128)(2,1)S(1)}, u32[]{:S(2)}, u32[]{:S(2)}) %collective-permute-start.58) | collective-permute-done | bytes 190496 | tf_op jit(solution)/shard_map/ppermute | solution.py:172
  453.3 4.9 collective-permute-done.45
  462.1 5.1 %collective-permute-done.50 = bf16[2,24,2432]{2,1,0:T(8,128)(2,1)S(1)} collective-permute-done((bf16[2,24,2432]{2,1,0:T(8,128)(2,1)S(1)}, bf16[2,24,2432]{2,1,0:T(8,128)(2,1)S(1)}, u32[]{:S(2)}, u32[]{:S(2)}) %collective-permute-start.50) | collective-permute-done | bytes 233504 | tf_op jit(solution)/shard_map/ppermute | solution.py:172
  (375 shorter events, 214.6 us)
Async XLA Ops:
  32.4 29.1 %collective-permute-start.11 = (bf16[4,24,2432]{2,1,0:T(8,128)(2,1)S(1)}, bf16[4,24,2432]{2,1,0:T(8,128)(2,1)S(1)}, u32[]{:S(2)}, u32[]{:S(2)}) collective-permute-start(bf16[4,24,2432]{2,1,0:T(8,128)(2,1)S(1)} %constant_dynamic-update-slice_fusion.refs_4_), channel_id=1, source_target_pairs={{0,1},{1,0},{2,3},{3,2},{4,5},{5,4},{6,7},{7,6},{8,9},{9,8},{10,11... | collective-permute-start | bytes 1400840 | tf_op jit(solution)/shard_map/ppermute | solution.py:172
  68.4 20.0 %collective-permute-start.17 = (bf16[4,24,3968]{2,1,0:T(8,128)(2,1)S(1)}, bf16[4,24,3968]{2,1,0:T(8,128)(2,1)S(1)}, u32[]{:S(2)}, u32[]{:S(2)}) collective-permute-start(bf16[4,24,3968]{2,1,0:T(8,128)(2,1)S(1)} %pad_maximum_fusion.3.refs_0_), channel_id=1, source_target_pairs={{0,2},{1,3},{2,0},{3,1},{4,6},{5,7},{6,4},{7,5},{8,10},{9,11},{10,... | collective-permute-start | bytes 2285576 | tf_op jit(solution)/shard_map/ppermute | solution.py:172
  71.1 22.8 %collective-permute-start.1 = (bf16[2,128,768]{2,1,0:T(8,128)(2,1)S(1)}, bf16[2,128,768]{2,1,0:T(8,128)(2,1)}, u32[]{:S(2)}, u32[]{:S(2)}) collective-permute-start(bf16[2,128,768]{2,1,0:T(8,128)(2,1)S(1)} %get-tuple-element.112), channel_id=1, source_target_pairs={{0,2},{1,3},{2,0},{3,1},{4,6},{5,7},{6,4},{7,5},{8,10},{9,11},{10,... | collective-permute-start | bytes 1179656 | tf_op jit(solution)/shard_map/ppermute | solution.py:172
  72.6 34.7 %collective-permute-start.22 = (bf16[4,24,3968]{2,1,0:T(8,128)(2,1)S(1)}, bf16[4,24,3968]{2,1,0:T(8,128)(2,1)}, u32[]{:S(2)}, u32[]{:S(2)}) collective-permute-start(bf16[4,24,3968]{2,1,0:T(8,128)(2,1)S(1)} %pad_maximum_fusion.4.refs_4_), channel_id=1, source_target_pairs={{0,1},{1,0},{2,3},{3,2},{4,5},{5,4},{6,7},{7,6},{8,9},{9,8},{10,11... | collective-permute-start | bytes 2285576 | tf_op jit(solution)/shard_map/ppermute | solution.py:172
  72.8 34.5 %collective-permute-start.16 = (bf16[4,24,3968]{2,1,0:T(8,128)(2,1)S(1)}, bf16[4,24,3968]{2,1,0:T(8,128)(2,1)}, u32[]{:S(2)}, u32[]{:S(2)}) collective-permute-start(bf16[4,24,3968]{2,1,0:T(8,128)(2,1)S(1)} %pad_maximum_fusion.3.refs_0_), channel_id=1, source_target_pairs={{0,1},{1,0},{2,3},{3,2},{4,5},{5,4},{6,7},{7,6},{8,9},{9,8},{10,11... | collective-permute-start | bytes 2285576 | tf_op jit(solution)/shard_map/ppermute | solution.py:172
  84.2 23.1 %collective-permute-start.24 = (bf16[4,24,3968]{2,1,0:T(8,128)(2,1)S(1)}, bf16[4,24,3968]{2,1,0:T(8,128)(2,1)}, u32[]{:S(2)}, u32[]{:S(2)}) collective-permute-start(bf16[4,24,3968]{2,1,0:T(8,128)(2,1)S(1)} %collective-permute-done.23.refs_6_), channel_id=1, source_target_pairs={{0,1},{1,0},{2,3},{3,2},{4,5},{5,4},{6,7},{7,6},{8,9},{9,8},{10,11... | collective-permute-start | bytes 2285576 | tf_op jit(solution)/shard_map/ppermute | solution.py:172
  124.9 26.8 %collective-permute-start.25 = (bf16[1,96,768]{2,1,0:T(8,128)(2,1)S(1)}, bf16[1,96,768]{2,1,0:T(8,128)(2,1)S(1)}, u32[]{:S(2)}, u32[]{:S(2)}) collective-permute-start(bf16[1,96,768]{2,1,0:T(8,128)(2,1)S(1)} %bitcast.304), channel_id=1, source_target_pairs={{0,8},{1,9},{2,10},{3,11},{4,12},{5,13},{6,14},{7,15},{8,0},{9,1},... | collective-permute-start | bytes 442376 | tf_op jit(solution)/shard_map/ppermute | solution.py:172
  126.0 25.7 %collective-permute-start.26 = (bf16[1,96,768]{2,1,0:T(8,128)(2,1)S(1)}, bf16[1,96,768]{2,1,0:T(8,128)(2,1)S(1)}, u32[]{:S(2)}, u32[]{:S(2)}) collective-permute-start(bf16[1,96,768]{2,1,0:T(8,128)(2,1)S(1)} %bitcast.305), channel_id=1, source_target_pairs={{0,16},{1,17},{2,18},{3,19},{4,20},{5,21},{6,22},{7,23},{8,24},{9,... | collective-permute-start | bytes 442376 | tf_op jit(solution)/shard_map/ppermute | solution.py:172
  126.0 25.7 %collective-permute-start.27 = (bf16[1,96,768]{2,1,0:T(8,128)(2,1)S(1)}, bf16[1,96,768]{2,1,0:T(8,128)(2,1)}, u32[]{:S(2)}, u32[]{:S(2)}) collective-permute-start(bf16[1,96,768]{2,1,0:T(8,128)(2,1)S(1)} %bitcast.306), channel_id=1, source_target_pairs={{0,24},{1,25},{2,26},{3,27},{4,28},{5,29},{6,30},{7,31},{8,16},{9,... | collective-permute-start | bytes 442376 | tf_op jit(solution)/shard_map/ppermute | solution.py:172
  167.1 25.9 %collective-permute-start.30 = (bf16[8,96,768]{2,1,0:T(8,128)(2,1)S(1)}, bf16[8,96,768]{2,1,0:T(8,128)(2,1)S(1)}, u32[]{:S(2)}, u32[]{:S(2)}) collective-permute-start(bf16[8,96,768]{2,1,0:T(8,128)(2,1)S(1)} %pad_maximum_fusion.2.refs_0_), channel_id=1, source_target_pairs={{0,4},{1,5},{2,6},{3,7},{4,0},{5,1},{6,2},{7,3},{8,12},{9,13},{10,... | collective-permute-start | bytes 3538952 | tf_op jit(solution)/shard_map/ppermute | solution.py:172
  170.8 62.7 %collective-permute-start.32 = (bf16[2,128,768]{2,1,0:T(8,128)(2,1)}, bf16[2,128,768]{2,1,0:T(8,128)(2,1)}, u32[]{:S(2)}, u32[]{:S(2)}) collective-permute-start(bf16[2,128,768]{2,1,0:T(8,128)(2,1)} %get-tuple-element.108), channel_id=1, source_target_pairs={{0,1},{1,0},{2,3},{3,2},{4,5},{5,4},{6,7},{7,6},{8,9},{9,8},{10,11... | collective-permute-start | bytes 1179656 | tf_op jit(solution)/shard_map/ppermute | solution.py:172
  170.8 63.8 %collective-permute-start.33 = (bf16[2,128,768]{2,1,0:T(8,128)(2,1)}, bf16[2,128,768]{2,1,0:T(8,128)(2,1)}, u32[]{:S(2)}, u32[]{:S(2)}) collective-permute-start(bf16[2,128,768]{2,1,0:T(8,128)(2,1)} %get-tuple-element.107), channel_id=1, source_target_pairs={{0,2},{1,3},{2,0},{3,1},{4,6},{5,7},{6,4},{7,5},{8,10},{9,11},{10,... | collective-permute-start | bytes 1179656 | tf_op jit(solution)/shard_map/ppermute | solution.py:172
  172.5 63.1 %collective-permute-start.34 = (bf16[2,128,768]{2,1,0:T(8,128)(2,1)}, bf16[2,128,768]{2,1,0:T(8,128)(2,1)}, u32[]{:S(2)}, u32[]{:S(2)}) collective-permute-start(bf16[2,128,768]{2,1,0:T(8,128)(2,1)} %get-tuple-element.106), channel_id=1, source_target_pairs={{0,3},{1,2},{2,1},{3,0},{4,7},{5,6},{6,5},{7,4},{8,11},{9,10},{10,... | collective-permute-start | bytes 1179656 | tf_op jit(solution)/shard_map/ppermute | solution.py:172
  173.4 65.7 %collective-permute-start.29 = (bf16[8,96,768]{2,1,0:T(8,128)(2,1)S(1)}, bf16[8,96,768]{2,1,0:T(8,128)(2,1)S(1)}, u32[]{:S(2)}, u32[]{:S(2)}) collective-permute-start(bf16[8,96,768]{2,1,0:T(8,128)(2,1)S(1)} %pad_maximum_fusion.2.refs_0_), channel_id=1, source_target_pairs={{0,1},{1,0},{2,3},{3,2},{4,5},{5,4},{6,7},{7,6},{8,9},{9,8},{10,11... | collective-permute-start | bytes 3538952 | tf_op jit(solution)/shard_map/ppermute | solution.py:172
  193.0 46.1 %collective-permute-start.31 = (bf16[8,96,768]{2,1,0:T(8,128)(2,1)S(1)}, bf16[8,96,768]{2,1,0:T(8,128)(2,1)}, u32[]{:S(2)}, u32[]{:S(2)}) collective-permute-start(bf16[8,96,768]{2,1,0:T(8,128)(2,1)S(1)} %collective-permute-done.30.refs_2_), channel_id=1, source_target_pairs={{0,1},{1,0},{2,3},{3,2},{4,5},{5,4},{6,7},{7,6},{8,9},{9,8},{10,11... | collective-permute-start | bytes 3538952 | tf_op jit(solution)/shard_map/ppermute | solution.py:172
  269.9 27.6 %collective-permute-start.35 = (bf16[16,96,768]{2,1,0:T(8,128)(2,1)}, bf16[16,96,768]{2,1,0:T(8,128)(2,1)}, u32[]{:S(2)}, u32[]{:S(2)}) collective-permute-start(bf16[16,96,768]{2,1,0:T(8,128)(2,1)} %dynamic-slice_bitcast_fusion.1), channel_id=1, source_target_pairs={{0,1},{1,0},{2,3},{3,2},{4,5},{5,4},{6,7},{7,6},{8,9},{9,8},{10,11... | collective-permute-start | bytes 7077896 | tf_op jit(solution)/shard_map/ppermute | solution.py:172
  324.0 28.6 %collective-permute-start.37 = (bf16[4,2,96,768]{3,2,0,1:T(8,128)(2,1)}, bf16[4,2,96,768]{3,2,0,1:T(8,128)(2,1)}, u32[]{:S(2)}, u32[]{:S(2)}) collective-permute-start(bf16[4,2,96,768]{3,2,0,1:T(8,128)(2,1)} %bitcast.265), channel_id=1, source_target_pairs={{0,2},{1,3},{2,0},{3,1},{4,6},{5,7},{6,4},{7,5},{8,10},{9,11},{10,... | collective-permute-start | bytes 3538952 | tf_op jit(solution)/shard_map/ppermute | solution.py:172
  331.7 54.7 %collective-permute-start.36 = (bf16[16,24,3968]{2,1,0:T(8,128)(2,1)}, bf16[16,24,3968]{2,1,0:T(8,128)(2,1)}, u32[]{:S(2)}, u32[]{:S(2)}) collective-permute-start(bf16[16,24,3968]{2,1,0:T(8,128)(2,1)} %dynamic-slice_bitcast_fusion), channel_id=1, source_target_pairs={{0,1},{1,0},{2,3},{3,2},{4,5},{5,4},{6,7},{7,6},{8,9},{9,8},{10,11... | collective-permute-start | bytes 9142280 | tf_op jit(solution)/shard_map/ppermute | solution.py:172
  357.6 116.7 %collective-permute-start.42 = (bf16[1,2,128,768]{3,2,1,0:T(8,128)(2,1)}, bf16[1,2,128,768]{3,2,1,0:T(8,128)(2,1)S(1)}, u32[]{:S(2)}, u32[]{:S(2)}) collective-permute-start(bf16[1,2,128,768]{3,2,1,0:T(8,128)(2,1)} %get-tuple-element.103), channel_id=1, source_target_pairs={{0,1},{1,0},{2,3},{3,2},{4,5},{5,4},{6,7},{7,6},{8,9},{9,8},{10,11... | collective-permute-start | bytes 1179656 | tf_op jit(solution)/shard_map/ppermute | solution.py:172
  378.6 95.8 %collective-permute-start.43 = (bf16[1,2,128,768]{3,2,1,0:T(8,128)(2,1)}, bf16[1,2,128,768]{3,2,1,0:T(8,128)(2,1)S(1)}, u32[]{:S(2)}, u32[]{:S(2)}) collective-permute-start(bf16[1,2,128,768]{3,2,1,0:T(8,128)(2,1)} %get-tuple-element.102), channel_id=1, source_target_pairs={{0,2},{1,3},{2,0},{3,1},{4,6},{5,7},{6,4},{7,5},{8,10},{9,11},{10,... | collective-permute-start | bytes 1179656 | tf_op jit(solution)/shard_map/ppermute | solution.py:172
  389.1 26.8 %collective-permute-start.39 = (bf16[2,2,24,3968]{3,2,1,0:T(8,128)(2,1)S(1)}, bf16[2,2,24,3968]{3,2,1,0:T(8,128)(2,1)S(1)}, u32[]{:S(2)}, u32[]{:S(2)}) collective-permute-start(bf16[2,2,24,3968]{3,2,1,0:T(8,128)(2,1)S(1)} %dynamic-slice_bitcast_fusion.4), channel_id=1, source_target_pairs={{0,4},{1,5},{2,6},{3,7},{4,0},{5,1},{6,2},{7,3},{8,12},{9,13},{10,... | collective-permute-start | bytes 2285576 | tf_op jit(solution)/shard_map/ppermute | solution.py:172
  389.8 26.1 %collective-permute-start.40 = (bf16[2,2,24,3968]{3,2,1,0:T(8,128)(2,1)S(1)}, bf16[2,2,24,3968]{3,2,1,0:T(8,128)(2,1)}, u32[]{:S(2)}, u32[]{:S(2)}) collective-permute-start(bf16[2,2,24,3968]{3,2,1,0:T(8,128)(2,1)S(1)} %dynamic-slice_bitcast_fusion.3), channel_id=1, source_target_pairs={{0,2},{1,3},{2,0},{3,1},{4,6},{5,7},{6,4},{7,5},{8,10},{9,11},{10,... | collective-permute-start | bytes 2285576 | tf_op jit(solution)/shard_map/ppermute | solution.py:172
  439.7 38.3 %collective-permute-start.44 = (bf16[1,2,128,768]{3,2,1,0:T(8,128)(2,1)S(1)}, bf16[1,2,128,768]{3,2,1,0:T(8,128)(2,1)S(1)}, u32[]{:S(2)}, u32[]{:S(2)}) collective-permute-start(bf16[1,2,128,768]{3,2,1,0:T(8,128)(2,1)S(1)} %copy-done.28), channel_id=1, source_target_pairs={{0,3},{1,2},{2,1},{3,0},{4,7},{5,6},{6,5},{7,4},{8,11},{9,10},{10,... | collective-permute-start | bytes 1179656 | tf_op jit(solution)/shard_map/ppermute | solution.py:172
  458.3 19.7 %collective-permute-start.47 = (bf16[1,2,128,768]{3,2,1,0:T(8,128)(2,1)S(1)}, bf16[1,2,128,768]{3,2,1,0:T(8,128)(2,1)S(1)}, u32[]{:S(2)}, u32[]{:S(2)}) collective-permute-start(bf16[1,2,128,768]{3,2,1,0:T(8,128)(2,1)S(1)} %get-tuple-element.99), channel_id=1, source_target_pairs={{0,1},{1,0},{2,3},{3,2},{4,5},{5,4},{6,7},{7,6},{8,9},{9,8},{10,11... | collective-permute-start | bytes 1179656 | tf_op jit(solution)/shard_map/ppermute | solution.py:172
  (92 other events, 898.3 us)

commit v6 on v5

--- a/solution.py
+++ b/solution.py
@@ -17,10 +17,6 @@
     centered = value - center
     spread = jnp.mean(centered * centered, -1, keepdims=True)
     return centered * lax.rsqrt(spread + 1e-12) * gain + shift
-
-
-def gelu_exact(value):
-    return jax.nn.gelu(value, approximate=False)
 
 
 def over_rows(left, right):
@@ -168,6 +164,42 @@
     return block.reshape(lead + (-1, 3, 128)).swapaxes(-3, -2).reshape(block.shape)
 
 
+def feed_forward_kernel(step, x_ref, w_ref, b_ref, active_ref, slope_ref):
+    x = x_ref[...]
+    for start in range(0, w_ref.shape[1], step):
+        part = slice(start, start + step)
+        hidden = nn(x, w_ref[:, part]) + b_ref[:, part]
+        bell = jnp.exp(hidden * hidden * -0.5)
+        share = 0.5 * (1.0 + lax.erf(hidden * 0.7071067811865476))
+        active_ref[:, part] = (hidden * share).astype(BF)
+        slope_ref[:, part] = (share + hidden * bell * 0.3989422804014327).astype(BF)
+
+
+def feed_forward(x, weight, bias):
+    rows, width = x.shape
+    inner = weight.shape[1]
+    block = 256
+    out = jax.ShapeDtypeStruct((rows, inner), BF)
+    return pl.pallas_call(
+        functools.partial(feed_forward_kernel, 512),
+        grid=(rows // block,),
+        in_specs=[
+            pl.BlockSpec((block, width), lambda i: (i, 0)),
+            pl.BlockSpec((width, inner), lambda i: (0, 0)),
+            pl.BlockSpec((1, inner), lambda i: (0, 0)),
+        ],
+        out_specs=[pl.BlockSpec((block, inner), lambda i: (i, 0))] * 2,
+        out_shape=[out, out],
+        compiler_params=pltpu.CompilerParams(vmem_limit_bytes=48 * 2**20),
+        name="feed_forward",
+        cost_estimate=pl.CostEstimate(
+            flops=2 * rows * width * inner,
+            bytes_accessed=4 * rows * inner + 2 * width * inner,
+            transcendentals=2 * rows * inner,
+        ),
+    )(x, weight, bias)
+
+
 def swap(block, distance, devices):
     return lax.ppermute(block, BOTH, [(i, i ^ distance) for i in range(devices)])
 
@@ -290,9 +322,11 @@
         self.parts = grown
         return [part[2] for part in grown]
 
-    def finish(self, spans=None):
+    def finish(self, spans=None, *done):
         pieces, piece_ids = [], []
         for held, ids, last, last_ids in self.parts:
+            if done:
+                last = after(last, *done)
             for b, b_ids in ((held, ids), (last, last_ids)):
                 pieces += [b, self.swapped(b, 1)]
                 piece_ids += b_ids + [i ^ 1 for i in b_ids]
@@ -427,7 +461,7 @@
     qkv_gather.along_z()
     flat = to_sequences(inputs, seat, members, devices)
     first_done = qkv_gather.first()
-    last_done = qkv_gather.second()
+    last_done = qkv_gather.second(flat)
     in_gather.along_z(first_done)
     in_gather.first(*last_done)
     wide_qkv, early = qkv_gather.finish([(0, 3 * width), (3 * width, early.shape[1])])
@@ -447,7 +481,7 @@
     mask = jnp.broadcast_to(mask[:, :, None], (kept, length, 128))
     mixed, logsum = attention_forward(packed, mask, length)
     wide_in, wide_out, late = in_gather.finish(
-        [(0, inner_width), (inner_width, width), (inner_width + width, late.shape[1])]
+        [(0, inner_width), (inner_width, width), (inner_width + width, late.shape[1])], mixed
     )
     wide_in = wide_in.reshape(width, inner_width)
     wide_out = wide_out.reshape(width, width)
@@ -471,10 +505,8 @@
     first_low = first.astype(BF)
     cot = to_sequences(after(cotangent, first_low), seat, members, devices)
     down_gather.second(first_low)
-    hidden = jnp.dot(first_low, wide_in, preferred_element_type=F32) + full_in_bias
-    active, gelu_pull = jax.vjp(gelu_exact, hidden)
-    active_low = active.astype(BF)
-    (wide_down,) = down_gather.finish()
+    active_low, slope = feed_forward(first_low, wide_in, full_in_bias[None])
+    (wide_down,) = down_gather.finish(None, active_low)
     wide_down = wide_down.reshape(inner_width, width)
     branch_two = jnp.dot(active_low, wide_down, preferred_element_type=F32) + full_down_bias
     result, norm_two_pull = jax.vjp(
@@ -486,15 +518,18 @@
     grad_second, grad_gain_two, grad_shift_two = norm_two_pull(cot.astype(F32))
     grad_branch_two = grad_second.astype(BF)
     grad_down = over_rows(active_low, grad_branch_two).astype(BF)
-    down_scatter = Scatter(grad_down.reshape(devices, -1, width), me, devices, "yx")
+    down_scatter = Scatter(grad_down.reshape(devices, -1, width), me, devices, "split")
     grad_down_bias = jnp.sum(grad_branch_two.astype(F32), 0)
-    (grad_hidden,) = gelu_pull(times_transposed(grad_branch_two, wide_down))
-    grad_hidden_low = grad_hidden.astype(BF)
+    grad_hidden_low = (
+        times_transposed(grad_branch_two, wide_down) * slope.astype(F32)
+    ).astype(BF)
     grad_in = over_rows(first_low, grad_hidden_low).astype(BF)
     grad_in_bias = jnp.sum(grad_hidden_low.astype(F32), 0)
     grad_hidden_low = after(grad_hidden_low, down_scatter.total)
     down_half = down_scatter.first()
     grad_first = times_transposed(grad_hidden_low, wide_in) + grad_second
+    grad_first = after(grad_first, *down_half)
+    down_quarter = down_scatter.second()
     grad_residual, grad_gain_one, grad_shift_one = norm_one_pull(grad_first)
     grad_branch_one = grad_residual.astype(BF)
     grad_out = over_rows(mixed, grad_branch_one).astype(BF)
@@ -523,12 +558,11 @@
         "split",
     )
     grad_mixed = times_transposed(grad_branch_one, wide_out).astype(BF)
-    grad_mixed = after(grad_mixed, in_scatter.total, *down_half)
+    grad_mixed = after(grad_mixed, in_scatter.total, *down_quarter)
     in_half = in_scatter.first()
-    down_quarter = down_scatter.second()
+    down_part = down_scatter.along_z()
     grad_packed, column_sums = attention_backward(packed, mask, logsum, grad_mixed, length)
-    grad_packed = after(grad_packed, *down_quarter, *in_half)
-    down_part = down_scatter.along_z()
+    grad_packed = after(grad_packed, down_part, *in_half)
     in_quarter = in_scatter.second()
     grad_qkv = over_rows(flat, grad_packed).astype(BF)
     column_sums = kind_major(column_sums.reshape(kept, 3 * width).sum(0))
@@ -541,7 +575,7 @@
         "split",
     )
     grad_inputs = (
-        times_transposed(after(grad_packed, grad_qkv), wide_qkv) + grad_residual
+        times_transposed(after(grad_packed, grad_qkv, *in_quarter), wide_qkv) + grad_residual
     ).astype(BF)
     grad_inputs = send_positions(
         grad_inputs.reshape(kept, members, local_len, width), members, devices

time: 497 us -> 437 us (0.88)
  matrix products: 111 us -> 57.9 us
  local copies, waits for them, and re-layouts: 49.4 us -> 33.3 us
  Pallas kernels: 58.1 us -> 70.4 us
  waiting for transfers between devices: 161 us -> 169 us
  other arithmetic: 44.6 us -> 38.7 us
    dot_general x1 -> x0, matrix products: 37 us -> none  [on_device(): jnp.dot(first_low, wide_in, preferred_element_type=F32) + full_in_bias]
    pallas_call x0 -> x1, Pallas kernels: none -> 14.8 us  [feed_forward(): pl.pallas_call(functools.partial(feed_forward_kernel, 512), grid=(rows //...]
    dot_general x4, matrix products: 30.7 us -> 17.7 us  [times_transposed(): lax.dot_general(left, right, (((1,), (1,)), ((), ())), preferred_element_...]
    ppermute x63 -> x65, waiting for transfers between devices: 161 us -> 169 us  [swap(): lax.ppermute(block, BOTH, [(i, i ^ distance) for i in range(devices)])]
    unnamed x117 -> x97, local copies, waits for them, and re-layouts: 20.4 us -> 14.1 us
    another operation x13 -> x9, local copies, waits for them, and re-layouts: 5.99 us -> 0.76 us  [pack_rows(): block = jnp.stack(rows, -2)]
    convert_element_type x11 -> x14, other arithmetic: 13.1 us -> 8.51 us  [fold(): return (pick(block, axis, digit).astype(F32) + got.astype(F32)).astype(BF)]
    ppermute x63 -> x65, starting transfers between devices: 64.7 us -> 60.8 us  [swap(): lax.ppermute(block, BOTH, [(i, i ^ distance) for i in range(devices)])]
  transfers between devices with their start and end apart: 63 -> 65, of which waited for: 25 -> 30; matrix products, arithmetic and copies ran while one was open for 26% -> 16% of each run, Pallas kernels for 9% -> 14%
where the time goes in v6:
time: 437 us; the launch traced here: 433 us
  waiting for transfers between devices  169 us (39%)
  Pallas kernels  70.4 us (16%)
  starting transfers between devices  60.8 us (14%)
  matrix products  57.9 us (13%)
  other arithmetic  38.7 us (9%)
  local copies, waits for them, and re-layouts  33.3 us (8%)
    ppermute x65, waiting for transfers between devices, swap(): lax.ppermute(block, BOTH, [(i, i ^ distance) for i in range(devices)])  169 us
    ppermute x65, starting transfers between devices, swap(): lax.ppermute(block, BOTH, [(i, i ^ distance) for i in range(devices)])  60.8 us
    pallas_call x1, Pallas kernels, attention_backward(): pl.pallas_call(backward_kernel, grid=(seqs, pairs), in_specs=[block(384),...  24.5 us
    dot_general x4, matrix products, over_rows(): lax.dot_general(left, right, (((0,), (0,)), ((), ())), preferred_element_...  21.1 us
    dot_general x4, matrix products, times_transposed(): lax.dot_general(left, right, (((1,), (1,)), ((), ())), preferred_element_...  17.7 us
    pallas_call x1, Pallas kernels, attention_forward(): pl.pallas_call(forward_kernel, grid=(seqs, pairs), in_specs=[block(384),...  17 us
    pallas_call x1, Pallas kernels, feed_forward(): pl.pallas_call(functools.partial(feed_forward_kernel, 512), grid=(rows //...  14.8 us
    unnamed x97, local copies, waits for them, and re-layouts  14.1 us
  transfers between devices with their start and end apart: 65, of which 30 were waited for; matrix products, arithmetic and copies ran while one was open for 16% of the time, Pallas kernels for 14%

profile of v6, /device:TPU:0, one launch (start us, length us, event | category | flops | bytes accessed | tf_op | source)
XLA Modules:
  0.0 432.5 jit_solution(15660559192732620707)
XLA Ops:
  26.2 9.7 %collective-permute-done.10 = bf16[2,24,2432]{2,1,0:T(8,128)(2,1)S(1)} collective-permute-done((bf16[2,24,2432]{2,1,0:T(8,128)(2,1)S(1)}, bf16[2,24,2432]{2,1,0:T(8,128)(2,1)S(1)}, u32[]{:S(2)}, u32[]{:S(2)}) %collective-permute-start.10) | collective-permute-done | bytes 233504 | tf_op jit(solution)/shard_map/ppermute | solution.py:204
  45.4 6.9 %collective-permute-done.12.refs_6_ = bf16[4,24,2432]{2,1,0:T(8,128)(2,1)S(1)} collective-permute-done((bf16[4,24,2432]{2,1,0:T(8,128)(2,1)S(1)}, bf16[4,24,2432]{2,1,0:T(8,128)(2,1)S(1)}, u32[]{:S(2)}, u32[]{:S(2)}) %collective-permute-start.12) | collective-permute-done | bytes 466976 | tf_op jit(solution)/shard_map/ppermute | solution.py:204
  55.8 6.8 %collective-permute-done.21 = bf16[2,24,3968]{2,1,0:T(8,128)(2,1)S(1)} collective-permute-done((bf16[2,24,3968]{2,1,0:T(8,128)(2,1)S(1)}, bf16[2,24,3968]{2,1,0:T(8,128)(2,1)S(1)}, u32[]{:S(2)}, u32[]{:S(2)}) %collective-permute-start.21) | collective-permute-done | bytes 380960 | tf_op jit(solution)/shard_map/ppermute | solution.py:204
  71.6 8.5 %add_convert_fusion.packed_ref = bf16[1024,2304]{1,0:T(8,128)(2,1)} fusion(bf16[1024,768]{1,0:T(8,128)(2,1)} %bitcast.308, bf16[768,2304]{1,0:T(8,128)(2,1)} %bitcast.289, f32[2304]{0:T(1024)S(1)} %add.443), kind=kOutput, calls=%fused_computation.1 | convolution fusion | flops 3628597248 | bytes 9839616 | tf_op jit(solution)/shard_map/dot_general | solution.py:474
  84.7 17.0 %attention_forward.1 = (bf16[1024,768]{1,0:T(8,128)(2,1)S(1)}, f32[12,2,512]{2,1,0:T(2,128)S(1)}) custom-call(bf16[1024,2304]{1,0:T(8,128)(2,1)} %add_convert_fusion.packed_ref, bf16[2,512,128]{2,1,0:T(8,128)(2,1)S(1)} %broadcast_in_dim.55.mask_ref), custom_call_target="tpu_custom_call" | custom-call | flops 6442450944 | bytes 6291456 | tf_op jit(solution)/shard_map/attention_forward/pallas_call | solution.py:117
  103.4 14.8 %collective-permute-done.28 = bf16[4,96,768]{2,1,0:T(8,128)(2,1)S(1)} collective-permute-done((bf16[4,96,768]{2,1,0:T(8,128)(2,1)S(1)}, bf16[4,96,768]{2,1,0:T(8,128)(2,1)S(1)}, u32[]{:S(2)}, u32[]{:S(2)}) %collective-permute-start.28) | collective-permute-done | bytes 589856 | tf_op jit(solution)/shard_map/ppermute | solution.py:204
  125.7 5.3 %fusion.47 = (f32[1024]{0:T(1024)S(1)}, f32[1024,768]{1,0:T(8,128)}) fusion(f32[768]{0:T(1024)S(1)} %reshape.435, bf16[1024,768]{1,0:T(8,128)(2,1)} %copy-done.5, bf16[768,768]{1,0:T(8,128)(2,1)} %bitcast.291, bf16[1024,768]{1,0:T(8,128)(2,1)} %bitcast.309), kind=kOutput, calls=%fused_computation.215 | convolution fusion | flops 1211104256 | bytes 7478272 | tf_op jit(solution)/shard_map/dot_general | solution.py:501
  137.7 14.8 %feed_forward.1 = (bf16[1024,3072]{1,0:T(8,128)(2,1)}, bf16[1024,3072]{1,0:T(8,128)(2,1)}) custom-call(bf16[1024,768]{1,0:T(8,128)(2,1)S(1)} %add_convert_fusion.3.x_ref, bf16[768,3072]{1,0:T(8,128)(2,1)} %bitcast.285, f32[1,3072]{1,0:T(1,128)S(1)} %reshape.438.b_ref), custom_call_target="tpu_custom_call" | custom-call | flops 4831838208 | bytes 17301504 | tf_op jit(solution)/shard_map/feed_forward/pallas_call | solution.py:183
  152.5 10.8 %collective-permute-done.30.refs_2_ = bf16[8,96,768]{2,1,0:T(8,128)(2,1)} collective-permute-done((bf16[8,96,768]{2,1,0:T(8,128)(2,1)S(1)}, bf16[8,96,768]{2,1,0:T(8,128)(2,1)}, u32[]{:S(2)}, u32[]{:S(2)}) %collective-permute-start.30) | collective-permute-done | bytes 1179680 | tf_op jit(solution)/shard_map/ppermute | solution.py:204
  168.1 9.3 %collective-permute-done.33 = bf16[2,128,768]{2,1,0:T(8,128)(2,1)} collective-permute-done((bf16[2,128,768]{2,1,0:T(8,128)(2,1)}, bf16[2,128,768]{2,1,0:T(8,128)(2,1)}, u32[]{:S(2)}, u32[]{:S(2)}) %collective-permute-start.33) | collective-permute-done | bytes 393248 | tf_op jit(solution)/shard_map/ppermute | solution.py:204
  178.4 5.4 %collective-permute-done.34 = bf16[2,128,768]{2,1,0:T(8,128)(2,1)} collective-permute-done((bf16[2,128,768]{2,1,0:T(8,128)(2,1)}, bf16[2,128,768]{2,1,0:T(8,128)(2,1)}, u32[]{:S(2)}, u32[]{:S(2)}) %collective-permute-start.34) | collective-permute-done | bytes 393248 | tf_op jit(solution)/shard_map/ppermute | solution.py:204
  202.5 5.5 %convolution_convert_fusion.1 = bf16[3072,768]{1,0:T(8,128)(2,1)S(1)} fusion(bf16[1024,3072]{1,0:T(8,128)(2,1)S(1)} %bitcast.339, bf16[1024,768]{1,0:T(8,128)(2,1)S(1)} %get-tuple-element.99), kind=kOutput, calls=%fused_computation.6 | convolution fusion | flops 4834197504 | bytes 12582912 | tf_op jit(solution)/shard_map/dot_general | solution.py:23
  212.7 7.4 %fusion.49 = (bf16[3072]{0:T(1024)(128)(2,1)S(1)}, bf16[1024,3072]{1,0:T(8,128)(2,1)}) fusion(bf16[1024,3072]{1,0:T(8,128)(2,1)S(1)} %bitcast.337, bf16[1024,768]{1,0:T(8,128)(2,1)S(1)} %get-tuple-element.99, bf16[3072,768]{1,0:T(8,128)(2,1)S(1)} %bitcast.284), kind=kOutput, calls=%fused_computation.217 | convolution fusion | flops 4844418048 | bytes 18880512 | tf_op jit(solution)/shard_map/dot_general | solution.py:29
  220.4 9.7 %convolution_convert_fusion = bf16[768,3072]{1,0:T(8,128)(2,1)} fusion(bf16[1024,768]{1,0:T(8,128)(2,1)S(1)} %add_convert_fusion.3.x_ref, bf16[1024,3072]{1,0:T(8,128)(2,1)} %get-tuple-element.70), kind=kOutput, calls=%fused_computation.5 | convolution fusion | flops 4834197504 | bytes 12582912 | tf_op jit(solution)/shard_map/dot_general | solution.py:23
  239.9 8.0 %collective-permute-done.36 = bf16[2,2,96,768]{3,2,0,1:T(8,128)(2,1)S(1)} collective-permute-done((bf16[2,2,96,768]{3,2,0,1:T(8,128)(2,1)S(1)}, bf16[2,2,96,768]{3,2,0,1:T(8,128)(2,1)S(1)}, u32[]{:S(2)}, u32[]{:S(2)}) %collective-permute-start.36) | collective-permute-done | bytes 589856 | tf_op jit(solution)/shard_map/ppermute | solution.py:204
  272.0 5.5 %collective-permute-done.39 = bf16[2,96,768]{2,1,0:T(8,128)(2,1)S(1)} collective-permute-done((bf16[2,96,768]{2,1,0:T(8,128)(2,1)S(1)}, bf16[2,96,768]{2,1,0:T(8,128)(2,1)S(1)}, u32[]{:S(2)}, u32[]{:S(2)}) %collective-permute-start.39) | collective-permute-done | bytes 294944 | tf_op jit(solution)/shard_map/ppermute | solution.py:204
  285.8 6.6 %collective-permute-done.42 = bf16[96,768]{1,0:T(8,128)(2,1)S(1)} collective-permute-done((bf16[96,768]{1,0:T(8,128)(2,1)S(1)}, bf16[96,768]{1,0:T(8,128)(2,1)S(1)}, u32[]{:S(2)}, u32[]{:S(2)}) %collective-permute-start.42) | collective-permute-done | bytes 147488 | tf_op jit(solution)/shard_map/ppermute | solution.py:204
  297.4 24.5 %attention_backward.1 = (bf16[1024,2304]{1,0:T(8,128)(2,1)}, f32[12,1,384]{2,1,0:T(1,128)S(1)}) custom-call(bf16[1024,2304]{1,0:T(8,128)(2,1)} %add_convert_fusion.packed_ref, bf16[2,512,128]{2,1,0:T(8,128)(2,1)S(1)} %broadcast_in_dim.55.mask_ref, f32[12,2,512]{2,1,0:T(2,128)S(1)} %get-tuple-element.67.logsum_ref, ...), custom_call_target="tpu_custom_call" | custom-call | flops 11274289152 | bytes 11010048 | tf_op jit(solution)/shard_map/attention_backward/pallas_call | solution.py:138
  326.4 16.6 %collective-permute-done.44 = bf16[2,2,24,3968]{3,2,0,1:T(8,128)(2,1)S(1)} collective-permute-done((bf16[2,2,24,3968]{3,2,0,1:T(8,128)(2,1)S(1)}, bf16[2,2,24,3968]{3,2,0,1:T(8,128)(2,1)S(1)}, u32[]{:S(2)}, u32[]{:S(2)}) %collective-permute-start.44) | collective-permute-done | bytes 761888 | tf_op jit(solution)/shard_map/ppermute | solution.py:204
  351.7 7.0 %collective-permute-done.50 = bf16[2,24,3968]{2,1,0:T(8,128)(2,1)S(1)} collective-permute-done((bf16[2,24,3968]{2,1,0:T(8,128)(2,1)S(1)}, bf16[2,24,3968]{2,1,0:T(8,128)(2,1)S(1)}, u32[]{:S(2)}, u32[]{:S(2)}) %collective-permute-start.50) | collective-permute-done | bytes 380960 | tf_op jit(solution)/shard_map/ppermute | solution.py:204
  368.6 9.9 %collective-permute-done.63 = bf16[24,3968]{1,0:T(8,128)(2,1)S(1)} collective-permute-done((bf16[24,3968]{1,0:T(8,128)(2,1)S(1)}, bf16[24,3968]{1,0:T(8,128)(2,1)S(1)}, u32[]{:S(2)}, u32[]{:S(2)}) %collective-permute-start.63) | collective-permute-done | bytes 190496 | tf_op jit(solution)/shard_map/ppermute | solution.py:204
  386.5 11.1 %collective-permute-done.52 = bf16[2,2,24,2432]{3,2,1,0:T(8,128)(2,1)S(1)} collective-permute-done((bf16[2,2,24,2432]{3,2,1,0:T(8,128)(2,1)S(1)}, bf16[2,2,24,2432]{3,2,1,0:T(8,128)(2,1)S(1)}, u32[]{:S(2)}, u32[]{:S(2)}) %collective-permute-start.52) | collective-permute-done | bytes 466976 | tf_op jit(solution)/shard_map/ppermute | solution.py:204
  399.0 7.0 %collective-permute-done.57 = bf16[2,24,2432]{2,1,0:T(8,128)(2,1)S(1)} collective-permute-done((bf16[2,24,2432]{2,1,0:T(8,128)(2,1)S(1)}, bf16[2,24,2432]{2,1,0:T(8,128)(2,1)S(1)}, u32[]{:S(2)}, u32[]{:S(2)}) %collective-permute-start.57) | collective-permute-done | bytes 233504 | tf_op jit(solution)/shard_map/ppermute | solution.py:204
  406.8 6.2 %collective-permute-done.59 = bf16[2,24,2432]{2,1,0:T(8,128)(2,1)S(1)} collective-permute-done((bf16[2,24,2432]{2,1,0:T(8,128)(2,1)S(1)}, bf16[2,24,2432]{2,1,0:T(8,128)(2,1)S(1)}, u32[]{:S(2)}, u32[]{:S(2)}) %collective-permute-start.59) | collective-permute-done | bytes 233504 | tf_op jit(solution)/shard_map/ppermute | solution.py:204
  (370 shorter events, 196.1 us)
Async XLA Ops:
  10.8 28.2 %collective-permute-start = (bf16[2,128,768]{2,1,0:T(8,128)(2,1)}, bf16[2,128,768]{2,1,0:T(8,128)(2,1)S(1)}, u32[]{:S(2)}, u32[]{:S(2)}) collective-permute-start(bf16[2,128,768]{2,1,0:T(8,128)(2,1)} %get-tuple-element.133), channel_id=1, source_target_pairs={{0,1},{1,0},{2,3},{3,2},{4,5},{5,4},{6,7},{7,6},{8,9},{9,8},{10,11... | collective-permute-start | bytes 1179656 | tf_op jit(solution)/shard_map/ppermute | solution.py:204
  10.8 28.2 %collective-permute-start.1 = (bf16[2,128,768]{2,1,0:T(8,128)(2,1)}, bf16[2,128,768]{2,1,0:T(8,128)(2,1)S(1)}, u32[]{:S(2)}, u32[]{:S(2)}) collective-permute-start(bf16[2,128,768]{2,1,0:T(8,128)(2,1)} %get-tuple-element.132), channel_id=1, source_target_pairs={{0,2},{1,3},{2,0},{3,1},{4,6},{5,7},{6,4},{7,5},{8,10},{9,11},{10,... | collective-permute-start | bytes 1179656 | tf_op jit(solution)/shard_map/ppermute | solution.py:204
  16.4 22.5 %collective-permute-start.2 = (bf16[2,128,768]{2,1,0:T(8,128)(2,1)S(1)}, bf16[2,128,768]{2,1,0:T(8,128)(2,1)S(1)}, u32[]{:S(2)}, u32[]{:S(2)}) collective-permute-start(bf16[2,128,768]{2,1,0:T(8,128)(2,1)S(1)} %get-tuple-element.131), channel_id=1, source_target_pairs={{0,3},{1,2},{2,1},{3,0},{4,7},{5,6},{6,5},{7,4},{8,11},{9,10},{10,... | collective-permute-start | bytes 1179656 | tf_op jit(solution)/shard_map/ppermute | solution.py:204
  18.1 17.8 %collective-permute-start.10 = (bf16[2,24,2432]{2,1,0:T(8,128)(2,1)S(1)}, bf16[2,24,2432]{2,1,0:T(8,128)(2,1)S(1)}, u32[]{:S(2)}, u32[]{:S(2)}) collective-permute-start(bf16[2,24,2432]{2,1,0:T(8,128)(2,1)S(1)} %pad_maximum_fusion.12), channel_id=1, source_target_pairs={{0,2},{1,3},{2,0},{3,1},{4,6},{5,7},{6,4},{7,5},{8,10},{9,11},{10,... | collective-permute-start | bytes 700424 | tf_op jit(solution)/shard_map/ppermute | solution.py:204
  24.5 19.4 %collective-permute-start.19 = (bf16[1,24,3968]{2,1,0:T(8,128)(2,1)S(1)}, bf16[1,24,3968]{2,1,0:T(8,128)(2,1)S(1)}, u32[]{:S(2)}, u32[]{:S(2)}) collective-permute-start(bf16[1,24,3968]{2,1,0:T(8,128)(2,1)S(1)} %fusion.26), channel_id=1, source_target_pairs={{0,16},{1,17},{2,18},{3,19},{4,20},{5,21},{6,22},{7,23},{8,24},{9,... | collective-permute-start | bytes 571400 | tf_op jit(solution)/shard_map/ppermute | solution.py:204
  43.9 20.2 %collective-permute-start.11 = (bf16[4,24,2432]{2,1,0:T(8,128)(2,1)S(1)}, bf16[4,24,2432]{2,1,0:T(8,128)(2,1)S(1)}, u32[]{:S(2)}, u32[]{:S(2)}) collective-permute-start(bf16[4,24,2432]{2,1,0:T(8,128)(2,1)S(1)} %pad_maximum_fusion.8.refs_4_), channel_id=1, source_target_pairs={{0,1},{1,0},{2,3},{3,2},{4,5},{5,4},{6,7},{7,6},{8,9},{9,8},{10,11... | collective-permute-start | bytes 1400840 | tf_op jit(solution)/shard_map/ppermute | solution.py:204
  44.3 19.8 %collective-permute-start.5 = (bf16[4,24,2432]{2,1,0:T(8,128)(2,1)S(1)}, bf16[4,24,2432]{2,1,0:T(8,128)(2,1)S(1)}, u32[]{:S(2)}, u32[]{:S(2)}) collective-permute-start(bf16[4,24,2432]{2,1,0:T(8,128)(2,1)S(1)} %pad_maximum_fusion.7.refs_0_), channel_id=1, source_target_pairs={{0,1},{1,0},{2,3},{3,2},{4,5},{5,4},{6,7},{7,6},{8,9},{9,8},{10,11... | collective-permute-start | bytes 1400840 | tf_op jit(solution)/shard_map/ppermute | solution.py:204
  69.5 32.2 %collective-permute-start.23 = (bf16[4,24,3968]{2,1,0:T(8,128)(2,1)S(1)}, bf16[4,24,3968]{2,1,0:T(8,128)(2,1)S(1)}, u32[]{:S(2)}, u32[]{:S(2)}) collective-permute-start(bf16[4,24,3968]{2,1,0:T(8,128)(2,1)S(1)} %pad_maximum_fusion.5.refs_4_), channel_id=1, source_target_pairs={{0,4},{1,5},{2,6},{3,7},{4,0},{5,1},{6,2},{7,3},{8,12},{9,13},{10,... | collective-permute-start | bytes 2285576 | tf_op jit(solution)/shard_map/ppermute | solution.py:204
  70.1 31.6 %collective-permute-start.17 = (bf16[4,24,3968]{2,1,0:T(8,128)(2,1)S(1)}, bf16[4,24,3968]{2,1,0:T(8,128)(2,1)S(1)}, u32[]{:S(2)}, u32[]{:S(2)}) collective-permute-start(bf16[4,24,3968]{2,1,0:T(8,128)(2,1)S(1)} %pad_maximum_fusion.4.refs_0_), channel_id=1, source_target_pairs={{0,2},{1,3},{2,0},{3,1},{4,6},{5,7},{6,4},{7,5},{8,10},{9,11},{10,... | collective-permute-start | bytes 2285576 | tf_op jit(solution)/shard_map/ppermute | solution.py:204
  80.1 22.2 %collective-permute-start.25 = (bf16[1,96,768]{2,1,0:T(8,128)(2,1)S(1)}, bf16[1,96,768]{2,1,0:T(8,128)(2,1)S(1)}, u32[]{:S(2)}, u32[]{:S(2)}) collective-permute-start(bf16[1,96,768]{2,1,0:T(8,128)(2,1)S(1)} %bitcast.327), channel_id=1, source_target_pairs={{0,8},{1,9},{2,10},{3,11},{4,12},{5,13},{6,14},{7,15},{8,0},{9,1},... | collective-permute-start | bytes 442376 | tf_op jit(solution)/shard_map/ppermute | solution.py:204
  80.5 21.8 %collective-permute-start.26 = (bf16[1,96,768]{2,1,0:T(8,128)(2,1)S(1)}, bf16[1,96,768]{2,1,0:T(8,128)(2,1)S(1)}, u32[]{:S(2)}, u32[]{:S(2)}) collective-permute-start(bf16[1,96,768]{2,1,0:T(8,128)(2,1)S(1)} %bitcast.328), channel_id=1, source_target_pairs={{0,16},{1,17},{2,18},{3,19},{4,20},{5,21},{6,22},{7,23},{8,24},{9,... | collective-permute-start | bytes 442376 | tf_op jit(solution)/shard_map/ppermute | solution.py:204
  81.5 21.2 %collective-permute-start.27 = (bf16[1,96,768]{2,1,0:T(8,128)(2,1)S(1)}, bf16[1,96,768]{2,1,0:T(8,128)(2,1)S(1)}, u32[]{:S(2)}, u32[]{:S(2)}) collective-permute-start(bf16[1,96,768]{2,1,0:T(8,128)(2,1)S(1)} %bitcast.329), channel_id=1, source_target_pairs={{0,24},{1,25},{2,26},{3,27},{4,28},{5,29},{6,30},{7,31},{8,16},{9,... | collective-permute-start | bytes 442376 | tf_op jit(solution)/shard_map/ppermute | solution.py:204
  136.0 27.3 %collective-permute-start.30 = (bf16[8,96,768]{2,1,0:T(8,128)(2,1)S(1)}, bf16[8,96,768]{2,1,0:T(8,128)(2,1)}, u32[]{:S(2)}, u32[]{:S(2)}) collective-permute-start(bf16[8,96,768]{2,1,0:T(8,128)(2,1)S(1)} %pad_maximum_fusion.3.refs_0_), channel_id=1, source_target_pairs={{0,4},{1,5},{2,6},{3,7},{4,0},{5,1},{6,2},{7,3},{8,12},{9,13},{10,... | collective-permute-start | bytes 3538952 | tf_op jit(solution)/shard_map/ppermute | solution.py:204
  137.5 49.3 %collective-permute-start.29 = (bf16[8,96,768]{2,1,0:T(8,128)(2,1)S(1)}, bf16[8,96,768]{2,1,0:T(8,128)(2,1)}, u32[]{:S(2)}, u32[]{:S(2)}) collective-permute-start(bf16[8,96,768]{2,1,0:T(8,128)(2,1)S(1)} %pad_maximum_fusion.3.refs_0_), channel_id=1, source_target_pairs={{0,1},{1,0},{2,3},{3,2},{4,5},{5,4},{6,7},{7,6},{8,9},{9,8},{10,11... | collective-permute-start | bytes 3538952 | tf_op jit(solution)/shard_map/ppermute | solution.py:204
  163.3 23.5 %collective-permute-start.31 = (bf16[8,96,768]{2,1,0:T(8,128)(2,1)}, bf16[8,96,768]{2,1,0:T(8,128)(2,1)}, u32[]{:S(2)}, u32[]{:S(2)}) collective-permute-start(bf16[8,96,768]{2,1,0:T(8,128)(2,1)} %collective-permute-done.30.refs_2_), channel_id=1, source_target_pairs={{0,1},{1,0},{2,3},{3,2},{4,5},{5,4},{6,7},{7,6},{8,9},{9,8},{10,11... | collective-permute-start | bytes 3538952 | tf_op jit(solution)/shard_map/ppermute | solution.py:204
  165.6 18.3 %collective-permute-start.34 = (bf16[2,128,768]{2,1,0:T(8,128)(2,1)}, bf16[2,128,768]{2,1,0:T(8,128)(2,1)}, u32[]{:S(2)}, u32[]{:S(2)}) collective-permute-start(bf16[2,128,768]{2,1,0:T(8,128)(2,1)} %get-tuple-element.126), channel_id=1, source_target_pairs={{0,3},{1,2},{2,1},{3,0},{4,7},{5,6},{6,5},{7,4},{8,11},{9,10},{10,... | collective-permute-start | bytes 1179656 | tf_op jit(solution)/shard_map/ppermute | solution.py:204
  211.9 18.2 %collective-permute-start.35 = (bf16[16,96,768]{2,1,0:T(8,128)(2,1)}, bf16[16,96,768]{2,1,0:T(8,128)(2,1)}, u32[]{:S(2)}, u32[]{:S(2)}) collective-permute-start(bf16[16,96,768]{2,1,0:T(8,128)(2,1)} %dynamic-slice_bitcast_fusion.1), channel_id=1, source_target_pairs={{0,1},{1,0},{2,3},{3,2},{4,5},{5,4},{6,7},{7,6},{8,9},{9,8},{10,11... | collective-permute-start | bytes 7077896 | tf_op jit(solution)/shard_map/ppermute | solution.py:204
  268.0 25.2 %collective-permute-start.38 = (bf16[16,24,3968]{2,1,0:T(8,128)(2,1)}, bf16[16,24,3968]{2,1,0:T(8,128)(2,1)}, u32[]{:S(2)}, u32[]{:S(2)}) collective-permute-start(bf16[16,24,3968]{2,1,0:T(8,128)(2,1)} %dynamic-slice_bitcast_fusion), channel_id=1, source_target_pairs={{0,1},{1,0},{2,3},{3,2},{4,5},{5,4},{6,7},{7,6},{8,9},{9,8},{10,11... | collective-permute-start | bytes 9142280 | tf_op jit(solution)/shard_map/ppermute | solution.py:204
  271.1 142.5 %collective-permute-start.47 = (bf16[1,2,128,768]{3,2,1,0:T(8,128)(2,1)}, bf16[1,2,128,768]{3,2,1,0:T(8,128)(2,1)S(1)}, u32[]{:S(2)}, u32[]{:S(2)}) collective-permute-start(bf16[1,2,128,768]{3,2,1,0:T(8,128)(2,1)} %get-tuple-element.123), channel_id=1, source_target_pairs={{0,1},{1,0},{2,3},{3,2},{4,5},{5,4},{6,7},{7,6},{8,9},{9,8},{10,11... | collective-permute-start | bytes 1179656 | tf_op jit(solution)/shard_map/ppermute | solution.py:204
  284.2 129.6 %collective-permute-start.48 = (bf16[1,2,128,768]{3,2,1,0:T(8,128)(2,1)}, bf16[1,2,128,768]{3,2,1,0:T(8,128)(2,1)S(1)}, u32[]{:S(2)}, u32[]{:S(2)}) collective-permute-start(bf16[1,2,128,768]{3,2,1,0:T(8,128)(2,1)} %get-tuple-element.122), channel_id=1, source_target_pairs={{0,2},{1,3},{2,0},{3,1},{4,6},{5,7},{6,4},{7,5},{8,10},{9,11},{10,... | collective-permute-start | bytes 1179656 | tf_op jit(solution)/shard_map/ppermute | solution.py:204
  324.0 19.0 %collective-permute-start.44 = (bf16[2,2,24,3968]{3,2,0,1:T(8,128)(2,1)S(1)}, bf16[2,2,24,3968]{3,2,0,1:T(8,128)(2,1)S(1)}, u32[]{:S(2)}, u32[]{:S(2)}) collective-permute-start(bf16[2,2,24,3968]{3,2,0,1:T(8,128)(2,1)S(1)} %bitcast.319), channel_id=1, source_target_pairs={{0,4},{1,5},{2,6},{3,7},{4,0},{5,1},{6,2},{7,3},{8,12},{9,13},{10,... | collective-permute-start | bytes 2285576 | tf_op jit(solution)/shard_map/ppermute | solution.py:204
  324.8 19.0 %collective-permute-start.45 = (bf16[2,2,24,3968]{3,2,0,1:T(8,128)(2,1)S(1)}, bf16[2,2,24,3968]{3,2,0,1:T(8,128)(2,1)S(1)}, u32[]{:S(2)}, u32[]{:S(2)}) collective-permute-start(bf16[2,2,24,3968]{3,2,0,1:T(8,128)(2,1)S(1)} %bitcast.320), channel_id=1, source_target_pairs={{0,2},{1,3},{2,0},{3,1},{4,6},{5,7},{6,4},{7,5},{8,10},{9,11},{10,... | collective-permute-start | bytes 2285576 | tf_op jit(solution)/shard_map/ppermute | solution.py:204
  368.6 47.4 %collective-permute-start.49 = (bf16[1,2,128,768]{3,2,1,0:T(8,128)(2,1)S(1)}, bf16[1,2,128,768]{3,2,1,0:T(8,128)(2,1)S(1)}, u32[]{:S(2)}, u32[]{:S(2)}) collective-permute-start(bf16[1,2,128,768]{3,2,1,0:T(8,128)(2,1)S(1)} %copy-done.21), channel_id=1, source_target_pairs={{0,3},{1,2},{2,1},{3,0},{4,7},{5,6},{6,5},{7,4},{8,11},{9,10},{10,... | collective-permute-start | bytes 1179656 | tf_op jit(solution)/shard_map/ppermute | solution.py:204
  397.6 18.8 %collective-permute-start.54 = (bf16[1,2,128,768]{3,2,1,0:T(8,128)(2,1)S(1)}, bf16[1,2,128,768]{3,2,1,0:T(8,128)(2,1)S(1)}, u32[]{:S(2)}, u32[]{:S(2)}) collective-permute-start(bf16[1,2,128,768]{3,2,1,0:T(8,128)(2,1)S(1)} %get-tuple-element.119), channel_id=1, source_target_pairs={{0,1},{1,0},{2,3},{3,2},{4,5},{5,4},{6,7},{7,6},{8,9},{9,8},{10,11... | collective-permute-start | bytes 1179656 | tf_op jit(solution)/shard_map/ppermute | solution.py:204
  (86 other events, 949.2 us)

commit v7 on v6

--- a/solution.py
+++ b/solution.py
@@ -272,65 +272,73 @@
     return out
 
 
+def fence(holders, *values):
+    arrays = [a for h in holders for a in h.arrays()]
+    kept = lax.optimization_barrier(tuple(arrays) + values)
+    at = 0
+    for h in holders:
+        count = len(h.arrays())
+        h.put(list(kept[at : at + count]))
+        at += count
+    return kept[at:]
+
+
 class Gather:
     def __init__(self, block, me, devices, plan):
         self.me, self.devices, self.plan = me, devices, plan
-        self.own, self.own_ids = block[None], [0]
+        self.held, self.ids = [block[None]], [[0]]
+
+    def arrays(self):
+        return self.held
+
+    def put(self, arrays):
+        self.held = arrays
 
     def swapped(self, block, distance):
         return swap(block, distance, self.devices)
 
-    def along_z(self, *done):
-        own, own_ids = self.own, self.own_ids
-        if done:
-            own = after(own, *done)
+    def along_z(self):
+        own, own_ids = self.held[0], self.ids[0]
         distance = 32
         while distance < self.devices:
             own = jnp.concatenate([own, self.swapped(own, distance)])
             own_ids = own_ids + [i ^ distance for i in own_ids]
             distance *= 2
-        far = [own] + [self.swapped(own, 8 * k) for k in (1, 2, 3)]
-        far_ids = [[i ^ (8 * k) for i in own_ids] for k in range(4)]
+        self.held = [own] + [self.swapped(own, 8 * k) for k in (1, 2, 3)]
+        self.ids = [[i ^ (8 * k) for i in own_ids] for k in range(4)]
+
+    def grow(self, order):
+        held, ids = [], []
+        for block, block_ids, distance in zip(self.held, self.ids, order):
+            held += [block, self.swapped(block, distance)]
+            ids += [block_ids, [i ^ distance for i in block_ids]]
+        self.held, self.ids = held, ids
+
+    def join(self, pairs):
+        self.held = [jnp.concatenate([self.held[i] for i in p]) for p in pairs]
+        self.ids = [[i for j in p for i in self.ids[j]] for p in pairs]
+
+    def first(self):
         if self.plan == "split":
-            parts = [((0, 1), (4, 2)), ((2, 3), (2, 4))]
+            self.join([(0, 1), (2, 3)])
+            self.grow((4, 2))
         else:
-            parts = [((0, 1, 2, 3), (4, 2) if self.plan == "xy" else (2, 4))]
-        self.parts = []
-        for which, order in parts:
-            held = jnp.concatenate([far[k] for k in which])
-            self.parts.append((held, [i for k in which for i in far_ids[k]], order))
-        return far[1]
-
-    def first(self, *done):
-        grown = []
-        for held, ids, order in self.parts:
-            if done:
-                held = after(held, *done)
-            got = self.swapped(held, order[0])
-            grown.append(
-                (jnp.concatenate([held, got]), ids + [i ^ order[0] for i in ids], order)
-            )
-        self.parts = grown
-        return grown[0][0]
-
-    def second(self, *done):
-        grown = []
-        for held, ids, order in self.parts:
-            if done:
-                held = after(held, *done)
-            grown.append((held, ids, self.swapped(held, order[1]), [i ^ order[1] for i in ids]))
-        self.parts = grown
-        return [part[2] for part in grown]
-
-    def finish(self, spans=None, *done):
-        pieces, piece_ids = [], []
-        for held, ids, last, last_ids in self.parts:
-            if done:
-                last = after(last, *done)
-            for b, b_ids in ((held, ids), (last, last_ids)):
-                pieces += [b, self.swapped(b, 1)]
-                piece_ids += b_ids + [i ^ 1 for i in b_ids]
-        return place(pieces, piece_ids, self.me, spans)
+            self.join([(0, 1, 2, 3)])
+            self.grow((4,) if self.plan == "xy" else (2,))
+
+    def second(self):
+        if self.plan == "split":
+            self.join([(0, 1), (2, 3)])
+            self.grow((2, 4))
+        else:
+            self.join([(0, 1)])
+            self.grow((2,) if self.plan == "xy" else (4,))
+
+    def core(self):
+        self.grow((1,) * len(self.held))
+
+    def finish(self, spans=None):
+        return place(self.held, [i for ids in self.ids for i in ids], self.me, spans)
 
 
 def pick(block, axis, index):
@@ -343,73 +351,104 @@
     return (pick(block, axis, digit).astype(F32) + got.astype(F32)).astype(BF)
 
 
+def core_sum(total, me, devices):
+    tail = total.shape[1:]
+    distance = devices // 2
+    while distance >= 32:
+        total = fold(total.reshape((2, distance) + tail), 0, me, distance, devices)
+        distance //= 2
+    return fold(total.reshape((16, 2) + tail), 1, me, 1, devices)
+
+
 class Scatter:
     def __init__(self, total, me, devices, plan):
         self.me, self.devices, self.plan = me, devices, plan
         self.tail = total.shape[1:]
-        distance = devices // 2
-        while distance >= 32:
-            total = self.fold(total.reshape((2, distance) + self.tail), 0, distance)
-            distance //= 2
-        self.total = self.fold(total.reshape((16, 2) + self.tail), 1, 1)
+        self.held = [total]
+
+    def arrays(self):
+        return self.held
+
+    def put(self, arrays):
+        self.held = arrays
 
     def fold(self, block, axis, distance):
         return fold(block, axis, self.me, distance, self.devices)
 
     def first(self):
-        total = self.total.reshape((4, 2, 2) + self.tail)
+        total = self.held[0].reshape((4, 2, 2) + self.tail)
         if self.plan == "split":
             z = (self.me // 8) % 4
             halves = total.reshape((2, 2, 2, 2) + self.tail)
-            self.parts = [
+            self.held = [
                 self.fold(pick(halves, 0, z // 2), 1, 4),
                 self.fold(pick(halves, 0, 1 - z // 2), 2, 2),
             ]
         elif self.plan == "xy":
-            self.parts = [self.fold(total, 1, 4)]
+            self.held = [self.fold(total, 1, 4)]
         else:
-            self.parts = [self.fold(total, 2, 2)]
-        return self.parts
+            self.held = [self.fold(total, 2, 2)]
 
     def second(self):
         z = (self.me // 8) % 4
         if self.plan == "split":
-            near = self.fold(self.parts[0], 1, 2)
-            away = self.fold(self.parts[1], 1, 4)
+            near = self.fold(self.held[0], 1, 2)
+            away = self.fold(self.held[1], 1, 4)
             odd = z % 2
-            self.mine = [
+            self.held = [
                 pick(near, 0, odd),
                 pick(near, 0, 1 - odd),
                 pick(away, 0, odd),
                 pick(away, 0, 1 - odd),
             ]
         else:
-            total = self.fold(self.parts[0], 1, 2 if self.plan == "xy" else 4)
-            self.mine = [pick(total, 0, z ^ k) for k in range(4)]
-        return self.mine
+            total = self.fold(self.held[0], 1, 2 if self.plan == "xy" else 4)
+            self.held = [pick(total, 0, z ^ k) for k in range(4)]
 
     def along_z(self):
-        got = [swap(self.mine[k], 8 * k, self.devices).astype(F32) for k in (1, 2, 3)]
-        return self.mine[0].astype(F32) + got[0] + got[1] + got[2]
-
-
-def to_sequences(block, seat, members, devices):
-    groups, count, width = block.shape
-    parts = block.reshape(members, groups // members, count, width)
-    pieces = [pick(parts, 0, seat)]
-    pieces += [swap(pick(parts, 0, seat ^ k), k, devices) for k in range(1, members)]
-    return jnp.stack(pieces, 1).reshape(groups * count, width)
-
-
-def send_positions(block, members, devices):
-    pieces = [block[:, 0][None]]
-    return pieces + [swap(block[:, k][None], k, devices) for k in range(1, members)]
-
-
-def put_positions(pieces, seat, *done):
-    pieces = [after(pieces[0], *done)] + pieces[1:]
-    (placed,) = place(pieces, list(range(len(pieces))), seat)
-    return placed.reshape((-1,) + placed.shape[2:])
+        total = self.held[0].astype(F32)
+        for k in (1, 2, 3):
+            total = total + swap(self.held[k], 8 * k, self.devices).astype(F32)
+        self.held = [total]
+
+
+class ToSequences:
+    def __init__(self, block, seat, members, devices):
+        groups, count, width = block.shape
+        parts = block.reshape(members, groups // members, count, width)
+        self.devices = devices
+        self.held = [pick(parts, 0, seat ^ k) for k in range(members)]
+
+    def arrays(self):
+        return self.held
+
+    def put(self, arrays):
+        self.held = arrays
+
+    def send(self, k):
+        self.held[k] = swap(self.held[k], k, self.devices)
+
+    def finish(self):
+        return jnp.stack(self.held, 1).reshape(-1, self.held[0].shape[-1])
+
+
+class ToPositions:
+    def __init__(self, block, members, devices):
+        self.devices = devices
+        self.held = [block[:, k][None] for k in range(members)]
+
+    def arrays(self):
+        return self.held
+
+    def put(self, arrays):
+        self.held = arrays
+
+    def send(self, k):
+        self.held[k] = swap(self.held[k], k, self.devices)
+
+    def finish(self, seat):
+        (placed,) = place(self.held, list(range(len(self.held))), seat)
+        return placed.reshape((-1,) + placed.shape[2:])
 
 
 def on_device(
@@ -458,14 +497,31 @@
         jnp.concatenate([in_weight, output_weight, late], 1), me, devices, "split"
     )
     down_gather = Gather(down_weight, me, devices, "yx")
+    near, far = range(1, (members + 1) // 2), range((members + 1) // 2, members)
+    flat = ToSequences(inputs, seat, members, devices)
+    for k in near:
+        flat.send(k)
+    for k in far[:1]:
+        flat.send(k)
     qkv_gather.along_z()
-    flat = to_sequences(inputs, seat, members, devices)
-    first_done = qkv_gather.first()
-    last_done = qkv_gather.second(flat)
-    in_gather.along_z(first_done)
-    in_gather.first(*last_done)
+    fence([qkv_gather])
+    qkv_gather.first()
+    fence([qkv_gather, flat])
+    for k in far[1:]:
+        flat.send(k)
+    qkv_gather.second()
+    in_gather.put([after(a, qkv_gather.held[0]) for a in in_gather.arrays()])
+    in_gather.along_z()
+    fence([qkv_gather])
+    qkv_gather.core()
+    fence([qkv_gather, in_gather, flat])
+    in_gather.first()
+    flat = flat.finish()
     wide_qkv, early = qkv_gather.finish([(0, 3 * width), (3 * width, early.shape[1])])
-    in_gather.second(wide_qkv)
+    (wide_qkv, early, flat) = fence([in_gather], wide_qkv, early, flat)
+    in_gather.second()
+    down_gather.put([after(a, wide_qkv) for a in down_gather.arrays()])
+    down_gather.along_z()
     wide_qkv = wide_qkv.reshape(width, 3 * width)
     full_query_bias, full_value_bias = [
         v.reshape(-1).astype(F32) for v in unpack_rows(early, [share, share])
@@ -473,16 +529,21 @@
     bias_vector = jnp.concatenate([full_query_bias, jnp.zeros((width,), F32), full_value_bias])
     packed = jnp.dot(flat, wide_qkv, preferred_element_type=F32) + pair_major(bias_vector)
     packed = packed.astype(BF)
-    down_gather.along_z(packed)
     mine = lax.dynamic_slice(lengths, (seat * kept,), (kept,))
     slots = jnp.arange(length, dtype=jnp.int32)
     positions = ((slots // local_len) ^ seat) * local_len + slots % local_len
     mask = jnp.where(positions[None, :] < mine[:, None], 0.0, -1e30).astype(BF)
     mask = jnp.broadcast_to(mask[:, :, None], (kept, length, 128))
     mixed, logsum = attention_forward(packed, mask, length)
+    (mixed, logsum, packed) = fence([in_gather, down_gather], mixed, logsum, packed)
+    in_gather.core()
+    down_gather.first()
+    fence([in_gather])
     wide_in, wide_out, late = in_gather.finish(
-        [(0, inner_width), (inner_width, width), (inner_width + width, late.shape[1])], mixed
-    )
+        [(0, inner_width), (inner_width, width), (inner_width + width, late.shape[1])]
+    )
+    (wide_in, wide_out, late) = fence([down_gather], wide_in, wide_out, late)
+    down_gather.second()
     wide_in = wide_in.reshape(width, inner_width)
     wide_out = wide_out.reshape(width, width)
     (
@@ -497,43 +558,64 @@
         v.reshape(-1).astype(F32)
         for v in unpack_rows(late, [v.shape[0] for v in late_vectors])
     ]
-    down_gather.first(mixed)
     attention_branch = jnp.dot(mixed, wide_out, preferred_element_type=F32) + full_out_bias
     first, norm_one_pull = jax.vjp(
         layer_norm, flat.astype(F32) + attention_branch, gain_one, shift_one
     )
     first_low = first.astype(BF)
-    cot = to_sequences(after(cotangent, first_low), seat, members, devices)
-    down_gather.second(first_low)
+    (first_low,) = fence([down_gather], first_low)
+    down_gather.core()
+    cot = ToSequences(after(cotangent, first_low), seat, members, devices)
+    for k in range(1, members):
+        cot.send(k)
     active_low, slope = feed_forward(first_low, wide_in, full_in_bias[None])
-    (wide_down,) = down_gather.finish(None, active_low)
+    (active_low, slope) = fence([down_gather, cot], active_low, slope)
+    (wide_down,) = down_gather.finish()
     wide_down = wide_down.reshape(inner_width, width)
     branch_two = jnp.dot(active_low, wide_down, preferred_element_type=F32) + full_down_bias
     result, norm_two_pull = jax.vjp(
         layer_norm, first_low.astype(F32) + branch_two, gain_two, shift_two
     )
-    outputs = send_positions(
-        result.astype(BF).reshape(kept, members, local_len, width), members, devices
-    )
-    grad_second, grad_gain_two, grad_shift_two = norm_two_pull(cot.astype(F32))
+    outputs = result.astype(BF).reshape(kept, members, local_len, width)
+    grad_second, grad_gain_two, grad_shift_two = norm_two_pull(cot.finish().astype(F32))
     grad_branch_two = grad_second.astype(BF)
+    grad_down_bias = jnp.sum(grad_branch_two.astype(F32), 0)
+    (outputs, grad_second, grad_branch_two, grad_gain_two, grad_shift_two, grad_down_bias) = fence(
+        [],
+        outputs,
+        grad_second,
+        grad_branch_two,
+        grad_gain_two,
+        grad_shift_two,
+        grad_down_bias,
+    )
+    outputs = ToPositions(outputs, members, devices)
+    for k in near:
+        outputs.send(k)
+    for k in far[:1]:
+        outputs.send(k)
     grad_down = over_rows(active_low, grad_branch_two).astype(BF)
-    down_scatter = Scatter(grad_down.reshape(devices, -1, width), me, devices, "split")
-    grad_down_bias = jnp.sum(grad_branch_two.astype(F32), 0)
+    (grad_down, grad_branch_two) = fence([outputs], grad_down, grad_branch_two)
+    for k in far[1:]:
+        outputs.send(k)
+    down_scatter = Scatter(
+        core_sum(grad_down.reshape(devices, -1, width), me, devices), me, devices, "split"
+    )
     grad_hidden_low = (
         times_transposed(grad_branch_two, wide_down) * slope.astype(F32)
     ).astype(BF)
+    grad_in_bias = jnp.sum(grad_hidden_low.astype(F32), 0)
+    (grad_hidden_low, grad_in_bias) = fence([outputs, down_scatter], grad_hidden_low, grad_in_bias)
+    down_scatter.first()
     grad_in = over_rows(first_low, grad_hidden_low).astype(BF)
-    grad_in_bias = jnp.sum(grad_hidden_low.astype(F32), 0)
-    grad_hidden_low = after(grad_hidden_low, down_scatter.total)
-    down_half = down_scatter.first()
+    (grad_in, grad_hidden_low) = fence([down_scatter], grad_in, grad_hidden_low)
+    down_scatter.second()
+    in_core = core_sum(grad_in.reshape(devices, share, inner_width), me, devices)
     grad_first = times_transposed(grad_hidden_low, wide_in) + grad_second
-    grad_first = after(grad_first, *down_half)
-    down_quarter = down_scatter.second()
     grad_residual, grad_gain_one, grad_shift_one = norm_one_pull(grad_first)
     grad_branch_one = grad_residual.astype(BF)
+    grad_out_bias = jnp.sum(grad_branch_one.astype(F32), 0)
     grad_out = over_rows(mixed, grad_branch_one).astype(BF)
-    grad_out_bias = jnp.sum(grad_branch_one.astype(F32), 0)
     late_sums = [
         grad_out_bias,
         grad_gain_one,
@@ -544,48 +626,47 @@
         grad_shift_two,
     ]
     late_block = pack_rows([v.reshape(devices, -1) for v in late_sums], share).astype(BF)
-    in_scatter = Scatter(
-        jnp.concatenate(
-            [
-                grad_in.reshape(devices, share, inner_width),
-                grad_out.reshape(devices, share, width),
-                late_block,
-            ],
-            2,
-        ),
-        me,
-        devices,
-        "split",
+    out_core = core_sum(
+        jnp.concatenate([grad_out.reshape(devices, share, width), late_block], 2), me, devices
     )
     grad_mixed = times_transposed(grad_branch_one, wide_out).astype(BF)
-    grad_mixed = after(grad_mixed, in_scatter.total, *down_quarter)
-    in_half = in_scatter.first()
-    down_part = down_scatter.along_z()
+    in_scatter = Scatter(jnp.concatenate([in_core, out_core], 2), me, devices, "split")
+    (grad_mixed, grad_residual) = fence([down_scatter, in_scatter], grad_mixed, grad_residual)
+    in_scatter.first()
+    down_scatter.along_z()
     grad_packed, column_sums = attention_backward(packed, mask, logsum, grad_mixed, length)
-    grad_packed = after(grad_packed, down_part, *in_half)
-    in_quarter = in_scatter.second()
+    (grad_packed, column_sums) = fence([in_scatter, down_scatter], grad_packed, column_sums)
+    in_scatter.second()
     grad_qkv = over_rows(flat, grad_packed).astype(BF)
     column_sums = kind_major(column_sums.reshape(kept, 3 * width).sum(0))
     early_sums = [column_sums[:width], column_sums[2 * width :]]
     early_block = pack_rows([v.reshape(devices, -1) for v in early_sums], share).astype(BF)
-    qkv_scatter = Scatter(
-        jnp.concatenate([grad_qkv.reshape(devices, share, 3 * width), early_block], 2),
-        me,
-        devices,
-        "split",
-    )
-    grad_inputs = (
-        times_transposed(after(grad_packed, grad_qkv, *in_quarter), wide_qkv) + grad_residual
-    ).astype(BF)
-    grad_inputs = send_positions(
+    grad_qkv = jnp.concatenate([grad_qkv.reshape(devices, share, 3 * width), early_block], 2)
+    (grad_qkv, grad_packed) = fence([], grad_qkv, grad_packed)
+    qkv_scatter = Scatter(core_sum(grad_qkv, me, devices), me, devices, "split")
+    grad_inputs = (times_transposed(grad_packed, wide_qkv) + grad_residual).astype(BF)
+    (grad_inputs,) = fence([in_scatter, qkv_scatter], grad_inputs)
+    qkv_scatter.first()
+    in_scatter.along_z()
+    grad_inputs = ToPositions(
         grad_inputs.reshape(kept, members, local_len, width), members, devices
     )
-    qkv_half = qkv_scatter.first()
-    in_part = in_scatter.along_z()
-    outputs = put_positions(outputs, seat, qkv_scatter.total)
-    qkv_quarter = qkv_scatter.second()
-    qkv_part = qkv_scatter.along_z()
-    grad_inputs = put_positions(grad_inputs, seat, *qkv_half)
+    for k in near:
+        grad_inputs.send(k)
+    for k in far[:1]:
+        grad_inputs.send(k)
+    fence([qkv_scatter])
+    qkv_scatter.second()
+    for k in far[1:]:
+        grad_inputs.send(k)
+    outputs.put([after(a, qkv_scatter.held[0]) for a in outputs.arrays()])
+    outputs = outputs.finish(seat)
+    (outputs,) = fence([qkv_scatter, grad_inputs], outputs)
+    qkv_scatter.along_z()
+    grad_inputs = grad_inputs.finish(seat)
+    (qkv_part,), (in_part,), (down_part,) = (
+        s.held for s in (qkv_scatter, in_scatter, down_scatter)
+    )
     early_out = unpack_rows(qkv_part[:, 3 * width :], [share, share])
     late_out = unpack_rows(
         in_part[:, inner_width + width :], [v.shape[0] for v in late_vectors]

time: 437 us -> 395 us (0.904)
  waiting for transfers between devices: 169 us -> 115 us
  local copies, waits for them, and re-layouts: 33.3 us -> 46.1 us
  other arithmetic: 38.7 us -> 30 us
  matrix products: 57.9 us -> 66.4 us
    ppermute x65 -> x66, waiting for transfers between devices: 169 us -> 115 us  [swap(): lax.ppermute(block, BOTH, [(i, i ^ distance) for i in range(devices)])]
    dot_general x4, matrix products: 17.7 us -> 26.7 us  [times_transposed(): lax.dot_general(left, right, (((1,), (1,)), ((), ())), preferred_element_...]
    squeeze x17 -> x20, local copies, waits for them, and re-layouts: 4.07 us -> 12.5 us  [pick(): return lax.dynamic_index_in_dim(block, index, axis, keepdims=False)]
    reduce_sum x7 -> x3, other arithmetic: 8.68 us -> 3.52 us  [layer_norm(): return centered * lax.rsqrt(spread + 1e-12) * gain + shift]
    concatenate x2 -> x11, local copies, waits for them, and re-layouts: 0.19 us -> 4.58 us  [the longest x10 4.47 us: join(): self.held = [jnp.concatenate([self.held[i] for i in p]) for p in pairs]]
    reduce_sum x2 -> x1, other arithmetic: 5.97 us -> 1.58 us  [layer_norm(): centered = value - center]
    convert_element_type x14 -> x15, other arithmetic: 8.51 us -> 12.4 us  [fold(): return (pick(block, axis, digit).astype(F32) + got.astype(F32)).astype(BF)]
    ppermute x65 -> x66, starting transfers between devices: 60.8 us -> 61.4 us  [swap(): lax.ppermute(block, BOTH, [(i, i ^ distance) for i in range(devices)])]
  transfers between devices with their start and end apart: 65 -> 66, of which waited for: 30 -> 22; matrix products, arithmetic and copies ran while one was open for 16% -> 27% of each run, Pallas kernels for 14% -> 17%
where the time goes in v7:
time: 395 us; the launch traced here: 392 us
  waiting for transfers between devices  115 us (29%)
  Pallas kernels  71.1 us (18%)
  matrix products  66.4 us (17%)
  starting transfers between devices  61.4 us (16%)
  local copies, waits for them, and re-layouts  46.1 us (12%)
  other arithmetic  30 us (8%)
    ppermute x66, waiting for transfers between devices, swap(): lax.ppermute(block, BOTH, [(i, i ^ distance) for i in range(devices)])  115 us
    ppermute x66, starting transfers between devices, swap(): lax.ppermute(block, BOTH, [(i, i ^ distance) for i in range(devices)])  61.4 us
    dot_general x4, matrix products, times_transposed(): lax.dot_general(left, right, (((1,), (1,)), ((), ())), preferred_element_...  26.7 us
    pallas_call x1, Pallas kernels, attention_backward(): pl.pallas_call(backward_kernel, grid=(seqs, pairs), in_specs=[block(384),...  24.8 us
    dot_general x4, matrix products, over_rows(): lax.dot_general(left, right, (((0,), (0,)), ((), ())), preferred_element_...  20.7 us
    pallas_call x1, Pallas kernels, attention_forward(): pl.pallas_call(forward_kernel, grid=(seqs, pairs), in_specs=[block(384),...  17 us
    pallas_call x1, Pallas kernels, feed_forward(): pl.pallas_call(functools.partial(feed_forward_kernel, 512), grid=(rows //...  15.1 us
    pallas_call x5, Pallas kernels, place(): pl.pallas_call(functools.partial(place_kernel, ids, counts, spans), in_sp...  14.3 us
  transfers between devices with their start and end apart: 66, of which 22 were waited for; matrix products, arithmetic and copies ran while one was open for 27% of the time, Pallas kernels for 17%

profile of v7, /device:TPU:0, one launch (start us, length us, event | category | flops | bytes accessed | tf_op | source)
XLA Modules:
  0.0 392.0 jit_solution(15956537020466047484)
XLA Ops:
  12.6 5.1 %collective-permute-done.1 = bf16[1,24,2432]{2,1,0:T(8,128)(2,1)S(1)} collective-permute-done((bf16[1,24,2432]{2,1,0:T(8,128)(2,1)S(1)}, bf16[1,24,2432]{2,1,0:T(8,128)(2,1)S(1)}, u32[]{:S(2)}, u32[]{:S(2)}) %collective-permute-start.1) | collective-permute-done | bytes 116768 | tf_op jit(solution)/shard_map/ppermute | solution.py:204
  36.0 4.4 %collective-permute-done.7.refs_2_ = bf16[4,24,2432]{2,1,0:T(8,128)(2,1)S(1)} collective-permute-done((bf16[4,24,2432]{2,1,0:T(8,128)(2,1)S(1)}, bf16[4,24,2432]{2,1,0:T(8,128)(2,1)S(1)}, u32[]{:S(2)}, u32[]{:S(2)}) %collective-permute-start.7) | collective-permute-done | bytes 466976 | tf_op jit(solution)/shard_map/ppermute | solution.py:204
  42.5 7.1 %collective-permute-done.14 = bf16[1,24,3968]{2,1,0:T(8,128)(2,1)S(1)} collective-permute-done((bf16[1,24,3968]{2,1,0:T(8,128)(2,1)S(1)}, bf16[1,24,3968]{2,1,0:T(8,128)(2,1)S(1)}, u32[]{:S(2)}, u32[]{:S(2)}) %collective-permute-start.14) | collective-permute-done | bytes 190496 | tf_op jit(solution)/shard_map/ppermute | solution.py:204
  50.2 10.4 %collective-permute-done.16 = bf16[2,128,768]{2,1,0:T(8,128)(2,1)S(1)} collective-permute-done((bf16[2,128,768]{2,1,0:T(8,128)(2,1)}, bf16[2,128,768]{2,1,0:T(8,128)(2,1)S(1)}, u32[]{:S(2)}, u32[]{:S(2)}) %collective-permute-start.16) | collective-permute-done | bytes 393248 | tf_op jit(solution)/shard_map/ppermute | solution.py:204
  88.7 8.4 %add_convert_fusion.packed_ref = bf16[1024,2304]{1,0:T(8,128)(2,1)} fusion(bf16[1024,768]{1,0:T(8,128)(2,1)} %bitcast.330, bf16[768,2304]{1,0:T(8,128)(2,1)} %bitcast.293, f32[2304]{0:T(1024)S(1)} %add.450), kind=kOutput, calls=%fused_computation.2 | convolution fusion | flops 3628597248 | bytes 9839616 | tf_op jit(solution)/shard_map/dot_general | solution.py:530
  97.4 17.0 %attention_forward.1 = (bf16[1024,768]{1,0:T(8,128)(2,1)S(1)}, f32[12,2,512]{2,1,0:T(2,128)S(1)}) custom-call(bf16[1024,2304]{1,0:T(8,128)(2,1)} %add_convert_fusion.packed_ref, bf16[2,512,128]{2,1,0:T(8,128)(2,1)S(1)} %broadcast_in_dim.57.mask_ref), custom_call_target="tpu_custom_call" | custom-call | flops 6442450944 | bytes 6291456 | tf_op jit(solution)/shard_map/attention_forward/pallas_call | solution.py:117
  124.8 9.9 %collective-permute-done.24 = bf16[4,96,768]{2,1,0:T(8,128)(2,1)S(1)} collective-permute-done((bf16[4,96,768]{2,1,0:T(8,128)(2,1)S(1)}, bf16[4,96,768]{2,1,0:T(8,128)(2,1)S(1)}, u32[]{:S(2)}, u32[]{:S(2)}) %collective-permute-start.24) | collective-permute-done | bytes 589856 | tf_op jit(solution)/shard_map/ppermute | solution.py:204
  135.8 5.3 %fusion.45 = (f32[1024]{0:T(1024)S(1)}, f32[1024,768]{1,0:T(8,128)}) fusion(f32[768]{0:T(1024)S(1)} %reshape.431, bf16[1024,768]{1,0:T(8,128)(2,1)} %copy-done.9, bf16[768,768]{1,0:T(8,128)(2,1)} %bitcast.295, bf16[1024,768]{1,0:T(8,128)(2,1)} %bitcast.331), kind=kOutput, calls=%fused_computation.231 | convolution fusion | flops 1211104256 | bytes 7478272 | tf_op jit(solution)/shard_map/dot_general | solution.py:561
  144.6 17.7 %collective-permute-done.29.refs_2_ = bf16[8,96,768]{2,1,0:T(8,128)(2,1)} collective-permute-done((bf16[8,96,768]{2,1,0:T(8,128)(2,1)S(1)}, bf16[8,96,768]{2,1,0:T(8,128)(2,1)}, u32[]{:S(2)}, u32[]{:S(2)}) %collective-permute-start.29) | collective-permute-done | bytes 1179680 | tf_op jit(solution)/shard_map/ppermute | solution.py:204
  167.6 15.1 %feed_forward.1 = (bf16[1024,3072]{1,0:T(8,128)(2,1)}, bf16[1024,3072]{1,0:T(8,128)(2,1)}) custom-call(bf16[1024,768]{1,0:T(8,128)(2,1)S(1)} %add_convert_fusion.3.x_ref, bf16[768,3072]{1,0:T(8,128)(2,1)} %bitcast.291, f32[1,3072]{1,0:T(1,128)S(1)} %reshape.434.b_ref), custom_call_target="tpu_custom_call" | custom-call | flops 4831838208 | bytes 17301504 | tf_op jit(solution)/shard_map/feed_forward/pallas_call | solution.py:183
  185.2 4.1 %place_blocks.7 = bf16[32,96,768]{2,1,0:T(8,128)(2,1)S(1)} custom-call(s32[1]{0:T(128)} %bitcast.17.me_ref, bf16[8,96,768]{2,1,0:T(8,128)(2,1)S(1)} %constant_dynamic-update-slice_fusion.20.refs_0_, bf16[8,96,768]{2,1,0:T(8,128)(2,1)} %collective-permute-done.30.refs_1_, bf16[8,96,768]{2,1,0:T(8,128)(2,1)} %collective-permute-done.29.refs_2_, ...), custom_call_target="tpu_custom_call" | custom-call | bytes 9437184 | tf_op jit(solution)/shard_map/place_blocks/pallas_call | solution.py:237
  189.4 5.3 %fusion.46 = (f32[1024]{0:T(1024)S(1)}, f32[1024,768]{1,0:T(8,128)S(1)}) fusion(f32[768]{0:T(1024)S(1)} %reshape.435, bf16[1024,3072]{1,0:T(8,128)(2,1)S(1)} %copy-done.42, bf16[3072,768]{1,0:T(8,128)(2,1)S(1)} %bitcast.289, bf16[1024,768]{1,0:T(8,128)(2,1)S(1)} %add_convert_fusion.3.x_ref), kind=kOutput, calls=%fused_computation.232 | convolution fusion | flops 4834982912 | bytes 15735808 | tf_op jit(solution)/shard_map/dot_general | solution.py:575
  202.8 5.7 %convolution_convert_fusion.1 = bf16[3072,768]{1,0:T(8,128)(2,1)S(1)} fusion(bf16[1024,3072]{1,0:T(8,128)(2,1)S(1)} %copy-done.42, bf16[1024,768]{1,0:T(8,128)(2,1)S(1)} %get-tuple-element.255), kind=kOutput, calls=%fused_computation.6 | convolution fusion | flops 4834197504 | bytes 12582912 | tf_op jit(solution)/shard_map/dot_general | solution.py:23
  208.6 5.0 %collective-permute-done.36.refs_2_ = bf16[1,2,128,768]{3,2,1,0:T(8,128)(2,1)S(1)} collective-permute-done((bf16[1,2,128,768]{3,2,1,0:T(8,128)(2,1)S(1)}, bf16[1,2,128,768]{3,2,1,0:T(8,128)(2,1)S(1)}, u32[]{:S(2)}, u32[]{:S(2)}) %collective-permute-start.36) | collective-permute-done | bytes 393248 | tf_op jit(solution)/shard_map/ppermute | solution.py:204
  216.2 8.7 %convert_reduce_fusion = (bf16[3072]{0:T(1024)(128)(2,1)S(1)}, bf16[1024,3072]{1,0:T(8,128)(2,1)S(1)}) fusion(bf16[1024,3072]{1,0:T(8,128)(2,1)} %get-tuple-element.256, bf16[1024,768]{1,0:T(8,128)(2,1)} %copy-done.22, bf16[3072,768]{1,0:T(8,128)(2,1)} %bitcast.290), kind=kOutput, calls=%fused_computation | convolution fusion | flops 4847563776 | bytes 18880512 | tf_op jit(solution)/shard_map/dot_general | solution.py:29
  234.4 6.8 %convolution_convert_fusion = bf16[768,3072]{1,0:T(8,128)(2,1)} fusion(bf16[1024,768]{1,0:T(8,128)(2,1)S(1)} %add_convert_fusion.3.x_ref, bf16[1024,3072]{1,0:T(8,128)(2,1)S(1)} %get-tuple-element.262), kind=kOutput, calls=%fused_computation.5 | convolution fusion | flops 4834197504 | bytes 12582912 | tf_op jit(solution)/shard_map/dot_general | solution.py:23
  241.3 4.9 %collective-permute-done.39 = bf16[2,2,96,768]{3,2,0,1:T(8,128)(2,1)} collective-permute-done((bf16[2,2,96,768]{3,2,0,1:T(8,128)(2,1)}, bf16[2,2,96,768]{3,2,0,1:T(8,128)(2,1)}, u32[]{:S(2)}, u32[]{:S(2)}) %collective-permute-start.39) | collective-permute-done | bytes 589856 | tf_op jit(solution)/shard_map/ppermute | solution.py:204
  254.3 10.3 %multiply_reduce_fusion = (bf16[768]{0:T(1024)(128)(2,1)}, f32[1024]{0:T(1024)S(1)}, bf16[768]{0:T(1024)(128)(2,1)}, f32[1024,768]{1,0:T(8,128)S(1)}) fusion(f32[1024,768]{1,0:T(8,128)S(1)} %copy-done.12, f32[1024]{0:T(1024)S(1)} %fusion.33, f32[1024]{0:T(1024)S(1)} %broadcast_multiply_fusion.1, f32[768]{0:T(1024)S(1)} %reshape.432, ...), kind=kOutput, calls=%fused_computation.25 | convolution fusion | flops 4838913024 | bytes 20465664 | tf_op jit(solution)/shard_map/dot_general | solution.py:29
  288.2 24.8 %attention_backward.1 = (bf16[1024,2304]{1,0:T(8,128)(2,1)}, f32[12,1,384]{2,1,0:T(1,128)S(1)}) custom-call(bf16[1024,2304]{1,0:T(8,128)(2,1)} %add_convert_fusion.packed_ref, bf16[2,512,128]{2,1,0:T(8,128)(2,1)S(1)} %broadcast_in_dim.57.mask_ref, f32[12,2,512]{2,1,0:T(2,128)S(1)} %get-tuple-element.274.logsum_ref, ...), custom_call_target="tpu_custom_call" | custom-call | flops 11274289152 | bytes 11010048 | tf_op jit(solution)/shard_map/attention_backward/pallas_call | solution.py:138
  319.2 6.7 %convolution_convert_fusion.2 = bf16[768,2304]{1,0:T(8,128)(2,1)S(1)} fusion(bf16[1024,768]{1,0:T(8,128)(2,1)} %bitcast.332, bf16[1024,2304]{1,0:T(8,128)(2,1)} %get-tuple-element.283), kind=kOutput, calls=%fused_computation.7 | convolution fusion | flops 3625648128 | bytes 9830400 | tf_op jit(solution)/shard_map/dot_general | solution.py:23
  329.0 6.2 %add_convert_fusion.1 = bf16[1024,768]{1,0:T(8,128)(2,1)S(1)} fusion(f32[1024,768]{1,0:T(8,128)S(1)} %copy-done.16, bf16[1024,2304]{1,0:T(8,128)(2,1)} %get-tuple-element.283, bf16[768,2304]{1,0:T(8,128)(2,1)S(1)} %bitcast.294), kind=kOutput, calls=%fused_computation.24 | convolution fusion | flops 3625451520 | bytes 12976128 | tf_op jit(solution)/shard_map/dot_general | solution.py:29
  342.7 5.0 %collective-permute-done.65 = bf16[24,3968]{1,0:T(8,128)(2,1)S(1)} collective-permute-done((bf16[24,3968]{1,0:T(8,128)(2,1)S(1)}, bf16[24,3968]{1,0:T(8,128)(2,1)S(1)}, u32[]{:S(2)}, u32[]{:S(2)}) %collective-permute-start.65) | collective-permute-done | bytes 190496 | tf_op jit(solution)/shard_map/ppermute | solution.py:204
  347.7 6.7 %collective-permute-done.64 = bf16[24,3968]{1,0:T(8,128)(2,1)S(1)} collective-permute-done((bf16[24,3968]{1,0:T(8,128)(2,1)S(1)}, bf16[24,3968]{1,0:T(8,128)(2,1)S(1)}, u32[]{:S(2)}, u32[]{:S(2)}) %collective-permute-start.64) | collective-permute-done | bytes 190496 | tf_op jit(solution)/shard_map/ppermute | solution.py:204
  360.4 16.2 %collective-permute-done.55 = bf16[2,24,2432]{2,1,0:T(8,128)(2,1)S(1)} collective-permute-done((bf16[2,24,2432]{2,1,0:T(8,128)(2,1)S(1)}, bf16[2,24,2432]{2,1,0:T(8,128)(2,1)S(1)}, u32[]{:S(2)}, u32[]{:S(2)}) %collective-permute-start.55) | collective-permute-done | bytes 233504 | tf_op jit(solution)/shard_map/ppermute | solution.py:204
  (375 shorter events, 172.6 us)
Async XLA Ops:
  41.9 18.7 %collective-permute-start.9 = (bf16[4,24,2432]{2,1,0:T(8,128)(2,1)S(1)}, bf16[4,24,2432]{2,1,0:T(8,128)(2,1)S(1)}, u32[]{:S(2)}, u32[]{:S(2)}) collective-permute-start(bf16[4,24,2432]{2,1,0:T(8,128)(2,1)S(1)} %constant_dynamic-update-slice_fusion.4.refs_0_), channel_id=1, source_target_pairs={{0,1},{1,0},{2,3},{3,2},{4,5},{5,4},{6,7},{7,6},{8,9},{9,8},{10,11... | collective-permute-start | bytes 1400840 | tf_op jit(solution)/shard_map/ppermute | solution.py:204
  76.7 37.6 %collective-permute-start.21 = (bf16[1,96,768]{2,1,0:T(8,128)(2,1)}, bf16[1,96,768]{2,1,0:T(8,128)(2,1)}, u32[]{:S(2)}, u32[]{:S(2)}) collective-permute-start(bf16[1,96,768]{2,1,0:T(8,128)(2,1)} %bitcast.23), channel_id=1, source_target_pairs={{0,8},{1,9},{2,10},{3,11},{4,12},{5,13},{6,14},{7,15},{8,0},{9,1},... | collective-permute-start | bytes 442376 | tf_op jit(solution)/shard_map/ppermute | solution.py:204
  78.5 35.9 %collective-permute-start.22 = (bf16[1,96,768]{2,1,0:T(8,128)(2,1)}, bf16[1,96,768]{2,1,0:T(8,128)(2,1)}, u32[]{:S(2)}, u32[]{:S(2)}) collective-permute-start(bf16[1,96,768]{2,1,0:T(8,128)(2,1)} %bitcast.23), channel_id=1, source_target_pairs={{0,16},{1,17},{2,18},{3,19},{4,20},{5,21},{6,22},{7,23},{8,24},{9,... | collective-permute-start | bytes 442376 | tf_op jit(solution)/shard_map/ppermute | solution.py:204
  79.4 34.9 %collective-permute-start.23 = (bf16[1,96,768]{2,1,0:T(8,128)(2,1)}, bf16[1,96,768]{2,1,0:T(8,128)(2,1)}, u32[]{:S(2)}, u32[]{:S(2)}) collective-permute-start(bf16[1,96,768]{2,1,0:T(8,128)(2,1)} %bitcast.23), channel_id=1, source_target_pairs={{0,24},{1,25},{2,26},{3,27},{4,28},{5,29},{6,30},{7,31},{8,16},{9,... | collective-permute-start | bytes 442376 | tf_op jit(solution)/shard_map/ppermute | solution.py:204
  83.1 31.2 %collective-permute-start.19 = (bf16[4,24,3968]{2,1,0:T(8,128)(2,1)S(1)}, bf16[4,24,3968]{2,1,0:T(8,128)(2,1)S(1)}, u32[]{:S(2)}, u32[]{:S(2)}) collective-permute-start(bf16[4,24,3968]{2,1,0:T(8,128)(2,1)S(1)} %constant_dynamic-update-slice_fusion.12.refs_0_), channel_id=1, source_target_pairs={{0,2},{1,3},{2,0},{3,1},{4,6},{5,7},{6,4},{7,5},{8,10},{9,11},{10,... | collective-permute-start | bytes 2285576 | tf_op jit(solution)/shard_map/ppermute | solution.py:204
  86.8 27.6 %collective-permute-start.20 = (bf16[4,24,3968]{2,1,0:T(8,128)(2,1)S(1)}, bf16[4,24,3968]{2,1,0:T(8,128)(2,1)S(1)}, u32[]{:S(2)}, u32[]{:S(2)}) collective-permute-start(bf16[4,24,3968]{2,1,0:T(8,128)(2,1)S(1)} %constant_dynamic-update-slice_fusion.14.refs_4_), channel_id=1, source_target_pairs={{0,4},{1,5},{2,6},{3,7},{4,0},{5,1},{6,2},{7,3},{8,12},{9,13},{10,... | collective-permute-start | bytes 2285576 | tf_op jit(solution)/shard_map/ppermute | solution.py:204
  135.1 27.3 %collective-permute-start.29 = (bf16[8,96,768]{2,1,0:T(8,128)(2,1)S(1)}, bf16[8,96,768]{2,1,0:T(8,128)(2,1)}, u32[]{:S(2)}, u32[]{:S(2)}) collective-permute-start(bf16[8,96,768]{2,1,0:T(8,128)(2,1)S(1)} %constant_dynamic-update-slice_fusion.20.refs_0_), channel_id=1, source_target_pairs={{0,4},{1,5},{2,6},{3,7},{4,0},{5,1},{6,2},{7,3},{8,12},{9,13},{10,... | collective-permute-start | bytes 3538952 | tf_op jit(solution)/shard_map/ppermute | solution.py:204
  162.4 22.8 %collective-permute-start.30 = (bf16[8,96,768]{2,1,0:T(8,128)(2,1)S(1)}, bf16[8,96,768]{2,1,0:T(8,128)(2,1)}, u32[]{:S(2)}, u32[]{:S(2)}) collective-permute-start(bf16[8,96,768]{2,1,0:T(8,128)(2,1)S(1)} %constant_dynamic-update-slice_fusion.20.refs_0_), channel_id=1, source_target_pairs={{0,1},{1,0},{2,3},{3,2},{4,5},{5,4},{6,7},{7,6},{8,9},{9,8},{10,11... | collective-permute-start | bytes 3538952 | tf_op jit(solution)/shard_map/ppermute | solution.py:204
  162.4 22.8 %collective-permute-start.31 = (bf16[8,96,768]{2,1,0:T(8,128)(2,1)}, bf16[8,96,768]{2,1,0:T(8,128)(2,1)}, u32[]{:S(2)}, u32[]{:S(2)}) collective-permute-start(bf16[8,96,768]{2,1,0:T(8,128)(2,1)} %collective-permute-done.29.refs_2_), channel_id=1, source_target_pairs={{0,1},{1,0},{2,3},{3,2},{4,5},{5,4},{6,7},{7,6},{8,9},{9,8},{10,11... | collective-permute-start | bytes 3538952 | tf_op jit(solution)/shard_map/ppermute | solution.py:204
  166.2 19.0 %collective-permute-start.34 = (bf16[2,128,768]{2,1,0:T(8,128)(2,1)S(1)}, bf16[2,128,768]{2,1,0:T(8,128)(2,1)S(1)}, u32[]{:S(2)}, u32[]{:S(2)}) collective-permute-start(bf16[2,128,768]{2,1,0:T(8,128)(2,1)S(1)} %get-tuple-element.354), channel_id=1, source_target_pairs={{0,3},{1,2},{2,1},{3,0},{4,7},{5,6},{6,5},{7,4},{8,11},{9,10},{10,... | collective-permute-start | bytes 1179656 | tf_op jit(solution)/shard_map/ppermute | solution.py:204
  250.5 26.9 %collective-permute-start.41 = (bf16[2,96,768]{2,1,0:T(8,128)(2,1)}, bf16[2,96,768]{2,1,0:T(8,128)(2,1)}, u32[]{:S(2)}, u32[]{:S(2)}) collective-permute-start(bf16[2,96,768]{2,1,0:T(8,128)(2,1)} %dynamic-slice_bitcast_fusion.17), channel_id=1, source_target_pairs={{0,2},{1,3},{2,0},{3,1},{4,6},{5,7},{6,4},{7,5},{8,10},{9,11},{10,... | collective-permute-start | bytes 884744 | tf_op jit(solution)/shard_map/ppermute | solution.py:204
  252.8 26.4 %collective-permute-start.42 = (bf16[2,96,768]{2,1,0:T(8,128)(2,1)}, bf16[2,96,768]{2,1,0:T(8,128)(2,1)}, u32[]{:S(2)}, u32[]{:S(2)}) collective-permute-start(bf16[2,96,768]{2,1,0:T(8,128)(2,1)} %dynamic-slice_bitcast_fusion.16), channel_id=1, source_target_pairs={{0,4},{1,5},{2,6},{3,7},{4,0},{5,1},{6,2},{7,3},{8,12},{9,13},{10,... | collective-permute-start | bytes 884744 | tf_op jit(solution)/shard_map/ppermute | solution.py:204
  282.6 31.1 %collective-permute-start.45 = (bf16[2,2,24,3968]{3,2,0,1:T(8,128)(2,1)S(1)}, bf16[2,2,24,3968]{3,2,0,1:T(8,128)(2,1)S(1)}, u32[]{:S(2)}, u32[]{:S(2)}) collective-permute-start(bf16[2,2,24,3968]{3,2,0,1:T(8,128)(2,1)S(1)} %bitcast.343), channel_id=1, source_target_pairs={{0,4},{1,5},{2,6},{3,7},{4,0},{5,1},{6,2},{7,3},{8,12},{9,13},{10,... | collective-permute-start | bytes 2285576 | tf_op jit(solution)/shard_map/ppermute | solution.py:204
  283.3 30.7 %collective-permute-start.46 = (bf16[2,2,24,3968]{3,2,0,1:T(8,128)(2,1)S(1)}, bf16[2,2,24,3968]{3,2,0,1:T(8,128)(2,1)S(1)}, u32[]{:S(2)}, u32[]{:S(2)}) collective-permute-start(bf16[2,2,24,3968]{3,2,0,1:T(8,128)(2,1)S(1)} %bitcast.342), channel_id=1, source_target_pairs={{0,2},{1,3},{2,0},{3,1},{4,6},{5,7},{6,4},{7,5},{8,10},{9,11},{10,... | collective-permute-start | bytes 2285576 | tf_op jit(solution)/shard_map/ppermute | solution.py:204
  283.8 29.1 %collective-permute-start.49 = (bf16[96,768]{1,0:T(8,128)(2,1)}, bf16[96,768]{1,0:T(8,128)(2,1)S(1)}, u32[]{:S(2)}, u32[]{:S(2)}) collective-permute-start(bf16[96,768]{1,0:T(8,128)(2,1)} %get-tuple-element.272), channel_id=1, source_target_pairs={{0,24},{1,25},{2,26},{3,27},{4,28},{5,29},{6,30},{7,31},{8,16},{9,... | collective-permute-start | bytes 442376 | tf_op jit(solution)/shard_map/ppermute | solution.py:204
  286.1 26.8 %collective-permute-start.48 = (bf16[96,768]{1,0:T(8,128)(2,1)}, bf16[96,768]{1,0:T(8,128)(2,1)S(1)}, u32[]{:S(2)}, u32[]{:S(2)}) collective-permute-start(bf16[96,768]{1,0:T(8,128)(2,1)} %get-tuple-element.271), channel_id=1, source_target_pairs={{0,16},{1,17},{2,18},{3,19},{4,20},{5,21},{6,22},{7,23},{8,24},{9,... | collective-permute-start | bytes 442376 | tf_op jit(solution)/shard_map/ppermute | solution.py:204
  286.2 26.7 %collective-permute-start.47 = (bf16[96,768]{1,0:T(8,128)(2,1)}, bf16[96,768]{1,0:T(8,128)(2,1)S(1)}, u32[]{:S(2)}, u32[]{:S(2)}) collective-permute-start(bf16[96,768]{1,0:T(8,128)(2,1)} %get-tuple-element.270), channel_id=1, source_target_pairs={{0,8},{1,9},{2,10},{3,11},{4,12},{5,13},{6,14},{7,15},{8,0},{9,1},... | collective-permute-start | bytes 442376 | tf_op jit(solution)/shard_map/ppermute | solution.py:204
  315.0 20.2 %collective-permute-start.50 = (bf16[2,24,3968]{2,1,0:T(8,128)(2,1)}, bf16[2,24,3968]{2,1,0:T(8,128)(2,1)}, u32[]{:S(2)}, u32[]{:S(2)}) collective-permute-start(bf16[2,24,3968]{2,1,0:T(8,128)(2,1)} %dynamic-slice_bitcast_fusion.15), channel_id=1, source_target_pairs={{0,2},{1,3},{2,0},{3,1},{4,6},{5,7},{6,4},{7,5},{8,10},{9,11},{10,... | collective-permute-start | bytes 1142792 | tf_op jit(solution)/shard_map/ppermute | solution.py:204
  317.3 19.0 %collective-permute-start.51 = (bf16[2,24,3968]{2,1,0:T(8,128)(2,1)}, bf16[2,24,3968]{2,1,0:T(8,128)(2,1)S(1)}, u32[]{:S(2)}, u32[]{:S(2)}) collective-permute-start(bf16[2,24,3968]{2,1,0:T(8,128)(2,1)} %dynamic-slice_bitcast_fusion.14), channel_id=1, source_target_pairs={{0,4},{1,5},{2,6},{3,7},{4,0},{5,1},{6,2},{7,3},{8,12},{9,13},{10,... | collective-permute-start | bytes 1142792 | tf_op jit(solution)/shard_map/ppermute | solution.py:204
  337.1 20.9 %collective-permute-start.54 = (bf16[2,2,24,2432]{3,2,1,0:T(8,128)(2,1)S(1)}, bf16[2,2,24,2432]{3,2,1,0:T(8,128)(2,1)S(1)}, u32[]{:S(2)}, u32[]{:S(2)}) collective-permute-start(bf16[2,2,24,2432]{3,2,1,0:T(8,128)(2,1)S(1)} %dynamic-slice_bitcast_fusion.4), channel_id=1, source_target_pairs={{0,2},{1,3},{2,0},{3,1},{4,6},{5,7},{6,4},{7,5},{8,10},{9,11},{10,... | collective-permute-start | bytes 1400840 | tf_op jit(solution)/shard_map/ppermute | solution.py:204
  337.6 20.4 %collective-permute-start.53 = (bf16[2,2,24,2432]{3,2,1,0:T(8,128)(2,1)S(1)}, bf16[2,2,24,2432]{3,2,1,0:T(8,128)(2,1)S(1)}, u32[]{:S(2)}, u32[]{:S(2)}) collective-permute-start(bf16[2,2,24,2432]{3,2,1,0:T(8,128)(2,1)S(1)} %dynamic-slice_bitcast_fusion.5), channel_id=1, source_target_pairs={{0,4},{1,5},{2,6},{3,7},{4,0},{5,1},{6,2},{7,3},{8,12},{9,13},{10,... | collective-permute-start | bytes 1400840 | tf_op jit(solution)/shard_map/ppermute | solution.py:204
  347.7 31.1 %collective-permute-start.57 = (bf16[1,2,128,768]{3,2,1,0:T(8,128)(2,1)S(1)}, bf16[1,2,128,768]{3,2,1,0:T(8,128)(2,1)S(1)}, u32[]{:S(2)}, u32[]{:S(2)}) collective-permute-start(bf16[1,2,128,768]{3,2,1,0:T(8,128)(2,1)S(1)} %get-tuple-element.348), channel_id=1, source_target_pairs={{0,1},{1,0},{2,3},{3,2},{4,5},{5,4},{6,7},{7,6},{8,9},{9,8},{10,11... | collective-permute-start | bytes 1179656 | tf_op jit(solution)/shard_map/ppermute | solution.py:204
  354.4 24.4 %collective-permute-start.58 = (bf16[1,2,128,768]{3,2,1,0:T(8,128)(2,1)S(1)}, bf16[1,2,128,768]{3,2,1,0:T(8,128)(2,1)S(1)}, u32[]{:S(2)}, u32[]{:S(2)}) collective-permute-start(bf16[1,2,128,768]{3,2,1,0:T(8,128)(2,1)S(1)} %get-tuple-element.347), channel_id=1, source_target_pairs={{0,2},{1,3},{2,0},{3,1},{4,6},{5,7},{6,4},{7,5},{8,10},{9,11},{10,... | collective-permute-start | bytes 1179656 | tf_op jit(solution)/shard_map/ppermute | solution.py:204
  356.0 22.8 %collective-permute-start.59 = (bf16[1,2,128,768]{3,2,1,0:T(8,128)(2,1)S(1)}, bf16[1,2,128,768]{3,2,1,0:T(8,128)(2,1)S(1)}, u32[]{:S(2)}, u32[]{:S(2)}) collective-permute-start(bf16[1,2,128,768]{3,2,1,0:T(8,128)(2,1)S(1)} %get-tuple-element.346), channel_id=1, source_target_pairs={{0,3},{1,2},{2,1},{3,0},{4,7},{5,6},{6,5},{7,4},{8,11},{9,10},{10,... | collective-permute-start | bytes 1179656 | tf_op jit(solution)/shard_map/ppermute | solution.py:204
  (87 other events, 960.2 us)

commit v8 on v7

--- a/solution.py
+++ b/solution.py
@@ -406,10 +406,11 @@
             self.held = [pick(total, 0, z ^ k) for k in range(4)]
 
     def along_z(self):
-        total = self.held[0].astype(F32)
-        for k in (1, 2, 3):
-            total = total + swap(self.held[k], 8 * k, self.devices).astype(F32)
-        self.held = [total]
+        sent = [swap(self.held[k], 8 * k, self.devices) for k in (1, 2, 3)]
+        self.held = [self.held[0]] + sent
+
+    def result(self):
+        return sum(block.astype(F32) for block in self.held)
 
 
 class ToSequences:
@@ -496,32 +497,25 @@
     in_gather = Gather(
         jnp.concatenate([in_weight, output_weight, late], 1), me, devices, "split"
     )
-    down_gather = Gather(down_weight, me, devices, "yx")
+    down_gather = Gather(down_weight, me, devices, "split")
     near, far = range(1, (members + 1) // 2), range((members + 1) // 2, members)
     flat = ToSequences(inputs, seat, members, devices)
-    for k in near:
-        flat.send(k)
-    for k in far[:1]:
+    for k in range(1, members):
         flat.send(k)
     qkv_gather.along_z()
     fence([qkv_gather])
     qkv_gather.first()
     fence([qkv_gather, flat])
-    for k in far[1:]:
-        flat.send(k)
     qkv_gather.second()
     in_gather.put([after(a, qkv_gather.held[0]) for a in in_gather.arrays()])
     in_gather.along_z()
     fence([qkv_gather])
     qkv_gather.core()
-    fence([qkv_gather, in_gather, flat])
-    in_gather.first()
+    fence([qkv_gather])
     flat = flat.finish()
     wide_qkv, early = qkv_gather.finish([(0, 3 * width), (3 * width, early.shape[1])])
     (wide_qkv, early, flat) = fence([in_gather], wide_qkv, early, flat)
-    in_gather.second()
-    down_gather.put([after(a, wide_qkv) for a in down_gather.arrays()])
-    down_gather.along_z()
+    in_gather.first()
     wide_qkv = wide_qkv.reshape(width, 3 * width)
     full_query_bias, full_value_bias = [
         v.reshape(-1).astype(F32) for v in unpack_rows(early, [share, share])
@@ -529,6 +523,10 @@
     bias_vector = jnp.concatenate([full_query_bias, jnp.zeros((width,), F32), full_value_bias])
     packed = jnp.dot(flat, wide_qkv, preferred_element_type=F32) + pair_major(bias_vector)
     packed = packed.astype(BF)
+    (packed,) = fence([in_gather], packed)
+    in_gather.second()
+    down_gather.put([after(a, packed) for a in down_gather.arrays()])
+    down_gather.along_z()
     mine = lax.dynamic_slice(lengths, (seat * kept,), (kept,))
     slots = jnp.arange(length, dtype=jnp.int32)
     positions = ((slots // local_len) ^ seat) * local_len + slots % local_len
@@ -646,27 +644,24 @@
     qkv_scatter = Scatter(core_sum(grad_qkv, me, devices), me, devices, "split")
     grad_inputs = (times_transposed(grad_packed, wide_qkv) + grad_residual).astype(BF)
     (grad_inputs,) = fence([in_scatter, qkv_scatter], grad_inputs)
+    grad_inputs = ToPositions(
+        grad_inputs.reshape(kept, members, local_len, width), members, devices
+    )
     qkv_scatter.first()
     in_scatter.along_z()
-    grad_inputs = ToPositions(
-        grad_inputs.reshape(kept, members, local_len, width), members, devices
-    )
-    for k in near:
+    fence([qkv_scatter, grad_inputs])
+    qkv_scatter.second()
+    fence([qkv_scatter, grad_inputs, in_scatter])
+    for k in range(1, members):
         grad_inputs.send(k)
-    for k in far[:1]:
-        grad_inputs.send(k)
-    fence([qkv_scatter])
-    qkv_scatter.second()
-    for k in far[1:]:
-        grad_inputs.send(k)
-    outputs.put([after(a, qkv_scatter.held[0]) for a in outputs.arrays()])
+    qkv_scatter.along_z()
+    outputs.put([after(a, *qkv_scatter.held[:1]) for a in outputs.arrays()])
     outputs = outputs.finish(seat)
-    (outputs,) = fence([qkv_scatter, grad_inputs], outputs)
-    qkv_scatter.along_z()
+    in_part = in_scatter.result()
+    down_part = down_scatter.result()
+    (in_part, outputs) = fence([qkv_scatter, grad_inputs], in_part, outputs)
+    qkv_part = qkv_scatter.result()
     grad_inputs = grad_inputs.finish(seat)
-    (qkv_part,), (in_part,), (down_part,) = (
-        s.held for s in (qkv_scatter, in_scatter, down_scatter)
-    )
     early_out = unpack_rows(qkv_part[:, 3 * width :], [share, share])
     late_out = unpack_rows(
         in_part[:, inner_width + width :], [v.shape[0] for v in late_vectors]

time: 395 us -> 385 us (0.975)
  waiting for transfers between devices: 115 us -> 83.1 us
  other arithmetic: 30 us -> 40 us
  starting transfers between devices: 61.4 us -> 70.4 us
    ppermute x66 -> x70, waiting for transfers between devices: 115 us -> 83.1 us  [swap(): lax.ppermute(block, BOTH, [(i, i ^ distance) for i in range(devices)])]
    ppermute x66 -> x70, starting transfers between devices: 61.4 us -> 70.4 us  [swap(): lax.ppermute(block, BOTH, [(i, i ^ distance) for i in range(devices)])]
    reduce_sum x3, other arithmetic: 3.52 us -> 7.88 us  [layer_norm(): return centered * lax.rsqrt(spread + 1e-12) * gain + shift]
    convert_element_type x9, local copies, waits for them, and re-layouts: 0.73 us -> 4.78 us  [on_device(): v.reshape(-1).astype(F32)]
    unnamed x110 -> x116, local copies, waits for them, and re-layouts: 14 us -> 13.1 us
  transfers between devices with their start and end apart: 66 -> 70, of which waited for: 22 -> 21; matrix products, arithmetic and copies ran while one was open for 27% -> 28% of each run, Pallas kernels for 17% -> 17%
where the time goes in v8:
time: 385 us; the launch traced here: 382 us
  waiting for transfers between devices  83.1 us (22%)
  Pallas kernels  72 us (19%)
  starting transfers between devices  70.4 us (18%)
  matrix products  65.2 us (17%)
  local copies, waits for them, and re-layouts  48.6 us (13%)
  other arithmetic  40 us (10%)
    ppermute x70, waiting for transfers between devices, swap(): lax.ppermute(block, BOTH, [(i, i ^ distance) for i in range(devices)])  83.1 us
    ppermute x70, starting transfers between devices, swap(): lax.ppermute(block, BOTH, [(i, i ^ distance) for i in range(devices)])  70.4 us
    dot_general x4, matrix products, times_transposed(): lax.dot_general(left, right, (((1,), (1,)), ((), ())), preferred_element_...  27.4 us
    pallas_call x1, Pallas kernels, attention_backward(): pl.pallas_call(backward_kernel, grid=(seqs, pairs), in_specs=[block(384),...  24.9 us
    dot_general x4, matrix products, over_rows(): lax.dot_general(left, right, (((0,), (0,)), ((), ())), preferred_element_...  20.7 us
    pallas_call x1, Pallas kernels, attention_forward(): pl.pallas_call(forward_kernel, grid=(seqs, pairs), in_specs=[block(384),...  17.1 us
    pallas_call x1, Pallas kernels, feed_forward(): pl.pallas_call(functools.partial(feed_forward_kernel, 512), grid=(rows //...  15 us
    pallas_call x5, Pallas kernels, place(): pl.pallas_call(functools.partial(place_kernel, ids, counts, spans), in_sp...  15 us
  transfers between devices with their start and end apart: 70, of which 21 were waited for; matrix products, arithmetic and copies ran while one was open for 28% of the time, Pallas kernels for 17%

profile of v8, /device:TPU:0, one launch (start us, length us, event | category | flops | bytes accessed | tf_op | source)
XLA Modules:
  0.0 381.6 jit_solution(4111456707327627379)
XLA Ops:
  12.5 5.2 %collective-permute-done.1 = bf16[1,24,2432]{2,1,0:T(8,128)(2,1)S(1)} collective-permute-done((bf16[1,24,2432]{2,1,0:T(8,128)(2,1)S(1)}, bf16[1,24,2432]{2,1,0:T(8,128)(2,1)S(1)}, u32[]{:S(2)}, u32[]{:S(2)}) %collective-permute-start.1) | collective-permute-done | bytes 116768 | tf_op jit(solution)/shard_map/ppermute | solution.py:204
  23.8 11.7 %collective-permute-done.4 = bf16[2,24,2432]{2,1,0:T(8,128)(2,1)S(1)} collective-permute-done((bf16[2,24,2432]{2,1,0:T(8,128)(2,1)S(1)}, bf16[2,24,2432]{2,1,0:T(8,128)(2,1)S(1)}, u32[]{:S(2)}, u32[]{:S(2)}) %collective-permute-start.4) | collective-permute-done | bytes 233504 | tf_op jit(solution)/shard_map/ppermute | solution.py:204
  39.1 8.9 %collective-permute-done.11.refs_2_ = bf16[4,24,2432]{2,1,0:T(8,128)(2,1)S(1)} collective-permute-done((bf16[4,24,2432]{2,1,0:T(8,128)(2,1)S(1)}, bf16[4,24,2432]{2,1,0:T(8,128)(2,1)S(1)}, u32[]{:S(2)}, u32[]{:S(2)}) %collective-permute-start.11) | collective-permute-done | bytes 466976 | tf_op jit(solution)/shard_map/ppermute | solution.py:204
  64.9 5.8 %collective-permute-done.9 = bf16[1,24,3968]{2,1,0:T(8,128)(2,1)} collective-permute-done((bf16[1,24,3968]{2,1,0:T(8,128)(2,1)}, bf16[1,24,3968]{2,1,0:T(8,128)(2,1)}, u32[]{:S(2)}, u32[]{:S(2)}) %collective-permute-start.9) | collective-permute-done | bytes 190496 | tf_op jit(solution)/shard_map/ppermute | solution.py:204
  77.0 8.5 %add_convert_fusion.packed_ref = bf16[1024,2304]{1,0:T(8,128)(2,1)} fusion(bf16[1024,768]{1,0:T(8,128)(2,1)} %bitcast.322, bf16[768,2304]{1,0:T(8,128)(2,1)} %bitcast.293, f32[2304]{0:T(1024)S(1)} %add.450), kind=kOutput, calls=%fused_computation.2 | convolution fusion | flops 3628597248 | bytes 9839616 | tf_op jit(solution)/shard_map/dot_general | solution.py:524
  94.2 17.1 %attention_forward.1 = (bf16[1024,768]{1,0:T(8,128)(2,1)S(1)}, f32[12,2,512]{2,1,0:T(2,128)S(1)}) custom-call(bf16[1024,2304]{1,0:T(8,128)(2,1)} %add_convert_fusion.packed_ref, bf16[2,512,128]{2,1,0:T(8,128)(2,1)S(1)} %broadcast_in_dim.57.mask_ref), custom_call_target="tpu_custom_call" | custom-call | flops 6442450944 | bytes 6291456 | tf_op jit(solution)/shard_map/attention_forward/pallas_call | solution.py:117
  136.5 4.0 %collective-permute-done.30.refs_2_ = bf16[4,96,768]{2,1,0:T(8,128)(2,1)S(1)} collective-permute-done((bf16[4,96,768]{2,1,0:T(8,128)(2,1)S(1)}, bf16[4,96,768]{2,1,0:T(8,128)(2,1)S(1)}, u32[]{:S(2)}, u32[]{:S(2)}) %collective-permute-start.30) | collective-permute-done | bytes 589856 | tf_op jit(solution)/shard_map/ppermute | solution.py:204
  150.3 5.2 %collective-permute-done.37 = bf16[2,128,768]{2,1,0:T(8,128)(2,1)} collective-permute-done((bf16[2,128,768]{2,1,0:T(8,128)(2,1)}, bf16[2,128,768]{2,1,0:T(8,128)(2,1)}, u32[]{:S(2)}, u32[]{:S(2)}) %collective-permute-start.37) | collective-permute-done | bytes 393248 | tf_op jit(solution)/shard_map/ppermute | solution.py:204
  156.0 15.0 %feed_forward.1 = (bf16[1024,3072]{1,0:T(8,128)(2,1)}, bf16[1024,3072]{1,0:T(8,128)(2,1)}) custom-call(bf16[1024,768]{1,0:T(8,128)(2,1)S(1)} %add_convert_fusion.3.x_ref, bf16[768,3072]{1,0:T(8,128)(2,1)} %bitcast.291, f32[1,3072]{1,0:T(1,128)S(1)} %reshape.434.b_ref), custom_call_target="tpu_custom_call" | custom-call | flops 4831838208 | bytes 17301504 | tf_op jit(solution)/shard_map/feed_forward/pallas_call | solution.py:183
  171.1 4.0 %place_blocks.7 = bf16[32,96,768]{2,1,0:T(8,128)(2,1)S(1)} custom-call(s32[1]{0:T(128)} %bitcast.17.me_ref, bf16[4,96,768]{2,1,0:T(8,128)(2,1)S(1)} %constant_dynamic-update-slice_fusion.20.refs_0_, bf16[4,96,768]{2,1,0:T(8,128)(2,1)} %collective-permute-done.32.refs_1_, bf16[4,96,768]{2,1,0:T(8,128)(2,1)S(1)} %collective-permute-done.30.refs_2_, ...), custom_call_target="tpu_custom_call" | custom-call | bytes 9437184 | tf_op jit(solution)/shard_map/place_blocks/pallas_call | solution.py:237
  175.2 5.3 %fusion.46 = (f32[1024]{0:T(1024)S(1)}, f32[1024,768]{1,0:T(8,128)S(1)}) fusion(f32[768]{0:T(1024)S(1)} %copy-done.33, bf16[1024,3072]{1,0:T(8,128)(2,1)S(1)} %copy-done.45, bf16[3072,768]{1,0:T(8,128)(2,1)S(1)} %bitcast.289, bf16[1024,768]{1,0:T(8,128)(2,1)S(1)} %add_convert_fusion.3.x_ref), kind=kOutput, calls=%fused_computation.234 | convolution fusion | flops 4834982912 | bytes 15735808 | tf_op jit(solution)/shard_map/dot_general | solution.py:573
  188.4 4.4 %convert_reduce_fusion.2 = (bf16[768]{0:T(1024)(128)(2,1)}, bf16[1024,768]{1,0:T(8,128)(2,1)S(1)}, f32[1024,768]{1,0:T(8,128)}, bf16[1024,768]{1,0:T(8,128)(2,1)S(1)}) fusion(f32[1024]{0:T(1024)S(1)} %negate_multiply_fusion.1, f32[1024]{0:T(1024)S(1)} %get-tuple-element.432, f32[1024,768]{1,0:T(8,128)S(1)} %get-tuple-element.437, ...), kind=kLoop, calls=%fused_computation.27 | loop fusion | flops 17300736 | bytes 11034112 | tf_op jit(solution)/shard_map/reduce_sum | solution.py:580
  194.7 5.7 %convolution_convert_fusion.1 = bf16[3072,768]{1,0:T(8,128)(2,1)S(1)} fusion(bf16[1024,3072]{1,0:T(8,128)(2,1)S(1)} %copy-done.45, bf16[1024,768]{1,0:T(8,128)(2,1)S(1)} %get-tuple-element.285), kind=kOutput, calls=%fused_computation.6 | convolution fusion | flops 4834197504 | bytes 12582912 | tf_op jit(solution)/shard_map/dot_general | solution.py:23
  200.4 4.5 %collective-permute-done.40.refs_2_ = bf16[1,2,128,768]{3,2,1,0:T(8,128)(2,1)S(1)} collective-permute-done((bf16[1,2,128,768]{3,2,1,0:T(8,128)(2,1)S(1)}, bf16[1,2,128,768]{3,2,1,0:T(8,128)(2,1)S(1)}, u32[]{:S(2)}, u32[]{:S(2)}) %collective-permute-start.40) | collective-permute-done | bytes 393248 | tf_op jit(solution)/shard_map/ppermute | solution.py:204
  211.6 9.4 %convert_reduce_fusion = (bf16[3072]{0:T(1024)(128)(2,1)}, bf16[1024,3072]{1,0:T(8,128)(2,1)S(1)}) fusion(bf16[1024,3072]{1,0:T(8,128)(2,1)} %get-tuple-element.286, bf16[1024,768]{1,0:T(8,128)(2,1)} %copy-done.23, bf16[3072,768]{1,0:T(8,128)(2,1)} %bitcast.290), kind=kOutput, calls=%fused_computation | convolution fusion | flops 4847563776 | bytes 18880512 | tf_op jit(solution)/shard_map/dot_general | solution.py:29
  221.0 4.1 %fusion.2 = bf16[16,96,768]{2,1,0:T(8,128)(2,1)S(1)} fusion(bf16[16,96,768]{2,1,0:T(8,128)(2,1)} %collective-permute-done.42, bf16[16,2,96,768]{3,2,1,0:T(8,128)(2,1)S(1)} %bitcast.316, s32[]{:T(128)S(6)} %select_n.257), kind=kLoop, calls=%fused_computation.13 | loop fusion | flops 4718592 | bytes 7077892 | tf_op jit(solution)/shard_map/convert_element_type | solution.py:351
  231.2 6.8 %convolution_convert_fusion = bf16[768,3072]{1,0:T(8,128)(2,1)} fusion(bf16[1024,768]{1,0:T(8,128)(2,1)S(1)} %add_convert_fusion.3.x_ref, bf16[1024,3072]{1,0:T(8,128)(2,1)S(1)} %get-tuple-element.292), kind=kOutput, calls=%fused_computation.5 | convolution fusion | flops 4834197504 | bytes 12582912 | tf_op jit(solution)/shard_map/dot_general | solution.py:23
  238.0 4.3 %collective-permute-done.43 = bf16[2,2,96,768]{3,2,0,1:T(8,128)(2,1)} collective-permute-done((bf16[2,2,96,768]{3,2,0,1:T(8,128)(2,1)}, bf16[2,2,96,768]{3,2,0,1:T(8,128)(2,1)}, u32[]{:S(2)}, u32[]{:S(2)}) %collective-permute-start.43) | collective-permute-done | bytes 589856 | tf_op jit(solution)/shard_map/ppermute | solution.py:204
  250.2 10.3 %multiply_reduce_fusion = (bf16[768]{0:T(1024)(128)(2,1)}, f32[1024]{0:T(1024)S(1)}, bf16[768]{0:T(1024)(128)(2,1)}, f32[1024,768]{1,0:T(8,128)S(1)}) fusion(f32[1024,768]{1,0:T(8,128)S(1)} %copy-done.13, f32[1024]{0:T(1024)S(1)} %fusion.33, f32[1024]{0:T(1024)S(1)} %broadcast_multiply_fusion.1, f32[768]{0:T(1024)S(1)} %reshape.432, ...), kind=kOutput, calls=%fused_computation.25 | convolution fusion | flops 4838913024 | bytes 20465664 | tf_op jit(solution)/shard_map/dot_general | solution.py:29
  282.6 24.9 %attention_backward.1 = (bf16[1024,2304]{1,0:T(8,128)(2,1)}, f32[12,1,384]{2,1,0:T(1,128)S(1)}) custom-call(bf16[1024,2304]{1,0:T(8,128)(2,1)} %add_convert_fusion.packed_ref, bf16[2,512,128]{2,1,0:T(8,128)(2,1)S(1)} %copy-done.2, f32[12,2,512]{2,1,0:T(2,128)S(1)} %copy-done.11, bf16[1024,768]{1,0:T(8,128)(2,1)S(1)} %convolution_convert_fusion.3.grad_ref), custom_call_target="tpu_custom_call" | custom-call | flops 11274289152 | bytes 11010048 | tf_op jit(solution)/shard_map/attention_backward/pallas_call | solution.py:138
  311.7 6.7 %convolution_convert_fusion.2 = bf16[768,2304]{1,0:T(8,128)(2,1)S(1)} fusion(bf16[1024,768]{1,0:T(8,128)(2,1)} %bitcast.324, bf16[1024,2304]{1,0:T(8,128)(2,1)} %get-tuple-element.313), kind=kOutput, calls=%fused_computation.7 | convolution fusion | flops 3625648128 | bytes 9830400 | tf_op jit(solution)/shard_map/dot_general | solution.py:23
  321.4 6.2 %add_convert_fusion.1 = bf16[1024,768]{1,0:T(8,128)(2,1)S(1)} fusion(f32[1024,768]{1,0:T(8,128)S(1)} %copy-done.18, bf16[1024,2304]{1,0:T(8,128)(2,1)} %get-tuple-element.313, bf16[768,2304]{1,0:T(8,128)(2,1)S(1)} %bitcast.294), kind=kOutput, calls=%fused_computation.24 | convolution fusion | flops 3625451520 | bytes 12976128 | tf_op jit(solution)/shard_map/dot_general | solution.py:29
  362.4 5.4 %collective-permute-done.68.refs_2_ = bf16[1,2,128,768]{3,2,1,0:T(8,128)(2,1)S(1)} collective-permute-done((bf16[1,2,128,768]{3,2,1,0:T(8,128)(2,1)S(1)}, bf16[1,2,128,768]{3,2,1,0:T(8,128)(2,1)S(1)}, u32[]{:S(2)}, u32[]{:S(2)}) %collective-permute-start.68) | collective-permute-done | bytes 393248 | tf_op jit(solution)/shard_map/ppermute | solution.py:204
  367.8 7.7 %collective-permute-done.69.refs_3_ = bf16[1,2,128,768]{3,2,1,0:T(8,128)(2,1)S(1)} collective-permute-done((bf16[1,2,128,768]{3,2,1,0:T(8,128)(2,1)S(1)}, bf16[1,2,128,768]{3,2,1,0:T(8,128)(2,1)S(1)}, u32[]{:S(2)}, u32[]{:S(2)}) %collective-permute-start.69) | collective-permute-done | bytes 393248 | tf_op jit(solution)/shard_map/ppermute | solution.py:204
  (391 shorter events, 188.1 us)
Async XLA Ops:
  10.6 25.0 %collective-permute-start.5 = (bf16[2,128,768]{2,1,0:T(8,128)(2,1)S(1)}, bf16[2,128,768]{2,1,0:T(8,128)(2,1)S(1)}, u32[]{:S(2)}, u32[]{:S(2)}) collective-permute-start(bf16[2,128,768]{2,1,0:T(8,128)(2,1)S(1)} %get-tuple-element.410), channel_id=1, source_target_pairs={{0,1},{1,0},{2,3},{3,2},{4,5},{5,4},{6,7},{7,6},{8,9},{9,8},{10,11... | collective-permute-start | bytes 1179656 | tf_op jit(solution)/shard_map/ppermute | solution.py:204
  10.6 25.0 %collective-permute-start.6 = (bf16[2,128,768]{2,1,0:T(8,128)(2,1)S(1)}, bf16[2,128,768]{2,1,0:T(8,128)(2,1)S(1)}, u32[]{:S(2)}, u32[]{:S(2)}) collective-permute-start(bf16[2,128,768]{2,1,0:T(8,128)(2,1)S(1)} %get-tuple-element.409), channel_id=1, source_target_pairs={{0,2},{1,3},{2,0},{3,1},{4,6},{5,7},{6,4},{7,5},{8,10},{9,11},{10,... | collective-permute-start | bytes 1179656 | tf_op jit(solution)/shard_map/ppermute | solution.py:204
  12.3 23.2 %collective-permute-start.7 = (bf16[2,128,768]{2,1,0:T(8,128)(2,1)S(1)}, bf16[2,128,768]{2,1,0:T(8,128)(2,1)S(1)}, u32[]{:S(2)}, u32[]{:S(2)}) collective-permute-start(bf16[2,128,768]{2,1,0:T(8,128)(2,1)S(1)} %get-tuple-element.408), channel_id=1, source_target_pairs={{0,3},{1,2},{2,1},{3,0},{4,7},{5,6},{6,5},{7,4},{8,11},{9,10},{10,... | collective-permute-start | bytes 1179656 | tf_op jit(solution)/shard_map/ppermute | solution.py:204
  53.0 17.6 %collective-permute-start.9 = (bf16[1,24,3968]{2,1,0:T(8,128)(2,1)}, bf16[1,24,3968]{2,1,0:T(8,128)(2,1)}, u32[]{:S(2)}, u32[]{:S(2)}) collective-permute-start(bf16[1,24,3968]{2,1,0:T(8,128)(2,1)} %fusion.24), channel_id=1, source_target_pairs={{0,16},{1,17},{2,18},{3,19},{4,20},{5,21},{6,22},{7,23},{8,24},{9,... | collective-permute-start | bytes 571400 | tf_op jit(solution)/shard_map/ppermute | solution.py:204
  85.5 27.0 %collective-permute-start.19 = (bf16[4,24,3968]{2,1,0:T(8,128)(2,1)S(1)}, bf16[4,24,3968]{2,1,0:T(8,128)(2,1)S(1)}, u32[]{:S(2)}, u32[]{:S(2)}) collective-permute-start(bf16[4,24,3968]{2,1,0:T(8,128)(2,1)S(1)} %constant_dynamic-update-slice_fusion.12.refs_0_), channel_id=1, source_target_pairs={{0,2},{1,3},{2,0},{3,1},{4,6},{5,7},{6,4},{7,5},{8,10},{9,11},{10,... | collective-permute-start | bytes 2285576 | tf_op jit(solution)/shard_map/ppermute | solution.py:204
  87.1 25.4 %collective-permute-start.20 = (bf16[4,24,3968]{2,1,0:T(8,128)(2,1)S(1)}, bf16[4,24,3968]{2,1,0:T(8,128)(2,1)S(1)}, u32[]{:S(2)}, u32[]{:S(2)}) collective-permute-start(bf16[4,24,3968]{2,1,0:T(8,128)(2,1)S(1)} %constant_dynamic-update-slice_fusion.14.refs_4_), channel_id=1, source_target_pairs={{0,4},{1,5},{2,6},{3,7},{4,0},{5,1},{6,2},{7,3},{8,12},{9,13},{10,... | collective-permute-start | bytes 2285576 | tf_op jit(solution)/shard_map/ppermute | solution.py:204
  87.8 24.7 %collective-permute-start.21 = (bf16[1,96,768]{2,1,0:T(8,128)(2,1)S(1)}, bf16[1,96,768]{2,1,0:T(8,128)(2,1)S(1)}, u32[]{:S(2)}, u32[]{:S(2)}) collective-permute-start(bf16[1,96,768]{2,1,0:T(8,128)(2,1)S(1)} %bitcast.340), channel_id=1, source_target_pairs={{0,8},{1,9},{2,10},{3,11},{4,12},{5,13},{6,14},{7,15},{8,0},{9,1},... | collective-permute-start | bytes 442376 | tf_op jit(solution)/shard_map/ppermute | solution.py:204
  91.6 20.9 %collective-permute-start.22 = (bf16[1,96,768]{2,1,0:T(8,128)(2,1)S(1)}, bf16[1,96,768]{2,1,0:T(8,128)(2,1)S(1)}, u32[]{:S(2)}, u32[]{:S(2)}) collective-permute-start(bf16[1,96,768]{2,1,0:T(8,128)(2,1)S(1)} %bitcast.341), channel_id=1, source_target_pairs={{0,16},{1,17},{2,18},{3,19},{4,20},{5,21},{6,22},{7,23},{8,24},{9,... | collective-permute-start | bytes 442376 | tf_op jit(solution)/shard_map/ppermute | solution.py:204
  92.5 20.0 %collective-permute-start.23 = (bf16[1,96,768]{2,1,0:T(8,128)(2,1)S(1)}, bf16[1,96,768]{2,1,0:T(8,128)(2,1)S(1)}, u32[]{:S(2)}, u32[]{:S(2)}) collective-permute-start(bf16[1,96,768]{2,1,0:T(8,128)(2,1)S(1)} %bitcast.342), channel_id=1, source_target_pairs={{0,24},{1,25},{2,26},{3,27},{4,28},{5,29},{6,30},{7,31},{8,16},{9,... | collective-permute-start | bytes 442376 | tf_op jit(solution)/shard_map/ppermute | solution.py:204
  144.8 26.2 %collective-permute-start.32 = (bf16[4,96,768]{2,1,0:T(8,128)(2,1)S(1)}, bf16[4,96,768]{2,1,0:T(8,128)(2,1)}, u32[]{:S(2)}, u32[]{:S(2)}) collective-permute-start(bf16[4,96,768]{2,1,0:T(8,128)(2,1)S(1)} %constant_dynamic-update-slice_fusion.20.refs_0_), channel_id=1, source_target_pairs={{0,1},{1,0},{2,3},{3,2},{4,5},{5,4},{6,7},{7,6},{8,9},{9,8},{10,11... | collective-permute-start | bytes 1769480 | tf_op jit(solution)/shard_map/ppermute | solution.py:204
  145.0 26.0 %collective-permute-start.33 = (bf16[4,96,768]{2,1,0:T(8,128)(2,1)S(1)}, bf16[4,96,768]{2,1,0:T(8,128)(2,1)}, u32[]{:S(2)}, u32[]{:S(2)}) collective-permute-start(bf16[4,96,768]{2,1,0:T(8,128)(2,1)S(1)} %collective-permute-done.30.refs_2_), channel_id=1, source_target_pairs={{0,1},{1,0},{2,3},{3,2},{4,5},{5,4},{6,7},{7,6},{8,9},{9,8},{10,11... | collective-permute-start | bytes 1769480 | tf_op jit(solution)/shard_map/ppermute | solution.py:204
  145.3 25.7 %collective-permute-start.34 = (bf16[4,96,768]{2,1,0:T(8,128)(2,1)S(1)}, bf16[4,96,768]{2,1,0:T(8,128)(2,1)}, u32[]{:S(2)}, u32[]{:S(2)}) collective-permute-start(bf16[4,96,768]{2,1,0:T(8,128)(2,1)S(1)} %constant_dynamic-update-slice_fusion.22.refs_4_), channel_id=1, source_target_pairs={{0,1},{1,0},{2,3},{3,2},{4,5},{5,4},{6,7},{7,6},{8,9},{9,8},{10,11... | collective-permute-start | bytes 1769480 | tf_op jit(solution)/shard_map/ppermute | solution.py:204
  145.6 25.5 %collective-permute-start.35 = (bf16[4,96,768]{2,1,0:T(8,128)(2,1)}, bf16[4,96,768]{2,1,0:T(8,128)(2,1)}, u32[]{:S(2)}, u32[]{:S(2)}) collective-permute-start(bf16[4,96,768]{2,1,0:T(8,128)(2,1)} %collective-permute-done.31.refs_6_), channel_id=1, source_target_pairs={{0,1},{1,0},{2,3},{3,2},{4,5},{5,4},{6,7},{7,6},{8,9},{9,8},{10,11... | collective-permute-start | bytes 1769480 | tf_op jit(solution)/shard_map/ppermute | solution.py:204
  247.6 23.9 %collective-permute-start.45 = (bf16[2,96,768]{2,1,0:T(8,128)(2,1)}, bf16[2,96,768]{2,1,0:T(8,128)(2,1)S(1)}, u32[]{:S(2)}, u32[]{:S(2)}) collective-permute-start(bf16[2,96,768]{2,1,0:T(8,128)(2,1)} %dynamic-slice_bitcast_fusion.17), channel_id=1, source_target_pairs={{0,2},{1,3},{2,0},{3,1},{4,6},{5,7},{6,4},{7,5},{8,10},{9,11},{10,... | collective-permute-start | bytes 884744 | tf_op jit(solution)/shard_map/ppermute | solution.py:204
  249.6 22.7 %collective-permute-start.46 = (bf16[2,96,768]{2,1,0:T(8,128)(2,1)}, bf16[2,96,768]{2,1,0:T(8,128)(2,1)}, u32[]{:S(2)}, u32[]{:S(2)}) collective-permute-start(bf16[2,96,768]{2,1,0:T(8,128)(2,1)} %dynamic-slice_bitcast_fusion.16), channel_id=1, source_target_pairs={{0,4},{1,5},{2,6},{3,7},{4,0},{5,1},{6,2},{7,3},{8,12},{9,13},{10,... | collective-permute-start | bytes 884744 | tf_op jit(solution)/shard_map/ppermute | solution.py:204
  275.8 31.7 %collective-permute-start.49 = (bf16[2,2,24,3968]{3,2,0,1:T(8,128)(2,1)S(1)}, bf16[2,2,24,3968]{3,2,0,1:T(8,128)(2,1)S(1)}, u32[]{:S(2)}, u32[]{:S(2)}) collective-permute-start(bf16[2,2,24,3968]{3,2,0,1:T(8,128)(2,1)S(1)} %bitcast.335), channel_id=1, source_target_pairs={{0,4},{1,5},{2,6},{3,7},{4,0},{5,1},{6,2},{7,3},{8,12},{9,13},{10,... | collective-permute-start | bytes 2285576 | tf_op jit(solution)/shard_map/ppermute | solution.py:204
  277.4 30.3 %collective-permute-start.50 = (bf16[2,2,24,3968]{3,2,0,1:T(8,128)(2,1)S(1)}, bf16[2,2,24,3968]{3,2,0,1:T(8,128)(2,1)S(1)}, u32[]{:S(2)}, u32[]{:S(2)}) collective-permute-start(bf16[2,2,24,3968]{3,2,0,1:T(8,128)(2,1)S(1)} %bitcast.334), channel_id=1, source_target_pairs={{0,2},{1,3},{2,0},{3,1},{4,6},{5,7},{6,4},{7,5},{8,10},{9,11},{10,... | collective-permute-start | bytes 2285576 | tf_op jit(solution)/shard_map/ppermute | solution.py:204
  278.2 29.7 %collective-permute-start.51 = (bf16[96,768]{1,0:T(8,128)(2,1)}, bf16[96,768]{1,0:T(8,128)(2,1)S(1)}, u32[]{:S(2)}, u32[]{:S(2)}) collective-permute-start(bf16[96,768]{1,0:T(8,128)(2,1)} %get-tuple-element.300), channel_id=1, source_target_pairs={{0,8},{1,9},{2,10},{3,11},{4,12},{5,13},{6,14},{7,15},{8,0},{9,1},... | collective-permute-start | bytes 442376 | tf_op jit(solution)/shard_map/ppermute | solution.py:204
  279.3 28.6 %collective-permute-start.52 = (bf16[96,768]{1,0:T(8,128)(2,1)}, bf16[96,768]{1,0:T(8,128)(2,1)}, u32[]{:S(2)}, u32[]{:S(2)}) collective-permute-start(bf16[96,768]{1,0:T(8,128)(2,1)} %get-tuple-element.301), channel_id=1, source_target_pairs={{0,16},{1,17},{2,18},{3,19},{4,20},{5,21},{6,22},{7,23},{8,24},{9,... | collective-permute-start | bytes 442376 | tf_op jit(solution)/shard_map/ppermute | solution.py:204
  281.1 26.8 %collective-permute-start.53 = (bf16[96,768]{1,0:T(8,128)(2,1)}, bf16[96,768]{1,0:T(8,128)(2,1)}, u32[]{:S(2)}, u32[]{:S(2)}) collective-permute-start(bf16[96,768]{1,0:T(8,128)(2,1)} %get-tuple-element.302), channel_id=1, source_target_pairs={{0,24},{1,25},{2,26},{3,27},{4,28},{5,29},{6,30},{7,31},{8,16},{9,... | collective-permute-start | bytes 442376 | tf_op jit(solution)/shard_map/ppermute | solution.py:204
  308.7 19.0 %collective-permute-start.54 = (bf16[2,24,3968]{2,1,0:T(8,128)(2,1)}, bf16[2,24,3968]{2,1,0:T(8,128)(2,1)}, u32[]{:S(2)}, u32[]{:S(2)}) collective-permute-start(bf16[2,24,3968]{2,1,0:T(8,128)(2,1)} %dynamic-slice_bitcast_fusion.15), channel_id=1, source_target_pairs={{0,2},{1,3},{2,0},{3,1},{4,6},{5,7},{6,4},{7,5},{8,10},{9,11},{10,... | collective-permute-start | bytes 1142792 | tf_op jit(solution)/shard_map/ppermute | solution.py:204
  310.6 18.2 %collective-permute-start.55 = (bf16[2,24,3968]{2,1,0:T(8,128)(2,1)}, bf16[2,24,3968]{2,1,0:T(8,128)(2,1)}, u32[]{:S(2)}, u32[]{:S(2)}) collective-permute-start(bf16[2,24,3968]{2,1,0:T(8,128)(2,1)} %dynamic-slice_bitcast_fusion.14), channel_id=1, source_target_pairs={{0,4},{1,5},{2,6},{3,7},{4,0},{5,1},{6,2},{7,3},{8,12},{9,13},{10,... | collective-permute-start | bytes 1142792 | tf_op jit(solution)/shard_map/ppermute | solution.py:204
  332.9 16.7 %collective-permute-start.61 = (bf16[24,3968]{1,0:T(8,128)(2,1)S(1)}, bf16[24,3968]{1,0:T(8,128)(2,1)S(1)}, u32[]{:S(2)}, u32[]{:S(2)}) collective-permute-start(bf16[24,3968]{1,0:T(8,128)(2,1)S(1)} %get-tuple-element.324), channel_id=1, source_target_pairs={{0,8},{1,9},{2,10},{3,11},{4,12},{5,13},{6,14},{7,15},{8,0},{9,1},... | collective-permute-start | bytes 571400 | tf_op jit(solution)/shard_map/ppermute | solution.py:204
  356.6 18.8 %collective-permute-start.69 = (bf16[1,2,128,768]{3,2,1,0:T(8,128)(2,1)S(1)}, bf16[1,2,128,768]{3,2,1,0:T(8,128)(2,1)S(1)}, u32[]{:S(2)}, u32[]{:S(2)}) collective-permute-start(bf16[1,2,128,768]{3,2,1,0:T(8,128)(2,1)S(1)} %get-tuple-element.334), channel_id=1, source_target_pairs={{0,3},{1,2},{2,1},{3,0},{4,7},{5,6},{6,5},{7,4},{8,11},{9,10},{10,... | collective-permute-start | bytes 1179656 | tf_op jit(solution)/shard_map/ppermute | solution.py:204
  (94 other events, 1055.0 us)

commit v9 on v8

--- a/solution.py
+++ b/solution.py
@@ -503,19 +503,20 @@
     for k in range(1, members):
         flat.send(k)
     qkv_gather.along_z()
-    fence([qkv_gather])
+    (in_block,) = fence([qkv_gather], in_gather.held[0])
+    in_gather.put([in_block])
     qkv_gather.first()
-    fence([qkv_gather, flat])
+    in_gather.along_z()
+    fence([qkv_gather, in_gather, flat])
     qkv_gather.second()
-    in_gather.put([after(a, qkv_gather.held[0]) for a in in_gather.arrays()])
-    in_gather.along_z()
     fence([qkv_gather])
     qkv_gather.core()
-    fence([qkv_gather])
+    fence([qkv_gather, in_gather])
+    in_gather.first()
     flat = flat.finish()
     wide_qkv, early = qkv_gather.finish([(0, 3 * width), (3 * width, early.shape[1])])
     (wide_qkv, early, flat) = fence([in_gather], wide_qkv, early, flat)
-    in_gather.first()
+    in_gather.second()
     wide_qkv = wide_qkv.reshape(width, 3 * width)
     full_query_bias, full_value_bias = [
         v.reshape(-1).astype(F32) for v in unpack_rows(early, [share, share])
@@ -523,8 +524,7 @@
     bias_vector = jnp.concatenate([full_query_bias, jnp.zeros((width,), F32), full_value_bias])
     packed = jnp.dot(flat, wide_qkv, preferred_element_type=F32) + pair_major(bias_vector)
     packed = packed.astype(BF)
-    (packed,) = fence([in_gather], packed)
-    in_gather.second()
+    (packed,) = fence([], packed)
     down_gather.put([after(a, packed) for a in down_gather.arrays()])
     down_gather.along_z()
     mine = lax.dynamic_slice(lengths, (seat * kept,), (kept,))
@@ -635,33 +635,37 @@
     grad_packed, column_sums = attention_backward(packed, mask, logsum, grad_mixed, length)
     (grad_packed, column_sums) = fence([in_scatter, down_scatter], grad_packed, column_sums)
     in_scatter.second()
+    grad_inputs = (times_transposed(grad_packed, wide_qkv) + grad_residual).astype(BF)
+    (grad_inputs, grad_packed) = fence([in_scatter], grad_inputs, grad_packed)
+    grad_inputs = ToPositions(
+        grad_inputs.reshape(kept, members, local_len, width), members, devices
+    )
+    for k in near:
+        grad_inputs.send(k)
+    for k in far[:1]:
+        grad_inputs.send(k)
+    in_scatter.along_z()
     grad_qkv = over_rows(flat, grad_packed).astype(BF)
     column_sums = kind_major(column_sums.reshape(kept, 3 * width).sum(0))
     early_sums = [column_sums[:width], column_sums[2 * width :]]
     early_block = pack_rows([v.reshape(devices, -1) for v in early_sums], share).astype(BF)
     grad_qkv = jnp.concatenate([grad_qkv.reshape(devices, share, 3 * width), early_block], 2)
-    (grad_qkv, grad_packed) = fence([], grad_qkv, grad_packed)
+    (grad_qkv,) = fence([grad_inputs], grad_qkv)
     qkv_scatter = Scatter(core_sum(grad_qkv, me, devices), me, devices, "split")
-    grad_inputs = (times_transposed(grad_packed, wide_qkv) + grad_residual).astype(BF)
-    (grad_inputs,) = fence([in_scatter, qkv_scatter], grad_inputs)
-    grad_inputs = ToPositions(
-        grad_inputs.reshape(kept, members, local_len, width), members, devices
-    )
+    for k in far[1:]:
+        grad_inputs.send(k)
+    fence([qkv_scatter])
     qkv_scatter.first()
-    in_scatter.along_z()
-    fence([qkv_scatter, grad_inputs])
+    fence([qkv_scatter, grad_inputs, in_scatter])
     qkv_scatter.second()
-    fence([qkv_scatter, grad_inputs, in_scatter])
-    for k in range(1, members):
-        grad_inputs.send(k)
+    down_part = down_scatter.result()
+    in_part = in_scatter.result()
+    outputs = outputs.finish(seat)
+    (in_part, down_part, outputs) = fence([qkv_scatter], in_part, down_part, outputs)
     qkv_scatter.along_z()
-    outputs.put([after(a, *qkv_scatter.held[:1]) for a in outputs.arrays()])
-    outputs = outputs.finish(seat)
-    in_part = in_scatter.result()
-    down_part = down_scatter.result()
-    (in_part, outputs) = fence([qkv_scatter, grad_inputs], in_part, outputs)
+    grad_inputs = grad_inputs.finish(seat)
+    (grad_inputs,) = fence([qkv_scatter], grad_inputs)
     qkv_part = qkv_scatter.result()
-    grad_inputs = grad_inputs.finish(seat)
     early_out = unpack_rows(qkv_part[:, 3 * width :], [share, share])
     late_out = unpack_rows(
         in_part[:, inner_width + width :], [v.shape[0] for v in late_vectors]

time: 385 us -> 389 us (1.010)
  waiting for transfers between devices: 83.1 us -> 93.5 us
  starting transfers between devices: 70.4 us -> 63.6 us
    ppermute x70, waiting for transfers between devices: 83.1 us -> 93.5 us  [swap(): lax.ppermute(block, BOTH, [(i, i ^ distance) for i in range(devices)])]
    ppermute x70, starting transfers between devices: 70.4 us -> 63.6 us  [swap(): lax.ppermute(block, BOTH, [(i, i ^ distance) for i in range(devices)])]
    unnamed x116 -> x122, local copies, waits for them, and re-layouts: 13.1 us -> 12.6 us
  transfers between devices with their start and end apart: 70 -> 70, of which waited for: 21 -> 34; matrix products, arithmetic and copies ran while one was open for 28% -> 27% of each run, Pallas kernels for 17% -> 17%
where the time goes in v9:
time: 389 us; the launch traced here: 385 us
  waiting for transfers between devices  93.5 us (24%)
  Pallas kernels  71 us (18%)
  matrix products  68 us (17%)
  starting transfers between devices  63.6 us (16%)
  local copies, waits for them, and re-layouts  48.1 us (12%)
  other arithmetic  38.7 us (10%)
    ppermute x70, waiting for transfers between devices, swap(): lax.ppermute(block, BOTH, [(i, i ^ distance) for i in range(devices)])  93.5 us
    ppermute x70, starting transfers between devices, swap(): lax.ppermute(block, BOTH, [(i, i ^ distance) for i in range(devices)])  63.6 us
    dot_general x4, matrix products, times_transposed(): lax.dot_general(left, right, (((1,), (1,)), ((), ())), preferred_element_...  30.1 us
    pallas_call x1, Pallas kernels, attention_backward(): pl.pallas_call(backward_kernel, grid=(seqs, pairs), in_specs=[block(384),...  24.7 us
    dot_general x4, matrix products, over_rows(): lax.dot_general(left, right, (((0,), (0,)), ((), ())), preferred_element_...  20.4 us
    pallas_call x1, Pallas kernels, attention_forward(): pl.pallas_call(forward_kernel, grid=(seqs, pairs), in_specs=[block(384),...  17 us
    pallas_call x1, Pallas kernels, feed_forward(): pl.pallas_call(functools.partial(feed_forward_kernel, 512), grid=(rows //...  15 us
    pallas_call x5, Pallas kernels, place(): pl.pallas_call(functools.partial(place_kernel, ids, counts, spans), in_sp...  14.2 us
  transfers between devices with their start and end apart: 70, of which 34 were waited for; matrix products, arithmetic and copies ran while one was open for 27% of the time, Pallas kernels for 17%

profile of v9, /device:TPU:0, one launch (start us, length us, event | category | flops | bytes accessed | tf_op | source)
XLA Modules:
  0.0 385.3 jit_solution(17961307564332902814)
XLA Ops:
  12.7 4.9 %collective-permute-done.1 = bf16[1,24,2432]{2,1,0:T(8,128)(2,1)S(1)} collective-permute-done((bf16[1,24,2432]{2,1,0:T(8,128)(2,1)S(1)}, bf16[1,24,2432]{2,1,0:T(8,128)(2,1)S(1)}, u32[]{:S(2)}, u32[]{:S(2)}) %collective-permute-start.1) | collective-permute-done | bytes 116768 | tf_op jit(solution)/shard_map/ppermute | solution.py:204
  20.7 5.4 %collective-permute-done.5 = bf16[1,24,3968]{2,1,0:T(8,128)(2,1)S(1)} collective-permute-done((bf16[1,24,3968]{2,1,0:T(8,128)(2,1)S(1)}, bf16[1,24,3968]{2,1,0:T(8,128)(2,1)S(1)}, u32[]{:S(2)}, u32[]{:S(2)}) %collective-permute-start.5) | collective-permute-done | bytes 190496 | tf_op jit(solution)/shard_map/ppermute | solution.py:204
  28.0 7.3 %collective-permute-done.6 = bf16[1,24,3968]{2,1,0:T(8,128)(2,1)S(1)} collective-permute-done((bf16[1,24,3968]{2,1,0:T(8,128)(2,1)S(1)}, bf16[1,24,3968]{2,1,0:T(8,128)(2,1)S(1)}, u32[]{:S(2)}, u32[]{:S(2)}) %collective-permute-start.6) | collective-permute-done | bytes 190496 | tf_op jit(solution)/shard_map/ppermute | solution.py:204
  48.2 6.6 %collective-permute-done.11.refs_2_ = bf16[4,24,2432]{2,1,0:T(8,128)(2,1)S(1)} collective-permute-done((bf16[4,24,2432]{2,1,0:T(8,128)(2,1)S(1)}, bf16[4,24,2432]{2,1,0:T(8,128)(2,1)S(1)}, u32[]{:S(2)}, u32[]{:S(2)}) %collective-permute-start.11) | collective-permute-done | bytes 466976 | tf_op jit(solution)/shard_map/ppermute | solution.py:204
  81.9 8.5 %add_convert_fusion.packed_ref = bf16[1024,2304]{1,0:T(8,128)(2,1)} fusion(bf16[1024,768]{1,0:T(8,128)(2,1)} %bitcast.322, bf16[768,2304]{1,0:T(8,128)(2,1)} %bitcast.293, f32[2304]{0:T(1024)S(1)} %add.450), kind=kOutput, calls=%fused_computation.2 | convolution fusion | flops 3628597248 | bytes 9839616 | tf_op jit(solution)/shard_map/dot_general | solution.py:525
  94.9 17.0 %attention_forward.1 = (bf16[1024,768]{1,0:T(8,128)(2,1)S(1)}, f32[12,2,512]{2,1,0:T(2,128)S(1)}) custom-call(bf16[1024,2304]{1,0:T(8,128)(2,1)} %add_convert_fusion.packed_ref, bf16[2,512,128]{2,1,0:T(8,128)(2,1)S(1)} %broadcast_in_dim.57.mask_ref), custom_call_target="tpu_custom_call" | custom-call | flops 6442450944 | bytes 6291456 | tf_op jit(solution)/shard_map/attention_forward/pallas_call | solution.py:117
  136.0 4.0 %collective-permute-done.30.refs_2_ = bf16[4,96,768]{2,1,0:T(8,128)(2,1)S(1)} collective-permute-done((bf16[4,96,768]{2,1,0:T(8,128)(2,1)S(1)}, bf16[4,96,768]{2,1,0:T(8,128)(2,1)S(1)}, u32[]{:S(2)}, u32[]{:S(2)}) %collective-permute-start.30) | collective-permute-done | bytes 589856 | tf_op jit(solution)/shard_map/ppermute | solution.py:204
  150.3 5.4 %collective-permute-done.37 = bf16[2,128,768]{2,1,0:T(8,128)(2,1)} collective-permute-done((bf16[2,128,768]{2,1,0:T(8,128)(2,1)}, bf16[2,128,768]{2,1,0:T(8,128)(2,1)}, u32[]{:S(2)}, u32[]{:S(2)}) %collective-permute-start.37) | collective-permute-done | bytes 393248 | tf_op jit(solution)/shard_map/ppermute | solution.py:204
  155.7 15.0 %feed_forward.1 = (bf16[1024,3072]{1,0:T(8,128)(2,1)}, bf16[1024,3072]{1,0:T(8,128)(2,1)}) custom-call(bf16[1024,768]{1,0:T(8,128)(2,1)S(1)} %add_convert_fusion.3.x_ref, bf16[768,3072]{1,0:T(8,128)(2,1)} %bitcast.291, f32[1,3072]{1,0:T(1,128)S(1)} %reshape.434.b_ref), custom_call_target="tpu_custom_call" | custom-call | flops 4831838208 | bytes 17301504 | tf_op jit(solution)/shard_map/feed_forward/pallas_call | solution.py:183
  170.8 4.0 %place_blocks.7 = bf16[32,96,768]{2,1,0:T(8,128)(2,1)S(1)} custom-call(s32[1]{0:T(128)} %bitcast.17.me_ref, bf16[4,96,768]{2,1,0:T(8,128)(2,1)S(1)} %constant_dynamic-update-slice_fusion.20.refs_0_, bf16[4,96,768]{2,1,0:T(8,128)(2,1)} %collective-permute-done.32.refs_1_, bf16[4,96,768]{2,1,0:T(8,128)(2,1)S(1)} %collective-permute-done.30.refs_2_, ...), custom_call_target="tpu_custom_call" | custom-call | bytes 9437184 | tf_op jit(solution)/shard_map/place_blocks/pallas_call | solution.py:237
  174.9 5.3 %fusion.46 = (f32[1024]{0:T(1024)S(1)}, f32[1024,768]{1,0:T(8,128)S(1)}) fusion(f32[768]{0:T(1024)S(1)} %copy-done.36, bf16[1024,3072]{1,0:T(8,128)(2,1)S(1)} %copy-done.48, bf16[3072,768]{1,0:T(8,128)(2,1)S(1)} %bitcast.289, bf16[1024,768]{1,0:T(8,128)(2,1)S(1)} %add_convert_fusion.3.x_ref), kind=kOutput, calls=%fused_computation.234 | convolution fusion | flops 4834982912 | bytes 15735808 | tf_op jit(solution)/shard_map/dot_general | solution.py:573
  188.1 4.4 %convert_reduce_fusion.2 = (bf16[768]{0:T(1024)(128)(2,1)}, bf16[1024,768]{1,0:T(8,128)(2,1)S(1)}, f32[1024,768]{1,0:T(8,128)}, bf16[1024,768]{1,0:T(8,128)(2,1)S(1)}) fusion(f32[1024]{0:T(1024)S(1)} %negate_multiply_fusion.1, f32[1024]{0:T(1024)S(1)} %get-tuple-element.424, f32[1024,768]{1,0:T(8,128)S(1)} %get-tuple-element.429, ...), kind=kLoop, calls=%fused_computation.27 | loop fusion | flops 17300736 | bytes 11034112 | tf_op jit(solution)/shard_map/reduce_sum | solution.py:580
  194.9 5.7 %convolution_convert_fusion.1 = bf16[3072,768]{1,0:T(8,128)(2,1)S(1)} fusion(bf16[1024,3072]{1,0:T(8,128)(2,1)S(1)} %copy-done.48, bf16[1024,768]{1,0:T(8,128)(2,1)S(1)} %get-tuple-element.284), kind=kOutput, calls=%fused_computation.6 | convolution fusion | flops 4834197504 | bytes 12582912 | tf_op jit(solution)/shard_map/dot_general | solution.py:23
  200.6 3.8 collective-permute-done.40.refs_2_
  211.8 9.0 %convert_reduce_fusion = (bf16[3072]{0:T(1024)(128)(2,1)}, bf16[1024,3072]{1,0:T(8,128)(2,1)S(1)}) fusion(bf16[1024,3072]{1,0:T(8,128)(2,1)} %get-tuple-element.285, bf16[1024,768]{1,0:T(8,128)(2,1)} %copy-done.25, bf16[3072,768]{1,0:T(8,128)(2,1)} %bitcast.290), kind=kOutput, calls=%fused_computation | convolution fusion | flops 4847563776 | bytes 18880512 | tf_op jit(solution)/shard_map/dot_general | solution.py:29
  220.8 4.1 %fusion.2 = bf16[16,96,768]{2,1,0:T(8,128)(2,1)S(1)} fusion(bf16[16,96,768]{2,1,0:T(8,128)(2,1)} %collective-permute-done.42, bf16[16,2,96,768]{3,2,1,0:T(8,128)(2,1)S(1)} %bitcast.316, s32[]{:T(128)S(6)} %select_n.257), kind=kLoop, calls=%fused_computation.13 | loop fusion | flops 4718592 | bytes 7077892 | tf_op jit(solution)/shard_map/convert_element_type | solution.py:351
  229.9 6.8 %convolution_convert_fusion = bf16[768,3072]{1,0:T(8,128)(2,1)} fusion(bf16[1024,768]{1,0:T(8,128)(2,1)S(1)} %add_convert_fusion.3.x_ref, bf16[1024,3072]{1,0:T(8,128)(2,1)S(1)} %get-tuple-element.291), kind=kOutput, calls=%fused_computation.5 | convolution fusion | flops 4834197504 | bytes 12582912 | tf_op jit(solution)/shard_map/dot_general | solution.py:23
  236.7 5.9 %collective-permute-done.43 = bf16[2,2,96,768]{3,2,0,1:T(8,128)(2,1)} collective-permute-done((bf16[2,2,96,768]{3,2,0,1:T(8,128)(2,1)}, bf16[2,2,96,768]{3,2,0,1:T(8,128)(2,1)}, u32[]{:S(2)}, u32[]{:S(2)}) %collective-permute-start.43) | collective-permute-done | bytes 589856 | tf_op jit(solution)/shard_map/ppermute | solution.py:204
  249.5 10.3 %multiply_reduce_fusion = (bf16[768]{0:T(1024)(128)(2,1)}, f32[1024]{0:T(1024)S(1)}, bf16[768]{0:T(1024)(128)(2,1)}, f32[1024,768]{1,0:T(8,128)S(1)}) fusion(f32[1024,768]{1,0:T(8,128)S(1)} %copy-done.14, f32[1024]{0:T(1024)S(1)} %fusion.33, f32[1024]{0:T(1024)S(1)} %broadcast_multiply_fusion.1, f32[768]{0:T(1024)S(1)} %reshape.432, ...), kind=kOutput, calls=%fused_computation.25 | convolution fusion | flops 4838913024 | bytes 20465664 | tf_op jit(solution)/shard_map/dot_general | solution.py:29
  280.5 24.7 %attention_backward.1 = (bf16[1024,2304]{1,0:T(8,128)(2,1)}, f32[12,1,384]{2,1,0:T(1,128)S(1)}) custom-call(bf16[1024,2304]{1,0:T(8,128)(2,1)} %add_convert_fusion.packed_ref, bf16[2,512,128]{2,1,0:T(8,128)(2,1)S(1)} %copy-done.4, f32[12,2,512]{2,1,0:T(2,128)S(1)} %copy-done.12, bf16[1024,768]{1,0:T(8,128)(2,1)S(1)} %convolution_convert_fusion.3.grad_ref), custom_call_target="tpu_custom_call" | custom-call | flops 11274289152 | bytes 11010048 | tf_op jit(solution)/shard_map/attention_backward/pallas_call | solution.py:138
  309.3 9.3 %add_convert_fusion.1 = bf16[1024,768]{1,0:T(8,128)(2,1)} fusion(f32[1024,768]{1,0:T(8,128)} %get-tuple-element.310, bf16[1024,2304]{1,0:T(8,128)(2,1)} %get-tuple-element.312, bf16[768,2304]{1,0:T(8,128)(2,1)} %bitcast.294), kind=kOutput, calls=%fused_computation.24 | convolution fusion | flops 3625451520 | bytes 12976128 | tf_op jit(solution)/shard_map/dot_general | solution.py:29
  323.4 6.4 %convolution_convert_fusion.2 = bf16[768,2304]{1,0:T(8,128)(2,1)S(1)} fusion(bf16[1024,768]{1,0:T(8,128)(2,1)S(1)} %bitcast.324, bf16[1024,2304]{1,0:T(8,128)(2,1)} %get-tuple-element.312), kind=kOutput, calls=%fused_computation.7 | convolution fusion | flops 3625648128 | bytes 9830400 | tf_op jit(solution)/shard_map/dot_general | solution.py:23
  353.3 7.5 %collective-permute-done.63 = bf16[24,3968]{1,0:T(8,128)(2,1)S(1)} collective-permute-done((bf16[24,3968]{1,0:T(8,128)(2,1)S(1)}, bf16[24,3968]{1,0:T(8,128)(2,1)S(1)}, u32[]{:S(2)}, u32[]{:S(2)}) %collective-permute-start.63) | collective-permute-done | bytes 190496 | tf_op jit(solution)/shard_map/ppermute | solution.py:204
  377.4 6.1 %collective-permute-done.68 = bf16[24,2432]{1,0:T(8,128)(2,1)S(1)} collective-permute-done((bf16[24,2432]{1,0:T(8,128)(2,1)S(1)}, bf16[24,2432]{1,0:T(8,128)(2,1)S(1)}, u32[]{:S(2)}, u32[]{:S(2)}) %collective-permute-start.68) | collective-permute-done | bytes 116768 | tf_op jit(solution)/shard_map/ppermute | solution.py:204
  (397 shorter events, 195.1 us)
Async XLA Ops:
  10.6 34.7 %collective-permute-start.8 = (bf16[2,128,768]{2,1,0:T(8,128)(2,1)S(1)}, bf16[2,128,768]{2,1,0:T(8,128)(2,1)S(1)}, u32[]{:S(2)}, u32[]{:S(2)}) collective-permute-start(bf16[2,128,768]{2,1,0:T(8,128)(2,1)S(1)} %get-tuple-element.402), channel_id=1, source_target_pairs={{0,1},{1,0},{2,3},{3,2},{4,5},{5,4},{6,7},{7,6},{8,9},{9,8},{10,11... | collective-permute-start | bytes 1179656 | tf_op jit(solution)/shard_map/ppermute | solution.py:204
  10.6 34.7 %collective-permute-start.9 = (bf16[2,128,768]{2,1,0:T(8,128)(2,1)S(1)}, bf16[2,128,768]{2,1,0:T(8,128)(2,1)S(1)}, u32[]{:S(2)}, u32[]{:S(2)}) collective-permute-start(bf16[2,128,768]{2,1,0:T(8,128)(2,1)S(1)} %get-tuple-element.401), channel_id=1, source_target_pairs={{0,2},{1,3},{2,0},{3,1},{4,6},{5,7},{6,4},{7,5},{8,10},{9,11},{10,... | collective-permute-start | bytes 1179656 | tf_op jit(solution)/shard_map/ppermute | solution.py:204
  12.6 32.8 %collective-permute-start.10 = (bf16[2,128,768]{2,1,0:T(8,128)(2,1)S(1)}, bf16[2,128,768]{2,1,0:T(8,128)(2,1)S(1)}, u32[]{:S(2)}, u32[]{:S(2)}) collective-permute-start(bf16[2,128,768]{2,1,0:T(8,128)(2,1)S(1)} %get-tuple-element.400), channel_id=1, source_target_pairs={{0,3},{1,2},{2,1},{3,0},{4,7},{5,6},{6,5},{7,4},{8,11},{9,10},{10,... | collective-permute-start | bytes 1179656 | tf_op jit(solution)/shard_map/ppermute | solution.py:204
  19.5 15.8 %collective-permute-start.6 = (bf16[1,24,3968]{2,1,0:T(8,128)(2,1)S(1)}, bf16[1,24,3968]{2,1,0:T(8,128)(2,1)S(1)}, u32[]{:S(2)}, u32[]{:S(2)}) collective-permute-start(bf16[1,24,3968]{2,1,0:T(8,128)(2,1)S(1)} %fusion.24), channel_id=1, source_target_pairs={{0,16},{1,17},{2,18},{3,19},{4,20},{5,21},{6,22},{7,23},{8,24},{9,... | collective-permute-start | bytes 571400 | tf_op jit(solution)/shard_map/ppermute | solution.py:204
  77.1 35.0 %collective-permute-start.19 = (bf16[4,24,3968]{2,1,0:T(8,128)(2,1)S(1)}, bf16[4,24,3968]{2,1,0:T(8,128)(2,1)S(1)}, u32[]{:S(2)}, u32[]{:S(2)}) collective-permute-start(bf16[4,24,3968]{2,1,0:T(8,128)(2,1)S(1)} %constant_dynamic-update-slice_fusion.12.refs_0_), channel_id=1, source_target_pairs={{0,2},{1,3},{2,0},{3,1},{4,6},{5,7},{6,4},{7,5},{8,10},{9,11},{10,... | collective-permute-start | bytes 2285576 | tf_op jit(solution)/shard_map/ppermute | solution.py:204
  79.7 32.4 %collective-permute-start.20 = (bf16[4,24,3968]{2,1,0:T(8,128)(2,1)S(1)}, bf16[4,24,3968]{2,1,0:T(8,128)(2,1)S(1)}, u32[]{:S(2)}, u32[]{:S(2)}) collective-permute-start(bf16[4,24,3968]{2,1,0:T(8,128)(2,1)S(1)} %constant_dynamic-update-slice_fusion.14.refs_4_), channel_id=1, source_target_pairs={{0,4},{1,5},{2,6},{3,7},{4,0},{5,1},{6,2},{7,3},{8,12},{9,13},{10,... | collective-permute-start | bytes 2285576 | tf_op jit(solution)/shard_map/ppermute | solution.py:204
  90.3 21.7 %collective-permute-start.21 = (bf16[1,96,768]{2,1,0:T(8,128)(2,1)S(1)}, bf16[1,96,768]{2,1,0:T(8,128)(2,1)S(1)}, u32[]{:S(2)}, u32[]{:S(2)}) collective-permute-start(bf16[1,96,768]{2,1,0:T(8,128)(2,1)S(1)} %bitcast.340), channel_id=1, source_target_pairs={{0,8},{1,9},{2,10},{3,11},{4,12},{5,13},{6,14},{7,15},{8,0},{9,1},... | collective-permute-start | bytes 442376 | tf_op jit(solution)/shard_map/ppermute | solution.py:204
  91.3 20.8 %collective-permute-start.22 = (bf16[1,96,768]{2,1,0:T(8,128)(2,1)S(1)}, bf16[1,96,768]{2,1,0:T(8,128)(2,1)S(1)}, u32[]{:S(2)}, u32[]{:S(2)}) collective-permute-start(bf16[1,96,768]{2,1,0:T(8,128)(2,1)S(1)} %bitcast.341), channel_id=1, source_target_pairs={{0,16},{1,17},{2,18},{3,19},{4,20},{5,21},{6,22},{7,23},{8,24},{9,... | collective-permute-start | bytes 442376 | tf_op jit(solution)/shard_map/ppermute | solution.py:204
  93.5 18.5 %collective-permute-start.23 = (bf16[1,96,768]{2,1,0:T(8,128)(2,1)S(1)}, bf16[1,96,768]{2,1,0:T(8,128)(2,1)S(1)}, u32[]{:S(2)}, u32[]{:S(2)}) collective-permute-start(bf16[1,96,768]{2,1,0:T(8,128)(2,1)S(1)} %bitcast.342), channel_id=1, source_target_pairs={{0,24},{1,25},{2,26},{3,27},{4,28},{5,29},{6,30},{7,31},{8,16},{9,... | collective-permute-start | bytes 442376 | tf_op jit(solution)/shard_map/ppermute | solution.py:204
  124.6 15.4 %collective-permute-start.30 = (bf16[4,96,768]{2,1,0:T(8,128)(2,1)S(1)}, bf16[4,96,768]{2,1,0:T(8,128)(2,1)S(1)}, u32[]{:S(2)}, u32[]{:S(2)}) collective-permute-start(bf16[4,96,768]{2,1,0:T(8,128)(2,1)S(1)} %constant_dynamic-update-slice_fusion.20.refs_0_), channel_id=1, source_target_pairs={{0,2},{1,3},{2,0},{3,1},{4,6},{5,7},{6,4},{7,5},{8,10},{9,11},{10,... | collective-permute-start | bytes 1769480 | tf_op jit(solution)/shard_map/ppermute | solution.py:204
  144.4 26.4 %collective-permute-start.32 = (bf16[4,96,768]{2,1,0:T(8,128)(2,1)S(1)}, bf16[4,96,768]{2,1,0:T(8,128)(2,1)}, u32[]{:S(2)}, u32[]{:S(2)}) collective-permute-start(bf16[4,96,768]{2,1,0:T(8,128)(2,1)S(1)} %constant_dynamic-update-slice_fusion.20.refs_0_), channel_id=1, source_target_pairs={{0,1},{1,0},{2,3},{3,2},{4,5},{5,4},{6,7},{7,6},{8,9},{9,8},{10,11... | collective-permute-start | bytes 1769480 | tf_op jit(solution)/shard_map/ppermute | solution.py:204
  144.6 26.2 %collective-permute-start.33 = (bf16[4,96,768]{2,1,0:T(8,128)(2,1)S(1)}, bf16[4,96,768]{2,1,0:T(8,128)(2,1)}, u32[]{:S(2)}, u32[]{:S(2)}) collective-permute-start(bf16[4,96,768]{2,1,0:T(8,128)(2,1)S(1)} %collective-permute-done.30.refs_2_), channel_id=1, source_target_pairs={{0,1},{1,0},{2,3},{3,2},{4,5},{5,4},{6,7},{7,6},{8,9},{9,8},{10,11... | collective-permute-start | bytes 1769480 | tf_op jit(solution)/shard_map/ppermute | solution.py:204
  144.9 25.9 %collective-permute-start.34 = (bf16[4,96,768]{2,1,0:T(8,128)(2,1)S(1)}, bf16[4,96,768]{2,1,0:T(8,128)(2,1)}, u32[]{:S(2)}, u32[]{:S(2)}) collective-permute-start(bf16[4,96,768]{2,1,0:T(8,128)(2,1)S(1)} %constant_dynamic-update-slice_fusion.22.refs_4_), channel_id=1, source_target_pairs={{0,1},{1,0},{2,3},{3,2},{4,5},{5,4},{6,7},{7,6},{8,9},{9,8},{10,11... | collective-permute-start | bytes 1769480 | tf_op jit(solution)/shard_map/ppermute | solution.py:204
  145.7 25.1 %collective-permute-start.35 = (bf16[4,96,768]{2,1,0:T(8,128)(2,1)}, bf16[4,96,768]{2,1,0:T(8,128)(2,1)}, u32[]{:S(2)}, u32[]{:S(2)}) collective-permute-start(bf16[4,96,768]{2,1,0:T(8,128)(2,1)} %collective-permute-done.31.refs_6_), channel_id=1, source_target_pairs={{0,1},{1,0},{2,3},{3,2},{4,5},{5,4},{6,7},{7,6},{8,9},{9,8},{10,11... | collective-permute-start | bytes 1769480 | tf_op jit(solution)/shard_map/ppermute | solution.py:204
  226.8 15.8 %collective-permute-start.43 = (bf16[2,2,96,768]{3,2,0,1:T(8,128)(2,1)}, bf16[2,2,96,768]{3,2,0,1:T(8,128)(2,1)}, u32[]{:S(2)}, u32[]{:S(2)}) collective-permute-start(bf16[2,2,96,768]{3,2,0,1:T(8,128)(2,1)} %bitcast.288), channel_id=1, source_target_pairs={{0,4},{1,5},{2,6},{3,7},{4,0},{5,1},{6,2},{7,3},{8,12},{9,13},{10,... | collective-permute-start | bytes 1769480 | tf_op jit(solution)/shard_map/ppermute | solution.py:204
  229.0 15.6 %collective-permute-start.44 = (bf16[2,2,96,768]{3,2,0,1:T(8,128)(2,1)}, bf16[2,2,96,768]{3,2,0,1:T(8,128)(2,1)}, u32[]{:S(2)}, u32[]{:S(2)}) collective-permute-start(bf16[2,2,96,768]{3,2,0,1:T(8,128)(2,1)} %bitcast.287), channel_id=1, source_target_pairs={{0,2},{1,3},{2,0},{3,1},{4,6},{5,7},{6,4},{7,5},{8,10},{9,11},{10,... | collective-permute-start | bytes 1769480 | tf_op jit(solution)/shard_map/ppermute | solution.py:204
  246.8 24.1 %collective-permute-start.45 = (bf16[2,96,768]{2,1,0:T(8,128)(2,1)}, bf16[2,96,768]{2,1,0:T(8,128)(2,1)S(1)}, u32[]{:S(2)}, u32[]{:S(2)}) collective-permute-start(bf16[2,96,768]{2,1,0:T(8,128)(2,1)} %dynamic-slice_bitcast_fusion.17), channel_id=1, source_target_pairs={{0,2},{1,3},{2,0},{3,1},{4,6},{5,7},{6,4},{7,5},{8,10},{9,11},{10,... | collective-permute-start | bytes 884744 | tf_op jit(solution)/shard_map/ppermute | solution.py:204
  247.9 23.1 %collective-permute-start.46 = (bf16[2,96,768]{2,1,0:T(8,128)(2,1)}, bf16[2,96,768]{2,1,0:T(8,128)(2,1)}, u32[]{:S(2)}, u32[]{:S(2)}) collective-permute-start(bf16[2,96,768]{2,1,0:T(8,128)(2,1)} %dynamic-slice_bitcast_fusion.16), channel_id=1, source_target_pairs={{0,4},{1,5},{2,6},{3,7},{4,0},{5,1},{6,2},{7,3},{8,12},{9,13},{10,... | collective-permute-start | bytes 884744 | tf_op jit(solution)/shard_map/ppermute | solution.py:204
  273.8 31.4 %collective-permute-start.49 = (bf16[2,2,24,3968]{3,2,0,1:T(8,128)(2,1)S(1)}, bf16[2,2,24,3968]{3,2,0,1:T(8,128)(2,1)S(1)}, u32[]{:S(2)}, u32[]{:S(2)}) collective-permute-start(bf16[2,2,24,3968]{3,2,0,1:T(8,128)(2,1)S(1)} %bitcast.335), channel_id=1, source_target_pairs={{0,4},{1,5},{2,6},{3,7},{4,0},{5,1},{6,2},{7,3},{8,12},{9,13},{10,... | collective-permute-start | bytes 2285576 | tf_op jit(solution)/shard_map/ppermute | solution.py:204
  274.4 31.1 %collective-permute-start.50 = (bf16[2,2,24,3968]{3,2,0,1:T(8,128)(2,1)S(1)}, bf16[2,2,24,3968]{3,2,0,1:T(8,128)(2,1)S(1)}, u32[]{:S(2)}, u32[]{:S(2)}) collective-permute-start(bf16[2,2,24,3968]{3,2,0,1:T(8,128)(2,1)S(1)} %bitcast.334), channel_id=1, source_target_pairs={{0,2},{1,3},{2,0},{3,1},{4,6},{5,7},{6,4},{7,5},{8,10},{9,11},{10,... | collective-permute-start | bytes 2285576 | tf_op jit(solution)/shard_map/ppermute | solution.py:204
  276.1 29.5 %collective-permute-start.51 = (bf16[96,768]{1,0:T(8,128)(2,1)S(1)}, bf16[96,768]{1,0:T(8,128)(2,1)S(1)}, u32[]{:S(2)}, u32[]{:S(2)}) collective-permute-start(bf16[96,768]{1,0:T(8,128)(2,1)S(1)} %get-tuple-element.299), channel_id=1, source_target_pairs={{0,8},{1,9},{2,10},{3,11},{4,12},{5,13},{6,14},{7,15},{8,0},{9,1},... | collective-permute-start | bytes 442376 | tf_op jit(solution)/shard_map/ppermute | solution.py:204
  277.2 28.5 %collective-permute-start.52 = (bf16[96,768]{1,0:T(8,128)(2,1)S(1)}, bf16[96,768]{1,0:T(8,128)(2,1)}, u32[]{:S(2)}, u32[]{:S(2)}) collective-permute-start(bf16[96,768]{1,0:T(8,128)(2,1)S(1)} %get-tuple-element.300), channel_id=1, source_target_pairs={{0,16},{1,17},{2,18},{3,19},{4,20},{5,21},{6,22},{7,23},{8,24},{9,... | collective-permute-start | bytes 442376 | tf_op jit(solution)/shard_map/ppermute | solution.py:204
  279.3 26.4 %collective-permute-start.53 = (bf16[96,768]{1,0:T(8,128)(2,1)S(1)}, bf16[96,768]{1,0:T(8,128)(2,1)}, u32[]{:S(2)}, u32[]{:S(2)}) collective-permute-start(bf16[96,768]{1,0:T(8,128)(2,1)S(1)} %get-tuple-element.301), channel_id=1, source_target_pairs={{0,24},{1,25},{2,26},{3,27},{4,28},{5,29},{6,30},{7,31},{8,16},{9,... | collective-permute-start | bytes 442376 | tf_op jit(solution)/shard_map/ppermute | solution.py:204
  344.0 16.8 %collective-permute-start.63 = (bf16[24,3968]{1,0:T(8,128)(2,1)S(1)}, bf16[24,3968]{1,0:T(8,128)(2,1)S(1)}, u32[]{:S(2)}, u32[]{:S(2)}) collective-permute-start(bf16[24,3968]{1,0:T(8,128)(2,1)S(1)} %get-tuple-element.321), channel_id=1, source_target_pairs={{0,16},{1,17},{2,18},{3,19},{4,20},{5,21},{6,22},{7,23},{8,24},{9,... | collective-permute-start | bytes 571400 | tf_op jit(solution)/shard_map/ppermute | solution.py:204
  (97 other events, 784.0 us)

commit v10 on v8

--- a/solution.py
+++ b/solution.py
@@ -198,6 +198,60 @@
             transcendentals=2 * rows * inner,
         ),
     )(x, weight, bias)
+
+
+def second_norm_kernel(
+    active_ref, weight_ref, first_ref, cot_ref, rows_ref, out_ref, grad_ref, low_ref, sums_ref
+):
+    bias, gain, shift = rows_ref[0:1, :], rows_ref[1:2, :], rows_ref[2:3, :]
+    value = first_ref[...].astype(F32) + (nn(active_ref[...], weight_ref[...]) + bias)
+    centered = value - jnp.mean(value, -1, keepdims=True)
+    scale = lax.rsqrt(jnp.mean(centered * centered, -1, keepdims=True) + 1e-12)
+    normal = centered * scale
+    out_ref[...] = (normal * gain + shift).astype(BF)
+    cot = cot_ref[...].astype(F32)
+    scaled = cot * gain
+    inner = jnp.mean(scaled * normal, -1, keepdims=True)
+    grad = scale * (scaled - jnp.mean(scaled, -1, keepdims=True) - normal * inner)
+    low = grad.astype(BF)
+    grad_ref[...] = grad
+    low_ref[...] = low
+
+    @pl.when(pl.program_id(0) == 0)
+    def _():
+        sums_ref[...] = jnp.zeros_like(sums_ref)
+
+    sums_ref[0:1, :] += jnp.sum(low.astype(F32), 0, keepdims=True)
+    sums_ref[1:2, :] += jnp.sum(cot * normal, 0, keepdims=True)
+    sums_ref[2:3, :] += jnp.sum(cot, 0, keepdims=True)
+
+
+def second_norm(active, weight, first, cot, bias, gain, shift):
+    rows, inner = active.shape
+    width = weight.shape[1]
+    block = 256
+    side = jnp.stack([bias, gain, shift] + [jnp.zeros_like(bias)] * 5)
+    tile = lambda size: pl.BlockSpec((block, size), lambda i: (i, 0))
+    whole = lambda count: pl.BlockSpec((count, width), lambda i: (0, 0))
+    return pl.pallas_call(
+        second_norm_kernel,
+        grid=(rows // block,),
+        in_specs=[tile(inner), whole(inner), tile(width), tile(width), whole(8)],
+        out_specs=[tile(width), tile(width), tile(width), whole(8)],
+        out_shape=[
+            jax.ShapeDtypeStruct((rows, width), BF),
+            jax.ShapeDtypeStruct((rows, width), F32),
+            jax.ShapeDtypeStruct((rows, width), BF),
+            jax.ShapeDtypeStruct((8, width), F32),
+        ],
+        compiler_params=pltpu.CompilerParams(vmem_limit_bytes=48 * 2**20),
+        name="second_norm",
+        cost_estimate=pl.CostEstimate(
+            flops=2 * rows * width * inner,
+            bytes_accessed=2 * (rows * inner + inner * width) + 12 * rows * width,
+            transcendentals=rows,
+        ),
+    )(active, weight, first, cot, side)
 
 
 def swap(block, distance, devices):
@@ -505,17 +559,18 @@
     qkv_gather.along_z()
     fence([qkv_gather])
     qkv_gather.first()
-    fence([qkv_gather, flat])
+    in_gather.put([after(a, qkv_gather.held[1]) for a in in_gather.arrays()])
+    in_gather.along_z()
+    in_gather.held[:2] = fence([qkv_gather, flat], *in_gather.held[:2])
     qkv_gather.second()
-    in_gather.put([after(a, qkv_gather.held[0]) for a in in_gather.arrays()])
-    in_gather.along_z()
-    fence([qkv_gather])
+    fence([qkv_gather, in_gather])
     qkv_gather.core()
     fence([qkv_gather])
+    in_gather.first()
     flat = flat.finish()
     wide_qkv, early = qkv_gather.finish([(0, 3 * width), (3 * width, early.shape[1])])
     (wide_qkv, early, flat) = fence([in_gather], wide_qkv, early, flat)
-    in_gather.first()
+    in_gather.second()
     wide_qkv = wide_qkv.reshape(width, 3 * width)
     full_query_bias, full_value_bias = [
         v.reshape(-1).astype(F32) for v in unpack_rows(early, [share, share])
@@ -523,8 +578,7 @@
     bias_vector = jnp.concatenate([full_query_bias, jnp.zeros((width,), F32), full_value_bias])
     packed = jnp.dot(flat, wide_qkv, preferred_element_type=F32) + pair_major(bias_vector)
     packed = packed.astype(BF)
-    (packed,) = fence([in_gather], packed)
-    in_gather.second()
+    (packed,) = fence([], packed)
     down_gather.put([after(a, packed) for a in down_gather.arrays()])
     down_gather.along_z()
     mine = lax.dynamic_slice(lengths, (seat * kept,), (kept,))
@@ -570,23 +624,14 @@
     (active_low, slope) = fence([down_gather, cot], active_low, slope)
     (wide_down,) = down_gather.finish()
     wide_down = wide_down.reshape(inner_width, width)
-    branch_two = jnp.dot(active_low, wide_down, preferred_element_type=F32) + full_down_bias
-    result, norm_two_pull = jax.vjp(
-        layer_norm, first_low.astype(F32) + branch_two, gain_two, shift_two
-    )
-    outputs = result.astype(BF).reshape(kept, members, local_len, width)
-    grad_second, grad_gain_two, grad_shift_two = norm_two_pull(cot.finish().astype(F32))
-    grad_branch_two = grad_second.astype(BF)
-    grad_down_bias = jnp.sum(grad_branch_two.astype(F32), 0)
-    (outputs, grad_second, grad_branch_two, grad_gain_two, grad_shift_two, grad_down_bias) = fence(
-        [],
-        outputs,
-        grad_second,
-        grad_branch_two,
-        grad_gain_two,
-        grad_shift_two,
-        grad_down_bias,
-    )
+    outputs, grad_second, grad_branch_two, norm_sums = second_norm(
+        active_low, wide_down, first_low, cot.finish(), full_down_bias, gain_two, shift_two
+    )
+    (outputs, grad_second, grad_branch_two, norm_sums) = fence(
+        [], outputs, grad_second, grad_branch_two, norm_sums
+    )
+    outputs = outputs.reshape(kept, members, local_len, width)
+    grad_down_bias, grad_gain_two, grad_shift_two = (norm_sums[i] for i in range(3))
     outputs = ToPositions(outputs, members, devices)
     for k in near:
         outputs.send(k)
@@ -651,8 +696,12 @@
     in_scatter.along_z()
     fence([qkv_scatter, grad_inputs])
     qkv_scatter.second()
+    for k in near:
+        grad_inputs.send(k)
+    for k in far[:1]:
+        grad_inputs.send(k)
     fence([qkv_scatter, grad_inputs, in_scatter])
-    for k in range(1, members):
+    for k in far[1:]:
         grad_inputs.send(k)
     qkv_scatter.along_z()
     outputs.put([after(a, *qkv_scatter.held[:1]) for a in outputs.arrays()])

time: 385 us -> 378 us (0.982)
  other arithmetic: 40 us -> 28.1 us
  Pallas kernels: 72 us -> 83.6 us
  starting transfers between devices: 70.4 us -> 66.2 us
    reduce_sum x4 -> x0, other arithmetic: 12.3 us -> none  [the longest x3 7.88 us: layer_norm(): return centered * lax.rsqrt(spread + 1e-12) * gain + shift]
    pallas_call x0 -> x1, Pallas kernels: none -> 12.2 us  [second_norm(): pl.pallas_call(second_norm_kernel, grid=(rows // block,), in_specs=[tile(...]
    dot_general x1 -> x0, matrix products: 5.27 us -> none  [on_device(): jnp.dot(active_low, wide_down, preferred_element_type=F32) + full_down_bias]
    ppermute x70, starting transfers between devices: 70.4 us -> 66.2 us  [swap(): lax.ppermute(block, BOTH, [(i, i ^ distance) for i in range(devices)])]
    reshape x9 -> x6, local copies, waits for them, and re-layouts: 4.65 us -> 0.53 us  [on_device(): v.reshape(devices, -1)]
    unnamed x116 -> x114, local copies, waits for them, and re-layouts: 13.1 us -> 13.1 us
  transfers between devices with their start and end apart: 70 -> 70, of which waited for: 21 -> 24; matrix products, arithmetic and copies ran while one was open for 28% -> 29% of each run, Pallas kernels for 17% -> 18%
where the time goes in v10:
time: 378 us; the launch traced here: 374 us
  Pallas kernels  83.6 us (22%)
  waiting for transfers between devices  82.7 us (22%)
  starting transfers between devices  66.2 us (18%)
  matrix products  63.5 us (17%)
  local copies, waits for them, and re-layouts  47.6 us (13%)
  other arithmetic  28.1 us (7%)
    ppermute x70, waiting for transfers between devices, swap(): lax.ppermute(block, BOTH, [(i, i ^ distance) for i in range(devices)])  82.7 us
    ppermute x70, starting transfers between devices, swap(): lax.ppermute(block, BOTH, [(i, i ^ distance) for i in range(devices)])  66.2 us
    dot_general x4, matrix products, times_transposed(): lax.dot_general(left, right, (((1,), (1,)), ((), ())), preferred_element_...  27.3 us
    pallas_call x1, Pallas kernels, attention_backward(): pl.pallas_call(backward_kernel, grid=(seqs, pairs), in_specs=[block(384),...  24.7 us
    dot_general x4, matrix products, over_rows(): lax.dot_general(left, right, (((0,), (0,)), ((), ())), preferred_element_...  23.9 us
    pallas_call x1, Pallas kernels, attention_forward(): pl.pallas_call(forward_kernel, grid=(seqs, pairs), in_specs=[block(384),...  17 us
    pallas_call x5, Pallas kernels, place(): pl.pallas_call(functools.partial(place_kernel, ids, counts, spans), in_sp...  14.9 us
    pallas_call x1, Pallas kernels, feed_forward(): pl.pallas_call(functools.partial(feed_forward_kernel, 512), grid=(rows //...  14.8 us
  transfers between devices with their start and end apart: 70, of which 24 were waited for; matrix products, arithmetic and copies ran while one was open for 29% of the time, Pallas kernels for 18%

profile of v10, /device:TPU:0, one launch (start us, length us, event | category | flops | bytes accessed | tf_op | source)
XLA Modules:
  0.0 374.0 jit_solution(1276125111797925007)
XLA Ops:
  12.7 5.0 %collective-permute-done.1 = bf16[1,24,2432]{2,1,0:T(8,128)(2,1)S(1)} collective-permute-done((bf16[1,24,2432]{2,1,0:T(8,128)(2,1)S(1)}, bf16[1,24,2432]{2,1,0:T(8,128)(2,1)S(1)}, u32[]{:S(2)}, u32[]{:S(2)}) %collective-permute-start.1) | collective-permute-done | bytes 116768 | tf_op jit(solution)/shard_map/ppermute | solution.py:258
  26.0 9.6 %collective-permute-done.4 = bf16[2,24,2432]{2,1,0:T(8,128)(2,1)S(1)} collective-permute-done((bf16[2,24,2432]{2,1,0:T(8,128)(2,1)S(1)}, bf16[2,24,2432]{2,1,0:T(8,128)(2,1)S(1)}, u32[]{:S(2)}, u32[]{:S(2)}) %collective-permute-start.4) | collective-permute-done | bytes 233504 | tf_op jit(solution)/shard_map/ppermute | solution.py:258
  43.4 12.4 %collective-permute-done.11 = bf16[1,24,3968]{2,1,0:T(8,128)(2,1)S(1)} collective-permute-done((bf16[1,24,3968]{2,1,0:T(8,128)(2,1)S(1)}, bf16[1,24,3968]{2,1,0:T(8,128)(2,1)S(1)}, u32[]{:S(2)}, u32[]{:S(2)}) %collective-permute-start.11) | collective-permute-done | bytes 190496 | tf_op jit(solution)/shard_map/ppermute | solution.py:258
  66.7 4.0 %collective-permute-done.14 = bf16[2,24,3968]{2,1,0:T(8,128)(2,1)} collective-permute-done((bf16[2,24,3968]{2,1,0:T(8,128)(2,1)}, bf16[2,24,3968]{2,1,0:T(8,128)(2,1)}, u32[]{:S(2)}, u32[]{:S(2)}) %collective-permute-start.14) | collective-permute-done | bytes 380960 | tf_op jit(solution)/shard_map/ppermute | solution.py:258
  77.3 8.5 %add_convert_fusion.packed_ref = bf16[1024,2304]{1,0:T(8,128)(2,1)} fusion(bf16[1024,768]{1,0:T(8,128)(2,1)} %bitcast.303, bf16[768,2304]{1,0:T(8,128)(2,1)} %bitcast.283, f32[2304]{0:T(1024)S(1)} %add.424), kind=kOutput, calls=%fused_computation.2 | convolution fusion | flops 3628597248 | bytes 9839616 | tf_op jit(solution)/shard_map/dot_general | solution.py:579
  92.1 17.0 %attention_forward.1 = (bf16[1024,768]{1,0:T(8,128)(2,1)S(1)}, f32[12,2,512]{2,1,0:T(2,128)S(1)}) custom-call(bf16[1024,2304]{1,0:T(8,128)(2,1)} %add_convert_fusion.packed_ref, bf16[2,512,128]{2,1,0:T(8,128)(2,1)S(1)} %broadcast_in_dim.46.mask_ref), custom_call_target="tpu_custom_call" | custom-call | flops 6442450944 | bytes 6291456 | tf_op jit(solution)/shard_map/attention_forward/pallas_call | solution.py:117
  124.0 3.8 %fusion.39 = (f32[1024]{0:T(1024)S(1)}, f32[1024,768]{1,0:T(8,128)S(1)}) fusion(f32[768]{0:T(1024)S(1)} %reshape.402, bf16[1024,768]{1,0:T(8,128)(2,1)} %copy-done.8, bf16[768,768]{1,0:T(8,128)(2,1)} %bitcast.285, bf16[1024,768]{1,0:T(8,128)(2,1)} %bitcast.304), kind=kOutput, calls=%fused_computation.217 | convolution fusion | flops 1211104256 | bytes 7478272 | tf_op jit(solution)/shard_map/dot_general | solution.py:613
  145.2 5.9 %collective-permute-done.37 = bf16[2,128,768]{2,1,0:T(8,128)(2,1)} collective-permute-done((bf16[2,128,768]{2,1,0:T(8,128)(2,1)}, bf16[2,128,768]{2,1,0:T(8,128)(2,1)}, u32[]{:S(2)}, u32[]{:S(2)}) %collective-permute-start.37) | collective-permute-done | bytes 393248 | tf_op jit(solution)/shard_map/ppermute | solution.py:258
  151.4 14.8 %feed_forward.1 = (bf16[1024,3072]{1,0:T(8,128)(2,1)}, bf16[1024,3072]{1,0:T(8,128)(2,1)}) custom-call(bf16[1024,768]{1,0:T(8,128)(2,1)S(1)} %add_convert_fusion.2.x_ref.first_ref, bf16[768,3072]{1,0:T(8,128)(2,1)} %bitcast.281, f32[1,3072]{1,0:T(1,128)S(1)} %reshape.405.b_ref), custom_call_target="tpu_custom_call" | custom-call | flops 4831838208 | bytes 17301504 | tf_op jit(solution)/shard_map/feed_forward/pallas_call | solution.py:183
  168.7 4.0 %place_blocks.7 = bf16[32,96,768]{2,1,0:T(8,128)(2,1)S(1)} custom-call(s32[1]{0:T(128)} %bitcast.17.me_ref, bf16[4,96,768]{2,1,0:T(8,128)(2,1)S(1)} %constant_dynamic-update-slice_fusion.20.refs_0_, bf16[4,96,768]{2,1,0:T(8,128)(2,1)} %collective-permute-done.32.refs_1_, bf16[4,96,768]{2,1,0:T(8,128)(2,1)S(1)} %collective-permute-done.30.refs_2_, ...), custom_call_target="tpu_custom_call" | custom-call | bytes 9437184 | tf_op jit(solution)/shard_map/place_blocks/pallas_call | solution.py:291
  174.9 12.2 %second_norm.1 = (bf16[1024,768]{1,0:T(8,128)(2,1)S(1)}, f32[1024,768]{1,0:T(8,128)}, bf16[1024,768]{1,0:T(8,128)(2,1)S(1)}, f32[8,768]{1,0:T(8,128)S(1)}) custom-call(bf16[1024,3072]{1,0:T(8,128)(2,1)} %get-tuple-element.265.active_ref, bf16[3072,768]{1,0:T(8,128)(2,1)} %bitcast.278, bf16[1024,768]{1,0:T(8,128)(2,1)S(1)} %add_convert_fusion.2.x_ref.first_ref, ...), custom_call_target="tpu_custom_call" | custom-call | flops 4831838208 | bytes 20447232 | tf_op jit(solution)/shard_map/second_norm/pallas_call | solution.py:236
  189.1 8.5 %convolution_convert_fusion.1 = bf16[3072,768]{1,0:T(8,128)(2,1)S(1)} fusion(bf16[1024,3072]{1,0:T(8,128)(2,1)} %get-tuple-element.265.active_ref, bf16[1024,768]{1,0:T(8,128)(2,1)S(1)} %get-tuple-element.285), kind=kOutput, calls=%fused_computation.6 | convolution fusion | flops 4834197504 | bytes 12582912 | tf_op jit(solution)/shard_map/dot_general | solution.py:23
  204.6 9.3 %convert_reduce_fusion = (bf16[3072]{0:T(1024)(128)(2,1)}, bf16[1024,3072]{1,0:T(8,128)(2,1)S(1)}) fusion(bf16[1024,3072]{1,0:T(8,128)(2,1)} %get-tuple-element.286, bf16[1024,768]{1,0:T(8,128)(2,1)} %copy-done.10, bf16[3072,768]{1,0:T(8,128)(2,1)} %bitcast.279), kind=kOutput, calls=%fused_computation | convolution fusion | flops 4847563776 | bytes 18880512 | tf_op jit(solution)/shard_map/dot_general | solution.py:29
  214.0 4.1 %fusion.2 = bf16[16,96,768]{2,1,0:T(8,128)(2,1)S(1)} fusion(bf16[16,96,768]{2,1,0:T(8,128)(2,1)} %collective-permute-done.42, bf16[16,2,96,768]{3,2,1,0:T(8,128)(2,1)S(1)} %bitcast.297, s32[]{:T(128)S(6)} %select_n.257), kind=kLoop, calls=%fused_computation.12 | loop fusion | flops 4718592 | bytes 7077892 | tf_op jit(solution)/shard_map/convert_element_type | solution.py:405
  223.2 7.3 %convolution_convert_fusion = bf16[768,3072]{1,0:T(8,128)(2,1)} fusion(bf16[1024,768]{1,0:T(8,128)(2,1)S(1)} %add_convert_fusion.2.x_ref.first_ref, bf16[1024,3072]{1,0:T(8,128)(2,1)S(1)} %get-tuple-element.292), kind=kOutput, calls=%fused_computation.5 | convolution fusion | flops 4834197504 | bytes 12582912 | tf_op jit(solution)/shard_map/dot_general | solution.py:23
  230.6 4.8 %collective-permute-done.43 = bf16[2,2,96,768]{3,2,0,1:T(8,128)(2,1)} collective-permute-done((bf16[2,2,96,768]{3,2,0,1:T(8,128)(2,1)}, bf16[2,2,96,768]{3,2,0,1:T(8,128)(2,1)}, u32[]{:S(2)}, u32[]{:S(2)}) %collective-permute-start.43) | collective-permute-done | bytes 589856 | tf_op jit(solution)/shard_map/ppermute | solution.py:258
  243.0 10.4 %multiply_reduce_fusion = (bf16[768]{0:T(1024)(128)(2,1)}, f32[1024]{0:T(1024)S(1)}, bf16[768]{0:T(1024)(128)(2,1)}, f32[1024,768]{1,0:T(8,128)S(1)}) fusion(f32[1024,768]{1,0:T(8,128)S(1)} %copy-done.14, f32[1024]{0:T(1024)S(1)} %fusion.29, f32[1024]{0:T(1024)S(1)} %broadcast_multiply_fusion, f32[768]{0:T(1024)S(1)} %reshape.403, ...), kind=kOutput, calls=%fused_computation.17 | convolution fusion | flops 4838913024 | bytes 20465664 | tf_op jit(solution)/shard_map/dot_general | solution.py:29
  274.6 24.7 %attention_backward.1 = (bf16[1024,2304]{1,0:T(8,128)(2,1)}, f32[12,1,384]{2,1,0:T(1,128)S(1)}) custom-call(bf16[1024,2304]{1,0:T(8,128)(2,1)} %add_convert_fusion.packed_ref, bf16[2,512,128]{2,1,0:T(8,128)(2,1)S(1)} %copy-done.2, f32[12,2,512]{2,1,0:T(2,128)S(1)} %copy-done.12, bf16[1024,768]{1,0:T(8,128)(2,1)S(1)} %convolution_convert_fusion.3.grad_ref), custom_call_target="tpu_custom_call" | custom-call | flops 11274289152 | bytes 11010048 | tf_op jit(solution)/shard_map/attention_backward/pallas_call | solution.py:138
  304.1 6.7 %convolution_convert_fusion.2 = bf16[768,2304]{1,0:T(8,128)(2,1)S(1)} fusion(bf16[1024,768]{1,0:T(8,128)(2,1)} %bitcast.305, bf16[1024,2304]{1,0:T(8,128)(2,1)} %get-tuple-element.311), kind=kOutput, calls=%fused_computation.7 | convolution fusion | flops 3625648128 | bytes 9830400 | tf_op jit(solution)/shard_map/dot_general | solution.py:23
  313.9 6.2 %add_convert_fusion.1 = bf16[1024,768]{1,0:T(8,128)(2,1)S(1)} fusion(f32[1024,768]{1,0:T(8,128)S(1)} %copy-done.18, bf16[1024,2304]{1,0:T(8,128)(2,1)} %get-tuple-element.311, bf16[768,2304]{1,0:T(8,128)(2,1)S(1)} %bitcast.284), kind=kOutput, calls=%fused_computation.16 | convolution fusion | flops 3625451520 | bytes 12976128 | tf_op jit(solution)/shard_map/dot_general | solution.py:29
  336.2 4.6 %collective-permute-done.59 = bf16[2,24,2432]{2,1,0:T(8,128)(2,1)S(1)} collective-permute-done((bf16[2,24,2432]{2,1,0:T(8,128)(2,1)S(1)}, bf16[2,24,2432]{2,1,0:T(8,128)(2,1)S(1)}, u32[]{:S(2)}, u32[]{:S(2)}) %collective-permute-start.59) | collective-permute-done | bytes 233504 | tf_op jit(solution)/shard_map/ppermute | solution.py:258
  343.1 9.4 %collective-permute-done.62.refs_2_ = bf16[1,2,128,768]{3,2,1,0:T(8,128)(2,1)S(1)} collective-permute-done((bf16[1,2,128,768]{3,2,1,0:T(8,128)(2,1)S(1)}, bf16[1,2,128,768]{3,2,1,0:T(8,128)(2,1)S(1)}, u32[]{:S(2)}, u32[]{:S(2)}) %collective-permute-start.62) | collective-permute-done | bytes 393248 | tf_op jit(solution)/shard_map/ppermute | solution.py:258
  358.9 4.4 %collective-permute-done.67 = bf16[24,2432]{1,0:T(8,128)(2,1)S(1)} collective-permute-done((bf16[24,2432]{1,0:T(8,128)(2,1)S(1)}, bf16[24,2432]{1,0:T(8,128)(2,1)S(1)}, u32[]{:S(2)}, u32[]{:S(2)}) %collective-permute-start.67) | collective-permute-done | bytes 116768 | tf_op jit(solution)/shard_map/ppermute | solution.py:258
  363.4 4.5 %collective-permute-done.69.refs_3_ = bf16[1,2,128,768]{3,2,1,0:T(8,128)(2,1)S(1)} collective-permute-done((bf16[1,2,128,768]{3,2,1,0:T(8,128)(2,1)S(1)}, bf16[1,2,128,768]{3,2,1,0:T(8,128)(2,1)S(1)}, u32[]{:S(2)}, u32[]{:S(2)}) %collective-permute-start.69) | collective-permute-done | bytes 393248 | tf_op jit(solution)/shard_map/ppermute | solution.py:258
  (388 shorter events, 169.5 us)
Async XLA Ops:
  10.6 25.0 %collective-permute-start.5 = (bf16[2,128,768]{2,1,0:T(8,128)(2,1)S(1)}, bf16[2,128,768]{2,1,0:T(8,128)(2,1)S(1)}, u32[]{:S(2)}, u32[]{:S(2)}) collective-permute-start(bf16[2,128,768]{2,1,0:T(8,128)(2,1)S(1)} %get-tuple-element.403), channel_id=1, source_target_pairs={{0,1},{1,0},{2,3},{3,2},{4,5},{5,4},{6,7},{7,6},{8,9},{9,8},{10,11... | collective-permute-start | bytes 1179656 | tf_op jit(solution)/shard_map/ppermute | solution.py:258
  10.6 25.0 %collective-permute-start.6 = (bf16[2,128,768]{2,1,0:T(8,128)(2,1)S(1)}, bf16[2,128,768]{2,1,0:T(8,128)(2,1)S(1)}, u32[]{:S(2)}, u32[]{:S(2)}) collective-permute-start(bf16[2,128,768]{2,1,0:T(8,128)(2,1)S(1)} %get-tuple-element.402), channel_id=1, source_target_pairs={{0,2},{1,3},{2,0},{3,1},{4,6},{5,7},{6,4},{7,5},{8,10},{9,11},{10,... | collective-permute-start | bytes 1179656 | tf_op jit(solution)/shard_map/ppermute | solution.py:258
  12.5 23.1 %collective-permute-start.7 = (bf16[2,128,768]{2,1,0:T(8,128)(2,1)S(1)}, bf16[2,128,768]{2,1,0:T(8,128)(2,1)S(1)}, u32[]{:S(2)}, u32[]{:S(2)}) collective-permute-start(bf16[2,128,768]{2,1,0:T(8,128)(2,1)S(1)} %get-tuple-element.401), channel_id=1, source_target_pairs={{0,3},{1,2},{2,1},{3,0},{4,7},{5,6},{6,5},{7,4},{8,11},{9,10},{10,... | collective-permute-start | bytes 1179656 | tf_op jit(solution)/shard_map/ppermute | solution.py:258
  36.5 19.4 %collective-permute-start.9 = (bf16[4,24,2432]{2,1,0:T(8,128)(2,1)S(1)}, bf16[4,24,2432]{2,1,0:T(8,128)(2,1)S(1)}, u32[]{:S(2)}, u32[]{:S(2)}) collective-permute-start(bf16[4,24,2432]{2,1,0:T(8,128)(2,1)S(1)} %constant_dynamic-update-slice_fusion.4.refs_0_), channel_id=1, source_target_pairs={{0,2},{1,3},{2,0},{3,1},{4,6},{5,7},{6,4},{7,5},{8,10},{9,11},{10,... | collective-permute-start | bytes 1400840 | tf_op jit(solution)/shard_map/ppermute | solution.py:258
  38.3 17.6 %collective-permute-start.10 = (bf16[4,24,2432]{2,1,0:T(8,128)(2,1)S(1)}, bf16[4,24,2432]{2,1,0:T(8,128)(2,1)S(1)}, u32[]{:S(2)}, u32[]{:S(2)}) collective-permute-start(bf16[4,24,2432]{2,1,0:T(8,128)(2,1)S(1)} %constant_dynamic-update-slice_fusion.6.refs_4_), channel_id=1, source_target_pairs={{0,4},{1,5},{2,6},{3,7},{4,0},{5,1},{6,2},{7,3},{8,12},{9,13},{10,... | collective-permute-start | bytes 1400840 | tf_op jit(solution)/shard_map/ppermute | solution.py:258
  72.8 36.5 %collective-permute-start.19 = (bf16[4,24,3968]{2,1,0:T(8,128)(2,1)S(1)}, bf16[4,24,3968]{2,1,0:T(8,128)(2,1)S(1)}, u32[]{:S(2)}, u32[]{:S(2)}) collective-permute-start(bf16[4,24,3968]{2,1,0:T(8,128)(2,1)S(1)} %constant_dynamic-update-slice_fusion.12.refs_0_), channel_id=1, source_target_pairs={{0,2},{1,3},{2,0},{3,1},{4,6},{5,7},{6,4},{7,5},{8,10},{9,11},{10,... | collective-permute-start | bytes 2285576 | tf_op jit(solution)/shard_map/ppermute | solution.py:258
  75.4 33.8 %collective-permute-start.20 = (bf16[4,24,3968]{2,1,0:T(8,128)(2,1)S(1)}, bf16[4,24,3968]{2,1,0:T(8,128)(2,1)S(1)}, u32[]{:S(2)}, u32[]{:S(2)}) collective-permute-start(bf16[4,24,3968]{2,1,0:T(8,128)(2,1)S(1)} %constant_dynamic-update-slice_fusion.14.refs_4_), channel_id=1, source_target_pairs={{0,4},{1,5},{2,6},{3,7},{4,0},{5,1},{6,2},{7,3},{8,12},{9,13},{10,... | collective-permute-start | bytes 2285576 | tf_op jit(solution)/shard_map/ppermute | solution.py:258
  85.8 23.4 %collective-permute-start.21 = (bf16[1,96,768]{2,1,0:T(8,128)(2,1)S(1)}, bf16[1,96,768]{2,1,0:T(8,128)(2,1)S(1)}, u32[]{:S(2)}, u32[]{:S(2)}) collective-permute-start(bf16[1,96,768]{2,1,0:T(8,128)(2,1)S(1)} %bitcast.324), channel_id=1, source_target_pairs={{0,8},{1,9},{2,10},{3,11},{4,12},{5,13},{6,14},{7,15},{8,0},{9,1},... | collective-permute-start | bytes 442376 | tf_op jit(solution)/shard_map/ppermute | solution.py:258
  89.3 19.9 %collective-permute-start.22 = (bf16[1,96,768]{2,1,0:T(8,128)(2,1)S(1)}, bf16[1,96,768]{2,1,0:T(8,128)(2,1)S(1)}, u32[]{:S(2)}, u32[]{:S(2)}) collective-permute-start(bf16[1,96,768]{2,1,0:T(8,128)(2,1)S(1)} %bitcast.325), channel_id=1, source_target_pairs={{0,16},{1,17},{2,18},{3,19},{4,20},{5,21},{6,22},{7,23},{8,24},{9,... | collective-permute-start | bytes 442376 | tf_op jit(solution)/shard_map/ppermute | solution.py:258
  90.4 18.8 %collective-permute-start.23 = (bf16[1,96,768]{2,1,0:T(8,128)(2,1)S(1)}, bf16[1,96,768]{2,1,0:T(8,128)(2,1)S(1)}, u32[]{:S(2)}, u32[]{:S(2)}) collective-permute-start(bf16[1,96,768]{2,1,0:T(8,128)(2,1)S(1)} %bitcast.326), channel_id=1, source_target_pairs={{0,24},{1,25},{2,26},{3,27},{4,28},{5,29},{6,30},{7,31},{8,16},{9,... | collective-permute-start | bytes 442376 | tf_op jit(solution)/shard_map/ppermute | solution.py:258
  140.2 26.0 %collective-permute-start.32 = (bf16[4,96,768]{2,1,0:T(8,128)(2,1)S(1)}, bf16[4,96,768]{2,1,0:T(8,128)(2,1)}, u32[]{:S(2)}, u32[]{:S(2)}) collective-permute-start(bf16[4,96,768]{2,1,0:T(8,128)(2,1)S(1)} %constant_dynamic-update-slice_fusion.20.refs_0_), channel_id=1, source_target_pairs={{0,1},{1,0},{2,3},{3,2},{4,5},{5,4},{6,7},{7,6},{8,9},{9,8},{10,11... | collective-permute-start | bytes 1769480 | tf_op jit(solution)/shard_map/ppermute | solution.py:258
  140.4 25.8 %collective-permute-start.33 = (bf16[4,96,768]{2,1,0:T(8,128)(2,1)S(1)}, bf16[4,96,768]{2,1,0:T(8,128)(2,1)}, u32[]{:S(2)}, u32[]{:S(2)}) collective-permute-start(bf16[4,96,768]{2,1,0:T(8,128)(2,1)S(1)} %collective-permute-done.30.refs_2_), channel_id=1, source_target_pairs={{0,1},{1,0},{2,3},{3,2},{4,5},{5,4},{6,7},{7,6},{8,9},{9,8},{10,11... | collective-permute-start | bytes 1769480 | tf_op jit(solution)/shard_map/ppermute | solution.py:258
  140.7 25.5 %collective-permute-start.34 = (bf16[4,96,768]{2,1,0:T(8,128)(2,1)S(1)}, bf16[4,96,768]{2,1,0:T(8,128)(2,1)}, u32[]{:S(2)}, u32[]{:S(2)}) collective-permute-start(bf16[4,96,768]{2,1,0:T(8,128)(2,1)S(1)} %constant_dynamic-update-slice_fusion.22.refs_4_), channel_id=1, source_target_pairs={{0,1},{1,0},{2,3},{3,2},{4,5},{5,4},{6,7},{7,6},{8,9},{9,8},{10,11... | collective-permute-start | bytes 1769480 | tf_op jit(solution)/shard_map/ppermute | solution.py:258
  141.1 25.1 %collective-permute-start.35 = (bf16[4,96,768]{2,1,0:T(8,128)(2,1)}, bf16[4,96,768]{2,1,0:T(8,128)(2,1)}, u32[]{:S(2)}, u32[]{:S(2)}) collective-permute-start(bf16[4,96,768]{2,1,0:T(8,128)(2,1)} %collective-permute-done.31.refs_6_), channel_id=1, source_target_pairs={{0,1},{1,0},{2,3},{3,2},{4,5},{5,4},{6,7},{7,6},{8,9},{9,8},{10,11... | collective-permute-start | bytes 1769480 | tf_op jit(solution)/shard_map/ppermute | solution.py:258
  239.8 24.3 %collective-permute-start.45 = (bf16[2,96,768]{2,1,0:T(8,128)(2,1)}, bf16[2,96,768]{2,1,0:T(8,128)(2,1)S(1)}, u32[]{:S(2)}, u32[]{:S(2)}) collective-permute-start(bf16[2,96,768]{2,1,0:T(8,128)(2,1)} %dynamic-slice_bitcast_fusion.17), channel_id=1, source_target_pairs={{0,2},{1,3},{2,0},{3,1},{4,6},{5,7},{6,4},{7,5},{8,10},{9,11},{10,... | collective-permute-start | bytes 884744 | tf_op jit(solution)/shard_map/ppermute | solution.py:258
  241.3 23.7 %collective-permute-start.46 = (bf16[2,96,768]{2,1,0:T(8,128)(2,1)}, bf16[2,96,768]{2,1,0:T(8,128)(2,1)}, u32[]{:S(2)}, u32[]{:S(2)}) collective-permute-start(bf16[2,96,768]{2,1,0:T(8,128)(2,1)} %dynamic-slice_bitcast_fusion.16), channel_id=1, source_target_pairs={{0,4},{1,5},{2,6},{3,7},{4,0},{5,1},{6,2},{7,3},{8,12},{9,13},{10,... | collective-permute-start | bytes 884744 | tf_op jit(solution)/shard_map/ppermute | solution.py:258
  268.4 30.8 %collective-permute-start.49 = (bf16[2,2,24,3968]{3,2,0,1:T(8,128)(2,1)S(1)}, bf16[2,2,24,3968]{3,2,0,1:T(8,128)(2,1)S(1)}, u32[]{:S(2)}, u32[]{:S(2)}) collective-permute-start(bf16[2,2,24,3968]{3,2,0,1:T(8,128)(2,1)S(1)} %bitcast.318), channel_id=1, source_target_pairs={{0,4},{1,5},{2,6},{3,7},{4,0},{5,1},{6,2},{7,3},{8,12},{9,13},{10,... | collective-permute-start | bytes 2285576 | tf_op jit(solution)/shard_map/ppermute | solution.py:258
  268.8 30.6 %collective-permute-start.50 = (bf16[2,2,24,3968]{3,2,0,1:T(8,128)(2,1)S(1)}, bf16[2,2,24,3968]{3,2,0,1:T(8,128)(2,1)S(1)}, u32[]{:S(2)}, u32[]{:S(2)}) collective-permute-start(bf16[2,2,24,3968]{3,2,0,1:T(8,128)(2,1)S(1)} %bitcast.317), channel_id=1, source_target_pairs={{0,2},{1,3},{2,0},{3,1},{4,6},{5,7},{6,4},{7,5},{8,10},{9,11},{10,... | collective-permute-start | bytes 2285576 | tf_op jit(solution)/shard_map/ppermute | solution.py:258
  270.2 29.4 %collective-permute-start.51 = (bf16[96,768]{1,0:T(8,128)(2,1)}, bf16[96,768]{1,0:T(8,128)(2,1)S(1)}, u32[]{:S(2)}, u32[]{:S(2)}) collective-permute-start(bf16[96,768]{1,0:T(8,128)(2,1)} %get-tuple-element.298), channel_id=1, source_target_pairs={{0,8},{1,9},{2,10},{3,11},{4,12},{5,13},{6,14},{7,15},{8,0},{9,1},... | collective-permute-start | bytes 442376 | tf_op jit(solution)/shard_map/ppermute | solution.py:258
  271.1 28.6 %collective-permute-start.52 = (bf16[96,768]{1,0:T(8,128)(2,1)}, bf16[96,768]{1,0:T(8,128)(2,1)}, u32[]{:S(2)}, u32[]{:S(2)}) collective-permute-start(bf16[96,768]{1,0:T(8,128)(2,1)} %get-tuple-element.299), channel_id=1, source_target_pairs={{0,16},{1,17},{2,18},{3,19},{4,20},{5,21},{6,22},{7,23},{8,24},{9,... | collective-permute-start | bytes 442376 | tf_op jit(solution)/shard_map/ppermute | solution.py:258
  273.2 26.5 %collective-permute-start.53 = (bf16[96,768]{1,0:T(8,128)(2,1)}, bf16[96,768]{1,0:T(8,128)(2,1)}, u32[]{:S(2)}, u32[]{:S(2)}) collective-permute-start(bf16[96,768]{1,0:T(8,128)(2,1)} %get-tuple-element.300), channel_id=1, source_target_pairs={{0,24},{1,25},{2,26},{3,27},{4,28},{5,29},{6,30},{7,31},{8,16},{9,... | collective-permute-start | bytes 442376 | tf_op jit(solution)/shard_map/ppermute | solution.py:258
  300.5 19.6 %collective-permute-start.54 = (bf16[2,24,3968]{2,1,0:T(8,128)(2,1)}, bf16[2,24,3968]{2,1,0:T(8,128)(2,1)}, u32[]{:S(2)}, u32[]{:S(2)}) collective-permute-start(bf16[2,24,3968]{2,1,0:T(8,128)(2,1)} %dynamic-slice_bitcast_fusion.15), channel_id=1, source_target_pairs={{0,2},{1,3},{2,0},{3,1},{4,6},{5,7},{6,4},{7,5},{8,10},{9,11},{10,... | collective-permute-start | bytes 1142792 | tf_op jit(solution)/shard_map/ppermute | solution.py:258
  302.0 19.3 %collective-permute-start.55 = (bf16[2,24,3968]{2,1,0:T(8,128)(2,1)}, bf16[2,24,3968]{2,1,0:T(8,128)(2,1)}, u32[]{:S(2)}, u32[]{:S(2)}) collective-permute-start(bf16[2,24,3968]{2,1,0:T(8,128)(2,1)} %dynamic-slice_bitcast_fusion.14), channel_id=1, source_target_pairs={{0,4},{1,5},{2,6},{3,7},{4,0},{5,1},{6,2},{7,3},{8,12},{9,13},{10,... | collective-permute-start | bytes 1142792 | tf_op jit(solution)/shard_map/ppermute | solution.py:258
  326.4 16.6 %collective-permute-start.64 = (bf16[24,3968]{1,0:T(8,128)(2,1)S(1)}, bf16[24,3968]{1,0:T(8,128)(2,1)S(1)}, u32[]{:S(2)}, u32[]{:S(2)}) collective-permute-start(bf16[24,3968]{1,0:T(8,128)(2,1)S(1)} %get-tuple-element.323), channel_id=1, source_target_pairs={{0,16},{1,17},{2,18},{3,19},{4,20},{5,21},{6,22},{7,23},{8,24},{9,... | collective-permute-start | bytes 571400 | tf_op jit(solution)/shard_map/ppermute | solution.py:258
  (93 other events, 832.1 us)

commit v11 on v10

--- a/solution.py
+++ b/solution.py
@@ -561,7 +561,7 @@
     qkv_gather.first()
     in_gather.put([after(a, qkv_gather.held[1]) for a in in_gather.arrays()])
     in_gather.along_z()
-    in_gather.held[:2] = fence([qkv_gather, flat], *in_gather.held[:2])
+    in_gather.held[:3] = fence([qkv_gather, flat], *in_gather.held[:3])
     qkv_gather.second()
     fence([qkv_gather, in_gather])
     qkv_gather.core()
@@ -581,13 +581,18 @@
     (packed,) = fence([], packed)
     down_gather.put([after(a, packed) for a in down_gather.arrays()])
     down_gather.along_z()
+    cot = ToSequences(after(cotangent, packed), seat, members, devices)
+    for k in range(1, members):
+        cot.send(k)
     mine = lax.dynamic_slice(lengths, (seat * kept,), (kept,))
     slots = jnp.arange(length, dtype=jnp.int32)
     positions = ((slots // local_len) ^ seat) * local_len + slots % local_len
     mask = jnp.where(positions[None, :] < mine[:, None], 0.0, -1e30).astype(BF)
     mask = jnp.broadcast_to(mask[:, :, None], (kept, length, 128))
     mixed, logsum = attention_forward(packed, mask, length)
-    (mixed, logsum, packed) = fence([in_gather, down_gather], mixed, logsum, packed)
+    (mixed, logsum, packed) = fence(
+        [in_gather, down_gather, cot], mixed, logsum, packed
+    )
     in_gather.core()
     down_gather.first()
     fence([in_gather])
@@ -617,11 +622,8 @@
     first_low = first.astype(BF)
     (first_low,) = fence([down_gather], first_low)
     down_gather.core()
-    cot = ToSequences(after(cotangent, first_low), seat, members, devices)
-    for k in range(1, members):
-        cot.send(k)
     active_low, slope = feed_forward(first_low, wide_in, full_in_bias[None])
-    (active_low, slope) = fence([down_gather, cot], active_low, slope)
+    (active_low, slope) = fence([down_gather], active_low, slope)
     (wide_down,) = down_gather.finish()
     wide_down = wide_down.reshape(inner_width, width)
     outputs, grad_second, grad_branch_two, norm_sums = second_norm(
@@ -692,14 +694,14 @@
     grad_inputs = ToPositions(
         grad_inputs.reshape(kept, members, local_len, width), members, devices
     )
+    for k in near:
+        grad_inputs.send(k)
+    for k in far[:1]:
+        grad_inputs.send(k)
     qkv_scatter.first()
     in_scatter.along_z()
     fence([qkv_scatter, grad_inputs])
     qkv_scatter.second()
-    for k in near:
-        grad_inputs.send(k)
-    for k in far[:1]:
-        grad_inputs.send(k)
     fence([qkv_scatter, grad_inputs, in_scatter])
     for k in far[1:]:
         grad_inputs.send(k)

time: 378 us -> 387 us (1.024)
  local copies, waits for them, and re-layouts: 47.6 us -> 51.7 us
  waiting for transfers between devices: 82.7 us -> 86.6 us
    ppermute x70, waiting for transfers between devices: 82.7 us -> 86.6 us  [swap(): lax.ppermute(block, BOTH, [(i, i ^ distance) for i in range(devices)])]
    unnamed x114 -> x126, local copies, waits for them, and re-layouts: 13.1 us -> 16.3 us
  transfers between devices with their start and end apart: 70 -> 70, of which waited for: 24 -> 24; matrix products, arithmetic and copies ran while one was open for 29% -> 30% of each run, Pallas kernels for 18% -> 17%
where the time goes in v11:
time: 387 us; the launch traced here: 382 us
  waiting for transfers between devices  86.6 us (22%)
  Pallas kernels  83.7 us (22%)
  starting transfers between devices  66.1 us (17%)
  matrix products  63.4 us (16%)
  local copies, waits for them, and re-layouts  51.7 us (13%)
  other arithmetic  28.4 us (7%)
    ppermute x70, waiting for transfers between devices, swap(): lax.ppermute(block, BOTH, [(i, i ^ distance) for i in range(devices)])  86.6 us
    ppermute x70, starting transfers between devices, swap(): lax.ppermute(block, BOTH, [(i, i ^ distance) for i in range(devices)])  66.1 us
    dot_general x4, matrix products, times_transposed(): lax.dot_general(left, right, (((1,), (1,)), ((), ())), preferred_element_...  27.1 us
    pallas_call x1, Pallas kernels, attention_backward(): pl.pallas_call(backward_kernel, grid=(seqs, pairs), in_specs=[block(384),...  24.7 us
    dot_general x4, matrix products, over_rows(): lax.dot_general(left, right, (((0,), (0,)), ((), ())), preferred_element_...  23.9 us
    pallas_call x1, Pallas kernels, attention_forward(): pl.pallas_call(forward_kernel, grid=(seqs, pairs), in_specs=[block(384),...  17 us
    unnamed x126, local copies, waits for them, and re-layouts  16.3 us
    pallas_call x5, Pallas kernels, place(): pl.pallas_call(functools.partial(place_kernel, ids, counts, spans), in_sp...  15.1 us
  transfers between devices with their start and end apart: 70, of which 24 were waited for; matrix products, arithmetic and copies ran while one was open for 30% of the time, Pallas kernels for 17%

profile of v11, /device:TPU:0, one launch (start us, length us, event | category | flops | bytes accessed | tf_op | source)
XLA Modules:
  0.0 382.4 jit_solution(9789362408814983769)
XLA Ops:
  12.7 5.0 %collective-permute-done.1 = bf16[1,24,2432]{2,1,0:T(8,128)(2,1)S(1)} collective-permute-done((bf16[1,24,2432]{2,1,0:T(8,128)(2,1)S(1)}, bf16[1,24,2432]{2,1,0:T(8,128)(2,1)S(1)}, u32[]{:S(2)}, u32[]{:S(2)}) %collective-permute-start.1) | collective-permute-done | bytes 116768 | tf_op jit(solution)/shard_map/ppermute | solution.py:258
  26.0 9.6 %collective-permute-done.4 = bf16[2,24,2432]{2,1,0:T(8,128)(2,1)S(1)} collective-permute-done((bf16[2,24,2432]{2,1,0:T(8,128)(2,1)S(1)}, bf16[2,24,2432]{2,1,0:T(8,128)(2,1)S(1)}, u32[]{:S(2)}, u32[]{:S(2)}) %collective-permute-start.4) | collective-permute-done | bytes 233504 | tf_op jit(solution)/shard_map/ppermute | solution.py:258
  37.5 9.4 %collective-permute-done.9 = bf16[1,24,3968]{2,1,0:T(8,128)(2,1)S(1)} collective-permute-done((bf16[1,24,3968]{2,1,0:T(8,128)(2,1)S(1)}, bf16[1,24,3968]{2,1,0:T(8,128)(2,1)S(1)}, u32[]{:S(2)}, u32[]{:S(2)}) %collective-permute-start.9) | collective-permute-done | bytes 190496 | tf_op jit(solution)/shard_map/ppermute | solution.py:258
  53.0 4.9 %collective-permute-done.12 = bf16[1,24,3968]{2,1,0:T(8,128)(2,1)S(1)} collective-permute-done((bf16[1,24,3968]{2,1,0:T(8,128)(2,1)S(1)}, bf16[1,24,3968]{2,1,0:T(8,128)(2,1)S(1)}, u32[]{:S(2)}, u32[]{:S(2)}) %collective-permute-start.12) | collective-permute-done | bytes 190496 | tf_op jit(solution)/shard_map/ppermute | solution.py:258
  72.1 4.0 %collective-permute-done.14 = bf16[2,24,3968]{2,1,0:T(8,128)(2,1)} collective-permute-done((bf16[2,24,3968]{2,1,0:T(8,128)(2,1)}, bf16[2,24,3968]{2,1,0:T(8,128)(2,1)}, u32[]{:S(2)}, u32[]{:S(2)}) %collective-permute-start.14) | collective-permute-done | bytes 380960 | tf_op jit(solution)/shard_map/ppermute | solution.py:258
  81.6 8.6 %add_convert_fusion.packed_ref = bf16[1024,2304]{1,0:T(8,128)(2,1)} fusion(bf16[1024,768]{1,0:T(8,128)(2,1)} %bitcast.303, bf16[768,2304]{1,0:T(8,128)(2,1)} %bitcast.283, f32[2304]{0:T(1024)S(1)} %add.424), kind=kOutput, calls=%fused_computation.2 | convolution fusion | flops 3628597248 | bytes 9839616 | tf_op jit(solution)/shard_map/dot_general | solution.py:579
  97.2 8.2 %collective-permute-done.22 = bf16[1,96,768]{2,1,0:T(8,128)(2,1)S(1)} collective-permute-done((bf16[1,96,768]{2,1,0:T(8,128)(2,1)S(1)}, bf16[1,96,768]{2,1,0:T(8,128)(2,1)S(1)}, u32[]{:S(2)}, u32[]{:S(2)}) %collective-permute-start.22) | collective-permute-done | bytes 147488 | tf_op jit(solution)/shard_map/ppermute | solution.py:258
  107.1 17.0 %attention_forward.1 = (bf16[1024,768]{1,0:T(8,128)(2,1)S(1)}, f32[12,2,512]{2,1,0:T(2,128)S(1)}) custom-call(bf16[1024,2304]{1,0:T(8,128)(2,1)} %add_convert_fusion.packed_ref, bf16[2,512,128]{2,1,0:T(8,128)(2,1)S(1)} %broadcast_in_dim.46.mask_ref), custom_call_target="tpu_custom_call" | custom-call | flops 6442450944 | bytes 6291456 | tf_op jit(solution)/shard_map/attention_forward/pallas_call | solution.py:117
  132.1 3.9 %place_blocks.6 = (bf16[32,24,3072]{2,1,0:T(8,128)(2,1)S(1)}, bf16[32,24,768]{2,1,0:T(8,128)(2,1)S(1)}, bf16[32,24,128]{2,1,0:T(8,128)(2,1)S(1)}) custom-call(s32[1]{0:T(128)} %bitcast.17.me_ref, bf16[4,24,3968]{2,1,0:T(8,128)(2,1)S(1)} %constant_dynamic-update-slice_fusion.12.refs_0_, bf16[4,24,3968]{2,1,0:T(8,128)(2,1)S(1)} %copy-done.2, ...), custom_call_target="tpu_custom_call" | custom-call | bytes 12189696 | tf_op jit(solution)/shard_map/place_blocks/pallas_call | solution.py:291
  145.6 3.8 fusion.39
  166.3 14.8 %feed_forward.1 = (bf16[1024,3072]{1,0:T(8,128)(2,1)}, bf16[1024,3072]{1,0:T(8,128)(2,1)}) custom-call(bf16[1024,768]{1,0:T(8,128)(2,1)S(1)} %add_convert_fusion.2.x_ref.first_ref, bf16[768,3072]{1,0:T(8,128)(2,1)} %bitcast.281, f32[1,3072]{1,0:T(1,128)S(1)} %reshape.405.b_ref), custom_call_target="tpu_custom_call" | custom-call | flops 4831838208 | bytes 17301504 | tf_op jit(solution)/shard_map/feed_forward/pallas_call | solution.py:183
  181.1 4.0 %place_blocks.7 = bf16[32,96,768]{2,1,0:T(8,128)(2,1)S(1)} custom-call(s32[1]{0:T(128)} %bitcast.17.me_ref, bf16[4,96,768]{2,1,0:T(8,128)(2,1)S(1)} %constant_dynamic-update-slice_fusion.20.refs_0_, bf16[4,96,768]{2,1,0:T(8,128)(2,1)} %collective-permute-done.35.refs_1_, bf16[4,96,768]{2,1,0:T(8,128)(2,1)S(1)} %collective-permute-done.33.refs_2_, ...), custom_call_target="tpu_custom_call" | custom-call | bytes 9437184 | tf_op jit(solution)/shard_map/place_blocks/pallas_call | solution.py:291
  187.3 12.1 %second_norm.1 = (bf16[1024,768]{1,0:T(8,128)(2,1)S(1)}, f32[1024,768]{1,0:T(8,128)}, bf16[1024,768]{1,0:T(8,128)(2,1)S(1)}, f32[8,768]{1,0:T(8,128)S(1)}) custom-call(bf16[1024,3072]{1,0:T(8,128)(2,1)} %get-tuple-element.267.active_ref, bf16[3072,768]{1,0:T(8,128)(2,1)} %bitcast.278, bf16[1024,768]{1,0:T(8,128)(2,1)S(1)} %add_convert_fusion.2.x_ref.first_ref, ...), custom_call_target="tpu_custom_call" | custom-call | flops 4831838208 | bytes 20447232 | tf_op jit(solution)/shard_map/second_norm/pallas_call | solution.py:236
  200.2 8.5 %convolution_convert_fusion.1 = bf16[3072,768]{1,0:T(8,128)(2,1)S(1)} fusion(bf16[1024,3072]{1,0:T(8,128)(2,1)} %get-tuple-element.267.active_ref, bf16[1024,768]{1,0:T(8,128)(2,1)S(1)} %get-tuple-element.287), kind=kOutput, calls=%fused_computation.6 | convolution fusion | flops 4834197504 | bytes 12582912 | tf_op jit(solution)/shard_map/dot_general | solution.py:23
  216.3 9.1 %convert_reduce_fusion = (bf16[3072]{0:T(1024)(128)(2,1)}, bf16[1024,3072]{1,0:T(8,128)(2,1)S(1)}) fusion(bf16[1024,3072]{1,0:T(8,128)(2,1)} %get-tuple-element.288, bf16[1024,768]{1,0:T(8,128)(2,1)} %copy-done.12, bf16[3072,768]{1,0:T(8,128)(2,1)} %bitcast.279), kind=kOutput, calls=%fused_computation | convolution fusion | flops 4847563776 | bytes 18880512 | tf_op jit(solution)/shard_map/dot_general | solution.py:29
  225.4 4.1 %fusion.2 = bf16[16,96,768]{2,1,0:T(8,128)(2,1)S(1)} fusion(bf16[16,96,768]{2,1,0:T(8,128)(2,1)} %collective-permute-done.42, bf16[16,2,96,768]{3,2,1,0:T(8,128)(2,1)S(1)} %bitcast.297, s32[]{:T(128)S(6)} %select_n.257), kind=kLoop, calls=%fused_computation.12 | loop fusion | flops 4718592 | bytes 7077892 | tf_op jit(solution)/shard_map/convert_element_type | solution.py:405
  234.9 7.3 %convolution_convert_fusion = bf16[768,3072]{1,0:T(8,128)(2,1)} fusion(bf16[1024,768]{1,0:T(8,128)(2,1)S(1)} %add_convert_fusion.2.x_ref.first_ref, bf16[1024,3072]{1,0:T(8,128)(2,1)S(1)} %get-tuple-element.294), kind=kOutput, calls=%fused_computation.5 | convolution fusion | flops 4834197504 | bytes 12582912 | tf_op jit(solution)/shard_map/dot_general | solution.py:23
  242.3 5.0 %collective-permute-done.43 = bf16[2,2,96,768]{3,2,0,1:T(8,128)(2,1)} collective-permute-done((bf16[2,2,96,768]{3,2,0,1:T(8,128)(2,1)}, bf16[2,2,96,768]{3,2,0,1:T(8,128)(2,1)}, u32[]{:S(2)}, u32[]{:S(2)}) %collective-permute-start.43) | collective-permute-done | bytes 589856 | tf_op jit(solution)/shard_map/ppermute | solution.py:258
  254.3 10.3 %multiply_reduce_fusion = (bf16[768]{0:T(1024)(128)(2,1)}, f32[1024]{0:T(1024)S(1)}, bf16[768]{0:T(1024)(128)(2,1)}, f32[1024,768]{1,0:T(8,128)S(1)}) fusion(f32[1024,768]{1,0:T(8,128)S(1)} %copy-done.16, f32[1024]{0:T(1024)S(1)} %fusion.29, f32[1024]{0:T(1024)S(1)} %broadcast_multiply_fusion, f32[768]{0:T(1024)S(1)} %reshape.403, ...), kind=kOutput, calls=%fused_computation.17 | convolution fusion | flops 4838913024 | bytes 20465664 | tf_op jit(solution)/shard_map/dot_general | solution.py:29
  286.6 24.7 %attention_backward.1 = (bf16[1024,2304]{1,0:T(8,128)(2,1)}, f32[12,1,384]{2,1,0:T(1,128)S(1)}) custom-call(bf16[1024,2304]{1,0:T(8,128)(2,1)} %add_convert_fusion.packed_ref, bf16[2,512,128]{2,1,0:T(8,128)(2,1)S(1)} %copy-done.4, f32[12,2,512]{2,1,0:T(2,128)S(1)} %copy-done.14, bf16[1024,768]{1,0:T(8,128)(2,1)S(1)} %convolution_convert_fusion.3.grad_ref), custom_call_target="tpu_custom_call" | custom-call | flops 11274289152 | bytes 11010048 | tf_op jit(solution)/shard_map/attention_backward/pallas_call | solution.py:138
  315.4 6.7 %convolution_convert_fusion.2 = bf16[768,2304]{1,0:T(8,128)(2,1)S(1)} fusion(bf16[1024,768]{1,0:T(8,128)(2,1)} %bitcast.305, bf16[1024,2304]{1,0:T(8,128)(2,1)} %get-tuple-element.313), kind=kOutput, calls=%fused_computation.7 | convolution fusion | flops 3625648128 | bytes 9830400 | tf_op jit(solution)/shard_map/dot_general | solution.py:23
  325.1 6.2 %add_convert_fusion.1 = bf16[1024,768]{1,0:T(8,128)(2,1)S(1)} fusion(f32[1024,768]{1,0:T(8,128)S(1)} %copy-done.20, bf16[1024,2304]{1,0:T(8,128)(2,1)} %get-tuple-element.313, bf16[768,2304]{1,0:T(8,128)(2,1)S(1)} %bitcast.284), kind=kOutput, calls=%fused_computation.16 | convolution fusion | flops 3625451520 | bytes 12976128 | tf_op jit(solution)/shard_map/dot_general | solution.py:29
  340.0 8.0 %collective-permute-done.58 = bf16[2,2,24,2432]{3,2,1,0:T(8,128)(2,1)S(1)} collective-permute-done((bf16[2,2,24,2432]{3,2,1,0:T(8,128)(2,1)S(1)}, bf16[2,2,24,2432]{3,2,1,0:T(8,128)(2,1)S(1)}, u32[]{:S(2)}, u32[]{:S(2)}) %collective-permute-start.58) | collective-permute-done | bytes 466976 | tf_op jit(solution)/shard_map/ppermute | solution.py:258
  371.7 4.6 %collective-permute-done.69.refs_3_ = bf16[1,2,128,768]{3,2,1,0:T(8,128)(2,1)S(1)} collective-permute-done((bf16[1,2,128,768]{3,2,1,0:T(8,128)(2,1)S(1)}, bf16[1,2,128,768]{3,2,1,0:T(8,128)(2,1)S(1)}, u32[]{:S(2)}, u32[]{:S(2)}) %collective-permute-start.69) | collective-permute-done | bytes 393248 | tf_op jit(solution)/shard_map/ppermute | solution.py:258
  (400 shorter events, 180.1 us)
Async XLA Ops:
  10.6 26.9 %collective-permute-start.5 = (bf16[2,128,768]{2,1,0:T(8,128)(2,1)S(1)}, bf16[2,128,768]{2,1,0:T(8,128)(2,1)S(1)}, u32[]{:S(2)}, u32[]{:S(2)}) collective-permute-start(bf16[2,128,768]{2,1,0:T(8,128)(2,1)S(1)} %get-tuple-element.405), channel_id=1, source_target_pairs={{0,1},{1,0},{2,3},{3,2},{4,5},{5,4},{6,7},{7,6},{8,9},{9,8},{10,11... | collective-permute-start | bytes 1179656 | tf_op jit(solution)/shard_map/ppermute | solution.py:258
  10.6 26.9 %collective-permute-start.6 = (bf16[2,128,768]{2,1,0:T(8,128)(2,1)S(1)}, bf16[2,128,768]{2,1,0:T(8,128)(2,1)S(1)}, u32[]{:S(2)}, u32[]{:S(2)}) collective-permute-start(bf16[2,128,768]{2,1,0:T(8,128)(2,1)S(1)} %get-tuple-element.404), channel_id=1, source_target_pairs={{0,2},{1,3},{2,0},{3,1},{4,6},{5,7},{6,4},{7,5},{8,10},{9,11},{10,... | collective-permute-start | bytes 1179656 | tf_op jit(solution)/shard_map/ppermute | solution.py:258
  12.5 25.0 %collective-permute-start.7 = (bf16[2,128,768]{2,1,0:T(8,128)(2,1)S(1)}, bf16[2,128,768]{2,1,0:T(8,128)(2,1)S(1)}, u32[]{:S(2)}, u32[]{:S(2)}) collective-permute-start(bf16[2,128,768]{2,1,0:T(8,128)(2,1)S(1)} %get-tuple-element.403), channel_id=1, source_target_pairs={{0,3},{1,2},{2,1},{3,0},{4,7},{5,6},{6,5},{7,4},{8,11},{9,10},{10,... | collective-permute-start | bytes 1179656 | tf_op jit(solution)/shard_map/ppermute | solution.py:258
  19.3 16.3 %collective-permute-start.4 = (bf16[2,24,2432]{2,1,0:T(8,128)(2,1)S(1)}, bf16[2,24,2432]{2,1,0:T(8,128)(2,1)S(1)}, u32[]{:S(2)}, u32[]{:S(2)}) collective-permute-start(bf16[2,24,2432]{2,1,0:T(8,128)(2,1)S(1)} %constant_dynamic-update-slice_fusion.2), channel_id=1, source_target_pairs={{0,2},{1,3},{2,0},{3,1},{4,6},{5,7},{6,4},{7,5},{8,10},{9,11},{10,... | collective-permute-start | bytes 700424 | tf_op jit(solution)/shard_map/ppermute | solution.py:258
  78.2 46.1 %collective-permute-start.19 = (bf16[4,24,3968]{2,1,0:T(8,128)(2,1)S(1)}, bf16[4,24,3968]{2,1,0:T(8,128)(2,1)S(1)}, u32[]{:S(2)}, u32[]{:S(2)}) collective-permute-start(bf16[4,24,3968]{2,1,0:T(8,128)(2,1)S(1)} %constant_dynamic-update-slice_fusion.12.refs_0_), channel_id=1, source_target_pairs={{0,2},{1,3},{2,0},{3,1},{4,6},{5,7},{6,4},{7,5},{8,10},{9,11},{10,... | collective-permute-start | bytes 2285576 | tf_op jit(solution)/shard_map/ppermute | solution.py:258
  80.8 43.5 %collective-permute-start.20 = (bf16[4,24,3968]{2,1,0:T(8,128)(2,1)S(1)}, bf16[4,24,3968]{2,1,0:T(8,128)(2,1)S(1)}, u32[]{:S(2)}, u32[]{:S(2)}) collective-permute-start(bf16[4,24,3968]{2,1,0:T(8,128)(2,1)S(1)} %constant_dynamic-update-slice_fusion.14.refs_4_), channel_id=1, source_target_pairs={{0,4},{1,5},{2,6},{3,7},{4,0},{5,1},{6,2},{7,3},{8,12},{9,13},{10,... | collective-permute-start | bytes 2285576 | tf_op jit(solution)/shard_map/ppermute | solution.py:258
  97.2 27.0 %collective-permute-start.24 = (bf16[2,128,768]{2,1,0:T(8,128)(2,1)S(1)}, bf16[2,128,768]{2,1,0:T(8,128)(2,1)S(1)}, u32[]{:S(2)}, u32[]{:S(2)}) collective-permute-start(bf16[2,128,768]{2,1,0:T(8,128)(2,1)S(1)} %get-tuple-element.401), channel_id=1, source_target_pairs={{0,1},{1,0},{2,3},{3,2},{4,5},{5,4},{6,7},{7,6},{8,9},{9,8},{10,11... | collective-permute-start | bytes 1179656 | tf_op jit(solution)/shard_map/ppermute | solution.py:258
  105.4 18.8 %collective-permute-start.25 = (bf16[2,128,768]{2,1,0:T(8,128)(2,1)S(1)}, bf16[2,128,768]{2,1,0:T(8,128)(2,1)S(1)}, u32[]{:S(2)}, u32[]{:S(2)}) collective-permute-start(bf16[2,128,768]{2,1,0:T(8,128)(2,1)S(1)} %get-tuple-element.400), channel_id=1, source_target_pairs={{0,2},{1,3},{2,0},{3,1},{4,6},{5,7},{6,4},{7,5},{8,10},{9,11},{10,... | collective-permute-start | bytes 1179656 | tf_op jit(solution)/shard_map/ppermute | solution.py:258
  106.9 17.3 %collective-permute-start.26 = (bf16[2,128,768]{2,1,0:T(8,128)(2,1)S(1)}, bf16[2,128,768]{2,1,0:T(8,128)(2,1)S(1)}, u32[]{:S(2)}, u32[]{:S(2)}) collective-permute-start(bf16[2,128,768]{2,1,0:T(8,128)(2,1)S(1)} %get-tuple-element.399), channel_id=1, source_target_pairs={{0,3},{1,2},{2,1},{3,0},{4,7},{5,6},{6,5},{7,4},{8,11},{9,10},{10,... | collective-permute-start | bytes 1179656 | tf_op jit(solution)/shard_map/ppermute | solution.py:258
  158.6 22.5 %collective-permute-start.35 = (bf16[4,96,768]{2,1,0:T(8,128)(2,1)S(1)}, bf16[4,96,768]{2,1,0:T(8,128)(2,1)}, u32[]{:S(2)}, u32[]{:S(2)}) collective-permute-start(bf16[4,96,768]{2,1,0:T(8,128)(2,1)S(1)} %constant_dynamic-update-slice_fusion.20.refs_0_), channel_id=1, source_target_pairs={{0,1},{1,0},{2,3},{3,2},{4,5},{5,4},{6,7},{7,6},{8,9},{9,8},{10,11... | collective-permute-start | bytes 1769480 | tf_op jit(solution)/shard_map/ppermute | solution.py:258
  158.6 22.5 %collective-permute-start.36 = (bf16[4,96,768]{2,1,0:T(8,128)(2,1)S(1)}, bf16[4,96,768]{2,1,0:T(8,128)(2,1)}, u32[]{:S(2)}, u32[]{:S(2)}) collective-permute-start(bf16[4,96,768]{2,1,0:T(8,128)(2,1)S(1)} %collective-permute-done.33.refs_2_), channel_id=1, source_target_pairs={{0,1},{1,0},{2,3},{3,2},{4,5},{5,4},{6,7},{7,6},{8,9},{9,8},{10,11... | collective-permute-start | bytes 1769480 | tf_op jit(solution)/shard_map/ppermute | solution.py:258
  159.1 22.0 %collective-permute-start.37 = (bf16[4,96,768]{2,1,0:T(8,128)(2,1)S(1)}, bf16[4,96,768]{2,1,0:T(8,128)(2,1)}, u32[]{:S(2)}, u32[]{:S(2)}) collective-permute-start(bf16[4,96,768]{2,1,0:T(8,128)(2,1)S(1)} %constant_dynamic-update-slice_fusion.22.refs_4_), channel_id=1, source_target_pairs={{0,1},{1,0},{2,3},{3,2},{4,5},{5,4},{6,7},{7,6},{8,9},{9,8},{10,11... | collective-permute-start | bytes 1769480 | tf_op jit(solution)/shard_map/ppermute | solution.py:258
  159.1 22.0 %collective-permute-start.38 = (bf16[4,96,768]{2,1,0:T(8,128)(2,1)}, bf16[4,96,768]{2,1,0:T(8,128)(2,1)}, u32[]{:S(2)}, u32[]{:S(2)}) collective-permute-start(bf16[4,96,768]{2,1,0:T(8,128)(2,1)} %collective-permute-done.34.refs_6_), channel_id=1, source_target_pairs={{0,1},{1,0},{2,3},{3,2},{4,5},{5,4},{6,7},{7,6},{8,9},{9,8},{10,11... | collective-permute-start | bytes 1769480 | tf_op jit(solution)/shard_map/ppermute | solution.py:258
  231.3 16.1 %collective-permute-start.43 = (bf16[2,2,96,768]{3,2,0,1:T(8,128)(2,1)}, bf16[2,2,96,768]{3,2,0,1:T(8,128)(2,1)}, u32[]{:S(2)}, u32[]{:S(2)}) collective-permute-start(bf16[2,2,96,768]{3,2,0,1:T(8,128)(2,1)} %bitcast.277), channel_id=1, source_target_pairs={{0,4},{1,5},{2,6},{3,7},{4,0},{5,1},{6,2},{7,3},{8,12},{9,13},{10,... | collective-permute-start | bytes 1769480 | tf_op jit(solution)/shard_map/ppermute | solution.py:258
  251.8 23.5 %collective-permute-start.45 = (bf16[2,96,768]{2,1,0:T(8,128)(2,1)}, bf16[2,96,768]{2,1,0:T(8,128)(2,1)S(1)}, u32[]{:S(2)}, u32[]{:S(2)}) collective-permute-start(bf16[2,96,768]{2,1,0:T(8,128)(2,1)} %dynamic-slice_bitcast_fusion.17), channel_id=1, source_target_pairs={{0,2},{1,3},{2,0},{3,1},{4,6},{5,7},{6,4},{7,5},{8,10},{9,11},{10,... | collective-permute-start | bytes 884744 | tf_op jit(solution)/shard_map/ppermute | solution.py:258
  253.0 23.2 %collective-permute-start.46 = (bf16[2,96,768]{2,1,0:T(8,128)(2,1)}, bf16[2,96,768]{2,1,0:T(8,128)(2,1)}, u32[]{:S(2)}, u32[]{:S(2)}) collective-permute-start(bf16[2,96,768]{2,1,0:T(8,128)(2,1)} %dynamic-slice_bitcast_fusion.16), channel_id=1, source_target_pairs={{0,4},{1,5},{2,6},{3,7},{4,0},{5,1},{6,2},{7,3},{8,12},{9,13},{10,... | collective-permute-start | bytes 884744 | tf_op jit(solution)/shard_map/ppermute | solution.py:258
  279.6 31.6 %collective-permute-start.49 = (bf16[2,2,24,3968]{3,2,0,1:T(8,128)(2,1)S(1)}, bf16[2,2,24,3968]{3,2,0,1:T(8,128)(2,1)S(1)}, u32[]{:S(2)}, u32[]{:S(2)}) collective-permute-start(bf16[2,2,24,3968]{3,2,0,1:T(8,128)(2,1)S(1)} %bitcast.318), channel_id=1, source_target_pairs={{0,4},{1,5},{2,6},{3,7},{4,0},{5,1},{6,2},{7,3},{8,12},{9,13},{10,... | collective-permute-start | bytes 2285576 | tf_op jit(solution)/shard_map/ppermute | solution.py:258
  280.5 30.9 %collective-permute-start.50 = (bf16[2,2,24,3968]{3,2,0,1:T(8,128)(2,1)S(1)}, bf16[2,2,24,3968]{3,2,0,1:T(8,128)(2,1)S(1)}, u32[]{:S(2)}, u32[]{:S(2)}) collective-permute-start(bf16[2,2,24,3968]{3,2,0,1:T(8,128)(2,1)S(1)} %bitcast.317), channel_id=1, source_target_pairs={{0,2},{1,3},{2,0},{3,1},{4,6},{5,7},{6,4},{7,5},{8,10},{9,11},{10,... | collective-permute-start | bytes 2285576 | tf_op jit(solution)/shard_map/ppermute | solution.py:258
  282.2 29.5 %collective-permute-start.51 = (bf16[96,768]{1,0:T(8,128)(2,1)}, bf16[96,768]{1,0:T(8,128)(2,1)S(1)}, u32[]{:S(2)}, u32[]{:S(2)}) collective-permute-start(bf16[96,768]{1,0:T(8,128)(2,1)} %get-tuple-element.300), channel_id=1, source_target_pairs={{0,8},{1,9},{2,10},{3,11},{4,12},{5,13},{6,14},{7,15},{8,0},{9,1},... | collective-permute-start | bytes 442376 | tf_op jit(solution)/shard_map/ppermute | solution.py:258
  282.8 28.9 %collective-permute-start.52 = (bf16[96,768]{1,0:T(8,128)(2,1)}, bf16[96,768]{1,0:T(8,128)(2,1)}, u32[]{:S(2)}, u32[]{:S(2)}) collective-permute-start(bf16[96,768]{1,0:T(8,128)(2,1)} %get-tuple-element.301), channel_id=1, source_target_pairs={{0,16},{1,17},{2,18},{3,19},{4,20},{5,21},{6,22},{7,23},{8,24},{9,... | collective-permute-start | bytes 442376 | tf_op jit(solution)/shard_map/ppermute | solution.py:258
  285.2 26.5 %collective-permute-start.53 = (bf16[96,768]{1,0:T(8,128)(2,1)}, bf16[96,768]{1,0:T(8,128)(2,1)}, u32[]{:S(2)}, u32[]{:S(2)}) collective-permute-start(bf16[96,768]{1,0:T(8,128)(2,1)} %get-tuple-element.302), channel_id=1, source_target_pairs={{0,24},{1,25},{2,26},{3,27},{4,28},{5,29},{6,30},{7,31},{8,16},{9,... | collective-permute-start | bytes 442376 | tf_op jit(solution)/shard_map/ppermute | solution.py:258
  312.5 18.8 %collective-permute-start.54 = (bf16[2,24,3968]{2,1,0:T(8,128)(2,1)}, bf16[2,24,3968]{2,1,0:T(8,128)(2,1)}, u32[]{:S(2)}, u32[]{:S(2)}) collective-permute-start(bf16[2,24,3968]{2,1,0:T(8,128)(2,1)} %dynamic-slice_bitcast_fusion.15), channel_id=1, source_target_pairs={{0,2},{1,3},{2,0},{3,1},{4,6},{5,7},{6,4},{7,5},{8,10},{9,11},{10,... | collective-permute-start | bytes 1142792 | tf_op jit(solution)/shard_map/ppermute | solution.py:258
  313.7 18.8 %collective-permute-start.55 = (bf16[2,24,3968]{2,1,0:T(8,128)(2,1)}, bf16[2,24,3968]{2,1,0:T(8,128)(2,1)}, u32[]{:S(2)}, u32[]{:S(2)}) collective-permute-start(bf16[2,24,3968]{2,1,0:T(8,128)(2,1)} %dynamic-slice_bitcast_fusion.14), channel_id=1, source_target_pairs={{0,4},{1,5},{2,6},{3,7},{4,0},{5,1},{6,2},{7,3},{8,12},{9,13},{10,... | collective-permute-start | bytes 1142792 | tf_op jit(solution)/shard_map/ppermute | solution.py:258
  339.1 22.3 %collective-permute-start.63 = (bf16[24,3968]{1,0:T(8,128)(2,1)S(1)}, bf16[24,3968]{1,0:T(8,128)(2,1)S(1)}, u32[]{:S(2)}, u32[]{:S(2)}) collective-permute-start(bf16[24,3968]{1,0:T(8,128)(2,1)S(1)} %get-tuple-element.324), channel_id=1, source_target_pairs={{0,8},{1,9},{2,10},{3,11},{4,12},{5,13},{6,14},{7,15},{8,0},{9,1},... | collective-permute-start | bytes 571400 | tf_op jit(solution)/shard_map/ppermute | solution.py:258
  (99 other events, 886.5 us)

commit v12 on v10

--- a/solution.py
+++ b/solution.py
@@ -388,8 +388,10 @@
             self.join([(0, 1)])
             self.grow((2,) if self.plan == "xy" else (4,))
 
-    def core(self):
-        self.grow((1,) * len(self.held))
+    def core(self, which=None):
+        for i in which or range(len(self.held)):
+            self.held.append(self.swapped(self.held[i], 1))
+            self.ids.append([j ^ 1 for j in self.ids[i]])
 
     def finish(self, spans=None):
         return place(self.held, [i for ids in self.ids for i in ids], self.me, spans)
@@ -596,6 +598,7 @@
     )
     (wide_in, wide_out, late) = fence([down_gather], wide_in, wide_out, late)
     down_gather.second()
+    down_gather.core((0, 2))
     wide_in = wide_in.reshape(width, inner_width)
     wide_out = wide_out.reshape(width, width)
     (
@@ -616,7 +619,7 @@
     )
     first_low = first.astype(BF)
     (first_low,) = fence([down_gather], first_low)
-    down_gather.core()
+    down_gather.core((1, 3))
     cot = ToSequences(after(cotangent, first_low), seat, members, devices)
     for k in range(1, members):
         cot.send(k)
@@ -692,14 +695,14 @@
     grad_inputs = ToPositions(
         grad_inputs.reshape(kept, members, local_len, width), members, devices
     )
+    for k in near:
+        grad_inputs.send(k)
+    for k in far[:1]:
+        grad_inputs.send(k)
     qkv_scatter.first()
     in_scatter.along_z()
     fence([qkv_scatter, grad_inputs])
     qkv_scatter.second()
-    for k in near:
-        grad_inputs.send(k)
-    for k in far[:1]:
-        grad_inputs.send(k)
     fence([qkv_scatter, grad_inputs, in_scatter])
     for k in far[1:]:
         grad_inputs.send(k)

time: 378 us -> 372 us (0.984)
  waiting for transfers between devices: 82.7 us -> 76.6 us
    ppermute x70, waiting for transfers between devices: 82.7 us -> 76.6 us  [swap(): lax.ppermute(block, BOTH, [(i, i ^ distance) for i in range(devices)])]
    unnamed x114 -> x118, local copies, waits for them, and re-layouts: 13.1 us -> 16.7 us
  transfers between devices with their start and end apart: 70 -> 70, of which waited for: 24 -> 21; matrix products, arithmetic and copies ran while one was open for 29% -> 29% of each run, Pallas kernels for 18% -> 18%
where the time goes in v12:
time: 372 us; the launch traced here: 368 us
  Pallas kernels  84.1 us (23%)
  waiting for transfers between devices  76.6 us (21%)
  starting transfers between devices  66.6 us (18%)
  matrix products  63.2 us (17%)
  local copies, waits for them, and re-layouts  49.2 us (13%)
  other arithmetic  26 us (7%)
    ppermute x70, waiting for transfers between devices, swap(): lax.ppermute(block, BOTH, [(i, i ^ distance) for i in range(devices)])  76.6 us
    ppermute x70, starting transfers between devices, swap(): lax.ppermute(block, BOTH, [(i, i ^ distance) for i in range(devices)])  66.6 us
    dot_general x4, matrix products, times_transposed(): lax.dot_general(left, right, (((1,), (1,)), ((), ())), preferred_element_...  27 us
    pallas_call x1, Pallas kernels, attention_backward(): pl.pallas_call(backward_kernel, grid=(seqs, pairs), in_specs=[block(384),...  24.7 us
    dot_general x4, matrix products, over_rows(): lax.dot_general(left, right, (((0,), (0,)), ((), ())), preferred_element_...  23.9 us
    pallas_call x1, Pallas kernels, attention_forward(): pl.pallas_call(forward_kernel, grid=(seqs, pairs), in_specs=[block(384),...  17.1 us
    unnamed x118, local copies, waits for them, and re-layouts  16.7 us
    pallas_call x5, Pallas kernels, place(): pl.pallas_call(functools.partial(place_kernel, ids, counts, spans), in_sp...  15.6 us
  transfers between devices with their start and end apart: 70, of which 21 were waited for; matrix products, arithmetic and copies ran while one was open for 29% of the time, Pallas kernels for 18%

profile of v12, /device:TPU:0, one launch (start us, length us, event | category | flops | bytes accessed | tf_op | source)
XLA Modules:
  0.0 368.0 jit_solution(12019467470942915859)
XLA Ops:
  12.7 5.0 %collective-permute-done.1 = bf16[1,24,2432]{2,1,0:T(8,128)(2,1)S(1)} collective-permute-done((bf16[1,24,2432]{2,1,0:T(8,128)(2,1)S(1)}, bf16[1,24,2432]{2,1,0:T(8,128)(2,1)S(1)}, u32[]{:S(2)}, u32[]{:S(2)}) %collective-permute-start.1) | collective-permute-done | bytes 116768 | tf_op jit(solution)/shard_map/ppermute | solution.py:258
  26.0 9.6 %collective-permute-done.4 = bf16[2,24,2432]{2,1,0:T(8,128)(2,1)S(1)} collective-permute-done((bf16[2,24,2432]{2,1,0:T(8,128)(2,1)S(1)}, bf16[2,24,2432]{2,1,0:T(8,128)(2,1)S(1)}, u32[]{:S(2)}, u32[]{:S(2)}) %collective-permute-start.4) | collective-permute-done | bytes 233504 | tf_op jit(solution)/shard_map/ppermute | solution.py:258
  43.4 12.4 %collective-permute-done.11 = bf16[1,24,3968]{2,1,0:T(8,128)(2,1)S(1)} collective-permute-done((bf16[1,24,3968]{2,1,0:T(8,128)(2,1)S(1)}, bf16[1,24,3968]{2,1,0:T(8,128)(2,1)S(1)}, u32[]{:S(2)}, u32[]{:S(2)}) %collective-permute-start.11) | collective-permute-done | bytes 190496 | tf_op jit(solution)/shard_map/ppermute | solution.py:258
  66.7 4.0 %collective-permute-done.14 = bf16[2,24,3968]{2,1,0:T(8,128)(2,1)} collective-permute-done((bf16[2,24,3968]{2,1,0:T(8,128)(2,1)}, bf16[2,24,3968]{2,1,0:T(8,128)(2,1)}, u32[]{:S(2)}, u32[]{:S(2)}) %collective-permute-start.14) | collective-permute-done | bytes 380960 | tf_op jit(solution)/shard_map/ppermute | solution.py:258
  77.4 8.5 %add_convert_fusion.packed_ref = bf16[1024,2304]{1,0:T(8,128)(2,1)} fusion(bf16[1024,768]{1,0:T(8,128)(2,1)} %bitcast.303, bf16[768,2304]{1,0:T(8,128)(2,1)} %bitcast.283, f32[2304]{0:T(1024)S(1)} %add.424), kind=kOutput, calls=%fused_computation.2 | convolution fusion | flops 3628597248 | bytes 9839616 | tf_op jit(solution)/shard_map/dot_general | solution.py:581
  85.9 3.5 collective-permute-start.21
  92.2 17.1 %attention_forward.1 = (bf16[1024,768]{1,0:T(8,128)(2,1)S(1)}, f32[12,2,512]{2,1,0:T(2,128)S(1)}) custom-call(bf16[1024,2304]{1,0:T(8,128)(2,1)} %add_convert_fusion.packed_ref, bf16[2,512,128]{2,1,0:T(8,128)(2,1)S(1)} %broadcast_in_dim.46.mask_ref), custom_call_target="tpu_custom_call" | custom-call | flops 6442450944 | bytes 6291456 | tf_op jit(solution)/shard_map/attention_forward/pallas_call | solution.py:117
  116.2 4.2 %place_blocks.6 = (bf16[32,24,3072]{2,1,0:T(8,128)(2,1)S(1)}, bf16[32,24,768]{2,1,0:T(8,128)(2,1)S(1)}, bf16[32,24,128]{2,1,0:T(8,128)(2,1)S(1)}) custom-call(s32[1]{0:T(128)} %bitcast.17.me_ref, bf16[4,24,3968]{2,1,0:T(8,128)(2,1)S(1)} %constant_dynamic-update-slice_fusion.12.refs_0_, bf16[4,24,3968]{2,1,0:T(8,128)(2,1)S(1)} %collective-permute-done.19.refs_1_, ...), custom_call_target="tpu_custom_call" | custom-call | bytes 12189696 | tf_op jit(solution)/shard_map/place_blocks/pallas_call | solution.py:291
  129.9 3.8 %fusion.39 = (f32[1024]{0:T(1024)S(1)}, f32[1024,768]{1,0:T(8,128)S(1)}) fusion(f32[768]{0:T(1024)S(1)} %reshape.402, bf16[1024,768]{1,0:T(8,128)(2,1)} %copy-done.10, bf16[768,768]{1,0:T(8,128)(2,1)} %bitcast.285, bf16[1024,768]{1,0:T(8,128)(2,1)} %bitcast.304), kind=kOutput, calls=%fused_computation.217 | convolution fusion | flops 1211104256 | bytes 7478272 | tf_op jit(solution)/shard_map/dot_general | solution.py:616
  138.8 5.0 %collective-permute-done.31.refs_3_ = bf16[4,96,768]{2,1,0:T(8,128)(2,1)} collective-permute-done((bf16[4,96,768]{2,1,0:T(8,128)(2,1)S(1)}, bf16[4,96,768]{2,1,0:T(8,128)(2,1)}, u32[]{:S(2)}, u32[]{:S(2)}) %collective-permute-start.31) | collective-permute-done | bytes 589856 | tf_op jit(solution)/shard_map/ppermute | solution.py:258
  147.8 14.7 %feed_forward.1 = (bf16[1024,3072]{1,0:T(8,128)(2,1)}, bf16[1024,3072]{1,0:T(8,128)(2,1)}) custom-call(bf16[1024,768]{1,0:T(8,128)(2,1)S(1)} %add_convert_fusion.2.x_ref.first_ref, bf16[768,3072]{1,0:T(8,128)(2,1)} %bitcast.281, f32[1,3072]{1,0:T(1,128)S(1)} %reshape.405.b_ref), custom_call_target="tpu_custom_call" | custom-call | flops 4831838208 | bytes 17301504 | tf_op jit(solution)/shard_map/feed_forward/pallas_call | solution.py:183
  166.8 4.1 %place_blocks.7 = bf16[32,96,768]{2,1,0:T(8,128)(2,1)S(1)} custom-call(s32[1]{0:T(128)} %bitcast.17.me_ref, bf16[4,96,768]{2,1,0:T(8,128)(2,1)S(1)} %constant_dynamic-update-slice_fusion.20.refs_0_, bf16[4,96,768]{2,1,0:T(8,128)(2,1)S(1)} %collective-permute-done.30.refs_1_, bf16[4,96,768]{2,1,0:T(8,128)(2,1)S(1)} %constant_dynamic-update-slice_fusion.22.refs_2_, ...), custom_call_target="tpu_custom_call" | custom-call | bytes 9437184 | tf_op jit(solution)/shard_map/place_blocks/pallas_call | solution.py:291
  173.0 12.1 %second_norm.1 = (bf16[1024,768]{1,0:T(8,128)(2,1)S(1)}, f32[1024,768]{1,0:T(8,128)}, bf16[1024,768]{1,0:T(8,128)(2,1)S(1)}, f32[8,768]{1,0:T(8,128)S(1)}) custom-call(bf16[1024,3072]{1,0:T(8,128)(2,1)} %get-tuple-element.269.active_ref, bf16[3072,768]{1,0:T(8,128)(2,1)} %bitcast.278, bf16[1024,768]{1,0:T(8,128)(2,1)S(1)} %add_convert_fusion.2.x_ref.first_ref, ...), custom_call_target="tpu_custom_call" | custom-call | flops 4831838208 | bytes 20447232 | tf_op jit(solution)/shard_map/second_norm/pallas_call | solution.py:236
  186.1 8.5 %convolution_convert_fusion.1 = bf16[3072,768]{1,0:T(8,128)(2,1)S(1)} fusion(bf16[1024,3072]{1,0:T(8,128)(2,1)} %get-tuple-element.269.active_ref, bf16[1024,768]{1,0:T(8,128)(2,1)S(1)} %get-tuple-element.289), kind=kOutput, calls=%fused_computation.6 | convolution fusion | flops 4834197504 | bytes 12582912 | tf_op jit(solution)/shard_map/dot_general | solution.py:23
  202.3 9.0 %convert_reduce_fusion = (bf16[3072]{0:T(1024)(128)(2,1)}, bf16[1024,3072]{1,0:T(8,128)(2,1)S(1)}) fusion(bf16[1024,3072]{1,0:T(8,128)(2,1)} %get-tuple-element.290, bf16[1024,768]{1,0:T(8,128)(2,1)} %copy-done.12, bf16[3072,768]{1,0:T(8,128)(2,1)} %bitcast.279), kind=kOutput, calls=%fused_computation | convolution fusion | flops 4847563776 | bytes 18880512 | tf_op jit(solution)/shard_map/dot_general | solution.py:29
  211.3 4.1 %fusion.2 = bf16[16,96,768]{2,1,0:T(8,128)(2,1)S(1)} fusion(bf16[16,96,768]{2,1,0:T(8,128)(2,1)} %collective-permute-done.42, bf16[16,2,96,768]{3,2,1,0:T(8,128)(2,1)S(1)} %bitcast.297, s32[]{:T(128)S(6)} %select_n.257), kind=kLoop, calls=%fused_computation.12 | loop fusion | flops 4718592 | bytes 7077892 | tf_op jit(solution)/shard_map/convert_element_type | solution.py:407
  221.1 7.3 %convolution_convert_fusion = bf16[768,3072]{1,0:T(8,128)(2,1)} fusion(bf16[1024,768]{1,0:T(8,128)(2,1)S(1)} %add_convert_fusion.2.x_ref.first_ref, bf16[1024,3072]{1,0:T(8,128)(2,1)S(1)} %get-tuple-element.296), kind=kOutput, calls=%fused_computation.5 | convolution fusion | flops 4834197504 | bytes 12582912 | tf_op jit(solution)/shard_map/dot_general | solution.py:23
  228.5 4.5 %collective-permute-done.43 = bf16[2,2,96,768]{3,2,0,1:T(8,128)(2,1)} collective-permute-done((bf16[2,2,96,768]{3,2,0,1:T(8,128)(2,1)}, bf16[2,2,96,768]{3,2,0,1:T(8,128)(2,1)}, u32[]{:S(2)}, u32[]{:S(2)}) %collective-permute-start.43) | collective-permute-done | bytes 589856 | tf_op jit(solution)/shard_map/ppermute | solution.py:258
  239.8 10.4 %multiply_reduce_fusion = (bf16[768]{0:T(1024)(128)(2,1)}, f32[1024]{0:T(1024)S(1)}, bf16[768]{0:T(1024)(128)(2,1)}, f32[1024,768]{1,0:T(8,128)S(1)}) fusion(f32[1024,768]{1,0:T(8,128)S(1)} %copy-done.16, f32[1024]{0:T(1024)S(1)} %fusion.29, f32[1024]{0:T(1024)S(1)} %broadcast_multiply_fusion, f32[768]{0:T(1024)S(1)} %reshape.403, ...), kind=kOutput, calls=%fused_computation.17 | convolution fusion | flops 4838913024 | bytes 20465664 | tf_op jit(solution)/shard_map/dot_general | solution.py:29
  272.8 24.7 %attention_backward.1 = (bf16[1024,2304]{1,0:T(8,128)(2,1)}, f32[12,1,384]{2,1,0:T(1,128)S(1)}) custom-call(bf16[1024,2304]{1,0:T(8,128)(2,1)} %add_convert_fusion.packed_ref, bf16[2,512,128]{2,1,0:T(8,128)(2,1)S(1)} %copy-done.4, f32[12,2,512]{2,1,0:T(2,128)S(1)} %copy-done.14, bf16[1024,768]{1,0:T(8,128)(2,1)S(1)} %convolution_convert_fusion.3.grad_ref), custom_call_target="tpu_custom_call" | custom-call | flops 11274289152 | bytes 11010048 | tf_op jit(solution)/shard_map/attention_backward/pallas_call | solution.py:138
  301.0 6.7 %convolution_convert_fusion.2 = bf16[768,2304]{1,0:T(8,128)(2,1)S(1)} fusion(bf16[1024,768]{1,0:T(8,128)(2,1)} %bitcast.305, bf16[1024,2304]{1,0:T(8,128)(2,1)} %get-tuple-element.315), kind=kOutput, calls=%fused_computation.7 | convolution fusion | flops 3625648128 | bytes 9830400 | tf_op jit(solution)/shard_map/dot_general | solution.py:23
  310.7 6.2 %add_convert_fusion.1 = bf16[1024,768]{1,0:T(8,128)(2,1)S(1)} fusion(f32[1024,768]{1,0:T(8,128)S(1)} %copy-done.20, bf16[1024,2304]{1,0:T(8,128)(2,1)} %get-tuple-element.315, bf16[768,2304]{1,0:T(8,128)(2,1)S(1)} %bitcast.284), kind=kOutput, calls=%fused_computation.16 | convolution fusion | flops 3625451520 | bytes 12976128 | tf_op jit(solution)/shard_map/dot_general | solution.py:29
  325.3 7.8 %collective-permute-done.58 = bf16[2,2,24,2432]{3,2,1,0:T(8,128)(2,1)S(1)} collective-permute-done((bf16[2,2,24,2432]{3,2,1,0:T(8,128)(2,1)S(1)}, bf16[2,2,24,2432]{3,2,1,0:T(8,128)(2,1)S(1)}, u32[]{:S(2)}, u32[]{:S(2)}) %collective-permute-start.58) | collective-permute-done | bytes 466976 | tf_op jit(solution)/shard_map/ppermute | solution.py:258
  357.9 4.1 %collective-permute-done.69.refs_3_ = bf16[1,2,128,768]{3,2,1,0:T(8,128)(2,1)S(1)} collective-permute-done((bf16[1,2,128,768]{3,2,1,0:T(8,128)(2,1)S(1)}, bf16[1,2,128,768]{3,2,1,0:T(8,128)(2,1)S(1)}, u32[]{:S(2)}, u32[]{:S(2)}) %collective-permute-start.69) | collective-permute-done | bytes 393248 | tf_op jit(solution)/shard_map/ppermute | solution.py:258
  (392 shorter events, 168.4 us)
Async XLA Ops:
  10.6 25.0 %collective-permute-start.5 = (bf16[2,128,768]{2,1,0:T(8,128)(2,1)S(1)}, bf16[2,128,768]{2,1,0:T(8,128)(2,1)S(1)}, u32[]{:S(2)}, u32[]{:S(2)}) collective-permute-start(bf16[2,128,768]{2,1,0:T(8,128)(2,1)S(1)} %get-tuple-element.407), channel_id=1, source_target_pairs={{0,1},{1,0},{2,3},{3,2},{4,5},{5,4},{6,7},{7,6},{8,9},{9,8},{10,11... | collective-permute-start | bytes 1179656 | tf_op jit(solution)/shard_map/ppermute | solution.py:258
  10.6 25.0 %collective-permute-start.6 = (bf16[2,128,768]{2,1,0:T(8,128)(2,1)S(1)}, bf16[2,128,768]{2,1,0:T(8,128)(2,1)S(1)}, u32[]{:S(2)}, u32[]{:S(2)}) collective-permute-start(bf16[2,128,768]{2,1,0:T(8,128)(2,1)S(1)} %get-tuple-element.406), channel_id=1, source_target_pairs={{0,2},{1,3},{2,0},{3,1},{4,6},{5,7},{6,4},{7,5},{8,10},{9,11},{10,... | collective-permute-start | bytes 1179656 | tf_op jit(solution)/shard_map/ppermute | solution.py:258
  12.5 23.1 %collective-permute-start.7 = (bf16[2,128,768]{2,1,0:T(8,128)(2,1)S(1)}, bf16[2,128,768]{2,1,0:T(8,128)(2,1)S(1)}, u32[]{:S(2)}, u32[]{:S(2)}) collective-permute-start(bf16[2,128,768]{2,1,0:T(8,128)(2,1)S(1)} %get-tuple-element.405), channel_id=1, source_target_pairs={{0,3},{1,2},{2,1},{3,0},{4,7},{5,6},{6,5},{7,4},{8,11},{9,10},{10,... | collective-permute-start | bytes 1179656 | tf_op jit(solution)/shard_map/ppermute | solution.py:258
  36.4 19.4 %collective-permute-start.9 = (bf16[4,24,2432]{2,1,0:T(8,128)(2,1)S(1)}, bf16[4,24,2432]{2,1,0:T(8,128)(2,1)S(1)}, u32[]{:S(2)}, u32[]{:S(2)}) collective-permute-start(bf16[4,24,2432]{2,1,0:T(8,128)(2,1)S(1)} %constant_dynamic-update-slice_fusion.4.refs_0_), channel_id=1, source_target_pairs={{0,2},{1,3},{2,0},{3,1},{4,6},{5,7},{6,4},{7,5},{8,10},{9,11},{10,... | collective-permute-start | bytes 1400840 | tf_op jit(solution)/shard_map/ppermute | solution.py:258
  38.2 17.6 %collective-permute-start.10 = (bf16[4,24,2432]{2,1,0:T(8,128)(2,1)S(1)}, bf16[4,24,2432]{2,1,0:T(8,128)(2,1)S(1)}, u32[]{:S(2)}, u32[]{:S(2)}) collective-permute-start(bf16[4,24,2432]{2,1,0:T(8,128)(2,1)S(1)} %constant_dynamic-update-slice_fusion.6.refs_2_), channel_id=1, source_target_pairs={{0,4},{1,5},{2,6},{3,7},{4,0},{5,1},{6,2},{7,3},{8,12},{9,13},{10,... | collective-permute-start | bytes 1400840 | tf_op jit(solution)/shard_map/ppermute | solution.py:258
  72.8 36.5 %collective-permute-start.19 = (bf16[4,24,3968]{2,1,0:T(8,128)(2,1)S(1)}, bf16[4,24,3968]{2,1,0:T(8,128)(2,1)S(1)}, u32[]{:S(2)}, u32[]{:S(2)}) collective-permute-start(bf16[4,24,3968]{2,1,0:T(8,128)(2,1)S(1)} %constant_dynamic-update-slice_fusion.12.refs_0_), channel_id=1, source_target_pairs={{0,2},{1,3},{2,0},{3,1},{4,6},{5,7},{6,4},{7,5},{8,10},{9,11},{10,... | collective-permute-start | bytes 2285576 | tf_op jit(solution)/shard_map/ppermute | solution.py:258
  75.4 33.9 %collective-permute-start.20 = (bf16[4,24,3968]{2,1,0:T(8,128)(2,1)S(1)}, bf16[4,24,3968]{2,1,0:T(8,128)(2,1)S(1)}, u32[]{:S(2)}, u32[]{:S(2)}) collective-permute-start(bf16[4,24,3968]{2,1,0:T(8,128)(2,1)S(1)} %constant_dynamic-update-slice_fusion.14.refs_2_), channel_id=1, source_target_pairs={{0,4},{1,5},{2,6},{3,7},{4,0},{5,1},{6,2},{7,3},{8,12},{9,13},{10,... | collective-permute-start | bytes 2285576 | tf_op jit(solution)/shard_map/ppermute | solution.py:258
  85.9 23.4 %collective-permute-start.21 = (bf16[1,96,768]{2,1,0:T(8,128)(2,1)S(1)}, bf16[1,96,768]{2,1,0:T(8,128)(2,1)S(1)}, u32[]{:S(2)}, u32[]{:S(2)}) collective-permute-start(bf16[1,96,768]{2,1,0:T(8,128)(2,1)S(1)} %bitcast.326), channel_id=1, source_target_pairs={{0,8},{1,9},{2,10},{3,11},{4,12},{5,13},{6,14},{7,15},{8,0},{9,1},... | collective-permute-start | bytes 442376 | tf_op jit(solution)/shard_map/ppermute | solution.py:258
  89.4 19.9 %collective-permute-start.22 = (bf16[1,96,768]{2,1,0:T(8,128)(2,1)S(1)}, bf16[1,96,768]{2,1,0:T(8,128)(2,1)S(1)}, u32[]{:S(2)}, u32[]{:S(2)}) collective-permute-start(bf16[1,96,768]{2,1,0:T(8,128)(2,1)S(1)} %bitcast.327), channel_id=1, source_target_pairs={{0,16},{1,17},{2,18},{3,19},{4,20},{5,21},{6,22},{7,23},{8,24},{9,... | collective-permute-start | bytes 442376 | tf_op jit(solution)/shard_map/ppermute | solution.py:258
  90.5 18.8 %collective-permute-start.23 = (bf16[1,96,768]{2,1,0:T(8,128)(2,1)S(1)}, bf16[1,96,768]{2,1,0:T(8,128)(2,1)S(1)}, u32[]{:S(2)}, u32[]{:S(2)}) collective-permute-start(bf16[1,96,768]{2,1,0:T(8,128)(2,1)S(1)} %bitcast.328), channel_id=1, source_target_pairs={{0,24},{1,25},{2,26},{3,27},{4,28},{5,29},{6,30},{7,31},{8,16},{9,... | collective-permute-start | bytes 442376 | tf_op jit(solution)/shard_map/ppermute | solution.py:258
  125.9 17.9 %collective-permute-start.32 = (bf16[4,96,768]{2,1,0:T(8,128)(2,1)S(1)}, bf16[4,96,768]{2,1,0:T(8,128)(2,1)}, u32[]{:S(2)}, u32[]{:S(2)}) collective-permute-start(bf16[4,96,768]{2,1,0:T(8,128)(2,1)S(1)} %constant_dynamic-update-slice_fusion.20.refs_0_), channel_id=1, source_target_pairs={{0,1},{1,0},{2,3},{3,2},{4,5},{5,4},{6,7},{7,6},{8,9},{9,8},{10,11... | collective-permute-start | bytes 1769480 | tf_op jit(solution)/shard_map/ppermute | solution.py:258
  143.8 21.6 %collective-permute-start.34 = (bf16[4,96,768]{2,1,0:T(8,128)(2,1)S(1)}, bf16[4,96,768]{2,1,0:T(8,128)(2,1)S(1)}, u32[]{:S(2)}, u32[]{:S(2)}) collective-permute-start(bf16[4,96,768]{2,1,0:T(8,128)(2,1)S(1)} %collective-permute-done.30.refs_1_), channel_id=1, source_target_pairs={{0,1},{1,0},{2,3},{3,2},{4,5},{5,4},{6,7},{7,6},{8,9},{9,8},{10,11... | collective-permute-start | bytes 1769480 | tf_op jit(solution)/shard_map/ppermute | solution.py:258
  143.9 21.5 %collective-permute-start.35 = (bf16[4,96,768]{2,1,0:T(8,128)(2,1)}, bf16[4,96,768]{2,1,0:T(8,128)(2,1)S(1)}, u32[]{:S(2)}, u32[]{:S(2)}) collective-permute-start(bf16[4,96,768]{2,1,0:T(8,128)(2,1)} %collective-permute-done.31.refs_3_), channel_id=1, source_target_pairs={{0,1},{1,0},{2,3},{3,2},{4,5},{5,4},{6,7},{7,6},{8,9},{9,8},{10,11... | collective-permute-start | bytes 1769480 | tf_op jit(solution)/shard_map/ppermute | solution.py:258
  146.5 18.9 %collective-permute-start.38 = (bf16[2,128,768]{2,1,0:T(8,128)(2,1)S(1)}, bf16[2,128,768]{2,1,0:T(8,128)(2,1)S(1)}, u32[]{:S(2)}, u32[]{:S(2)}) collective-permute-start(bf16[2,128,768]{2,1,0:T(8,128)(2,1)S(1)} %get-tuple-element.401), channel_id=1, source_target_pairs={{0,3},{1,2},{2,1},{3,0},{4,7},{5,6},{6,5},{7,4},{8,11},{9,10},{10,... | collective-permute-start | bytes 1179656 | tf_op jit(solution)/shard_map/ppermute | solution.py:258
  238.0 22.9 %collective-permute-start.45 = (bf16[2,96,768]{2,1,0:T(8,128)(2,1)}, bf16[2,96,768]{2,1,0:T(8,128)(2,1)S(1)}, u32[]{:S(2)}, u32[]{:S(2)}) collective-permute-start(bf16[2,96,768]{2,1,0:T(8,128)(2,1)} %dynamic-slice_bitcast_fusion.17), channel_id=1, source_target_pairs={{0,2},{1,3},{2,0},{3,1},{4,6},{5,7},{6,4},{7,5},{8,10},{9,11},{10,... | collective-permute-start | bytes 884744 | tf_op jit(solution)/shard_map/ppermute | solution.py:258
  239.1 22.6 %collective-permute-start.46 = (bf16[2,96,768]{2,1,0:T(8,128)(2,1)}, bf16[2,96,768]{2,1,0:T(8,128)(2,1)}, u32[]{:S(2)}, u32[]{:S(2)}) collective-permute-start(bf16[2,96,768]{2,1,0:T(8,128)(2,1)} %dynamic-slice_bitcast_fusion.16), channel_id=1, source_target_pairs={{0,4},{1,5},{2,6},{3,7},{4,0},{5,1},{6,2},{7,3},{8,12},{9,13},{10,... | collective-permute-start | bytes 884744 | tf_op jit(solution)/shard_map/ppermute | solution.py:258
  265.3 32.3 %collective-permute-start.49 = (bf16[2,2,24,3968]{3,2,0,1:T(8,128)(2,1)S(1)}, bf16[2,2,24,3968]{3,2,0,1:T(8,128)(2,1)S(1)}, u32[]{:S(2)}, u32[]{:S(2)}) collective-permute-start(bf16[2,2,24,3968]{3,2,0,1:T(8,128)(2,1)S(1)} %bitcast.318), channel_id=1, source_target_pairs={{0,4},{1,5},{2,6},{3,7},{4,0},{5,1},{6,2},{7,3},{8,12},{9,13},{10,... | collective-permute-start | bytes 2285576 | tf_op jit(solution)/shard_map/ppermute | solution.py:258
  266.7 31.0 %collective-permute-start.50 = (bf16[2,2,24,3968]{3,2,0,1:T(8,128)(2,1)S(1)}, bf16[2,2,24,3968]{3,2,0,1:T(8,128)(2,1)S(1)}, u32[]{:S(2)}, u32[]{:S(2)}) collective-permute-start(bf16[2,2,24,3968]{3,2,0,1:T(8,128)(2,1)S(1)} %bitcast.317), channel_id=1, source_target_pairs={{0,2},{1,3},{2,0},{3,1},{4,6},{5,7},{6,4},{7,5},{8,10},{9,11},{10,... | collective-permute-start | bytes 2285576 | tf_op jit(solution)/shard_map/ppermute | solution.py:258
  268.4 29.4 %collective-permute-start.51 = (bf16[96,768]{1,0:T(8,128)(2,1)}, bf16[96,768]{1,0:T(8,128)(2,1)S(1)}, u32[]{:S(2)}, u32[]{:S(2)}) collective-permute-start(bf16[96,768]{1,0:T(8,128)(2,1)} %get-tuple-element.302), channel_id=1, source_target_pairs={{0,8},{1,9},{2,10},{3,11},{4,12},{5,13},{6,14},{7,15},{8,0},{9,1},... | collective-permute-start | bytes 442376 | tf_op jit(solution)/shard_map/ppermute | solution.py:258
  269.3 28.6 %collective-permute-start.52 = (bf16[96,768]{1,0:T(8,128)(2,1)}, bf16[96,768]{1,0:T(8,128)(2,1)}, u32[]{:S(2)}, u32[]{:S(2)}) collective-permute-start(bf16[96,768]{1,0:T(8,128)(2,1)} %get-tuple-element.303), channel_id=1, source_target_pairs={{0,16},{1,17},{2,18},{3,19},{4,20},{5,21},{6,22},{7,23},{8,24},{9,... | collective-permute-start | bytes 442376 | tf_op jit(solution)/shard_map/ppermute | solution.py:258
  271.3 26.6 %collective-permute-start.53 = (bf16[96,768]{1,0:T(8,128)(2,1)}, bf16[96,768]{1,0:T(8,128)(2,1)}, u32[]{:S(2)}, u32[]{:S(2)}) collective-permute-start(bf16[96,768]{1,0:T(8,128)(2,1)} %get-tuple-element.304), channel_id=1, source_target_pairs={{0,24},{1,25},{2,26},{3,27},{4,28},{5,29},{6,30},{7,31},{8,16},{9,... | collective-permute-start | bytes 442376 | tf_op jit(solution)/shard_map/ppermute | solution.py:258
  298.7 18.2 %collective-permute-start.54 = (bf16[2,24,3968]{2,1,0:T(8,128)(2,1)}, bf16[2,24,3968]{2,1,0:T(8,128)(2,1)}, u32[]{:S(2)}, u32[]{:S(2)}) collective-permute-start(bf16[2,24,3968]{2,1,0:T(8,128)(2,1)} %dynamic-slice_bitcast_fusion.15), channel_id=1, source_target_pairs={{0,2},{1,3},{2,0},{3,1},{4,6},{5,7},{6,4},{7,5},{8,10},{9,11},{10,... | collective-permute-start | bytes 1142792 | tf_op jit(solution)/shard_map/ppermute | solution.py:258
  299.9 18.2 %collective-permute-start.55 = (bf16[2,24,3968]{2,1,0:T(8,128)(2,1)}, bf16[2,24,3968]{2,1,0:T(8,128)(2,1)}, u32[]{:S(2)}, u32[]{:S(2)}) collective-permute-start(bf16[2,24,3968]{2,1,0:T(8,128)(2,1)} %dynamic-slice_bitcast_fusion.14), channel_id=1, source_target_pairs={{0,4},{1,5},{2,6},{3,7},{4,0},{5,1},{6,2},{7,3},{8,12},{9,13},{10,... | collective-permute-start | bytes 1142792 | tf_op jit(solution)/shard_map/ppermute | solution.py:258
  325.3 21.8 %collective-permute-start.63 = (bf16[24,3968]{1,0:T(8,128)(2,1)S(1)}, bf16[24,3968]{1,0:T(8,128)(2,1)S(1)}, u32[]{:S(2)}, u32[]{:S(2)}) collective-permute-start(bf16[24,3968]{1,0:T(8,128)(2,1)S(1)} %get-tuple-element.326), channel_id=1, source_target_pairs={{0,8},{1,9},{2,10},{3,11},{4,12},{5,13},{6,14},{7,15},{8,0},{9,1},... | collective-permute-start | bytes 571400 | tf_op jit(solution)/shard_map/ppermute | solution.py:258
  (95 other events, 861.2 us)
